TPU v7x, 256 devices: a whole 4x4x8 slice. The times are simulated.
256 devices in a mesh: dp: 16 (over y, z_hi), node: 16 (over z_lo, x, core).
Axes of the slice: x: 4, y: 4, z: 8 (z_hi: 4, z_lo: 2; z = z_hi * 2 + z_lo), core: 2. Of those that a mesh axis runs over, the one named last changes fastest.
Arguments:
- tokens: bfloat16 [81920, 8192], P(('dp', 'node')), may hold values from -60 to 60
- norm_gain: float32 [8192], replicated, may hold values from 0.1 to 1.9
- weight_values: bfloat16 [8192, 512], P('node'), may hold values from -127 to 127, as said below
- weight_scale: bfloat16 [8192, 4], P('node'), may hold values from 4.9829483e-05 to 0.00049972534
- key_cotangent: bfloat16 [81920, 512], P(('dp', 'node')), may hold values from -8 to 8
Outputs:
- projected: bfloat16 [81920, 512], P(('dp', 'node'))
- token_grads: bfloat16 [81920, 8192], P(('dp', 'node'))
- weight_grads: float32 [8192, 512], P('node')
- gain_grads: float32 [8192], replicated
Inputs may be any that keep to these rules, and one draw needn't show every extreme that they name: `weight_values`: entries are whole numbers.
All inputs are finite; a program needn't handle non-finite values.
Results may differ from a plain program's by a relative error of at most 0.0057.
Values may be sent and summed in bfloat16 or wider, within the bound.
No kernel may reach another device: no remote copies, remote signals or barrier semaphores. Data moves between devices by JAX's collectives and lax.ppermute only.
A program may use at most 128 MiB of HBM per device.

v0:
```python
import jax
import jax.numpy as jnp
from jax import lax
from jax.sharding import PartitionSpec as P


def widen_weight(values, scales):
    row_count = values.shape[0]
    block_count = scales.shape[1]
    block = values.shape[1] // block_count
    shaped = values.astype(jnp.float32).reshape(row_count, block_count, block)
    return (
        (shaped * scales.astype(jnp.float32)[:, :, None])
        .reshape(row_count, block_count * block)
        .astype(jnp.bfloat16)
    )


def shards(tokens, norm_gain, weight_values, weight_scale, key_cotangent):
    wide = tokens.astype(jnp.float32)
    inverse = lax.rsqrt(jnp.mean(wide * wide, axis=1, keepdims=True) + 1e-05)
    scaled = wide * inverse
    normed = (scaled * norm_gain).astype(jnp.bfloat16)
    width = tokens.shape[1]
    columns = weight_values.shape[1]
    pieces = (
        lax.all_gather(weight_values, "node", axis=0, tiled=True),
        lax.all_gather(weight_scale, "node", axis=0, tiled=True),
    )
    weight_piece = widen_weight(pieces[0], pieces[1])
    inputs = normed
    key_sums = jnp.dot(inputs, weight_piece, preferred_element_type=jnp.float32)
    pieces = (
        lax.all_gather(weight_values, "node", axis=0, tiled=True),
        lax.all_gather(weight_scale, "node", axis=0, tiled=True),
    )
    weight_piece = widen_weight(pieces[0], pieces[1])
    partial_grads = lax.dot_general(
        key_cotangent, weight_piece, (((1,), (1,)), ((), ())), preferred_element_type=jnp.float32
    )
    projected = key_sums.astype(jnp.bfloat16)
    gained = partial_grads * norm_gain
    moment = jnp.mean(wide * gained, axis=1, keepdims=True)
    token_grads = (inverse * gained - wide * inverse**3 * moment).astype(jnp.bfloat16)
    gain_terms = jnp.sum(partial_grads * scaled, axis=0)
    block_count = weight_scale.shape[1]
    block = columns // block_count
    group = lax.axis_size("node")
    shard = width // group

    def quantize_rows(owner):
        inputs = lax.dynamic_slice_in_dim(normed, owner * shard, shard, 1)
        local_grads = lax.dot_general(
            inputs, key_cotangent, (((0,), (0,)), ((), ())), preferred_element_type=jnp.float32
        )
        blocked = local_grads.reshape(shard, block_count, block)
        peaks = (jnp.max(jnp.abs(blocked), axis=2) + 1e-06).astype(jnp.bfloat16)
        peak_wide = lax.optimization_barrier(peaks).astype(jnp.float32)
        levels = (blocked / peak_wide[:, :, None]).astype(jnp.bfloat16)
        return (levels.reshape(shard, columns), peaks)

    levels, peaks = lax.map(quantize_rows, jnp.arange(group, dtype=jnp.int32))
    got_levels, got_peaks = (
        lax.all_to_all(levels, "node", split_axis=0, concat_axis=0, tiled=True),
        lax.all_to_all(peaks, "node", split_axis=0, concat_axis=0, tiled=True),
    )
    group_total = jnp.sum(
        got_levels.astype(jnp.float32).reshape(group, shard, block_count, block)
        * got_peaks.astype(jnp.float32)[:, :, :, None],
        axis=0,
    ).reshape(shard, columns)
    devices = lax.axis_size("dp") * group
    weight_grads = lax.psum(group_total, "dp") / devices
    gain_grads = lax.psum(gain_terms, ("dp", "node")) / devices
    return (projected, token_grads, weight_grads, gain_grads)


def solution(mesh):
    placed = (
        P(("dp", "node"), None),
        P(),
        P("node", None),
        P("node", None),
        P(("dp", "node"), None),
    )
    return jax.shard_map(
        shards,
        mesh=mesh,
        in_specs=placed,
        out_specs=(P(("dp", "node"), None), P(("dp", "node"), None), P("node", None), P()),
        check_vma=False,
    )
```

profile of v0, /device:TPU:1, one launch (start us, length us, event | category | flops | bytes accessed | tf_op | source)
XLA Modules:
  0.0 533.1 jit_solution(12061469767737460450)
XLA Ops:
  7.9 21.8 %all_gather.9 = bf16[8192,4]{0,1:T(4,128)(2,1)S(1)} all-gather(bf16[512,4]{0,1:T(4,128)(2,1)} %param.10), channel_id=1, replica_groups=mesh['dp'=16,'node'=16] {'node'}, dimensions={0}, use_global_device_ids=true | all-gather | bytes 69632 | tf_op jit(solution)/shard_map/all_gather | solution.py:28
  29.7 2.4 copy.10
  32.1 3.8 fusion.10
  36.0 32.9 %all-gather.2.cloned.1.call-done = bf16[8192,512]{1,0:T(8,128)(2,1)} async-done(((bf16[512,512]{1,0:T(8,128)(2,1)}), bf16[8192,512]{1,0:T(8,128)(2,1)}) %all-gather.2.cloned.1.call-update) | async-done | bytes 8388624 | tf_op jit(solution)/shard_map/all_gather | solution.py:27
  68.8 16.8 %mul.90 = f32[8192,4,128]{2,1,0:T(4,128)} broadcast(f32[8192,4]{1,0:T(8,128)} %copy.10), dimensions={0,1} | broadcast | bytes 16908288 | tf_op jit(solution)/shard_map/mul | solution.py:13
  85.6 13.6 %fusion.9 = (f32[8192]{0:T(1024)S(1)}, f32[320]{0:T(512)S(1)}, f32[320,8192]{1,0:T(8,128)}) fusion(bf16[320,8192]{1,0:T(8,128)(2,1)S(1)} %bitcast.42, f32[320]{0:T(512)S(1)} %get-tuple-element.64, f32[8192]{0:T(1024)S(1)} %copy-done.1, bf16[320,512]{1,0:T(8,128)(2,1)S(1)} %copy-done, f32[1024,8,4,128]{3,2,1,0:T(4,128)} %bitcast.39, ...), kind=kOutput, calls=%fused_computation.21 | convolution fusion | flops 2715279104 | bytes 41290240 | tf_op jit(solution)/shard_map/dot_general | solution.py:38
  99.3 10.9 %fusion.13 = (bf16[320,8192]{1,0:T(8,128)(2,1)}, bf16[320,8192]{1,0:T(8,128)(2,1)}) fusion(bf16[320,8192]{1,0:T(8,128)(2,1)S(1)} %bitcast.42, f32[320,8192]{1,0:T(8,128)} %get-tuple-element.65, f32[320]{0:T(512)S(1)} %broadcast_multiply_fusion.2, f32[320]{0:T(512)S(1)} %get-tuple-element.63, f32[8192]{0:T(1024)S(1)} %copy-done.1, f32[320]{0:T(512)S(1)} %get-tuple-element.64), kind=kLoop, calls=%fused_computation.25 | loop fusion | flops 26214400 | bytes 26251008 | tf_op jit(solution)/shard_map/convert_element_type | solution.py:44
  110.2 58.7 %while.12 = (s32[]{:T(128)}, bf16[16,512,512]{1,2,0:T(8,128)(2,1)}, bf16[16,512,4]{1,2,0:T(4,128)(2,1)S(1)}, s32[16]{0:T(128)S(1)}, bf16[320,8192]{1,0:T(8,128)(...) while((s32[]{:T(128)}, bf16[16,512,512]{1,2,0:T(8,128)(2,1)}, ...), condition=%wide.region_4.0_spmd, body=%wide.region_2.4_spmd.sunk | while | flops 168824832 | bytes 3322035 | solution.py:62
  111.4 1.5 bitcast_reduce_fusion.2
  115.1 1.5 bitcast_reduce_fusion.2
  118.8 1.5 bitcast_reduce_fusion.2
  126.1 1.5 bitcast_reduce_fusion.2
  129.7 1.5 bitcast_reduce_fusion.2
  133.4 1.5 bitcast_reduce_fusion.2
  148.1 1.5 bitcast_reduce_fusion.2
  151.7 1.5 bitcast_reduce_fusion.2
  159.1 1.5 bitcast_reduce_fusion.2
  162.7 1.5 bitcast_reduce_fusion.2
  168.8 10.8 %all_to_all.10 = bf16[16,512,4]{1,2,0:T(4,128)(2,1)S(1)} all-to-all(bf16[16,512,4]{1,2,0:T(4,128)(2,1)S(1)} %get-tuple-element.38), channel_id=1, replica_groups=mesh['dp'=16,'node'=16] {'node'}, dimensions={0} | all-to-all | bytes 131072 | tf_op jit(solution)/shard_map/all_to_all | solution.py:65
  179.6 4.9 all-to-all-start
  184.5 175.5 %psum.15 = f32[8192]{0:T(1024)S(1)} all-reduce(f32[8192]{0:T(1024)S(1)} %get-tuple-element.43), channel_id=1, replica_groups=mesh['dp'=16,'node'=16] {'dp','node'}, use_global_device_ids=true, to_apply=%region_8.9 | all-reduce | flops 8192 | bytes 65536 | tf_op jit(solution)/shard_map/psum | solution.py:74
  360.7 6.1 %fusion.5 = f32[512,512]{0,1:T(8,128)} fusion(bf16[16,512,512]{1,2,0:T(8,128)(2,1)} %all-to-all-done, f32[16,512,4]{1,2,0:T(4,128)S(1)} %convert_element_type.61), kind=kLoop, calls=%fused_computation.16 | loop fusion | flops 12320768 | bytes 9568256 | tf_op jit(solution)/shard_map/reduce_sum | solution.py:67
  366.8 13.5 %convolution_convert_fusion = bf16[320,512]{1,0:T(8,128)(2,1)} fusion(bf16[320,8192]{1,0:T(8,128)(2,1)} %get-tuple-element.144, f32[1024,8,4,128]{3,2,1,0:T(4,128)} %bitcast.40, bf16[8192,512]{1,0:T(8,128)(2,1)} %all-gather.2.cloned.1.call-done), kind=kOutput, calls=%fused_computation.27 | convolution fusion | flops 2697101312 | bytes 30736384 | tf_op jit(solution)/shard_map/dot_general | solution.py:32
  380.3 143.3 %all-reduce.2.cloned.1.call-done = f32[512,512]{0,1:T(8,128)} async-done(((f32[512,512]{0,1:T(8,128)}), f32[512,512]{0,1:T(8,128)}) %all-reduce.2.cloned.1.call-update) | async-done | bytes 1048592 | tf_op jit(solution)/shard_map/psum | solution.py:73
  (93 shorter events, 37.2 us)
Async XLA Ops:
  7.2 61.7 %all-gather.2.cloned.1.call-start = ((), (), s32[]{:S(2)}) async-start(), calls=%async_computation.2 | async-start | bytes 8912896 | tf_op jit(solution)/shard_map/all_gather | solution.py:27
  32.1 53.5 %slice-start = ((s8[5242880]{0:T(1024)(128)(4,1)}), s8[1048576]{0:T(1024)(128)(4,1)S(1)}, s32[]{:S(2)}) async-start(s8[5242880]{0:T(1024)(128)(4,1)} %bitcast.41), calls=%async_computation.4 | async-start | bytes 2097152
  68.8 16.8 %slice-start.1 = ((s8[5242880]{0:T(1024)(128)(4,1)}), s8[4194304]{0:T(1024)(128)(4,1)S(1)}, s32[]{:S(2)}) async-start(s8[5242880]{0:T(1024)(128)(4,1)} %bitcast.41), calls=%async_computation.5 | async-start | bytes 8388608
  68.8 16.8 %copy-start = (bf16[320,512]{1,0:T(8,128)(2,1)S(1)}, bf16[320,512]{1,0:T(8,128)(2,1)}, u32[]{:S(2)}) copy-start(bf16[320,512]{1,0:T(8,128)(2,1)} %param.11) | copy-start | bytes 983044
  68.8 16.8 %copy-start.1 = (f32[8192]{0:T(1024)S(1)}, f32[8192]{0:T(1024)}, u32[]{:S(2)}) copy-start(f32[8192]{0:T(1024)} %param.8) | copy-start | bytes 98308
  179.6 181.1 %all-to-all-start = ((bf16[16,512,512]{1,2,0:T(8,128)(2,1)}), bf16[16,512,512]{1,2,0:T(8,128)(2,1)}, u32[]{:S(2)}, u32[]{:S(2)}) async-start(bf16[16,512,512]{1,2,0:T(8,128)(2,1)} %get-tuple-element.37), calls=%async_computation | async-start | bytes 16777216 | tf_op jit(solution)/shard_map/all_to_all | solution.py:64
  184.5 339.1 %all-reduce.2.cloned.1.call-start = ((), (), s32[]{:S(2)}) async-start(), calls=%async_computation.3 | async-start | bytes 2097152 | tf_op jit(solution)/shard_map/psum | solution.py:73
Sparse Core Ops, SparseCore 0:
  9.8 58.9 all-gather.1
  366.9 156.6 all-reduce.1
where the time goes:
time: 543 us; the launch traced here: 533 us
  blocking collectives  208 us (38%)
  waiting for transfers between devices  177 us (33%)
  matrix products  50.8 us (9%)
  other arithmetic  37.7 us (7%)
  local copies, waits for them, and re-layouts  29.8 us (5%)
  between operations  14.1 us (3%)
  loops' own time  10.8 us (2%)
    psum x1, blocking collectives, shards(): gain_grads = lax.psum(gain_terms, ('dp', 'node')) / devices  176 us
    psum x1, waiting for transfers between devices, shards(): weight_grads = lax.psum(group_total, 'dp') / devices  143 us
    all_gather x1, waiting for transfers between devices, shards(): lax.all_gather(weight_values, 'node', axis=0, tiled=True)  32.9 us
    dot_general x16, matrix products, quantize_rows(): lax.dot_general(inputs, key_cotangent, (((0,), (0,)), ((), ())), preferre...  23.7 us
    all_gather x1, blocking collectives, shards(): lax.all_gather(weight_scale, 'node', axis=0, tiled=True)  21.8 us
    mul x1, local copies, waits for them, and re-layouts, widen_weight(): shaped * scales.astype(jnp.float32)[:, :, None]  16.8 us
    dynamic_update_slice x32, other arithmetic, shards(): levels, peaks = lax.map(quantize_rows, jnp.arange(group, dtype=jnp.int32))  14.8 us
    dot_general x1, matrix products, shards(): lax.dot_general(key_cotangent, weight_piece, (((1,), (1,)), ((), ())), pr...  13.6 us
  transfers between devices with their start and end apart: 3, of which 2 were waited for; matrix products, arithmetic and copies ran while one was open for 4% of the time, Pallas kernels for 0%

commit v1 on v0

v1 whole, which is shorter than its diff:
```python
import functools

import jax
import jax.numpy as jnp
from jax import lax
from jax.experimental import pallas as pl
from jax.experimental.pallas import tpu as pltpu
from jax.sharding import Mesh, PartitionSpec as P

NODE = ("zl", "x", "c")
EVERY = ("y", "zh", "zl", "x", "c")
TILE = 128
GROUPS = 4
Y_MASKS = ((1, 3), (3, 1), (1, 3), (3, 1))
LIMIT = 48 * 2**20


def widen_weight(values, scales):
    rows, blocks = scales.shape
    block = values.shape[1] // blocks
    shaped = values.astype(jnp.float32).reshape(rows, blocks, block)
    return (
        (shaped * scales.astype(jnp.float32)[:, :, None])
        .reshape(rows, blocks * block)
        .astype(jnp.bfloat16)
    )


def norm_kernel(tab_ref, tok_ref, gain_ref, own_ref, oth_ref, inv_ref):
    rows, width = tok_ref.shape
    total = jnp.zeros((rows, TILE), jnp.float32)
    for t in range(width // TILE):
        wide = tok_ref[:, t * TILE : (t + 1) * TILE].astype(jnp.float32)
        total = total + wide * wide
    mean = jnp.sum(total, axis=1, keepdims=True) / width
    inverse = lax.rsqrt(mean + 1e-05)
    inv_ref[...] = inverse
    for side, out_ref in enumerate((own_ref, oth_ref)):
        for r in range(width // TILE // 2):
            at = pl.multiple_of(tab_ref[side, r] * TILE, TILE)
            wide = tok_ref[:, pl.ds(at, TILE)].astype(jnp.float32)
            scaled = wide * inverse * gain_ref[:, pl.ds(at, TILE)]
            out_ref[:, r * TILE : (r + 1) * TILE] = scaled.astype(jnp.bfloat16)


def norm_tiles(tokens, gain, table):
    rows, width = tokens.shape
    step = 64 if rows % 64 == 0 else rows
    half = pl.BlockSpec((step, width // 2), lambda i, tab: (i, 0))
    return pl.pallas_call(
        norm_kernel,
        grid_spec=pltpu.PrefetchScalarGridSpec(
            num_scalar_prefetch=1,
            grid=(rows // step,),
            in_specs=[
                pl.BlockSpec((step, width), lambda i, tab: (i, 0)),
                pl.BlockSpec((1, width), lambda i, tab: (0, 0)),
            ],
            out_specs=[half, half, pl.BlockSpec((step, 1), lambda i, tab: (i, 0))],
        ),
        out_shape=[
            jax.ShapeDtypeStruct((rows, width // 2), jnp.bfloat16),
            jax.ShapeDtypeStruct((rows, width // 2), jnp.bfloat16),
            jax.ShapeDtypeStruct((rows, 1), jnp.float32),
        ],
        compiler_params=pltpu.CompilerParams(vmem_limit_bytes=LIMIT),
        cost_estimate=pl.CostEstimate(
            flops=6 * rows * width, bytes_accessed=4 * rows * width, transcendentals=rows
        ),
    )(table, tokens, gain)


def place(group, rz, ry, rx):
    first, second = Y_MASKS[group]
    y1, y2 = next(
        (a, b) for a in (0, 1) for b in (0, 1) if (a * first) ^ (b * second) == ry
    )
    if group < 2:
        return y1, (rz * 2 + y2) * 4 + rx
    return rz, (y1 * 2 + y2) * 4 + rx


def grad_kernel(own_ref, got_ref, cot_own_ref, cot_got_ref, *out_refs):
    span = 2 * TILE
    cot_own = cot_own_ref[...]
    cot_got = cot_got_ref[...]
    for pair in range(own_ref.shape[1] // span):
        part = slice(pair * span, (pair + 1) * span)
        grads = jnp.dot(cot_own, own_ref[:, part], preferred_element_type=jnp.float32)
        grads += jnp.dot(cot_got, got_ref[:, part], preferred_element_type=jnp.float32)
        for which in range(2):
            tile = pair * 2 + which
            for group in range(GROUPS):
                piece = grads[
                    group * TILE : (group + 1) * TILE, which * TILE : (which + 1) * TILE
                ]
                sent, at = place(group, tile // 16, tile // 4 % 4, tile % 4)
                if sent:
                    out_refs[group][at] = piece.astype(jnp.bfloat16)
                else:
                    out_refs[GROUPS + group][at] = piece


def grad_tiles(own, got, cot_own, cot_got):
    rows, width = own.shape
    tiles = width // TILE // 2
    shape = (tiles, TILE, TILE)
    outs = pl.pallas_call(
        grad_kernel,
        out_shape=[jax.ShapeDtypeStruct(shape, jnp.bfloat16)] * GROUPS
        + [jax.ShapeDtypeStruct(shape, jnp.float32)] * GROUPS,
        compiler_params=pltpu.CompilerParams(vmem_limit_bytes=LIMIT),
        cost_estimate=pl.CostEstimate(
            flops=4 * rows * width * GROUPS * TILE,
            bytes_accessed=4 * rows * width + 6 * GROUPS * tiles * TILE * TILE,
            transcendentals=0,
        ),
    )(own, got, cot_own, cot_got)
    return outs[:GROUPS], outs[GROUPS:]


def project_kernel(tok_ref, inv_ref, gain_ref, w_ref, cot_ref, proj_ref, grads_ref, acc, moment, *, width):
    phase, step = pl.program_id(0), pl.program_id(1)
    last = pl.num_programs(1) - 1
    inverse = inv_ref[...]

    @pl.when(phase == 0)
    def _():
        wide = tok_ref[...].astype(jnp.float32)
        normed = (wide * inverse * gain_ref[...]).astype(jnp.bfloat16)
        sums = jnp.dot(normed, w_ref[...], preferred_element_type=jnp.float32)

        @pl.when(step == 0)
        def _():
            acc[...] = sums

        @pl.when(step > 0)
        def _():
            acc[...] += sums

        @pl.when(step == last)
        def _():
            keys = acc[...]
            proj_ref[...] = keys.astype(jnp.bfloat16)
            inner = jnp.sum(cot_ref[...].astype(jnp.float32) * keys, axis=1, keepdims=True)
            moment[...] = inverse * inverse * inner / width

    @pl.when(phase == 1)
    def _():
        partial = lax.dot_general(
            cot_ref[...], w_ref[...], (((1,), (1,)), ((), ())), preferred_element_type=jnp.float32
        )
        wide = tok_ref[...].astype(jnp.float32)
        grads = inverse * gain_ref[...] * partial - wide * moment[...]
        grads_ref[...] = grads.astype(jnp.bfloat16)


def project(tokens, inverse, gain, weight, cotangent):
    rows, width = tokens.shape
    columns = cotangent.shape[1]
    span = 1024
    return pl.pallas_call(
        functools.partial(project_kernel, width=width),
        grid=(2, width // span),
        in_specs=[
            pl.BlockSpec((rows, span), lambda p, i: (0, i)),
            pl.BlockSpec((rows, 1), lambda p, i: (0, 0)),
            pl.BlockSpec((1, span), lambda p, i: (0, i)),
            pl.BlockSpec((span, columns), lambda p, i: (i, 0)),
            pl.BlockSpec((rows, columns), lambda p, i: (0, 0)),
        ],
        out_specs=[
            pl.BlockSpec((rows, columns), lambda p, i: (0, 0)),
            pl.BlockSpec((rows, span), lambda p, i: (0, i * p)),
        ],
        out_shape=[
            jax.ShapeDtypeStruct((rows, columns), jnp.bfloat16),
            jax.ShapeDtypeStruct((rows, width), jnp.bfloat16),
        ],
        scratch_shapes=[
            pltpu.VMEM((rows, columns), jnp.float32),
            pltpu.VMEM((rows, 1), jnp.float32),
        ],
        compiler_params=pltpu.CompilerParams(vmem_limit_bytes=LIMIT),
        cost_estimate=pl.CostEstimate(
            flops=4 * rows * width * columns,
            bytes_accessed=6 * rows * width + 4 * width * columns,
            transcendentals=0,
        ),
    )(tokens, inverse, gain, weight, cotangent)


def swap(array, axis, mask):
    size = lax.axis_size(axis)
    return lax.ppermute(array, axis, [(i, i ^ mask) for i in range(size)])


def swap_z(array, odd):
    size = lax.axis_size("zh") * lax.axis_size("zl")
    if odd:
        pairs = [(i, (i + 1 if i % 2 else i - 1) % size) for i in range(size)]
    else:
        pairs = [(i, i ^ 1) for i in range(size)]
    return lax.ppermute(array, ("zh", "zl"), pairs)


def halve(total):
    half = total.shape[0] // 2
    return total[half:].astype(jnp.bfloat16), total[:half]


def reduce_grads(sent, kept):
    moves = (
        lambda a: swap(a, "y", 1),
        lambda a: swap(a, "y", 3),
        lambda a: swap_z(a, False),
        lambda a: swap_z(a, True),
    )
    for order in ((0, 1, 2, 3), (2, 3, 0, 1)):
        got = [moves[m](s) for m, s in zip(order, sent)]
        totals = [k + g.astype(jnp.float32) for k, g in zip(kept, got)]
        sent, kept = zip(*[halve(t) for t in totals])
    got_even = swap(jnp.stack([sent[0], sent[2]]), "y", 3)
    got_odd = swap(jnp.stack([sent[1], sent[3]]), "y", 1)
    got = (got_even[0], got_odd[0], got_even[1], got_odd[1])
    total = jnp.stack([k + g.astype(jnp.float32) for k, g in zip(kept, got)], axis=1)
    out = total[0]
    for mask in (1, 3, 2):
        out = out + swap(total[mask].astype(jnp.bfloat16), "x", mask).astype(jnp.float32)
    send = out.astype(jnp.bfloat16)
    for mask in (1, 3, 2):
        out = out + swap(send, "zh", mask).astype(jnp.float32)
    return out


def shards(tokens, norm_gain, weight_values, weight_scale, key_cotangent):
    y, zl, x, c = (lax.axis_index(a) for a in ("y", "zl", "x", "c"))
    width = tokens.shape[1]
    columns = weight_values.shape[1]
    gain = norm_gain.reshape(1, width)
    own_weight = widen_weight(weight_values, weight_scale)
    weight = lax.all_gather(own_weight, NODE, axis=0, tiled=True)

    label = jnp.arange(32, dtype=jnp.int32)
    chip = (zl ^ (label // 16)) * 4 + (x ^ (label % 4))
    quarter = y ^ (label // 4 % 4)
    table = jnp.stack([(chip * 2 + side) * 4 + quarter for side in (c, 1 - c)])
    own, other, inverse = norm_tiles(tokens, gain, table)

    cot_own = key_cotangent.T
    cot_got = swap(cot_own, "c", 1)
    got = swap(other, "c", 1)
    sent, kept = grad_tiles(own, got, cot_own, cot_got)
    devices = 1
    for axis in EVERY:
        devices *= lax.axis_size(axis)
    mine = reduce_grads(sent, kept) / devices

    projected, token_grads = project(tokens, inverse, gain, weight, key_cotangent)

    mine = mine.reshape(columns, TILE)
    shard = columns
    node = (zl * 4 + x) * 2 + c
    my_weight = lax.dynamic_slice_in_dim(own_weight, y * TILE, TILE, 0).T.astype(jnp.float32)
    my_gain = lax.dynamic_slice_in_dim(norm_gain, node * shard + y * TILE, TILE, 0)
    gain_part = jnp.sum(my_weight * mine, axis=0, keepdims=True) / my_gain[None, :]
    high = gain_part.astype(jnp.bfloat16)
    low = (gain_part - high.astype(jnp.float32)).astype(jnp.bfloat16)
    packed = jnp.concatenate(
        [mine.astype(jnp.bfloat16), high, low, jnp.zeros((14, TILE), jnp.bfloat16)], axis=0
    )
    pieces = jnp.stack([packed] + [swap(packed, "y", mask) for mask in (1, 2, 3)])
    ordered = [lax.dynamic_index_in_dim(pieces, y ^ q, 0, keepdims=False) for q in range(4)]
    weight_grads = jnp.concatenate([p[:columns] for p in ordered], axis=1)
    weight_grads = weight_grads.astype(jnp.float32).T
    gains = jnp.concatenate(
        [p[columns].astype(jnp.float32) + p[columns + 1].astype(jnp.float32) for p in ordered]
    )
    pair = swap(gains, "c", 1)
    gains = jnp.where(c == 0, jnp.concatenate([gains, pair]), jnp.concatenate([pair, gains]))
    rows = jnp.stack([gains] + [swap(gains, "x", mask) for mask in (1, 2, 3)])
    gains = jnp.concatenate([lax.dynamic_index_in_dim(rows, x ^ q, 0, keepdims=False) for q in range(4)])
    pair = swap(gains, "zl", 1)
    gain_grads = jnp.where(zl == 0, jnp.concatenate([gains, pair]), jnp.concatenate([pair, gains]))
    return (projected, token_grads, weight_grads, gain_grads)


def solution(mesh):
    fine = Mesh(mesh.devices.reshape(4, 4, 2, 4, 2), EVERY)
    rows = P(EVERY, None)
    return jax.shard_map(
        shards,
        mesh=fine,
        in_specs=(rows, P(), P(NODE, None), P(NODE, None), rows),
        out_specs=(rows, rows, P(NODE, None), P()),
        check_vma=False,
    )
```

time: 543 us -> 164 us (0.30); the launches traced: 533 us -> 162 us
  blocking collectives: 208 us -> 0 us
  waiting for transfers between devices: 177 us -> 50.9 us
  matrix products: 50.8 us -> 0 us
  starting transfers between devices: 4.98 us -> 52.1 us
  other arithmetic: 37.7 us -> 6.61 us
  Pallas kernels: 0 us -> 31 us
  local copies, waits for them, and re-layouts: 29.8 us -> 7.38 us
  loops' own time: 10.8 us -> 0 us
    psum x1 -> x0, blocking collectives: 176 us -> none  [shards(): gain_grads = lax.psum(gain_terms, ('dp', 'node')) / devices]
    psum x1 -> x0, waiting for transfers between devices: 143 us -> none  [shards(): weight_grads = lax.psum(group_total, 'dp') / devices]
    ppermute x0 -> x26, starting transfers between devices: none -> 52 us  [the longest x22 40.6 us: swap(): return lax.ppermute(array, axis, [(i, i ^ mask) for i in range(size)])]
    ppermute x0 -> x26, waiting for transfers between devices: none -> 50.9 us  [the longest x22 29.2 us: swap(): return lax.ppermute(array, axis, [(i, i ^ mask) for i in range(size)])]
    dot_general x18 -> x0, matrix products: 50.8 us -> none  [the longest x16 23.7 us: quantize_rows(): lax.dot_general(inputs, key_cotangent, (((0,), (0,)), ((), ())), preferre...]
    all_gather x1, waiting for transfers between devices: 32.9 us -> 0.01 us  [shards(): weight = lax.all_gather(own_weight, NODE, axis=0, tiled=True)]
    pallas_call x0 -> x3, Pallas kernels: none -> 31 us  [the longest x1 18 us: project(): pl.pallas_call(functools.partial(project_kernel, width=width), grid=(2, w...]
    all_gather x1 -> x0, blocking collectives: 21.8 us -> none  [shards(): lax.all_gather(weight_scale, 'node', axis=0, tiled=True)]
  transfers between devices with their start and end apart: 3 -> 27, of which waited for: 2 -> 17; matrix products, arithmetic and copies ran while one was open for 4% -> 4% of each run, Pallas kernels for 0% -> 8%
where the time goes in v1:
time: 164 us; the launch traced here: 162 us
  starting transfers between devices  52.1 us (32%)
  waiting for transfers between devices  50.9 us (31%)
  Pallas kernels  31 us (19%)
  between operations  14.5 us (9%)
  local copies, waits for them, and re-layouts  7.38 us (4%)
  other arithmetic  6.61 us (4%)
    ppermute x22, starting transfers between devices, swap(): return lax.ppermute(array, axis, [(i, i ^ mask) for i in range(size)])  40.6 us
    ppermute x22, waiting for transfers between devices, swap(): return lax.ppermute(array, axis, [(i, i ^ mask) for i in range(size)])  29.2 us
    ppermute x4, waiting for transfers between devices, swap_z(): return lax.ppermute(array, ('zh', 'zl'), pairs)  21.7 us
    pallas_call x1, Pallas kernels, project(): pl.pallas_call(functools.partial(project_kernel, width=width), grid=(2, w...  18 us
    ppermute x4, starting transfers between devices, swap_z(): return lax.ppermute(array, ('zh', 'zl'), pairs)  11.4 us
    pallas_call x1, Pallas kernels, grad_tiles(): pl.pallas_call(grad_kernel, out_shape=[jax.ShapeDtypeStruct(shape, jnp.bf...  7.02 us
    pallas_call x1, Pallas kernels, norm_tiles(): pl.pallas_call(norm_kernel, grid_spec=pltpu.PrefetchScalarGridSpec(num_sc...  5.94 us
    unnamed x37, local copies, waits for them, and re-layouts  5.07 us
  transfers between devices with their start and end apart: 27, of which 17 were waited for; matrix products, arithmetic and copies ran while one was open for 4% of the time, Pallas kernels for 8%

profile of v1, /device:TPU:1, one launch (start us, length us, event | category | flops | bytes accessed | tf_op | source)
XLA Modules:
  0.0 162.5 jit_solution(15746046772599509153)
XLA Ops:
  8.7 2.0 %fusion = bf16[512,512]{1,0:T(8,128)(2,1)} fusion(f32[64,8,4,128]{3,2,1,0:T(4,128)S(1)} %bitcast.115, bf16[512,512]{1,0:T(8,128)(2,1)} %param.7), kind=kLoop, calls=%fused_computation.1 | loop fusion | flops 786432 | bytes 2097152 | tf_op jit(solution)/shard_map/convert_element_type | solution.py:25
  11.6 5.9 %shard_map.84 = (bf16[320,4096]{1,0:T(8,128)(2,1)S(1)}, bf16[320,4096]{1,0:T(8,128)(2,1)S(1)}, f32[320,1]{1,0:T(8,128)S(1)}) custom-call(s32[2,32]{1,0:T(2,128)S(1)} %pad_add_fusion.tab_ref, bf16[320,8192]{1,0:T(8,128)(2,1)} %tok_ref.3, f32[1,8192]{1,0:T(1,128)S(1)} %bitcast.113), custom_call_target="tpu_custom_call" | custom-call | flops 15728640 | bytes 10485760 | tf_op jit(solution)/shard_map/pallas_call | solution.py:50
  19.0 3.2 %collective-permute-start = (bf16[320,4096]{1,0:T(8,128)(2,1)S(1)}, bf16[320,4096]{1,0:T(8,128)(2,1)}, u32[]{:S(2)}, u32[]{:S(2)}) collective-permute-start(bf16[320,4096]{1,0:T(8,128)(2,1)S(1)} %get-tuple-element.21), channel_id=1, source_target_pairs={{0,1},{1,0},{2,3},{3,2},{4,5},{5,4},{6,7},{7,6},{8,9},{9,8},{10,11... | collective-permute-start | bytes 7864328 | tf_op jit(solution)/shard_map/ppermute | solution.py:195
  22.6 4.7 %collective-permute-done.1.cot_got_ref = bf16[512,320]{1,0:T(8,128)(2,1)S(1)} collective-permute-done((bf16[512,320]{1,0:T(8,128)(2,1)S(1)}, bf16[512,320]{1,0:T(8,128)(2,1)S(1)}, u32[]{:S(2)}, u32[]{:S(2)}) %collective-permute-start.1) | collective-permute-done | bytes 327712 | tf_op jit(solution)/shard_map/ppermute | solution.py:195
  27.5 7.0 %shard_map.86 = (bf16[16,128,128]{2,1,0:T(8,128)(2,1)S(1)}, bf16[16,128,128]{2,1,0:T(8,128)(2,1)S(1)}, bf16[16,128,128]{2,1,0:T(8,128)(2,1)S(1)}, bf16[16,128,12...) custom-call(bf16[320,4096]{1,0:T(8,128)(2,1)} %copy-done.4, ...), custom_call_target="tpu_custom_call" | custom-call | flops 2684354560 | bytes 11534336 | tf_op jit(solution)/shard_map/pallas_call | solution.py:108
  36.1 4.7 %collective-permute-start.9 = (bf16[16,128,128]{2,1,0:T(8,128)(2,1)S(1)}, bf16[16,128,128]{2,1,0:T(8,128)(2,1)S(1)}, u32[]{:S(2)}, u32[]{:S(2)}) collective-permute-start(bf16[16,128,128]{2,1,0:T(8,128)(2,1)S(1)} %get-tuple-element.29), channel_id=1, source_target_pairs={{0,56},{8,16},{16,8},{24,32},{32,24},{40,48},{48,40},{56,0},{1,57}... | collective-permute-start | bytes 1572872 | tf_op jit(solution)/shard_map/ppermute | solution.py:204
  40.8 1.9 %collective-permute-start.7 = (bf16[16,128,128]{2,1,0:T(8,128)(2,1)S(1)}, bf16[16,128,128]{2,1,0:T(8,128)(2,1)S(1)}, u32[]{:S(2)}, u32[]{:S(2)}) collective-permute-start(bf16[16,128,128]{2,1,0:T(8,128)(2,1)S(1)} %get-tuple-element.27), channel_id=1, source_target_pairs={{0,192},{64,128},{128,64},{192,0},{1,193},{65,129},{129,65},{193,1... | collective-permute-start | bytes 1572872 | tf_op jit(solution)/shard_map/ppermute | solution.py:195
  42.7 16.9 %collective-permute-done.4 = bf16[16,128,128]{2,1,0:T(8,128)(2,1)S(1)} collective-permute-done((bf16[16,128,128]{2,1,0:T(8,128)(2,1)S(1)}, bf16[16,128,128]{2,1,0:T(8,128)(2,1)S(1)}, u32[]{:S(2)}, u32[]{:S(2)}) %collective-permute-start.4) | collective-permute-done | bytes 524320 | tf_op jit(solution)/shard_map/ppermute | solution.py:204
  61.8 1.9 %collective-permute-start.10 = (bf16[8,128,128]{2,1,0:T(8,128)(2,1)S(1)}, bf16[8,128,128]{2,1,0:T(8,128)(2,1)S(1)}, u32[]{:S(2)}, u32[]{:S(2)}) collective-permute-start(bf16[8,128,128]{2,1,0:T(8,128)(2,1)S(1)} %slice.261), channel_id=1, source_target_pairs={{0,192},{64,128},{128,64},{192,0},{1,193},{65,129},{129,65},{193,1... | collective-permute-start | bytes 786440 | tf_op jit(solution)/shard_map/ppermute | solution.py:195
  63.8 5.0 %collective-permute-start.8 = (bf16[8,128,128]{2,1,0:T(8,128)(2,1)S(1)}, bf16[8,128,128]{2,1,0:T(8,128)(2,1)S(1)}, u32[]{:S(2)}, u32[]{:S(2)}) collective-permute-start(bf16[8,128,128]{2,1,0:T(8,128)(2,1)S(1)} %slice.262), channel_id=1, source_target_pairs={{0,56},{8,16},{16,8},{24,32},{32,24},{40,48},{48,40},{56,0},{1,57}... | collective-permute-start | bytes 786440 | tf_op jit(solution)/shard_map/ppermute | solution.py:204
  68.9 4.8 %collective-permute-done.3 = bf16[8,128,128]{2,1,0:T(8,128)(2,1)S(1)} collective-permute-done((bf16[8,128,128]{2,1,0:T(8,128)(2,1)S(1)}, bf16[8,128,128]{2,1,0:T(8,128)(2,1)S(1)}, u32[]{:S(2)}, u32[]{:S(2)}) %collective-permute-start.3) | collective-permute-done | bytes 262176 | tf_op jit(solution)/shard_map/ppermute | solution.py:204
  76.2 4.7 %collective-permute-done.6 = bf16[2,4,128,128]{3,2,1,0:T(8,128)(2,1)S(1)} collective-permute-done((bf16[2,4,128,128]{3,2,1,0:T(8,128)(2,1)S(1)}, bf16[2,4,128,128]{3,2,1,0:T(8,128)(2,1)S(1)}, u32[]{:S(2)}, u32[]{:S(2)}) %collective-permute-start.6) | collective-permute-done | bytes 262176 | tf_op jit(solution)/shard_map/ppermute | solution.py:195
  82.0 2.5 %collective-permute-start.13 = (bf16[4,128,128]{2,1,0:T(8,128)(2,1)S(1)}, bf16[4,128,128]{2,1,0:T(8,128)(2,1)S(1)}, u32[]{:S(2)}, u32[]{:S(2)}) collective-permute-start(bf16[4,128,128]{2,1,0:T(8,128)(2,1)S(1)} %get-tuple-element.42), channel_id=1, source_target_pairs={{0,6},{2,4},{4,2},{6,0},{1,7},{3,5},{5,3},{7,1},{8,14},{10,12},{12... | collective-permute-start | bytes 393224 | tf_op jit(solution)/shard_map/ppermute | solution.py:195
  85.8 2.0 %collective-permute-done.13 = bf16[4,128,128]{2,1,0:T(8,128)(2,1)S(1)} collective-permute-done((bf16[4,128,128]{2,1,0:T(8,128)(2,1)S(1)}, bf16[4,128,128]{2,1,0:T(8,128)(2,1)S(1)}, u32[]{:S(2)}, u32[]{:S(2)}) %collective-permute-start.13) | collective-permute-done | bytes 131104 | tf_op jit(solution)/shard_map/ppermute | solution.py:195
  87.8 2.1 %collective-permute-done.14 = bf16[4,128,128]{2,1,0:T(8,128)(2,1)S(1)} collective-permute-done((bf16[4,128,128]{2,1,0:T(8,128)(2,1)S(1)}, bf16[4,128,128]{2,1,0:T(8,128)(2,1)S(1)}, u32[]{:S(2)}, u32[]{:S(2)}) %collective-permute-start.14) | collective-permute-done | bytes 131104 | tf_op jit(solution)/shard_map/ppermute | solution.py:195
  89.9 3.0 %collective-permute-start.15 = (bf16[4,128,128]{2,1,0:T(8,128)(2,1)S(1)}, bf16[4,128,128]{2,1,0:T(8,128)(2,1)S(1)}, u32[]{:S(2)}, u32[]{:S(2)}) collective-permute-start(bf16[4,128,128]{2,1,0:T(8,128)(2,1)S(1)} %fusion.13), channel_id=1, source_target_pairs={{0,16},{16,0},{32,48},{48,32},{1,17},{17,1},{33,49},{49,33},{2,18}... | collective-permute-start | bytes 393224 | tf_op jit(solution)/shard_map/ppermute | solution.py:195
  93.0 4.0 %collective-permute-start.16 = (bf16[4,128,128]{2,1,0:T(8,128)(2,1)S(1)}, bf16[4,128,128]{2,1,0:T(8,128)(2,1)S(1)}, u32[]{:S(2)}, u32[]{:S(2)}) collective-permute-start(bf16[4,128,128]{2,1,0:T(8,128)(2,1)S(1)} %fusion.13), channel_id=1, source_target_pairs={{0,48},{16,32},{32,16},{48,0},{1,49},{17,33},{33,17},{49,1},{2,50}... | collective-permute-start | bytes 393224 | tf_op jit(solution)/shard_map/ppermute | solution.py:195
  99.9 6.5 %collective-permute-done.17 = bf16[4,128,128]{2,1,0:T(8,128)(2,1)S(1)} collective-permute-done((bf16[4,128,128]{2,1,0:T(8,128)(2,1)S(1)}, bf16[4,128,128]{2,1,0:T(8,128)(2,1)S(1)}, u32[]{:S(2)}, u32[]{:S(2)}) %collective-permute-start.17) | collective-permute-done | bytes 131104 | tf_op jit(solution)/shard_map/ppermute | solution.py:195
  112.4 2.5 %collective-permute-done.19 = bf16[528,128]{0,1:T(8,128)(2,1)S(1)} collective-permute-done((bf16[528,128]{0,1:T(8,128)(2,1)S(1)}, bf16[528,128]{0,1:T(8,128)(2,1)S(1)}, u32[]{:S(2)}, u32[]{:S(2)}) %collective-permute-start.19) | collective-permute-done | bytes 135200 | tf_op jit(solution)/shard_map/ppermute | solution.py:195
  117.0 6.2 %collective-permute-start.21 = (f32[512]{0:T(512)S(1)}, f32[512]{0:T(512)S(1)}, u32[]{:S(2)}, u32[]{:S(2)}) collective-permute-start(f32[512]{0:T(512)S(1)} %pad_maximum_fusion.6), channel_id=1, source_target_pairs={{0,1},{1,0},{2,3},{3,2},{4,5},{5,4},{6,7},{7,6},{8,9},{9,8},{10,11... | collective-permute-start | bytes 6152 | tf_op jit(solution)/shard_map/ppermute | solution.py:195
  126.7 2.1 %collective-permute-start.24 = (f32[1024]{0:T(1024)S(1)}, f32[1024]{0:T(1024)S(1)}, u32[]{:S(2)}, u32[]{:S(2)}) collective-permute-start(f32[1024]{0:T(1024)S(1)} %broadcast_select_fusion.2), channel_id=1, source_target_pairs={{0,6},{2,4},{4,2},{6,0},{1,7},{3,5},{5,3},{7,1},{8,14},{10,12},{12... | collective-permute-start | bytes 12296 | tf_op jit(solution)/shard_map/ppermute | solution.py:195
  130.4 2.9 %collective-permute-start.25 = (f32[4096]{0:T(1024)S(1)}, f32[4096]{0:T(1024)S(1)}, u32[]{:S(2)}, u32[]{:S(2)}) collective-permute-start(f32[4096]{0:T(1024)S(1)} %pad_maximum_fusion.5), channel_id=1, source_target_pairs={{0,8},{8,0},{1,9},{9,1},{2,10},{10,2},{3,11},{11,3},{4,12},{12,4},... | collective-permute-start | bytes 49160 | tf_op jit(solution)/shard_map/ppermute | solution.py:195
  135.1 2.5 %copy-done = bf16[320,8192]{1,0:T(8,128)(2,1)S(1)} copy-done((bf16[320,8192]{1,0:T(8,128)(2,1)S(1)}, bf16[320,8192]{1,0:T(8,128)(2,1)}, u32[]{:S(2)}) %copy-start) | copy-done | bytes 5242904
  137.6 18.0 %shard_map.85 = (bf16[320,512]{1,0:T(8,128)(2,1)}, bf16[320,8192]{1,0:T(8,128)(2,1)}) custom-call(bf16[320,8192]{1,0:T(8,128)(2,1)S(1)} %copy-done, f32[320,1]{1,0:T(8,128)S(1)} %get-tuple-element.17.inv_ref, f32[1,8192]{1,0:T(1,128)S(1)} %bitcast.114, bf16[8192,512]{1,0:T(8,128)(2,1)} %all-gather.2.cloned.1.call-done.w_ref, bf16[320,512]{1,0:T(8,128)(2,1)S(1)} %copy-done.1), custom_call_target="tpu_custom_call" | custom-call | flops 5368709120 | bytes 32505856 | tf_op jit(solution)/shard_map/pallas_call | solution.py:162
  (127 shorter events, 31.0 us)
Async XLA Ops:
  7.2 128.0 %all-gather.2.cloned.1.call-start = ((), (), s32[]{:S(2)}) async-start(), calls=%async_computation | async-start | bytes 8912896 | tf_op jit(solution)/shard_map/all_gather | solution.py:242
  19.0 8.5 %collective-permute-start = (bf16[320,4096]{1,0:T(8,128)(2,1)S(1)}, bf16[320,4096]{1,0:T(8,128)(2,1)}, u32[]{:S(2)}, u32[]{:S(2)}) collective-permute-start(bf16[320,4096]{1,0:T(8,128)(2,1)S(1)} %get-tuple-element.21), channel_id=1, source_target_pairs={{0,1},{1,0},{2,3},{3,2},{4,5},{5,4},{6,7},{7,6},{8,9},{9,8},{10,11... | collective-permute-start | bytes 7864328 | tf_op jit(solution)/shard_map/ppermute | solution.py:195
  22.5 4.8 %collective-permute-start.1 = (bf16[512,320]{1,0:T(8,128)(2,1)S(1)}, bf16[512,320]{1,0:T(8,128)(2,1)S(1)}, u32[]{:S(2)}, u32[]{:S(2)}) collective-permute-start(bf16[512,320]{1,0:T(8,128)(2,1)S(1)} %bitcast.111), channel_id=1, source_target_pairs={{0,1},{1,0},{2,3},{3,2},{4,5},{5,4},{6,7},{7,6},{8,9},{9,8},{10,11... | collective-permute-start | bytes 983048 | tf_op jit(solution)/shard_map/ppermute | solution.py:195
  34.6 25.1 %collective-permute-start.4 = (bf16[16,128,128]{2,1,0:T(8,128)(2,1)S(1)}, bf16[16,128,128]{2,1,0:T(8,128)(2,1)S(1)}, u32[]{:S(2)}, u32[]{:S(2)}) collective-permute-start(bf16[16,128,128]{2,1,0:T(8,128)(2,1)S(1)} %get-tuple-element.25), channel_id=1, source_target_pairs={{0,8},{8,0},{16,24},{24,16},{32,40},{40,32},{48,56},{56,48},{1,9},... | collective-permute-start | bytes 1572872 | tf_op jit(solution)/shard_map/ppermute | solution.py:204
  34.8 25.1 %collective-permute-start.2 = (bf16[16,128,128]{2,1,0:T(8,128)(2,1)S(1)}, bf16[16,128,128]{2,1,0:T(8,128)(2,1)S(1)}, u32[]{:S(2)}, u32[]{:S(2)}) collective-permute-start(bf16[16,128,128]{2,1,0:T(8,128)(2,1)S(1)} %get-tuple-element.23), channel_id=1, source_target_pairs={{0,64},{64,0},{128,192},{192,128},{1,65},{65,1},{129,193},{193,129... | collective-permute-start | bytes 1572872 | tf_op jit(solution)/shard_map/ppermute | solution.py:195
  36.1 25.5 %collective-permute-start.9 = (bf16[16,128,128]{2,1,0:T(8,128)(2,1)S(1)}, bf16[16,128,128]{2,1,0:T(8,128)(2,1)S(1)}, u32[]{:S(2)}, u32[]{:S(2)}) collective-permute-start(bf16[16,128,128]{2,1,0:T(8,128)(2,1)S(1)} %get-tuple-element.29), channel_id=1, source_target_pairs={{0,56},{8,16},{16,8},{24,32},{32,24},{40,48},{48,40},{56,0},{1,57}... | collective-permute-start | bytes 1572872 | tf_op jit(solution)/shard_map/ppermute | solution.py:204
  40.8 22.9 %collective-permute-start.7 = (bf16[16,128,128]{2,1,0:T(8,128)(2,1)S(1)}, bf16[16,128,128]{2,1,0:T(8,128)(2,1)S(1)}, u32[]{:S(2)}, u32[]{:S(2)}) collective-permute-start(bf16[16,128,128]{2,1,0:T(8,128)(2,1)S(1)} %get-tuple-element.27), channel_id=1, source_target_pairs={{0,192},{64,128},{128,64},{192,0},{1,193},{65,129},{129,65},{193,1... | collective-permute-start | bytes 1572872 | tf_op jit(solution)/shard_map/ppermute | solution.py:195
  59.8 9.0 %collective-permute-start.5 = (bf16[8,128,128]{2,1,0:T(8,128)(2,1)S(1)}, bf16[8,128,128]{2,1,0:T(8,128)(2,1)S(1)}, u32[]{:S(2)}, u32[]{:S(2)}) collective-permute-start(bf16[8,128,128]{2,1,0:T(8,128)(2,1)S(1)} %slice.263), channel_id=1, source_target_pairs={{0,64},{64,0},{128,192},{192,128},{1,65},{65,1},{129,193},{193,129... | collective-permute-start | bytes 786440 | tf_op jit(solution)/shard_map/ppermute | solution.py:195
  60.1 13.5 %collective-permute-start.3 = (bf16[8,128,128]{2,1,0:T(8,128)(2,1)S(1)}, bf16[8,128,128]{2,1,0:T(8,128)(2,1)S(1)}, u32[]{:S(2)}, u32[]{:S(2)}) collective-permute-start(bf16[8,128,128]{2,1,0:T(8,128)(2,1)S(1)} %slice.264), channel_id=1, source_target_pairs={{0,8},{8,0},{16,24},{24,16},{32,40},{40,32},{48,56},{56,48},{1,9},... | collective-permute-start | bytes 786440 | tf_op jit(solution)/shard_map/ppermute | solution.py:204
  61.8 13.8 %collective-permute-start.10 = (bf16[8,128,128]{2,1,0:T(8,128)(2,1)S(1)}, bf16[8,128,128]{2,1,0:T(8,128)(2,1)S(1)}, u32[]{:S(2)}, u32[]{:S(2)}) collective-permute-start(bf16[8,128,128]{2,1,0:T(8,128)(2,1)S(1)} %slice.261), channel_id=1, source_target_pairs={{0,192},{64,128},{128,64},{192,0},{1,193},{65,129},{129,65},{193,1... | collective-permute-start | bytes 786440 | tf_op jit(solution)/shard_map/ppermute | solution.py:195
  63.8 11.8 %collective-permute-start.8 = (bf16[8,128,128]{2,1,0:T(8,128)(2,1)S(1)}, bf16[8,128,128]{2,1,0:T(8,128)(2,1)S(1)}, u32[]{:S(2)}, u32[]{:S(2)}) collective-permute-start(bf16[8,128,128]{2,1,0:T(8,128)(2,1)S(1)} %slice.262), channel_id=1, source_target_pairs={{0,56},{8,16},{16,8},{24,32},{32,24},{40,48},{48,40},{56,0},{1,57}... | collective-permute-start | bytes 786440 | tf_op jit(solution)/shard_map/ppermute | solution.py:204
  73.8 7.1 %collective-permute-start.6 = (bf16[2,4,128,128]{3,2,1,0:T(8,128)(2,1)S(1)}, bf16[2,4,128,128]{3,2,1,0:T(8,128)(2,1)S(1)}, u32[]{:S(2)}, u32[]{:S(2)}) collective-permute-start(bf16[2,4,128,128]{3,2,1,0:T(8,128)(2,1)S(1)} %pad_maximum_fusion.2), channel_id=1, source_target_pairs={{0,192},{64,128},{128,64},{192,0},{1,193},{65,129},{129,65},{193,1... | collective-permute-start | bytes 786440 | tf_op jit(solution)/shard_map/ppermute | solution.py:195
  75.8 5.7 %collective-permute-start.11 = (bf16[2,4,128,128]{3,2,1,0:T(8,128)(2,1)S(1)}, bf16[2,4,128,128]{3,2,1,0:T(8,128)(2,1)S(1)}, u32[]{:S(2)}, u32[]{:S(2)}) collective-permute-start(bf16[2,4,128,128]{3,2,1,0:T(8,128)(2,1)S(1)} %pad_maximum_fusion.3), channel_id=1, source_target_pairs={{0,64},{64,0},{128,192},{192,128},{1,65},{65,1},{129,193},{193,129... | collective-permute-start | bytes 786440 | tf_op jit(solution)/shard_map/ppermute | solution.py:195
  81.7 4.1 %collective-permute-start.12 = (bf16[4,128,128]{2,1,0:T(8,128)(2,1)S(1)}, bf16[4,128,128]{2,1,0:T(8,128)(2,1)S(1)}, u32[]{:S(2)}, u32[]{:S(2)}) collective-permute-start(bf16[4,128,128]{2,1,0:T(8,128)(2,1)S(1)} %get-tuple-element.40), channel_id=1, source_target_pairs={{0,2},{2,0},{4,6},{6,4},{1,3},{3,1},{5,7},{7,5},{8,10},{10,8},{12,... | collective-permute-start | bytes 393224 | tf_op jit(solution)/shard_map/ppermute | solution.py:195
  82.0 5.8 %collective-permute-start.13 = (bf16[4,128,128]{2,1,0:T(8,128)(2,1)S(1)}, bf16[4,128,128]{2,1,0:T(8,128)(2,1)S(1)}, u32[]{:S(2)}, u32[]{:S(2)}) collective-permute-start(bf16[4,128,128]{2,1,0:T(8,128)(2,1)S(1)} %get-tuple-element.42), channel_id=1, source_target_pairs={{0,6},{2,4},{4,2},{6,0},{1,7},{3,5},{5,3},{7,1},{8,14},{10,12},{12... | collective-permute-start | bytes 393224 | tf_op jit(solution)/shard_map/ppermute | solution.py:195
  84.5 5.4 %collective-permute-start.14 = (bf16[4,128,128]{2,1,0:T(8,128)(2,1)S(1)}, bf16[4,128,128]{2,1,0:T(8,128)(2,1)S(1)}, u32[]{:S(2)}, u32[]{:S(2)}) collective-permute-start(bf16[4,128,128]{2,1,0:T(8,128)(2,1)S(1)} %get-tuple-element.41), channel_id=1, source_target_pairs={{0,4},{2,6},{4,0},{6,2},{1,5},{3,7},{5,1},{7,3},{8,12},{10,14},{12... | collective-permute-start | bytes 393224 | tf_op jit(solution)/shard_map/ppermute | solution.py:195
  89.9 8.8 %collective-permute-start.15 = (bf16[4,128,128]{2,1,0:T(8,128)(2,1)S(1)}, bf16[4,128,128]{2,1,0:T(8,128)(2,1)S(1)}, u32[]{:S(2)}, u32[]{:S(2)}) collective-permute-start(bf16[4,128,128]{2,1,0:T(8,128)(2,1)S(1)} %fusion.13), channel_id=1, source_target_pairs={{0,16},{16,0},{32,48},{48,32},{1,17},{17,1},{33,49},{49,33},{2,18}... | collective-permute-start | bytes 393224 | tf_op jit(solution)/shard_map/ppermute | solution.py:195
  93.0 7.0 %collective-permute-start.16 = (bf16[4,128,128]{2,1,0:T(8,128)(2,1)S(1)}, bf16[4,128,128]{2,1,0:T(8,128)(2,1)S(1)}, u32[]{:S(2)}, u32[]{:S(2)}) collective-permute-start(bf16[4,128,128]{2,1,0:T(8,128)(2,1)S(1)} %fusion.13), channel_id=1, source_target_pairs={{0,48},{16,32},{32,16},{48,0},{1,49},{17,33},{33,17},{49,1},{2,50}... | collective-permute-start | bytes 393224 | tf_op jit(solution)/shard_map/ppermute | solution.py:195
  96.9 9.5 %collective-permute-start.17 = (bf16[4,128,128]{2,1,0:T(8,128)(2,1)S(1)}, bf16[4,128,128]{2,1,0:T(8,128)(2,1)S(1)}, u32[]{:S(2)}, u32[]{:S(2)}) collective-permute-start(bf16[4,128,128]{2,1,0:T(8,128)(2,1)S(1)} %fusion.13), channel_id=1, source_target_pairs={{0,32},{16,48},{32,0},{48,16},{1,33},{17,49},{33,1},{49,17},{2,34}... | collective-permute-start | bytes 393224 | tf_op jit(solution)/shard_map/ppermute | solution.py:195
  108.1 4.3 %collective-permute-start.18 = (bf16[528,128]{0,1:T(8,128)(2,1)S(1)}, bf16[528,128]{0,1:T(8,128)(2,1)S(1)}, u32[]{:S(2)}, u32[]{:S(2)}) collective-permute-start(bf16[528,128]{0,1:T(8,128)(2,1)S(1)} %maximum_maximum_fusion), channel_id=1, source_target_pairs={{0,64},{64,0},{128,192},{192,128},{1,65},{65,1},{129,193},{193,129... | collective-permute-start | bytes 405512 | tf_op jit(solution)/shard_map/ppermute | solution.py:195
  108.5 6.4 %collective-permute-start.19 = (bf16[528,128]{0,1:T(8,128)(2,1)S(1)}, bf16[528,128]{0,1:T(8,128)(2,1)S(1)}, u32[]{:S(2)}, u32[]{:S(2)}) collective-permute-start(bf16[528,128]{0,1:T(8,128)(2,1)S(1)} %maximum_maximum_fusion), channel_id=1, source_target_pairs={{0,128},{64,192},{128,0},{192,64},{1,129},{65,193},{129,1},{193,65... | collective-permute-start | bytes 405512 | tf_op jit(solution)/shard_map/ppermute | solution.py:195
  110.4 6.2 %collective-permute-start.20 = (bf16[528,128]{0,1:T(8,128)(2,1)S(1)}, bf16[528,128]{0,1:T(8,128)(2,1)S(1)}, u32[]{:S(2)}, u32[]{:S(2)}) collective-permute-start(bf16[528,128]{0,1:T(8,128)(2,1)S(1)} %maximum_maximum_fusion), channel_id=1, source_target_pairs={{0,192},{64,128},{128,64},{192,0},{1,193},{65,129},{129,65},{193,1... | collective-permute-start | bytes 405512 | tf_op jit(solution)/shard_map/ppermute | solution.py:195
  117.0 7.4 %collective-permute-start.21 = (f32[512]{0:T(512)S(1)}, f32[512]{0:T(512)S(1)}, u32[]{:S(2)}, u32[]{:S(2)}) collective-permute-start(f32[512]{0:T(512)S(1)} %pad_maximum_fusion.6), channel_id=1, source_target_pairs={{0,1},{1,0},{2,3},{3,2},{4,5},{5,4},{6,7},{7,6},{8,9},{9,8},{10,11... | collective-permute-start | bytes 6152 | tf_op jit(solution)/shard_map/ppermute | solution.py:195
  124.5 4.3 %collective-permute-start.22 = (f32[1024]{0:T(1024)S(1)}, f32[1024]{0:T(1024)S(1)}, u32[]{:S(2)}, u32[]{:S(2)}) collective-permute-start(f32[1024]{0:T(1024)S(1)} %broadcast_select_fusion.2), channel_id=1, source_target_pairs={{0,2},{2,0},{4,6},{6,4},{1,3},{3,1},{5,7},{7,5},{8,10},{10,8},{12,... | collective-permute-start | bytes 12296 | tf_op jit(solution)/shard_map/ppermute | solution.py:195
  (9 other events, 90.4 us)
Sparse Core Ops, SparseCore 0:
  10.9 75.7 all-gather.1

commit v2 on v1

v2 whole, which is shorter than its diff:
```python
import functools

import jax
import jax.numpy as jnp
from jax import lax
from jax.experimental import pallas as pl
from jax.experimental.pallas import tpu as pltpu
from jax.sharding import Mesh, PartitionSpec as P

NODE = ("zl", "x", "c")
EVERY = ("y", "zh", "zl", "x", "c")
TILE = 128
GROUPS = 4
Y_MASKS = ((1, 3), (3, 1), (1, 3), (3, 1))
LIMIT = 48 * 2**20


def widen_weight(values, scales):
    rows, blocks = scales.shape
    block = values.shape[1] // blocks
    shaped = values.astype(jnp.float32).reshape(rows, blocks, block)
    return (
        (shaped * scales.astype(jnp.float32)[:, :, None])
        .reshape(rows, blocks * block)
        .astype(jnp.bfloat16)
    )


def norm_kernel(tab_ref, tok_ref, gain_ref, out_ref, inv_ref):
    rows, width = tok_ref.shape
    total = jnp.zeros((rows, TILE), jnp.float32)
    for t in range(width // TILE):
        wide = tok_ref[:, t * TILE : (t + 1) * TILE].astype(jnp.float32)
        total = total + wide * wide
    mean = jnp.sum(total, axis=1, keepdims=True) / width
    inverse = lax.rsqrt(mean + 1e-05)
    inv_ref[...] = inverse
    for r in range(width // TILE // 2):
        at = pl.multiple_of(tab_ref[r] * TILE, TILE)
        wide = tok_ref[:, pl.ds(at, TILE)].astype(jnp.float32)
        scaled = wide * inverse * gain_ref[:, pl.ds(at, TILE)]
        out_ref[:, r * TILE : (r + 1) * TILE] = scaled.astype(jnp.bfloat16)


def norm_tiles(tokens, gain, table):
    rows, width = tokens.shape
    step = 64 if rows % 64 == 0 else rows
    return pl.pallas_call(
        norm_kernel,
        grid_spec=pltpu.PrefetchScalarGridSpec(
            num_scalar_prefetch=1,
            grid=(rows // step,),
            in_specs=[
                pl.BlockSpec((step, width), lambda i, tab: (i, 0)),
                pl.BlockSpec((1, width), lambda i, tab: (0, 0)),
            ],
            out_specs=[
                pl.BlockSpec((step, width // 2), lambda i, tab: (i, 0)),
                pl.BlockSpec((step, 1), lambda i, tab: (i, 0)),
            ],
        ),
        out_shape=[
            jax.ShapeDtypeStruct((rows, width // 2), jnp.bfloat16),
            jax.ShapeDtypeStruct((rows, 1), jnp.float32),
        ],
        compiler_params=pltpu.CompilerParams(vmem_limit_bytes=LIMIT),
        cost_estimate=pl.CostEstimate(
            flops=6 * rows * width, bytes_accessed=3 * rows * width, transcendentals=rows
        ),
    )(table, tokens, gain)


def split(group, ry):
    first, second = Y_MASKS[group]
    return next((a, b) for a in (0, 1) for b in (0, 1) if (a * first) ^ (b * second) == ry)


def grad_kernel(tab_ref, tok_ref, gain_ref, inv_ref, got_ref, cot_own_ref, cot_got_ref, *refs):
    sent_refs, kept_refs, normed = refs[:GROUPS], refs[GROUPS : 2 * GROUPS], refs[-1]
    y = tab_ref[8]
    rz = 1 - pl.program_id(0) // 4
    inverse = inv_ref[...]
    for ry in range(4):
        at = pl.multiple_of((y ^ ry) * TILE, TILE)
        wide = tok_ref[:, pl.ds(at, TILE)].astype(jnp.float32)
        scaled = wide * inverse * gain_ref[:, pl.ds(at, TILE)]
        normed[:, ry * TILE : (ry + 1) * TILE] = scaled.astype(jnp.bfloat16)
    span = 2 * TILE
    for pair in range(2):
        part = slice(pair * span, (pair + 1) * span)
        grads = jnp.dot(cot_own_ref[...], normed[:, part], preferred_element_type=jnp.float32)
        grads += jnp.dot(cot_got_ref[...], got_ref[:, part], preferred_element_type=jnp.float32)
        for which in range(2):
            ry = pair * 2 + which
            for group in range(GROUPS):
                piece = grads[
                    group * TILE : (group + 1) * TILE, which * TILE : (which + 1) * TILE
                ]
                y1, y2 = split(group, ry)
                if group < 2:
                    if y1:
                        sent_refs[group][0, y2, 0] = piece.astype(jnp.bfloat16)
                    else:
                        kept_refs[group][0, y2, 0] = piece
                else:

                    @pl.when(rz == 1)
                    def _(piece=piece, group=group, y1=y1, y2=y2):
                        sent_refs[group][y1, y2, 0] = piece.astype(jnp.bfloat16)

                    @pl.when(rz == 0)
                    def _(piece=piece, group=group, y1=y1, y2=y2):
                        kept_refs[group][y1, y2, 0] = piece


def grad_tiles(tokens, inverse, gain, got, cot_own, cot_got, table):
    rows = tokens.shape[0]
    columns = cot_own.shape[0]
    span = 4 * TILE
    shape = (2, 2, 4, TILE, TILE)
    y_block = (1, 2, 1, TILE, TILE)
    z_block = (2, 2, 1, TILE, TILE)

    def by_y(j, tab):
        return (1 - j // 4, 0, j % 4, 0, 0)

    def sent_z(j, tab):
        return (0, 0, jnp.minimum(j, 3), 0, 0)

    def kept_z(j, tab):
        return (0, 0, jnp.maximum(j - 4, 0), 0, 0)

    def whole(j, tab):
        return (0, 0)

    def rel(j, tab):
        return (0, (1 - j // 4) * 4 + j % 4)

    outs = pl.pallas_call(
        grad_kernel,
        grid_spec=pltpu.PrefetchScalarGridSpec(
            num_scalar_prefetch=1,
            grid=(8,),
            in_specs=[
                pl.BlockSpec((rows, span), lambda j, tab: (0, tab[j])),
                pl.BlockSpec((1, span), lambda j, tab: (0, tab[j])),
                pl.BlockSpec((rows, 1), whole),
                pl.BlockSpec((rows, span), rel),
                pl.BlockSpec((columns, rows), whole),
                pl.BlockSpec((columns, rows), whole),
            ],
            out_specs=[pl.BlockSpec(y_block, by_y)] * 2
            + [pl.BlockSpec(z_block, sent_z)] * 2
            + [pl.BlockSpec(y_block, by_y)] * 2
            + [pl.BlockSpec(z_block, kept_z)] * 2,
            scratch_shapes=[pltpu.VMEM((rows, span), jnp.bfloat16)],
        ),
        out_shape=[jax.ShapeDtypeStruct(shape, jnp.bfloat16)] * GROUPS
        + [jax.ShapeDtypeStruct(shape, jnp.float32)] * GROUPS,
        compiler_params=pltpu.CompilerParams(vmem_limit_bytes=LIMIT),
        cost_estimate=pl.CostEstimate(
            flops=4 * rows * 8 * span * columns,
            bytes_accessed=4 * rows * 8 * span + 6 * GROUPS * 16 * TILE * TILE,
            transcendentals=0,
        ),
    )(table, tokens, gain, inverse, got, cot_own, cot_got)
    return outs[:GROUPS], outs[GROUPS:]


def forward_kernel(tab_ref, tok_ref, inv_ref, gain_ref, cot_ref, *refs, width):
    w_refs, (proj_ref, moment_ref, acc) = refs[:4], refs[4:]
    step = pl.program_id(0)
    inverse = inv_ref[...]

    @pl.when(step == 0)
    def _():
        acc[...] = jnp.zeros_like(acc)

    wide = tok_ref[...].astype(jnp.float32)
    normed = (wide * inverse * gain_ref[...]).astype(jnp.bfloat16)
    for which in range(4):

        @pl.when(step // 4 == which)
        def _(which=which):
            acc[...] += jnp.dot(normed, w_refs[which][0], preferred_element_type=jnp.float32)

    @pl.when(step == pl.num_programs(0) - 1)
    def _():
        keys = acc[...]
        proj_ref[...] = keys.astype(jnp.bfloat16)
        inner = jnp.sum(cot_ref[...].astype(jnp.float32) * keys, axis=1, keepdims=True)
        moment_ref[...] = inverse * inverse * inner / width


def weight_specs(span, columns):
    return [
        pl.BlockSpec((1, span, columns), lambda j, tab, a=a: (jnp.clip(j - 4 * a, 0, 3), 0, 0))
        for a in range(4)
    ]


def forward(tokens, inverse, gain, cotangent, weights, table):
    rows, width = tokens.shape
    columns = cotangent.shape[1]
    span = weights[0].shape[1]

    def whole(j, tab):
        return (0, 0)

    def block(j, tab):
        return (0, tab[j])

    return pl.pallas_call(
        functools.partial(forward_kernel, width=width),
        grid_spec=pltpu.PrefetchScalarGridSpec(
            num_scalar_prefetch=1,
            grid=(width // span,),
            in_specs=[
                pl.BlockSpec((rows, span), block),
                pl.BlockSpec((rows, 1), whole),
                pl.BlockSpec((1, span), block),
                pl.BlockSpec((rows, columns), whole),
            ]
            + weight_specs(span, columns),
            out_specs=[pl.BlockSpec((rows, columns), whole), pl.BlockSpec((rows, 1), whole)],
            scratch_shapes=[pltpu.VMEM((rows, columns), jnp.float32)],
        ),
        out_shape=[
            jax.ShapeDtypeStruct((rows, columns), jnp.bfloat16),
            jax.ShapeDtypeStruct((rows, 1), jnp.float32),
        ],
        compiler_params=pltpu.CompilerParams(vmem_limit_bytes=LIMIT),
        cost_estimate=pl.CostEstimate(
            flops=2 * rows * width * columns,
            bytes_accessed=2 * rows * width + 2 * width * columns,
            transcendentals=0,
        ),
    )(table, tokens, inverse, gain, cotangent, *weights)


def backward_kernel(tab_ref, tok_ref, inv_ref, gain_ref, cot_ref, moment_ref, *refs):
    w_refs, grads_ref = refs[:4], refs[4]
    step = pl.program_id(0)
    for which in range(4):

        @pl.when(step // 4 == which)
        def _(which=which):
            partial = lax.dot_general(
                cot_ref[...],
                w_refs[which][0],
                (((1,), (1,)), ((), ())),
                preferred_element_type=jnp.float32,
            )
            wide = tok_ref[...].astype(jnp.float32)
            grads = inv_ref[...] * gain_ref[...] * partial - wide * moment_ref[...]
            grads_ref[...] = grads.astype(jnp.bfloat16)


def backward(tokens, inverse, gain, cotangent, moment, weights, table):
    rows, width = tokens.shape
    columns = cotangent.shape[1]
    span = weights[0].shape[1]

    def whole(j, tab):
        return (0, 0)

    def block(j, tab):
        return (0, tab[j])

    return pl.pallas_call(
        backward_kernel,
        grid_spec=pltpu.PrefetchScalarGridSpec(
            num_scalar_prefetch=1,
            grid=(width // span,),
            in_specs=[
                pl.BlockSpec((rows, span), block),
                pl.BlockSpec((rows, 1), whole),
                pl.BlockSpec((1, span), block),
                pl.BlockSpec((rows, columns), whole),
                pl.BlockSpec((rows, 1), whole),
            ]
            + weight_specs(span, columns),
            out_specs=pl.BlockSpec((rows, span), block),
        ),
        out_shape=jax.ShapeDtypeStruct((rows, width), jnp.bfloat16),
        compiler_params=pltpu.CompilerParams(vmem_limit_bytes=LIMIT),
        cost_estimate=pl.CostEstimate(
            flops=2 * rows * width * columns,
            bytes_accessed=4 * rows * width + 2 * width * columns,
            transcendentals=0,
        ),
    )(table, tokens, inverse, gain, cotangent, moment, *weights)


def swap(array, axis, mask):
    size = lax.axis_size(axis)
    return lax.ppermute(array, axis, [(i, i ^ mask) for i in range(size)])


def swap_z(array, odd):
    size = lax.axis_size("zh") * lax.axis_size("zl")
    if odd:
        pairs = [(i, (i + 1 if i % 2 else i - 1) % size) for i in range(size)]
    else:
        pairs = [(i, i ^ 1) for i in range(size)]
    return lax.ppermute(array, ("zh", "zl"), pairs)


def halve(total):
    return total[1].astype(jnp.bfloat16), total[0]


def reduce_grads(sent, kept):
    moves = (
        lambda a: swap(a, "y", 1),
        lambda a: swap(a, "y", 3),
        lambda a: swap_z(a, False),
        lambda a: swap_z(a, True),
    )
    for order in ((0, 1, 2, 3), (2, 3, 0, 1)):
        got = [moves[m](s) for m, s in zip(order, sent)]
        totals = [k + g.astype(jnp.float32) for k, g in zip(kept, got)]
        sent, kept = zip(*[halve(t) for t in totals])
    got_even = swap(jnp.stack([sent[0], sent[2]]), "y", 3)
    got_odd = swap(jnp.stack([sent[1], sent[3]]), "y", 1)
    got = (got_even[0], got_odd[0], got_even[1], got_odd[1])
    total = jnp.stack([k + g.astype(jnp.float32) for k, g in zip(kept, got)], axis=1)
    out = total[0]
    for mask in (1, 3, 2):
        out = out + swap(total[mask].astype(jnp.bfloat16), "x", mask).astype(jnp.float32)
    for mask in (1, 3):
        send = out.astype(jnp.bfloat16)
        out = send.astype(jnp.float32) + swap(send, "zh", mask).astype(jnp.float32)
    return out


def gather_weight(own):
    up = swap_z(own, False)
    near, far = swap(own, "x", 1), swap(own, "x", 3)
    up_near, up_far = swap(up, "x", 1), swap(up, "x", 3)
    half = own.shape[0] // 2
    top = swap(jnp.stack([far[:half], up_far[:half]]), "x", 1)
    low = swap(jnp.stack([near[half:], up_near[half:]]), "x", 3)
    first = jnp.stack([own, up, near, far])
    second = jnp.concatenate(
        [up_near[None], up_far[None], jnp.concatenate([top, low], axis=1)], axis=0
    )
    return (first, second, swap(first, "c", 1), swap(second, "c", 1))


ORDER = ((0, 0), (1, 0), (0, 1), (0, 3), (1, 1), (1, 3), (0, 2), (1, 2))


def order_kernel(tab_ref, in_ref, out_ref):
    nodes, quarters = in_ref.shape[:2]
    for node in range(nodes):
        for quarter in range(quarters):
            row = in_ref[tab_ref[node], pl.ds(tab_ref[nodes] ^ quarter, 1)]
            out_ref[node * quarters + quarter, :] = row[0]


def order_rows(rows, table):
    nodes, quarters, lanes = rows.shape
    return pl.pallas_call(
        order_kernel,
        grid_spec=pltpu.PrefetchScalarGridSpec(
            num_scalar_prefetch=1,
            grid=(1,),
            in_specs=[pl.BlockSpec(rows.shape, lambda i, tab: (0, 0, 0))],
            out_specs=pl.BlockSpec((nodes * quarters, lanes), lambda i, tab: (0, 0)),
        ),
        out_shape=jax.ShapeDtypeStruct((nodes * quarters, lanes), rows.dtype),
    )(table.astype(jnp.int32), rows)


def shards(tokens, norm_gain, weight_values, weight_scale, key_cotangent):
    y, zl, x, c = (lax.axis_index(a) for a in ("y", "zl", "x", "c"))
    width = tokens.shape[1]
    columns = weight_values.shape[1]
    gain = norm_gain.reshape(1, width)
    own_weight = widen_weight(weight_values, weight_scale)
    weights = gather_weight(own_weight)
    shards_at = jnp.stack(
        [((zl ^ rz) * 4 + (x ^ rx)) * 2 + (c ^ rc) for rc in (0, 1) for rz, rx in ORDER]
    ).astype(jnp.int32)

    label = jnp.arange(32, dtype=jnp.int32)
    chip = (zl ^ (label // 16)) * 4 + (x ^ (label // 4 % 4))
    other_at = (chip * 2 + 1 - c) * 4 + (y ^ (label % 4))
    own_at = jnp.stack(
        [((zl ^ rz) * 4 + (x ^ rx)) * 2 + c for rz in (1, 0) for rx in range(4)] + [y]
    ).astype(jnp.int32)
    cot_own = key_cotangent.T
    cot_got = swap(cot_own, "c", 1)
    other, inverse = norm_tiles(tokens, gain, other_at)
    got = swap(other, "c", 1)
    sent, kept = grad_tiles(tokens, inverse, gain, got, cot_own, cot_got, own_at)
    devices = 1
    for axis in EVERY:
        devices *= lax.axis_size(axis)
    mine = reduce_grads(sent, kept) / devices

    projected, moment = forward(tokens, inverse, gain, key_cotangent, weights, shards_at)
    token_grads = backward(tokens, inverse, gain, key_cotangent, moment, weights, shards_at)

    mine = mine.reshape(columns, TILE)
    node = (zl * 4 + x) * 2 + c
    my_weight = lax.dynamic_slice_in_dim(own_weight, y * TILE, TILE, 0).T.astype(jnp.float32)
    my_gain = lax.dynamic_slice_in_dim(gain, node * columns + y * TILE, TILE, 1)
    gain_part = jnp.sum(my_weight * mine, axis=0, keepdims=True) / my_gain
    high = gain_part.astype(jnp.bfloat16)
    low = (gain_part - high.astype(jnp.float32)).astype(jnp.bfloat16)
    packed = jnp.concatenate(
        [mine.astype(jnp.bfloat16), high, low, jnp.zeros((14, TILE), jnp.bfloat16)], axis=0
    )
    pieces = [packed] + [swap(packed, "y", mask) for mask in (1, 2, 3)]
    stacked = jnp.stack([p[:columns] for p in pieces])
    ordered = [lax.dynamic_index_in_dim(stacked, y ^ q, 0, keepdims=False) for q in range(4)]
    weight_grads = jnp.concatenate(ordered, axis=1).astype(jnp.float32).T
    tails = jnp.stack([p[columns : columns + 2].astype(jnp.float32) for p in pieces])
    gains = (tails[:, 0] + tails[:, 1])[None]
    gains = jnp.concatenate([gains, swap(gains, "c", 1)])
    gains = jnp.concatenate([gains] + [swap(gains, "x", mask) for mask in (1, 2, 3)])
    gains = jnp.concatenate([gains, swap(gains, "zl", 1)])
    node_at = jnp.arange(16, dtype=jnp.int32)
    table = (node_at // 8 ^ zl) * 8 + (node_at // 2 % 4 ^ x) * 2 + (node_at % 2 ^ c)
    gain_grads = order_rows(gains, jnp.append(table, y)).reshape(width)
    return (projected, token_grads, weight_grads, gain_grads)


def solution(mesh):
    fine = Mesh(mesh.devices.reshape(4, 4, 2, 4, 2), EVERY)
    rows = P(EVERY, None)
    return jax.shard_map(
        shards,
        mesh=fine,
        in_specs=(rows, P(), P(NODE, None), P(NODE, None), rows),
        out_specs=(rows, rows, P(NODE, None), P()),
        check_vma=False,
    )
```

time: 164 us -> 185 us (1.13)
  Pallas kernels: 31 us -> 55.3 us
  between operations: 14.5 us -> 1.26 us
  waiting for transfers between devices: 50.9 us -> 60.5 us
    pallas_call x2 -> x4, Pallas kernels: 25 us -> 48.4 us  [the longest x1 15.8 us: forward(): pl.pallas_call(functools.partial(forward_kernel, width=width), grid_spec=...]
    ppermute x22 -> x29, waiting for transfers between devices: 29.2 us -> 41.3 us  [swap(): return lax.ppermute(array, axis, [(i, i ^ mask) for i in range(size)])]
    ppermute x4 -> x5, waiting for transfers between devices: 21.7 us -> 19.2 us  [swap_z(): return lax.ppermute(array, ('zh', 'zl'), pairs)]
    concatenate x2 -> x3, other arithmetic: 0.02 us -> 2.11 us  [the longest x1 1.5 us: gather_weight(): jnp.concatenate([up_near[None], up_far[None], jnp.concatenate([top, low],...]
    unnamed x37 -> x36, local copies, waits for them, and re-layouts: 5.07 us -> 3.65 us
    ppermute x4 -> x5, starting transfers between devices: 11.4 us -> 11.3 us  [swap_z(): return lax.ppermute(array, ('zh', 'zl'), pairs)]
    ppermute x22 -> x29, starting transfers between devices: 40.6 us -> 40.6 us  [swap(): return lax.ppermute(array, axis, [(i, i ^ mask) for i in range(size)])]
  transfers between devices with their start and end apart: 27 -> 34, of which waited for: 17 -> 19; matrix products, arithmetic and copies ran while one was open for 4% -> 4% of each run, Pallas kernels for 8% -> 25%
where the time goes in v2:
time: 185 us; the launch traced here: 183 us
  waiting for transfers between devices  60.5 us (33%)
  Pallas kernels  55.3 us (30%)
  starting transfers between devices  51.9 us (28%)
  other arithmetic  7.15 us (4%)
  local copies, waits for them, and re-layouts  6.9 us (4%)
    ppermute x29, waiting for transfers between devices, swap(): return lax.ppermute(array, axis, [(i, i ^ mask) for i in range(size)])  41.3 us
    ppermute x29, starting transfers between devices, swap(): return lax.ppermute(array, axis, [(i, i ^ mask) for i in range(size)])  40.6 us
    ppermute x5, waiting for transfers between devices, swap_z(): return lax.ppermute(array, ('zh', 'zl'), pairs)  19.2 us
    pallas_call x1, Pallas kernels, forward(): pl.pallas_call(functools.partial(forward_kernel, width=width), grid_spec=...  15.8 us
    pallas_call x1, Pallas kernels, backward(): pl.pallas_call(backward_kernel, grid_spec=pltpu.PrefetchScalarGridSpec(nu...  15.5 us
    pallas_call x1, Pallas kernels, grad_tiles(): pl.pallas_call(grad_kernel, grid_spec=pltpu.PrefetchScalarGridSpec(num_sc...  15.1 us
    ppermute x5, starting transfers between devices, swap_z(): return lax.ppermute(array, ('zh', 'zl'), pairs)  11.3 us
    pallas_call x1, Pallas kernels, norm_tiles(): pl.pallas_call(norm_kernel, grid_spec=pltpu.PrefetchScalarGridSpec(num_sc...  6.91 us
  transfers between devices with their start and end apart: 34, of which 19 were waited for; matrix products, arithmetic and copies ran while one was open for 4% of the time, Pallas kernels for 25%

profile of v2, /device:TPU:1, one launch (start us, length us, event | category | flops | bytes accessed | tf_op | source)
XLA Modules:
  0.0 183.0 jit_solution(6499911292262645195)
XLA Ops:
  1.4 6.9 %shard_map.84 = (bf16[320,4096]{1,0:T(8,128)(2,1)}, f32[320,1]{1,0:T(8,128)S(1)}) custom-call(s32[32]{0:T(128)S(1)} %fusion.20.tab_ref, bf16[320,8192]{1,0:T(8,128)(2,1)} %tok_ref.7, f32[1,8192]{1,0:T(1,128)S(1)} %bitcast.139), custom_call_target="tpu_custom_call" | custom-call | flops 15728640 | bytes 7864320 | tf_op jit(solution)/shard_map/pallas_call | solution.py:48
  8.3 3.2 %collective-permute-start.9 = (bf16[320,4096]{1,0:T(8,128)(2,1)}, bf16[320,4096]{1,0:T(8,128)(2,1)}, u32[]{:S(2)}, u32[]{:S(2)}) collective-permute-start(bf16[320,4096]{1,0:T(8,128)(2,1)} %get-tuple-element.19), channel_id=1, source_target_pairs={{0,1},{1,0},{2,3},{3,2},{4,5},{5,4},{6,7},{7,6},{8,9},{9,8},{10,11... | collective-permute-start | bytes 7864328 | tf_op jit(solution)/shard_map/ppermute | solution.py:297
  12.7 2.4 %collective-permute-start.2 = (bf16[512,512]{1,0:T(8,128)(2,1)S(1)}, bf16[512,512]{1,0:T(8,128)(2,1)S(1)}, u32[]{:S(2)}, u32[]{:S(2)}) collective-permute-start(bf16[512,512]{1,0:T(8,128)(2,1)S(1)} %fusion), channel_id=1, source_target_pairs={{0,6},{2,4},{4,2},{6,0},{1,7},{3,5},{5,3},{7,1},{8,14},{10,12},{12... | collective-permute-start | bytes 1572872 | tf_op jit(solution)/shard_map/ppermute | solution.py:297
  15.0 11.3 %collective-permute-done = bf16[512,512]{1,0:T(8,128)(2,1)} collective-permute-done((bf16[512,512]{1,0:T(8,128)(2,1)S(1)}, bf16[512,512]{1,0:T(8,128)(2,1)}, u32[]{:S(2)}, u32[]{:S(2)}) %collective-permute-start) | collective-permute-done | bytes 524320 | tf_op jit(solution)/shard_map/ppermute | solution.py:306
  28.9 11.5 %collective-permute-done.4 = bf16[512,512]{1,0:T(8,128)(2,1)S(1)} collective-permute-done((bf16[512,512]{1,0:T(8,128)(2,1)}, bf16[512,512]{1,0:T(8,128)(2,1)S(1)}, u32[]{:S(2)}, u32[]{:S(2)}) %collective-permute-start.4) | collective-permute-done | bytes 524320 | tf_op jit(solution)/shard_map/ppermute | solution.py:297
  40.6 1.9 %collective-permute-done.3 = bf16[512,512]{1,0:T(8,128)(2,1)S(1)} collective-permute-done((bf16[512,512]{1,0:T(8,128)(2,1)}, bf16[512,512]{1,0:T(8,128)(2,1)S(1)}, u32[]{:S(2)}, u32[]{:S(2)}) %collective-permute-start.3) | collective-permute-done | bytes 524320 | tf_op jit(solution)/shard_map/ppermute | solution.py:297
  44.4 15.1 %shard_map.87 = (bf16[2,2,4,128,128]{4,3,2,1,0:T(8,128)(2,1)S(1)}, bf16[2,2,4,128,128]{4,3,2,1,0:T(8,128)(2,1)S(1)}, bf16[2,2,4,128,128]{4,3,2,1,0:T(8,128)(2,1)...) custom-call(s32[9]{0:T(128)S(1)} %stack.176.tab_ref, ...), custom_call_target="tpu_custom_call" | custom-call | flops 2684354560 | bytes 11534336 | tf_op jit(solution)/shard_map/pallas_call | solution.py:139
  65.4 4.7 %collective-permute-start.18 = (bf16[2,2,4,128,128]{4,3,2,1,0:T(8,128)(2,1)S(1)}, bf16[2,2,4,128,128]{4,3,2,1,0:T(8,128)(2,1)S(1)}, u32[]{:S(2)}, u32[]{:S(2)}) collective-permute-start(bf16[2,2,4,128,128]{4,3,2,1,0:T(8,128)(2,1)S(1)} %get-tuple-element.27), channel_id=1, source_target_pairs={{0,56},{8,16},{16,8},{24,32},{32,24},{40,48},{48,40},{56,0},{1,57}... | collective-permute-start | bytes 1572872 | tf_op jit(solution)/shard_map/ppermute | solution.py:306
  72.4 4.8 %collective-permute-done.11 = bf16[2,2,4,128,128]{4,3,2,1,0:T(8,128)(2,1)S(1)} collective-permute-done((bf16[2,2,4,128,128]{4,3,2,1,0:T(8,128)(2,1)S(1)}, bf16[2,2,4,128,128]{4,3,2,1,0:T(8,128)(2,1)S(1)}, u32[]{:S(2)}, u32[]{:S(2)}) %collective-permute-start.11) | collective-permute-done | bytes 524320 | tf_op jit(solution)/shard_map/ppermute | solution.py:297
  78.6 3.0 %collective-permute-done.18 = bf16[2,2,4,128,128]{4,3,2,1,0:T(8,128)(2,1)S(1)} collective-permute-done((bf16[2,2,4,128,128]{4,3,2,1,0:T(8,128)(2,1)S(1)}, bf16[2,2,4,128,128]{4,3,2,1,0:T(8,128)(2,1)S(1)}, u32[]{:S(2)}, u32[]{:S(2)}) %collective-permute-start.18) | collective-permute-done | bytes 524320 | tf_op jit(solution)/shard_map/ppermute | solution.py:306
  81.8 2.3 %collective-permute-done.16 = bf16[2,2,4,128,128]{4,3,2,1,0:T(8,128)(2,1)S(1)} collective-permute-done((bf16[2,2,4,128,128]{4,3,2,1,0:T(8,128)(2,1)S(1)}, bf16[2,2,4,128,128]{4,3,2,1,0:T(8,128)(2,1)S(1)}, u32[]{:S(2)}, u32[]{:S(2)}) %collective-permute-start.16) | collective-permute-done | bytes 524320 | tf_op jit(solution)/shard_map/ppermute | solution.py:297
  84.4 6.5 %collective-permute-start.17 = (bf16[2,4,128,128]{3,2,1,0:T(8,128)(2,1)S(1)}, bf16[2,4,128,128]{3,2,1,0:T(8,128)(2,1)S(1)}, u32[]{:S(2)}, u32[]{:S(2)}) collective-permute-start(bf16[2,4,128,128]{3,2,1,0:T(8,128)(2,1)S(1)} %fusion.7), channel_id=1, source_target_pairs={{0,56},{8,16},{16,8},{24,32},{32,24},{40,48},{48,40},{56,0},{1,57}... | collective-permute-start | bytes 786440 | tf_op jit(solution)/shard_map/ppermute | solution.py:306
  91.3 3.2 %collective-permute-done.17 = bf16[2,4,128,128]{3,2,1,0:T(8,128)(2,1)S(1)} collective-permute-done((bf16[2,4,128,128]{3,2,1,0:T(8,128)(2,1)S(1)}, bf16[2,4,128,128]{3,2,1,0:T(8,128)(2,1)S(1)}, u32[]{:S(2)}, u32[]{:S(2)}) %collective-permute-start.17) | collective-permute-done | bytes 262176 | tf_op jit(solution)/shard_map/ppermute | solution.py:306
  94.8 3.0 %collective-permute-done.15 = bf16[2,4,128,128]{3,2,1,0:T(8,128)(2,1)S(1)} collective-permute-done((bf16[2,4,128,128]{3,2,1,0:T(8,128)(2,1)S(1)}, bf16[2,4,128,128]{3,2,1,0:T(8,128)(2,1)S(1)}, u32[]{:S(2)}, u32[]{:S(2)}) %collective-permute-start.15) | collective-permute-done | bytes 262176 | tf_op jit(solution)/shard_map/ppermute | solution.py:297
  97.9 2.4 %collective-permute-done.20 = bf16[2,4,128,128]{3,2,1,0:T(8,128)(2,1)S(1)} collective-permute-done((bf16[2,4,128,128]{3,2,1,0:T(8,128)(2,1)S(1)}, bf16[2,4,128,128]{3,2,1,0:T(8,128)(2,1)S(1)}, u32[]{:S(2)}, u32[]{:S(2)}) %collective-permute-start.20) | collective-permute-done | bytes 262176 | tf_op jit(solution)/shard_map/ppermute | solution.py:297
  100.6 2.2 %collective-permute-start.22 = (bf16[4,128,128]{2,1,0:T(8,128)(2,1)S(1)}, bf16[4,128,128]{2,1,0:T(8,128)(2,1)S(1)}, u32[]{:S(2)}, u32[]{:S(2)}) collective-permute-start(bf16[4,128,128]{2,1,0:T(8,128)(2,1)S(1)} %get-tuple-element.50), channel_id=1, source_target_pairs={{0,6},{2,4},{4,2},{6,0},{1,7},{3,5},{5,3},{7,1},{8,14},{10,12},{12... | collective-permute-start | bytes 393224 | tf_op jit(solution)/shard_map/ppermute | solution.py:297
  106.1 2.0 %collective-permute-done.23 = bf16[4,128,128]{2,1,0:T(8,128)(2,1)S(1)} collective-permute-done((bf16[4,128,128]{2,1,0:T(8,128)(2,1)S(1)}, bf16[4,128,128]{2,1,0:T(8,128)(2,1)S(1)}, u32[]{:S(2)}, u32[]{:S(2)}) %collective-permute-start.23) | collective-permute-done | bytes 131104 | tf_op jit(solution)/shard_map/ppermute | solution.py:297
  109.1 5.1 %collective-permute-done.24 = bf16[4,128,128]{2,1,0:T(8,128)(2,1)S(1)} collective-permute-done((bf16[4,128,128]{2,1,0:T(8,128)(2,1)S(1)}, bf16[4,128,128]{2,1,0:T(8,128)(2,1)S(1)}, u32[]{:S(2)}, u32[]{:S(2)}) %collective-permute-start.24) | collective-permute-done | bytes 131104 | tf_op jit(solution)/shard_map/ppermute | solution.py:297
  115.6 15.8 %shard_map.85 = (bf16[320,512]{1,0:T(8,128)(2,1)}, f32[320,1]{1,0:T(8,128)S(1)}) custom-call(s32[16]{0:T(128)S(1)} %stack.163.tab_ref, bf16[320,8192]{1,0:T(8,128)(2,1)} %tok_ref.7, f32[320,1]{1,0:T(8,128)S(1)} %get-tuple-element.16.inv_ref, f32[1,8192]{1,0:T(1,128)S(1)} %bitcast.141, bf16[320,512]{1,0:T(8,128)(2,1)S(1)} %copy-done, ...), custom_call_target="tpu_custom_call" | custom-call | flops 2684354560 | bytes 13631488 | tf_op jit(solution)/shard_map/pallas_call | solution.py:213
  136.0 15.5 %shard_map.86 = bf16[320,8192]{1,0:T(8,128)(2,1)} custom-call(s32[16]{0:T(128)S(1)} %stack.163.tab_ref, bf16[320,8192]{1,0:T(8,128)(2,1)} %tok_ref.7, f32[320,1]{1,0:T(8,128)S(1)} %get-tuple-element.16.inv_ref, f32[1,8192]{1,0:T(1,128)S(1)} %bitcast.142, bf16[320,512]{1,0:T(8,128)(2,1)S(1)} %copy-done, f32[320,1]{1,0:T(8,128)S(1)} %get-tuple-element.18.moment_ref, ...), custom_call_target="tpu_custom_call" | custom-call | flops 2684354560 | bytes 18874368 | tf_op jit(solution)/shard_map/pallas_call | solution.py:270
  151.4 2.2 %collective-permute-start.27 = (bf16[528,128]{1,0:T(8,128)(2,1)S(1)}, bf16[528,128]{1,0:T(8,128)(2,1)S(1)}, u32[]{:S(2)}, u32[]{:S(2)}) collective-permute-start(bf16[528,128]{1,0:T(8,128)(2,1)S(1)} %maximum_maximum_fusion.1), channel_id=1, source_target_pairs={{0,128},{64,192},{128,0},{192,64},{1,129},{65,193},{129,1},{193,65... | collective-permute-start | bytes 405512 | tf_op jit(solution)/shard_map/ppermute | solution.py:297
  158.8 11.3 %collective-permute-start.29 = (f32[1,4,128]{2,1,0:T(4,128)S(1)}, f32[1,4,128]{2,1,0:T(4,128)S(1)}, u32[]{:S(2)}, u32[]{:S(2)}) collective-permute-start(f32[1,4,128]{2,1,0:T(4,128)S(1)} %get-tuple-element.41), channel_id=1, source_target_pairs={{0,1},{1,0},{2,3},{3,2},{4,5},{5,4},{6,7},{7,6},{8,9},{9,8},{10,11... | collective-permute-start | bytes 6152 | tf_op jit(solution)/shard_map/ppermute | solution.py:297
  176.9 2.0 %collective-permute-start.33 = (f32[8,4,128]{2,1,0:T(4,128)S(1)}, f32[8,4,128]{2,1,0:T(4,128)S(1)}, u32[]{:S(2)}, u32[]{:S(2)}) collective-permute-start(f32[8,4,128]{2,1,0:T(4,128)S(1)} %get-tuple-element.57), channel_id=1, source_target_pairs={{0,8},{8,0},{1,9},{9,1},{2,10},{10,2},{3,11},{11,3},{4,12},{12,4},... | collective-permute-start | bytes 49160 | tf_op jit(solution)/shard_map/ppermute | solution.py:297
  181.0 2.1 %shard_map.88 = f32[64,128]{1,0:T(8,128)} custom-call(s32[17]{0:T(128)} %pad_add_fusion.tab_ref, f32[16,4,128]{2,1,0:T(4,128)} %copy-done.13), custom_call_target="tpu_custom_call" | custom-call | tf_op jit(solution)/shard_map/pallas_call | solution.py:364
  (152 shorter events, 41.4 us)
Async XLA Ops:
  8.3 36.1 %collective-permute-start.9 = (bf16[320,4096]{1,0:T(8,128)(2,1)}, bf16[320,4096]{1,0:T(8,128)(2,1)}, u32[]{:S(2)}, u32[]{:S(2)}) collective-permute-start(bf16[320,4096]{1,0:T(8,128)(2,1)} %get-tuple-element.19), channel_id=1, source_target_pairs={{0,1},{1,0},{2,3},{3,2},{4,5},{5,4},{6,7},{7,6},{8,9},{9,8},{10,11... | collective-permute-start | bytes 7864328 | tf_op jit(solution)/shard_map/ppermute | solution.py:297
  12.5 13.7 %collective-permute-start = (bf16[512,512]{1,0:T(8,128)(2,1)S(1)}, bf16[512,512]{1,0:T(8,128)(2,1)}, u32[]{:S(2)}, u32[]{:S(2)}) collective-permute-start(bf16[512,512]{1,0:T(8,128)(2,1)S(1)} %fusion), channel_id=1, source_target_pairs={{0,8},{8,0},{16,24},{24,16},{32,40},{40,32},{48,56},{56,48},{1,9},... | collective-permute-start | bytes 1572872 | tf_op jit(solution)/shard_map/ppermute | solution.py:306
  12.7 16.0 %collective-permute-start.2 = (bf16[512,512]{1,0:T(8,128)(2,1)S(1)}, bf16[512,512]{1,0:T(8,128)(2,1)S(1)}, u32[]{:S(2)}, u32[]{:S(2)}) collective-permute-start(bf16[512,512]{1,0:T(8,128)(2,1)S(1)} %fusion), channel_id=1, source_target_pairs={{0,6},{2,4},{4,2},{6,0},{1,7},{3,5},{5,3},{7,1},{8,14},{10,12},{12... | collective-permute-start | bytes 1572872 | tf_op jit(solution)/shard_map/ppermute | solution.py:297
  15.0 13.8 %collective-permute-start.1 = (bf16[512,512]{1,0:T(8,128)(2,1)S(1)}, bf16[512,512]{1,0:T(8,128)(2,1)S(1)}, u32[]{:S(2)}, u32[]{:S(2)}) collective-permute-start(bf16[512,512]{1,0:T(8,128)(2,1)S(1)} %fusion), channel_id=1, source_target_pairs={{0,2},{2,0},{4,6},{6,4},{1,3},{3,1},{5,7},{7,5},{8,10},{10,8},{12,... | collective-permute-start | bytes 1572872 | tf_op jit(solution)/shard_map/ppermute | solution.py:297
  26.3 14.1 %collective-permute-start.4 = (bf16[512,512]{1,0:T(8,128)(2,1)}, bf16[512,512]{1,0:T(8,128)(2,1)S(1)}, u32[]{:S(2)}, u32[]{:S(2)}) collective-permute-start(bf16[512,512]{1,0:T(8,128)(2,1)} %collective-permute-done), channel_id=1, source_target_pairs={{0,6},{2,4},{4,2},{6,0},{1,7},{3,5},{5,3},{7,1},{8,14},{10,12},{12... | collective-permute-start | bytes 1572872 | tf_op jit(solution)/shard_map/ppermute | solution.py:297
  27.5 16.9 %collective-permute-start.10 = (bf16[512,320]{1,0:T(8,128)(2,1)S(1)}, bf16[512,320]{1,0:T(8,128)(2,1)S(1)}, u32[]{:S(2)}, u32[]{:S(2)}) collective-permute-start(bf16[512,320]{1,0:T(8,128)(2,1)S(1)} %bitcast.137), channel_id=1, source_target_pairs={{0,1},{1,0},{2,3},{3,2},{4,5},{5,4},{6,7},{7,6},{8,9},{9,8},{10,11... | collective-permute-start | bytes 983048 | tf_op jit(solution)/shard_map/ppermute | solution.py:297
  28.7 13.8 %collective-permute-start.3 = (bf16[512,512]{1,0:T(8,128)(2,1)}, bf16[512,512]{1,0:T(8,128)(2,1)S(1)}, u32[]{:S(2)}, u32[]{:S(2)}) collective-permute-start(bf16[512,512]{1,0:T(8,128)(2,1)} %collective-permute-done), channel_id=1, source_target_pairs={{0,2},{2,0},{4,6},{6,4},{1,3},{3,1},{5,7},{7,5},{8,10},{10,8},{12,... | collective-permute-start | bytes 1572872 | tf_op jit(solution)/shard_map/ppermute | solution.py:297
  40.5 22.2 %collective-permute-start.5 = (bf16[2,256,512]{2,1,0:T(8,128)(2,1)S(1)}, bf16[2,256,512]{2,1,0:T(8,128)(2,1)S(1)}, u32[]{:S(2)}, u32[]{:S(2)}) collective-permute-start(bf16[2,256,512]{2,1,0:T(8,128)(2,1)S(1)} %pad_maximum_fusion.2), channel_id=1, source_target_pairs={{0,2},{2,0},{4,6},{6,4},{1,3},{3,1},{5,7},{7,5},{8,10},{10,8},{12,... | collective-permute-start | bytes 1572872 | tf_op jit(solution)/shard_map/ppermute | solution.py:297
  42.6 20.0 %collective-permute-start.6 = (bf16[2,256,512]{2,1,0:T(8,128)(2,1)S(1)}, bf16[2,256,512]{2,1,0:T(8,128)(2,1)S(1)}, u32[]{:S(2)}, u32[]{:S(2)}) collective-permute-start(bf16[2,256,512]{2,1,0:T(8,128)(2,1)S(1)} %pad_maximum_fusion.3), channel_id=1, source_target_pairs={{0,6},{2,4},{4,2},{6,0},{1,7},{3,5},{5,3},{7,1},{8,14},{10,12},{12... | collective-permute-start | bytes 1572872 | tf_op jit(solution)/shard_map/ppermute | solution.py:297
  59.5 12.2 %collective-permute-start.13 = (bf16[2,2,4,128,128]{4,3,2,1,0:T(8,128)(2,1)S(1)}, bf16[2,2,4,128,128]{4,3,2,1,0:T(8,128)(2,1)S(1)}, u32[]{:S(2)}, u32[]{:S(2)}) collective-permute-start(bf16[2,2,4,128,128]{4,3,2,1,0:T(8,128)(2,1)S(1)} %get-tuple-element.23), channel_id=1, source_target_pairs={{0,8},{8,0},{16,24},{24,16},{32,40},{40,32},{48,56},{56,48},{1,9},... | collective-permute-start | bytes 1572872 | tf_op jit(solution)/shard_map/ppermute | solution.py:306
  61.1 54.4 %collective-permute-start.7 = (bf16[4,512,512]{2,1,0:T(8,128)(2,1)S(1)}, bf16[4,512,512]{2,1,0:T(8,128)(2,1)}, u32[]{:S(2)}, u32[]{:S(2)}) collective-permute-start(bf16[4,512,512]{2,1,0:T(8,128)(2,1)S(1)} %pad_maximum_fusion.refs_0_), channel_id=1, source_target_pairs={{0,1},{1,0},{2,3},{3,2},{4,5},{5,4},{6,7},{7,6},{8,9},{9,8},{10,11... | collective-permute-start | bytes 6291464 | tf_op jit(solution)/shard_map/ppermute | solution.py:297
  64.1 51.4 %collective-permute-start.8 = (bf16[4,512,512]{2,1,0:T(8,128)(2,1)}, bf16[4,512,512]{2,1,0:T(8,128)(2,1)}, u32[]{:S(2)}, u32[]{:S(2)}) collective-permute-start(bf16[4,512,512]{2,1,0:T(8,128)(2,1)} %maximum_maximum_fusion.refs_1_), channel_id=1, source_target_pairs={{0,1},{1,0},{2,3},{3,2},{4,5},{5,4},{6,7},{7,6},{8,9},{9,8},{10,11... | collective-permute-start | bytes 6291464 | tf_op jit(solution)/shard_map/ppermute | solution.py:297
  64.2 13.0 %collective-permute-start.11 = (bf16[2,2,4,128,128]{4,3,2,1,0:T(8,128)(2,1)S(1)}, bf16[2,2,4,128,128]{4,3,2,1,0:T(8,128)(2,1)S(1)}, u32[]{:S(2)}, u32[]{:S(2)}) collective-permute-start(bf16[2,2,4,128,128]{4,3,2,1,0:T(8,128)(2,1)S(1)} %get-tuple-element.21), channel_id=1, source_target_pairs={{0,64},{64,0},{128,192},{192,128},{1,65},{65,1},{129,193},{193,129... | collective-permute-start | bytes 1572872 | tf_op jit(solution)/shard_map/ppermute | solution.py:297
  65.4 16.2 %collective-permute-start.18 = (bf16[2,2,4,128,128]{4,3,2,1,0:T(8,128)(2,1)S(1)}, bf16[2,2,4,128,128]{4,3,2,1,0:T(8,128)(2,1)S(1)}, u32[]{:S(2)}, u32[]{:S(2)}) collective-permute-start(bf16[2,2,4,128,128]{4,3,2,1,0:T(8,128)(2,1)S(1)} %get-tuple-element.27), channel_id=1, source_target_pairs={{0,56},{8,16},{16,8},{24,32},{32,24},{40,48},{48,40},{56,0},{1,57}... | collective-permute-start | bytes 1572872 | tf_op jit(solution)/shard_map/ppermute | solution.py:306
  71.7 12.4 %collective-permute-start.16 = (bf16[2,2,4,128,128]{4,3,2,1,0:T(8,128)(2,1)S(1)}, bf16[2,2,4,128,128]{4,3,2,1,0:T(8,128)(2,1)S(1)}, u32[]{:S(2)}, u32[]{:S(2)}) collective-permute-start(bf16[2,2,4,128,128]{4,3,2,1,0:T(8,128)(2,1)S(1)} %get-tuple-element.25), channel_id=1, source_target_pairs={{0,192},{64,128},{128,64},{192,0},{1,193},{65,129},{129,65},{193,1... | collective-permute-start | bytes 1572872 | tf_op jit(solution)/shard_map/ppermute | solution.py:297
  77.2 7.2 %collective-permute-start.14 = (bf16[2,4,128,128]{3,2,1,0:T(8,128)(2,1)S(1)}, bf16[2,4,128,128]{3,2,1,0:T(8,128)(2,1)S(1)}, u32[]{:S(2)}, u32[]{:S(2)}) collective-permute-start(bf16[2,4,128,128]{3,2,1,0:T(8,128)(2,1)S(1)} %fusion.6), channel_id=1, source_target_pairs={{0,64},{64,0},{128,192},{192,128},{1,65},{65,1},{129,193},{193,129... | collective-permute-start | bytes 786440 | tf_op jit(solution)/shard_map/ppermute | solution.py:297
  81.6 9.3 %collective-permute-start.12 = (bf16[2,4,128,128]{3,2,1,0:T(8,128)(2,1)S(1)}, bf16[2,4,128,128]{3,2,1,0:T(8,128)(2,1)S(1)}, u32[]{:S(2)}, u32[]{:S(2)}) collective-permute-start(bf16[2,4,128,128]{3,2,1,0:T(8,128)(2,1)S(1)} %fusion.5), channel_id=1, source_target_pairs={{0,8},{8,0},{16,24},{24,16},{32,40},{40,32},{48,56},{56,48},{1,9},... | collective-permute-start | bytes 786440 | tf_op jit(solution)/shard_map/ppermute | solution.py:306
  84.0 7.2 %collective-permute-start.19 = (bf16[2,4,128,128]{3,2,1,0:T(8,128)(2,1)S(1)}, bf16[2,4,128,128]{3,2,1,0:T(8,128)(2,1)S(1)}, u32[]{:S(2)}, u32[]{:S(2)}) collective-permute-start(bf16[2,4,128,128]{3,2,1,0:T(8,128)(2,1)S(1)} %fusion.8), channel_id=1, source_target_pairs={{0,192},{64,128},{128,64},{192,0},{1,193},{65,129},{129,65},{193,1... | collective-permute-start | bytes 786440 | tf_op jit(solution)/shard_map/ppermute | solution.py:297
  84.4 10.2 %collective-permute-start.17 = (bf16[2,4,128,128]{3,2,1,0:T(8,128)(2,1)S(1)}, bf16[2,4,128,128]{3,2,1,0:T(8,128)(2,1)S(1)}, u32[]{:S(2)}, u32[]{:S(2)}) collective-permute-start(bf16[2,4,128,128]{3,2,1,0:T(8,128)(2,1)S(1)} %fusion.7), channel_id=1, source_target_pairs={{0,56},{8,16},{16,8},{24,32},{32,24},{40,48},{48,40},{56,0},{1,57}... | collective-permute-start | bytes 786440 | tf_op jit(solution)/shard_map/ppermute | solution.py:306
  91.0 6.8 %collective-permute-start.15 = (bf16[2,4,128,128]{3,2,1,0:T(8,128)(2,1)S(1)}, bf16[2,4,128,128]{3,2,1,0:T(8,128)(2,1)S(1)}, u32[]{:S(2)}, u32[]{:S(2)}) collective-permute-start(bf16[2,4,128,128]{3,2,1,0:T(8,128)(2,1)S(1)} %pad_maximum_fusion.5), channel_id=1, source_target_pairs={{0,192},{64,128},{128,64},{192,0},{1,193},{65,129},{129,65},{193,1... | collective-permute-start | bytes 786440 | tf_op jit(solution)/shard_map/ppermute | solution.py:297
  108.1 6.0 %collective-permute-start.24 = (bf16[4,128,128]{2,1,0:T(8,128)(2,1)S(1)}, bf16[4,128,128]{2,1,0:T(8,128)(2,1)S(1)}, u32[]{:S(2)}, u32[]{:S(2)}) collective-permute-start(bf16[4,128,128]{2,1,0:T(8,128)(2,1)S(1)} %fusion.12), channel_id=1, source_target_pairs={{0,16},{16,0},{32,48},{48,32},{1,17},{17,1},{33,49},{49,33},{2,18}... | collective-permute-start | bytes 393224 | tf_op jit(solution)/shard_map/ppermute | solution.py:297
  114.2 17.1 %collective-permute-start.25 = (bf16[4,128,128]{2,1,0:T(8,128)(2,1)S(1)}, bf16[4,128,128]{2,1,0:T(8,128)(2,1)S(1)}, u32[]{:S(2)}, u32[]{:S(2)}) collective-permute-start(bf16[4,128,128]{2,1,0:T(8,128)(2,1)S(1)} %add_convert_fusion), channel_id=1, source_target_pairs={{0,48},{16,32},{32,16},{48,0},{1,49},{17,33},{33,17},{49,1},{2,50}... | collective-permute-start | bytes 393224 | tf_op jit(solution)/shard_map/ppermute | solution.py:297
  135.9 19.4 %collective-permute-start.26 = (bf16[528,128]{1,0:T(8,128)(2,1)S(1)}, bf16[528,128]{1,0:T(8,128)(2,1)S(1)}, u32[]{:S(2)}, u32[]{:S(2)}) collective-permute-start(bf16[528,128]{1,0:T(8,128)(2,1)S(1)} %maximum_maximum_fusion.1), channel_id=1, source_target_pairs={{0,64},{64,0},{128,192},{192,128},{1,65},{65,1},{129,193},{193,129... | collective-permute-start | bytes 405512 | tf_op jit(solution)/shard_map/ppermute | solution.py:297
  158.8 12.1 %collective-permute-start.29 = (f32[1,4,128]{2,1,0:T(4,128)S(1)}, f32[1,4,128]{2,1,0:T(4,128)S(1)}, u32[]{:S(2)}, u32[]{:S(2)}) collective-permute-start(f32[1,4,128]{2,1,0:T(4,128)S(1)} %get-tuple-element.41), channel_id=1, source_target_pairs={{0,1},{1,0},{2,3},{3,2},{4,5},{5,4},{6,7},{7,6},{8,9},{9,8},{10,11... | collective-permute-start | bytes 6152 | tf_op jit(solution)/shard_map/ppermute | solution.py:297
  (25 other events, 239.1 us)

commit v3 on v1

v3 whole, which is shorter than its diff:
```python
import functools

import jax
import jax.numpy as jnp
from jax import lax
from jax.experimental import pallas as pl
from jax.experimental.pallas import tpu as pltpu
from jax.sharding import Mesh, PartitionSpec as P

NODE = ("zl", "x", "c")
EVERY = ("y", "zh", "zl", "x", "c")
TILE = 128
GROUPS = 4
Y_MASKS = ((1, 3), (3, 1), (1, 3), (3, 1))
LIMIT = 48 * 2**20


def widen_kernel(values_ref, scales_ref, out_ref):
    blocks = scales_ref.shape[1]
    block = values_ref.shape[1] // blocks
    for k in range(blocks):
        part = slice(k * block, (k + 1) * block)
        wide = values_ref[:, part].astype(jnp.float32)
        scale = scales_ref[:, k : k + 1].astype(jnp.float32)
        out_ref[:, part] = (wide * scale).astype(jnp.bfloat16)


def widen_weight(values, scales):
    return pl.pallas_call(
        widen_kernel, out_shape=jax.ShapeDtypeStruct(values.shape, jnp.bfloat16)
    )(values, scales)


def norm_kernel(tab_ref, tok_ref, gain_ref, own_ref, oth_ref, inv_ref):
    rows, width = tok_ref.shape
    total = jnp.zeros((rows, TILE), jnp.float32)
    for t in range(width // TILE):
        wide = tok_ref[:, t * TILE : (t + 1) * TILE].astype(jnp.float32)
        total = total + wide * wide
    mean = jnp.sum(total, axis=1, keepdims=True) / width
    inverse = lax.rsqrt(mean + 1e-05)
    inv_ref[...] = inverse
    for side, out_ref in enumerate((own_ref, oth_ref)):
        for r in range(width // TILE // 2):
            at = pl.multiple_of(tab_ref[side, r] * TILE, TILE)
            wide = tok_ref[:, pl.ds(at, TILE)].astype(jnp.float32)
            scaled = wide * inverse * gain_ref[:, pl.ds(at, TILE)]
            out_ref[:, r * TILE : (r + 1) * TILE] = scaled.astype(jnp.bfloat16)


def norm_tiles(tokens, gain, table):
    rows, width = tokens.shape
    step = 64 if rows % 64 == 0 else rows
    half = pl.BlockSpec((step, width // 2), lambda i, tab: (i, 0))
    return pl.pallas_call(
        norm_kernel,
        grid_spec=pltpu.PrefetchScalarGridSpec(
            num_scalar_prefetch=1,
            grid=(rows // step,),
            in_specs=[
                pl.BlockSpec((step, width), lambda i, tab: (i, 0)),
                pl.BlockSpec((1, width), lambda i, tab: (0, 0)),
            ],
            out_specs=[half, half, pl.BlockSpec((step, 1), lambda i, tab: (i, 0))],
        ),
        out_shape=[
            jax.ShapeDtypeStruct((rows, width // 2), jnp.bfloat16),
            jax.ShapeDtypeStruct((rows, width // 2), jnp.bfloat16),
            jax.ShapeDtypeStruct((rows, 1), jnp.float32),
        ],
        compiler_params=pltpu.CompilerParams(vmem_limit_bytes=LIMIT),
        cost_estimate=pl.CostEstimate(
            flops=6 * rows * width, bytes_accessed=4 * rows * width, transcendentals=rows
        ),
    )(table, tokens, gain)


def place(group, rz, ry, rx):
    first, second = Y_MASKS[group]
    y1, y2 = next(
        (a, b) for a in (0, 1) for b in (0, 1) if (a * first) ^ (b * second) == ry
    )
    if group < 2:
        return y1, (rz * 2 + y2) * 4 + rx
    return rz, (y1 * 2 + y2) * 4 + rx


def grad_kernel(own_ref, got_ref, cot_own_ref, cot_got_ref, *out_refs):
    span = 2 * TILE
    cot_own = cot_own_ref[...]
    cot_got = cot_got_ref[...]
    for pair in range(own_ref.shape[1] // span):
        part = slice(pair * span, (pair + 1) * span)
        grads = jnp.dot(cot_own, own_ref[:, part], preferred_element_type=jnp.float32)
        grads += jnp.dot(cot_got, got_ref[:, part], preferred_element_type=jnp.float32)
        for which in range(2):
            tile = pair * 2 + which
            for group in range(GROUPS):
                piece = grads[
                    group * TILE : (group + 1) * TILE, which * TILE : (which + 1) * TILE
                ]
                sent, at = place(group, tile // 16, tile // 4 % 4, tile % 4)
                if sent:
                    out_refs[group][at] = piece.astype(jnp.bfloat16)
                else:
                    out_refs[GROUPS + group][at] = piece


def grad_tiles(own, got, cot_own, cot_got):
    rows, width = own.shape
    tiles = width // TILE // 2
    shape = (tiles, TILE, TILE)
    outs = pl.pallas_call(
        grad_kernel,
        out_shape=[jax.ShapeDtypeStruct(shape, jnp.bfloat16)] * GROUPS
        + [jax.ShapeDtypeStruct(shape, jnp.float32)] * GROUPS,
        compiler_params=pltpu.CompilerParams(vmem_limit_bytes=LIMIT),
        cost_estimate=pl.CostEstimate(
            flops=4 * rows * width * GROUPS * TILE,
            bytes_accessed=4 * rows * width + 6 * GROUPS * tiles * TILE * TILE,
            transcendentals=0,
        ),
    )(own, got, cot_own, cot_got)
    return outs[:GROUPS], outs[GROUPS:]


def forward_kernel(tab_ref, tok_ref, inv_ref, gain_ref, cot_ref, *refs):
    w_refs, (proj_ref, moment_ref, acc) = refs[:-3], refs[-3:]
    inverse = inv_ref[...]
    acc[...] = jnp.zeros_like(acc)
    for k, (slot, pieces) in enumerate(PIECES):
        span = tok_ref.shape[1] // len(PIECES)
        at = pl.multiple_of(tab_ref[k] * span, span)
        wide = tok_ref[:, pl.ds(at, span)].astype(jnp.float32)
        normed = (wide * inverse * gain_ref[:, pl.ds(at, span)]).astype(jnp.bfloat16)
        part = span // len(pieces)
        for h, which in enumerate(pieces):
            acc[...] += jnp.dot(
                normed[:, h * part : (h + 1) * part],
                w_refs[which][slot],
                preferred_element_type=jnp.float32,
            )
    keys = acc[...]
    proj_ref[...] = keys.astype(jnp.bfloat16)
    inner = jnp.sum(cot_ref[...].astype(jnp.float32) * keys, axis=1, keepdims=True)
    moment_ref[...] = inverse * inverse * inner / tok_ref.shape[1]


def backward_kernel(tab_ref, tok_ref, inv_ref, gain_ref, cot_ref, moment_ref, *refs):
    w_refs, grads_ref = refs[:-1], refs[-1]
    inverse, moment, cot = inv_ref[...], moment_ref[...], cot_ref[...]
    for k, (slot, pieces) in enumerate(PIECES):
        span = tok_ref.shape[1] // len(PIECES)
        part = span // len(pieces)
        for h, which in enumerate(pieces):
            at = pl.multiple_of(tab_ref[k] * span + h * part, part)
            partial = lax.dot_general(
                cot, w_refs[which][slot], (((1,), (1,)), ((), ())), preferred_element_type=jnp.float32
            )
            wide = tok_ref[:, pl.ds(at, part)].astype(jnp.float32)
            grads = inverse * gain_ref[:, pl.ds(at, part)] * partial - wide * moment
            grads_ref[:, pl.ds(at, part)] = grads.astype(jnp.bfloat16)


def forward(tokens, inverse, gain, cotangent, weights, table):
    rows, width = tokens.shape
    columns = cotangent.shape[1]
    count = len(weights)
    return pl.pallas_call(
        forward_kernel,
        in_specs=[pl.BlockSpec(memory_space=pltpu.SMEM)]
        + [pl.BlockSpec(memory_space=pltpu.VMEM)] * (4 + count),
        out_specs=[pl.BlockSpec(memory_space=pltpu.VMEM)] * 2,
        out_shape=[
            jax.ShapeDtypeStruct((rows, columns), jnp.bfloat16),
            jax.ShapeDtypeStruct((rows, 1), jnp.float32),
        ],
        scratch_shapes=[pltpu.VMEM((rows, columns), jnp.float32)],
        compiler_params=pltpu.CompilerParams(vmem_limit_bytes=LIMIT),
        cost_estimate=pl.CostEstimate(
            flops=2 * rows * width * columns,
            bytes_accessed=2 * rows * width + 2 * width * columns,
            transcendentals=0,
        ),
    )(table, tokens, inverse, gain, cotangent, *weights)


def backward(tokens, inverse, gain, cotangent, moment, weights, table):
    rows, width = tokens.shape
    columns = cotangent.shape[1]
    count = len(weights)
    return pl.pallas_call(
        backward_kernel,
        in_specs=[pl.BlockSpec(memory_space=pltpu.SMEM)]
        + [pl.BlockSpec(memory_space=pltpu.VMEM)] * (5 + count),
        out_specs=pl.BlockSpec(memory_space=pltpu.VMEM),
        out_shape=jax.ShapeDtypeStruct((rows, width), jnp.bfloat16),
        compiler_params=pltpu.CompilerParams(vmem_limit_bytes=LIMIT),
        cost_estimate=pl.CostEstimate(
            flops=2 * rows * width * columns,
            bytes_accessed=4 * rows * width + 2 * width * columns,
            transcendentals=0,
        ),
    )(table, tokens, inverse, gain, cotangent, moment, *weights)


def swap(array, axis, mask):
    size = lax.axis_size(axis)
    return lax.ppermute(array, axis, [(i, i ^ mask) for i in range(size)])


def swap_z(array, odd):
    size = lax.axis_size("zh") * lax.axis_size("zl")
    if odd:
        pairs = [(i, (i + 1 if i % 2 else i - 1) % size) for i in range(size)]
    else:
        pairs = [(i, i ^ 1) for i in range(size)]
    return lax.ppermute(array, ("zh", "zl"), pairs)


def halve(total):
    half = total.shape[0] // 2
    return total[half:].astype(jnp.bfloat16), total[:half]


def tie(first, *others):
    return lax.optimization_barrier((first, *others))[0]


def exchange(sent, order):
    moves = (
        lambda a: swap(a, "y", 1),
        lambda a: swap(a, "y", 3),
        lambda a: swap_z(a, False),
        lambda a: swap_z(a, True),
    )
    return [moves[m](s) for m, s in zip(order, sent)]


def add_halve(kept, got):
    return zip(*[halve(k + g.astype(jnp.float32)) for k, g in zip(kept, got)])


PIECES = tuple((k % 8, (k // 8,)) for k in range(16))


def pack_kernel(tab_ref, sent_ref, got_ref, weight_ref, gain_ref, out_ref, *, devices):
    columns = sent_ref.shape[0]
    mine = (sent_ref[...].astype(jnp.float32) + got_ref[...].astype(jnp.float32)) / devices
    out_ref[:columns, :] = mine.astype(jnp.bfloat16)
    rows = pl.ds(pl.multiple_of(tab_ref[0] * TILE, TILE), TILE)
    weight = weight_ref[rows, :].astype(jnp.float32).T
    gain = gain_ref[:, pl.ds(pl.multiple_of(tab_ref[1] * TILE, TILE), TILE)]
    part = jnp.sum(weight * mine, axis=0, keepdims=True) / gain
    high = part.astype(jnp.bfloat16).astype(jnp.float32)
    tail = out_ref.shape[0] - columns
    row = lax.broadcasted_iota(jnp.int32, (tail, TILE), 0)
    ends = jnp.where(row == 0, high, jnp.where(row == 1, part - high, 0.0))
    out_ref[columns:, :] = ends.astype(jnp.bfloat16)


def pack(sent, got, weight, gain, table, devices):
    vmem = pl.BlockSpec(memory_space=pltpu.VMEM)
    return pl.pallas_call(
        functools.partial(pack_kernel, devices=devices),
        in_specs=[pl.BlockSpec(memory_space=pltpu.SMEM)] + [vmem] * 4,
        out_specs=vmem,
        out_shape=jax.ShapeDtypeStruct((sent.shape[0] + 16, TILE), jnp.bfloat16),
    )(table, sent, got, weight, gain)


def finish_kernel(tab_ref, *refs):
    parts, (weight_ref, gain_ref) = refs[:4], refs[4:]
    columns = weight_ref.shape[1]
    for k, part in enumerate(parts):
        quarter = tab_ref[0] ^ k
        rows = pl.ds(pl.multiple_of(quarter * TILE, TILE), TILE)
        weight_ref[rows, :] = part[:columns, :].astype(jnp.float32).T
        ends = part[columns:, :].astype(jnp.float32)
        gain_ref[pl.ds(quarter, 1), :] = ends[0:1] + ends[1:2]


def finish(parts, table):
    vmem = pl.BlockSpec(memory_space=pltpu.VMEM)
    columns = parts[0].shape[0] - 16
    return pl.pallas_call(
        finish_kernel,
        in_specs=[pl.BlockSpec(memory_space=pltpu.SMEM)] + [vmem] * 4,
        out_specs=[vmem] * 2,
        out_shape=[
            jax.ShapeDtypeStruct((4 * TILE, columns), jnp.float32),
            jax.ShapeDtypeStruct((4, TILE), jnp.float32),
        ],
    )(table, *parts)


def order_kernel(tab_ref, in_ref, out_ref):
    for node in range(in_ref.shape[0]):
        out_ref[node] = in_ref[tab_ref[node]]


def order(rows, table):
    vmem = pl.BlockSpec(memory_space=pltpu.VMEM)
    return pl.pallas_call(
        order_kernel,
        in_specs=[pl.BlockSpec(memory_space=pltpu.SMEM), vmem],
        out_specs=vmem,
        out_shape=jax.ShapeDtypeStruct(rows.shape, rows.dtype),
    )(table, rows)


def shards(tokens, norm_gain, weight_values, weight_scale, key_cotangent):
    y, zl, x, c = (lax.axis_index(a) for a in ("y", "zl", "x", "c"))
    width = tokens.shape[1]
    columns = weight_values.shape[1]
    gain = norm_gain.reshape(1, width)
    devices = 1
    for axis in EVERY:
        devices *= lax.axis_size(axis)
    label = jnp.arange(32, dtype=jnp.int32)
    chip = (zl ^ (label // 16)) * 4 + (x ^ (label % 4))
    quarter = y ^ (label // 4 % 4)
    table = jnp.stack([(chip * 2 + side) * 4 + quarter for side in (c, 1 - c)])
    shards_at = jnp.arange(16, dtype=jnp.int32) ^ (zl * 8)

    own_weight = widen_weight(weight_values, weight_scale)
    up = swap_z(own_weight, False)
    weights = [lax.all_gather(part, ("x", "c"), axis=0) for part in (own_weight, up)]
    cot_own = key_cotangent.T
    cot_got = swap(cot_own, "c", 1)
    mine, other, inverse = norm_tiles(tie(tokens, own_weight, cot_own), gain, table)
    got = swap(other, "c", 1)
    sent, kept = grad_tiles(mine, got, cot_own, cot_got)

    moved = exchange(sent, (0, 1, 2, 3))
    sent, kept = add_halve(kept, moved)
    moved = exchange(sent, (2, 3, 0, 1))
    sent, kept = add_halve(kept, moved)
    even = swap(jnp.stack([sent[0], sent[2]]), "y", 3)
    odd = swap(jnp.stack([sent[1], sent[3]]), "y", 1)
    moved = (even[0], odd[0], even[1], odd[1])
    total = jnp.stack([k + m.astype(jnp.float32) for k, m in zip(kept, moved)], axis=1)
    out = total[0]
    for mask in (1, 3, 2):
        out = out + swap(total[mask].astype(jnp.bfloat16), "x", mask).astype(jnp.float32)
    send = out.astype(jnp.bfloat16)

    send, *weights = lax.optimization_barrier((send, *weights))
    arrived = swap(send, "zh", 1)
    projected, moment = forward(tokens, inverse, gain, key_cotangent, weights, shards_at)
    arrived, moment = lax.optimization_barrier((arrived, moment))
    send = (send.astype(jnp.float32) + arrived.astype(jnp.float32)).astype(jnp.bfloat16)
    arrived = swap(send, "zh", 3)

    node = (zl * 4 + x) * 2 + c
    at = jnp.stack([y, node * 4 + y]).astype(jnp.int32)
    packed = pack(
        send.reshape(columns, TILE), arrived.reshape(columns, TILE), own_weight, gain, at, devices
    )
    packed, moment = lax.optimization_barrier((packed, moment))
    pieces = [packed] + [swap(packed, "y", mask) for mask in (1, 2, 3)]
    token_grads = backward(tokens, inverse, gain, key_cotangent, moment, weights, shards_at)
    pieces[3] = tie(pieces[3], token_grads)
    weight_grads, gains = finish(pieces, at)
    gains = gains[None]
    gains = jnp.concatenate([gains, swap(gains, "c", 1)])
    gains = jnp.concatenate([gains] + [swap(gains, "x", mask) for mask in (1, 2, 3)])
    gains = jnp.concatenate([gains, swap(gains, "zl", 1)])
    nodes = jnp.arange(16, dtype=jnp.int32)
    relative = (nodes // 8 ^ zl) * 8 + (nodes // 2 % 4 ^ x) * 2 + (nodes % 2 ^ c)
    gain_grads = order(gains, relative.astype(jnp.int32)).reshape(width)
    return (projected, token_grads, weight_grads, gain_grads)


def solution(mesh):
    fine = Mesh(mesh.devices.reshape(4, 4, 2, 4, 2), EVERY)
    rows = P(EVERY, None)
    return jax.shard_map(
        shards,
        mesh=fine,
        in_specs=(rows, P(), P(NODE, None), P(NODE, None), rows),
        out_specs=(rows, rows, P(NODE, None), P()),
        check_vma=False,
    )
```

time: 164 us -> 166 us (1.012)
  local copies, waits for them, and re-layouts: 7.38 us -> 15.5 us
  starting transfers between devices: 52.1 us -> 44.1 us
  Pallas kernels: 31 us -> 38.9 us
  waiting for transfers between devices: 50.9 us -> 47.3 us
    unnamed x37 -> x42, local copies, waits for them, and re-layouts: 5.07 us -> 15.2 us
    ppermute x4 -> x5, waiting for transfers between devices: 21.7 us -> 13.7 us  [swap_z(): return lax.ppermute(array, ('zh', 'zl'), pairs)]
    pallas_call x1 -> x6, Pallas kernels: 18 us -> 24.6 us  [the longest x1 9.4 us: backward(): pl.pallas_call(backward_kernel, in_specs=[pl.BlockSpec(memory_space=pltpu...]
    ppermute x22 -> x21, starting transfers between devices: 40.6 us -> 34.4 us  [swap(): return lax.ppermute(array, axis, [(i, i ^ mask) for i in range(size)])]
    ppermute x22 -> x21, waiting for transfers between devices: 29.2 us -> 33.6 us  [swap(): return lax.ppermute(array, axis, [(i, i ^ mask) for i in range(size)])]
    convert_element_type x5 -> x2, other arithmetic: 3.22 us -> 0.11 us  [the longest x1 0.07 us: shards(): send = out.astype(jnp.bfloat16)]
    add x9, other arithmetic: 0.85 us -> 3.6 us  [the longest x8 3.08 us: add_halve(): return zip(*[halve(k + g.astype(jnp.float32)) for k, g in zip(kept, got)])]
    ppermute x4 -> x5, starting transfers between devices: 11.4 us -> 9.56 us  [swap_z(): return lax.ppermute(array, ('zh', 'zl'), pairs)]
  transfers between devices with their start and end apart: 27 -> 28, of which waited for: 17 -> 14; matrix products, arithmetic and copies ran while one was open for 4% -> 4% of each run, Pallas kernels for 8% -> 19%
where the time goes in v3:
time: 166 us
  waiting for transfers between devices  47.3 us (28%)
  starting transfers between devices  44.1 us (27%)
  Pallas kernels  38.9 us (23%)
  local copies, waits for them, and re-layouts  15.5 us (9%)
  between operations  14.4 us (9%)
  other arithmetic  5.43 us (3%)
    ppermute x21, starting transfers between devices, swap(): return lax.ppermute(array, axis, [(i, i ^ mask) for i in range(size)])  34.4 us
    ppermute x21, waiting for transfers between devices, swap(): return lax.ppermute(array, axis, [(i, i ^ mask) for i in range(size)])  33.6 us
    unnamed x42, local copies, waits for them, and re-layouts  15.2 us
    ppermute x5, waiting for transfers between devices, swap_z(): return lax.ppermute(array, ('zh', 'zl'), pairs)  13.7 us
    ppermute x5, starting transfers between devices, swap_z(): return lax.ppermute(array, ('zh', 'zl'), pairs)  9.56 us
    pallas_call x1, Pallas kernels, backward(): pl.pallas_call(backward_kernel, in_specs=[pl.BlockSpec(memory_space=pltpu...  9.4 us
    pallas_call x1, Pallas kernels, grad_tiles(): pl.pallas_call(grad_kernel, out_shape=[jax.ShapeDtypeStruct(shape, jnp.bf...  8.36 us
    pallas_call x1, Pallas kernels, forward(): pl.pallas_call(forward_kernel, in_specs=[pl.BlockSpec(memory_space=pltpu....  7.41 us
  transfers between devices with their start and end apart: 28, of which 14 were waited for; matrix products, arithmetic and copies ran while one was open for 4% of the time, Pallas kernels for 19%

profile of v3, /device:TPU:1, one launch (start us, length us, event | category | flops | bytes accessed | tf_op | source)
XLA Modules:
  0.0 165.6 jit_solution(14990022745092669067)
XLA Ops:
  8.7 2.1 %shard_map.84.weight_ref = bf16[512,512]{1,0:T(8,128)(2,1)} custom-call(bf16[512,512]{1,0:T(8,128)(2,1)} %values_ref.1, bf16[512,4]{1,0:T(8,128)(2,1)} %copy.9.scales_ref), custom_call_target="tpu_custom_call" | custom-call | tf_op jit(solution)/shard_map/pallas_call | solution.py:29
  12.9 5.9 %shard_map.85 = (bf16[320,4096]{1,0:T(8,128)(2,1)S(1)}, bf16[320,4096]{1,0:T(8,128)(2,1)S(1)}, f32[320,1]{1,0:T(8,128)S(1)}) custom-call(s32[2,32]{1,0:T(2,128)S(1)} %pad_add_fusion.tab_ref, bf16[320,8192]{1,0:T(8,128)(2,1)} %tok_ref.4, f32[1,8192]{1,0:T(1,128)S(1)} %bitcast.73), custom_call_target="tpu_custom_call" | custom-call | flops 15728640 | bytes 10485760 | tf_op jit(solution)/shard_map/pallas_call | solution.py:55
  20.4 3.2 %collective-permute-start = (bf16[320,4096]{1,0:T(8,128)(2,1)S(1)}, bf16[320,4096]{1,0:T(8,128)(2,1)}, u32[]{:S(2)}, u32[]{:S(2)}) collective-permute-start(bf16[320,4096]{1,0:T(8,128)(2,1)S(1)} %get-tuple-element.31), channel_id=1, source_target_pairs={{0,1},{1,0},{2,3},{3,2},{4,5},{5,4},{6,7},{7,6},{8,9},{9,8},{10,11... | collective-permute-start | bytes 7864328 | tf_op jit(solution)/shard_map/ppermute | solution.py:209
  23.6 13.7 %collective-permute-done.15 = bf16[512,512]{1,0:T(8,128)(2,1)} collective-permute-done((bf16[512,512]{1,0:T(8,128)(2,1)S(1)}, bf16[512,512]{1,0:T(8,128)(2,1)}, u32[]{:S(2)}, u32[]{:S(2)}) %collective-permute-start.15) | collective-permute-done | bytes 524320 | tf_op jit(solution)/shard_map/ppermute | solution.py:218
  40.5 8.4 %shard_map.86 = (bf16[16,128,128]{2,1,0:T(8,128)(2,1)S(1)}, bf16[16,128,128]{2,1,0:T(8,128)(2,1)}, bf16[16,128,128]{2,1,0:T(8,128)(2,1)S(1)}, bf16[16,128,128]{2...) custom-call(bf16[320,4096]{1,0:T(8,128)(2,1)} %copy-done.8, ...), custom_call_target="tpu_custom_call" | custom-call | flops 2684354560 | bytes 11534336 | tf_op jit(solution)/shard_map/pallas_call | solution.py:113
  51.7 5.4 %collective-permute-start.9 = (bf16[16,128,128]{2,1,0:T(8,128)(2,1)}, bf16[16,128,128]{2,1,0:T(8,128)(2,1)}, u32[]{:S(2)}, u32[]{:S(2)}) collective-permute-start(bf16[16,128,128]{2,1,0:T(8,128)(2,1)} %get-tuple-element.39), channel_id=1, source_target_pairs={{0,56},{8,16},{16,8},{24,32},{32,24},{40,48},{48,40},{56,0},{1,57}... | collective-permute-start | bytes 1572872 | tf_op jit(solution)/shard_map/ppermute | solution.py:218
  57.1 8.0 %collective-permute-done.7 = bf16[16,128,128]{2,1,0:T(8,128)(2,1)} collective-permute-done((bf16[16,128,128]{2,1,0:T(8,128)(2,1)}, bf16[16,128,128]{2,1,0:T(8,128)(2,1)}, u32[]{:S(2)}, u32[]{:S(2)}) %collective-permute-start.7) | collective-permute-done | bytes 524320 | tf_op jit(solution)/shard_map/ppermute | solution.py:209
  66.3 4.1 %collective-permute-start.8 = (bf16[8,128,128]{2,1,0:T(8,128)(2,1)S(1)}, bf16[8,128,128]{2,1,0:T(8,128)(2,1)S(1)}, u32[]{:S(2)}, u32[]{:S(2)}) collective-permute-start(bf16[8,128,128]{2,1,0:T(8,128)(2,1)S(1)} %slice.188), channel_id=1, source_target_pairs={{0,56},{8,16},{16,8},{24,32},{32,24},{40,48},{48,40},{56,0},{1,57}... | collective-permute-start | bytes 786440 | tf_op jit(solution)/shard_map/ppermute | solution.py:218
  72.0 2.7 %collective-permute-start.10 = (bf16[8,128,128]{2,1,0:T(8,128)(2,1)S(1)}, bf16[8,128,128]{2,1,0:T(8,128)(2,1)S(1)}, u32[]{:S(2)}, u32[]{:S(2)}) collective-permute-start(bf16[8,128,128]{2,1,0:T(8,128)(2,1)S(1)} %slice.187), channel_id=1, source_target_pairs={{0,192},{64,128},{128,64},{192,0},{1,193},{65,129},{129,65},{193,1... | collective-permute-start | bytes 786440 | tf_op jit(solution)/shard_map/ppermute | solution.py:209
  75.2 4.6 %collective-permute-done.10 = bf16[8,128,128]{2,1,0:T(8,128)(2,1)S(1)} collective-permute-done((bf16[8,128,128]{2,1,0:T(8,128)(2,1)S(1)}, bf16[8,128,128]{2,1,0:T(8,128)(2,1)S(1)}, u32[]{:S(2)}, u32[]{:S(2)}) %collective-permute-start.10) | collective-permute-done | bytes 262176 | tf_op jit(solution)/shard_map/ppermute | solution.py:209
  83.1 4.0 %collective-permute-done.11 = bf16[2,4,128,128]{3,2,1,0:T(8,128)(2,1)S(1)} collective-permute-done((bf16[2,4,128,128]{3,2,1,0:T(8,128)(2,1)S(1)}, bf16[2,4,128,128]{3,2,1,0:T(8,128)(2,1)S(1)}, u32[]{:S(2)}, u32[]{:S(2)}) %collective-permute-start.11) | collective-permute-done | bytes 262176 | tf_op jit(solution)/shard_map/ppermute | solution.py:209
  88.5 2.8 %collective-permute-start.14 = (bf16[4,128,128]{2,1,0:T(8,128)(2,1)S(1)}, bf16[4,128,128]{2,1,0:T(8,128)(2,1)S(1)}, u32[]{:S(2)}, u32[]{:S(2)}) collective-permute-start(bf16[4,128,128]{2,1,0:T(8,128)(2,1)S(1)} %get-tuple-element.53), channel_id=1, source_target_pairs={{0,4},{2,6},{4,0},{6,2},{1,5},{3,7},{5,1},{7,3},{8,12},{10,14},{12... | collective-permute-start | bytes 393224 | tf_op jit(solution)/shard_map/ppermute | solution.py:209
  93.9 2.4 %collective-permute-done.13 = bf16[4,128,128]{2,1,0:T(8,128)(2,1)S(1)} collective-permute-done((bf16[4,128,128]{2,1,0:T(8,128)(2,1)S(1)}, bf16[4,128,128]{2,1,0:T(8,128)(2,1)S(1)}, u32[]{:S(2)}, u32[]{:S(2)}) %collective-permute-start.13) | collective-permute-done | bytes 131104 | tf_op jit(solution)/shard_map/ppermute | solution.py:209
  98.0 2.2 %copy-done = bf16[4096,512]{1,0:T(8,128)(2,1)S(1)} copy-done((bf16[4096,512]{1,0:T(8,128)(2,1)S(1)}, bf16[4096,512]{1,0:T(8,128)(2,1)}, u32[]{:S(2)}) %copy-start) | copy-done | bytes 4194328
  100.2 7.4 %shard_map.87 = (bf16[320,512]{1,0:T(8,128)(2,1)}, f32[320,1]{1,0:T(8,128)S(1)}) custom-call(s32[16]{0:T(128)S(1)} %iota_xor_fusion.tab_ref, bf16[320,8192]{1,0:T(8,128)(2,1)} %tok_ref.4, f32[320,1]{1,0:T(8,128)S(1)} %get-tuple-element.29.inv_ref, f32[1,8192]{1,0:T(1,128)S(1)} %bitcast.74, bf16[320,512]{1,0:T(8,128)(2,1)S(1)} %copy-done.2, ...), custom_call_target="tpu_custom_call" | custom-call | flops 2684354560 | bytes 13631488 | tf_op jit(solution)/shard_map/pallas_call | solution.py:169
  109.7 4.1 %collective-permute-done.17 = bf16[4,128,128]{2,1,0:T(8,128)(2,1)S(1)} collective-permute-done((bf16[4,128,128]{2,1,0:T(8,128)(2,1)S(1)}, bf16[4,128,128]{2,1,0:T(8,128)(2,1)S(1)}, u32[]{:S(2)}, u32[]{:S(2)}) %collective-permute-start.17) | collective-permute-done | bytes 131104 | tf_op jit(solution)/shard_map/ppermute | solution.py:209
  117.9 2.4 %collective-permute-start.20 = (bf16[528,128]{1,0:T(8,128)(2,1)}, bf16[528,128]{1,0:T(8,128)(2,1)S(1)}, u32[]{:S(2)}, u32[]{:S(2)}) collective-permute-start(bf16[528,128]{1,0:T(8,128)(2,1)} %shard_map.88.refs_0_), channel_id=1, source_target_pairs={{0,192},{64,128},{128,64},{192,0},{1,193},{65,129},{129,65},{193,1... | collective-permute-start | bytes 405512 | tf_op jit(solution)/shard_map/ppermute | solution.py:209
  120.3 2.2 %copy-done.1 = bf16[4096,512]{1,0:T(8,128)(2,1)S(1)} copy-done((bf16[4096,512]{1,0:T(8,128)(2,1)S(1)}, bf16[4096,512]{1,0:T(8,128)(2,1)}, u32[]{:S(2)}) %copy-start.1) | copy-done | bytes 4194328
  122.5 9.4 %shard_map.89 = bf16[320,8192]{1,0:T(8,128)(2,1)} custom-call(s32[16]{0:T(128)S(1)} %iota_xor_fusion.tab_ref, bf16[320,8192]{1,0:T(8,128)(2,1)} %tok_ref.4, f32[320,1]{1,0:T(8,128)S(1)} %get-tuple-element.29.inv_ref, f32[1,8192]{1,0:T(1,128)S(1)} %bitcast.75, bf16[320,512]{1,0:T(8,128)(2,1)S(1)} %copy-done.2, f32[320,1]{1,0:T(8,128)S(1)} %get-tuple-element.47.moment_ref, ...), custom_call_target="tpu_custom_call" | custom-call | flops 2684354560 | bytes 18874368 | tf_op jit(solution)/shard_map/pallas_call | solution.py:192
  133.3 2.3 %shard_map.90 = (f32[512,512]{1,0:T(8,128)}, f32[4,128]{1,0:T(4,128)}) custom-call(s32[2]{0:T(128)} %pad_add_fusion.1.tab_ref, bf16[528,128]{1,0:T(8,128)(2,1)} %shard_map.88.refs_0_, bf16[528,128]{1,0:T(8,128)(2,1)} %copy-done.13, bf16[528,128]{1,0:T(8,128)(2,1)} %copy-done.14, bf16[528,128]{1,0:T(8,128)(2,1)} %copy-done.15), custom_call_target="tpu_custom_call" | custom-call | tf_op jit(solution)/shard_map/pallas_call | solution.py:286
  135.5 10.3 %collective-permute-start.21 = (f32[1,4,128]{2,1,0:T(4,128)}, f32[1,4,128]{2,1,0:T(4,128)S(1)}, u32[]{:S(2)}, u32[]{:S(2)}) collective-permute-start(f32[1,4,128]{2,1,0:T(4,128)} %bitcast.83), channel_id=1, source_target_pairs={{0,1},{1,0},{2,3},{3,2},{4,5},{5,4},{6,7},{7,6},{8,9},{9,8},{10,11... | collective-permute-start | bytes 6152 | tf_op jit(solution)/shard_map/ppermute | solution.py:209
  147.6 2.9 %collective-permute-start.23 = (f32[2,4,128]{2,1,0:T(4,128)S(1)}, f32[2,4,128]{2,1,0:T(4,128)S(1)}, u32[]{:S(2)}, u32[]{:S(2)}) collective-permute-start(f32[2,4,128]{2,1,0:T(4,128)S(1)} %pad_maximum_fusion.3), channel_id=1, source_target_pairs={{0,4},{2,6},{4,0},{6,2},{1,5},{3,7},{5,1},{7,3},{8,12},{10,14},{12... | collective-permute-start | bytes 12296 | tf_op jit(solution)/shard_map/ppermute | solution.py:209
  151.6 2.6 %collective-permute-done.24 = f32[2,4,128]{2,1,0:T(4,128)S(1)} collective-permute-done((f32[2,4,128]{2,1,0:T(4,128)S(1)}, f32[2,4,128]{2,1,0:T(4,128)S(1)}, u32[]{:S(2)}, u32[]{:S(2)}) %collective-permute-start.24) | collective-permute-done | bytes 4128 | tf_op jit(solution)/shard_map/ppermute | solution.py:209
  154.7 2.1 %collective-permute-done.25 = f32[8,4,128]{2,1,0:T(4,128)S(1)} collective-permute-done((f32[8,4,128]{2,1,0:T(4,128)S(1)}, f32[8,4,128]{2,1,0:T(4,128)S(1)}, u32[]{:S(2)}, u32[]{:S(2)}) %collective-permute-start.25) | collective-permute-done | bytes 16416 | tf_op jit(solution)/shard_map/ppermute | solution.py:209
  (117 shorter events, 36.0 us)
Async XLA Ops:
  7.2 89.2 %all-gather.5.cloned.1.call-start = ((), (), s32[]{:S(2)}) async-start(), calls=%async_computation | async-start | bytes 4718592 | tf_op jit(solution)/shard_map/all_gather | solution.py:328
  10.8 85.6 %all-gather.7.cloned.1.call-start = ((), (), s32[]{:S(2)}) async-start(), calls=%async_computation.1 | async-start | bytes 4718592 | tf_op jit(solution)/shard_map/all_gather | solution.py:328
  20.4 19.2 %collective-permute-start = (bf16[320,4096]{1,0:T(8,128)(2,1)S(1)}, bf16[320,4096]{1,0:T(8,128)(2,1)}, u32[]{:S(2)}, u32[]{:S(2)}) collective-permute-start(bf16[320,4096]{1,0:T(8,128)(2,1)S(1)} %get-tuple-element.31), channel_id=1, source_target_pairs={{0,1},{1,0},{2,3},{3,2},{4,5},{5,4},{6,7},{7,6},{8,9},{9,8},{10,11... | collective-permute-start | bytes 7864328 | tf_op jit(solution)/shard_map/ppermute | solution.py:209
  23.6 13.7 %collective-permute-start.15 = (bf16[512,512]{1,0:T(8,128)(2,1)S(1)}, bf16[512,512]{1,0:T(8,128)(2,1)}, u32[]{:S(2)}, u32[]{:S(2)}) collective-permute-start(bf16[512,512]{1,0:T(8,128)(2,1)S(1)} %copy-done.11), channel_id=1, source_target_pairs={{0,8},{8,0},{16,24},{24,16},{32,40},{40,32},{48,56},{56,48},{1,9},... | collective-permute-start | bytes 1572872 | tf_op jit(solution)/shard_map/ppermute | solution.py:218
  50.5 14.6 %collective-permute-start.7 = (bf16[16,128,128]{2,1,0:T(8,128)(2,1)}, bf16[16,128,128]{2,1,0:T(8,128)(2,1)}, u32[]{:S(2)}, u32[]{:S(2)}) collective-permute-start(bf16[16,128,128]{2,1,0:T(8,128)(2,1)} %get-tuple-element.37), channel_id=1, source_target_pairs={{0,192},{64,128},{128,64},{192,0},{1,193},{65,129},{129,65},{193,1... | collective-permute-start | bytes 1572872 | tf_op jit(solution)/shard_map/ppermute | solution.py:209
  51.7 18.7 %collective-permute-start.9 = (bf16[16,128,128]{2,1,0:T(8,128)(2,1)}, bf16[16,128,128]{2,1,0:T(8,128)(2,1)}, u32[]{:S(2)}, u32[]{:S(2)}) collective-permute-start(bf16[16,128,128]{2,1,0:T(8,128)(2,1)} %get-tuple-element.39), channel_id=1, source_target_pairs={{0,56},{8,16},{16,8},{24,32},{32,24},{40,48},{48,40},{56,0},{1,57}... | collective-permute-start | bytes 1572872 | tf_op jit(solution)/shard_map/ppermute | solution.py:218
  57.1 17.6 %collective-permute-start.2 = (bf16[16,128,128]{2,1,0:T(8,128)(2,1)}, bf16[16,128,128]{2,1,0:T(8,128)(2,1)S(1)}, u32[]{:S(2)}, u32[]{:S(2)}) collective-permute-start(bf16[16,128,128]{2,1,0:T(8,128)(2,1)} %copy-done.10), channel_id=1, source_target_pairs={{0,64},{64,0},{128,192},{192,128},{1,65},{65,1},{129,193},{193,129... | collective-permute-start | bytes 1572872 | tf_op jit(solution)/shard_map/ppermute | solution.py:209
  57.1 17.8 %collective-permute-start.4 = (bf16[16,128,128]{2,1,0:T(8,128)(2,1)}, bf16[16,128,128]{2,1,0:T(8,128)(2,1)S(1)}, u32[]{:S(2)}, u32[]{:S(2)}) collective-permute-start(bf16[16,128,128]{2,1,0:T(8,128)(2,1)} %copy-done.9), channel_id=1, source_target_pairs={{0,8},{8,0},{16,24},{24,16},{32,40},{40,32},{48,56},{56,48},{1,9},... | collective-permute-start | bytes 1572872 | tf_op jit(solution)/shard_map/ppermute | solution.py:218
  66.3 13.5 %collective-permute-start.8 = (bf16[8,128,128]{2,1,0:T(8,128)(2,1)S(1)}, bf16[8,128,128]{2,1,0:T(8,128)(2,1)S(1)}, u32[]{:S(2)}, u32[]{:S(2)}) collective-permute-start(bf16[8,128,128]{2,1,0:T(8,128)(2,1)S(1)} %slice.188), channel_id=1, source_target_pairs={{0,56},{8,16},{16,8},{24,32},{32,24},{40,48},{48,40},{56,0},{1,57}... | collective-permute-start | bytes 786440 | tf_op jit(solution)/shard_map/ppermute | solution.py:218
  72.0 7.8 %collective-permute-start.10 = (bf16[8,128,128]{2,1,0:T(8,128)(2,1)S(1)}, bf16[8,128,128]{2,1,0:T(8,128)(2,1)S(1)}, u32[]{:S(2)}, u32[]{:S(2)}) collective-permute-start(bf16[8,128,128]{2,1,0:T(8,128)(2,1)S(1)} %slice.187), channel_id=1, source_target_pairs={{0,192},{64,128},{128,64},{192,0},{1,193},{65,129},{129,65},{193,1... | collective-permute-start | bytes 786440 | tf_op jit(solution)/shard_map/ppermute | solution.py:209
  74.8 6.6 %collective-permute-start.3 = (bf16[8,128,128]{2,1,0:T(8,128)(2,1)S(1)}, bf16[8,128,128]{2,1,0:T(8,128)(2,1)S(1)}, u32[]{:S(2)}, u32[]{:S(2)}) collective-permute-start(bf16[8,128,128]{2,1,0:T(8,128)(2,1)S(1)} %slice.190), channel_id=1, source_target_pairs={{0,8},{8,0},{16,24},{24,16},{32,40},{40,32},{48,56},{56,48},{1,9},... | collective-permute-start | bytes 786440 | tf_op jit(solution)/shard_map/ppermute | solution.py:218
  75.1 6.2 %collective-permute-start.5 = (bf16[8,128,128]{2,1,0:T(8,128)(2,1)S(1)}, bf16[8,128,128]{2,1,0:T(8,128)(2,1)S(1)}, u32[]{:S(2)}, u32[]{:S(2)}) collective-permute-start(bf16[8,128,128]{2,1,0:T(8,128)(2,1)S(1)} %slice.189), channel_id=1, source_target_pairs={{0,64},{64,0},{128,192},{192,128},{1,65},{65,1},{129,193},{193,129... | collective-permute-start | bytes 786440 | tf_op jit(solution)/shard_map/ppermute | solution.py:209
  80.0 7.1 %collective-permute-start.11 = (bf16[2,4,128,128]{3,2,1,0:T(8,128)(2,1)S(1)}, bf16[2,4,128,128]{3,2,1,0:T(8,128)(2,1)S(1)}, u32[]{:S(2)}, u32[]{:S(2)}) collective-permute-start(bf16[2,4,128,128]{3,2,1,0:T(8,128)(2,1)S(1)} %pad_maximum_fusion.2), channel_id=1, source_target_pairs={{0,64},{64,0},{128,192},{192,128},{1,65},{65,1},{129,193},{193,129... | collective-permute-start | bytes 786440 | tf_op jit(solution)/shard_map/ppermute | solution.py:209
  81.6 6.7 %collective-permute-start.6 = (bf16[2,4,128,128]{3,2,1,0:T(8,128)(2,1)S(1)}, bf16[2,4,128,128]{3,2,1,0:T(8,128)(2,1)S(1)}, u32[]{:S(2)}, u32[]{:S(2)}) collective-permute-start(bf16[2,4,128,128]{3,2,1,0:T(8,128)(2,1)S(1)} %pad_maximum_fusion.1), channel_id=1, source_target_pairs={{0,192},{64,128},{128,64},{192,0},{1,193},{65,129},{129,65},{193,1... | collective-permute-start | bytes 786440 | tf_op jit(solution)/shard_map/ppermute | solution.py:209
  88.5 5.4 %collective-permute-start.14 = (bf16[4,128,128]{2,1,0:T(8,128)(2,1)S(1)}, bf16[4,128,128]{2,1,0:T(8,128)(2,1)S(1)}, u32[]{:S(2)}, u32[]{:S(2)}) collective-permute-start(bf16[4,128,128]{2,1,0:T(8,128)(2,1)S(1)} %get-tuple-element.53), channel_id=1, source_target_pairs={{0,4},{2,6},{4,0},{6,2},{1,5},{3,7},{5,1},{7,3},{8,12},{10,14},{12... | collective-permute-start | bytes 393224 | tf_op jit(solution)/shard_map/ppermute | solution.py:209
  91.2 5.0 %collective-permute-start.13 = (bf16[4,128,128]{2,1,0:T(8,128)(2,1)S(1)}, bf16[4,128,128]{2,1,0:T(8,128)(2,1)S(1)}, u32[]{:S(2)}, u32[]{:S(2)}) collective-permute-start(bf16[4,128,128]{2,1,0:T(8,128)(2,1)S(1)} %get-tuple-element.54), channel_id=1, source_target_pairs={{0,6},{2,4},{4,2},{6,0},{1,7},{3,5},{5,3},{7,1},{8,14},{10,12},{12... | collective-permute-start | bytes 393224 | tf_op jit(solution)/shard_map/ppermute | solution.py:209
  92.1 4.2 %collective-permute-start.12 = (bf16[4,128,128]{2,1,0:T(8,128)(2,1)S(1)}, bf16[4,128,128]{2,1,0:T(8,128)(2,1)S(1)}, u32[]{:S(2)}, u32[]{:S(2)}) collective-permute-start(bf16[4,128,128]{2,1,0:T(8,128)(2,1)S(1)} %get-tuple-element.52), channel_id=1, source_target_pairs={{0,2},{2,0},{4,6},{6,4},{1,3},{3,1},{5,7},{7,5},{8,10},{10,8},{12,... | collective-permute-start | bytes 393224 | tf_op jit(solution)/shard_map/ppermute | solution.py:209
  96.4 11.2 %collective-permute-start.16 = (bf16[4,128,128]{2,1,0:T(8,128)(2,1)S(1)}, bf16[4,128,128]{2,1,0:T(8,128)(2,1)S(1)}, u32[]{:S(2)}, u32[]{:S(2)}) collective-permute-start(bf16[4,128,128]{2,1,0:T(8,128)(2,1)S(1)} %fusion.3), channel_id=1, source_target_pairs={{0,16},{16,0},{32,48},{48,32},{1,17},{17,1},{33,49},{49,33},{2,18}... | collective-permute-start | bytes 393224 | tf_op jit(solution)/shard_map/ppermute | solution.py:209
  107.7 6.1 %collective-permute-start.17 = (bf16[4,128,128]{2,1,0:T(8,128)(2,1)S(1)}, bf16[4,128,128]{2,1,0:T(8,128)(2,1)S(1)}, u32[]{:S(2)}, u32[]{:S(2)}) collective-permute-start(bf16[4,128,128]{2,1,0:T(8,128)(2,1)S(1)} %add_convert_fusion), channel_id=1, source_target_pairs={{0,48},{16,32},{32,16},{48,0},{1,49},{17,33},{33,17},{49,1},{2,50}... | collective-permute-start | bytes 393224 | tf_op jit(solution)/shard_map/ppermute | solution.py:209
  116.4 15.5 %collective-permute-start.18 = (bf16[528,128]{1,0:T(8,128)(2,1)}, bf16[528,128]{1,0:T(8,128)(2,1)S(1)}, u32[]{:S(2)}, u32[]{:S(2)}) collective-permute-start(bf16[528,128]{1,0:T(8,128)(2,1)} %shard_map.88.refs_0_), channel_id=1, source_target_pairs={{0,64},{64,0},{128,192},{192,128},{1,65},{65,1},{129,193},{193,129... | collective-permute-start | bytes 405512 | tf_op jit(solution)/shard_map/ppermute | solution.py:209
  116.4 15.5 %collective-permute-start.19 = (bf16[528,128]{1,0:T(8,128)(2,1)}, bf16[528,128]{1,0:T(8,128)(2,1)S(1)}, u32[]{:S(2)}, u32[]{:S(2)}) collective-permute-start(bf16[528,128]{1,0:T(8,128)(2,1)} %shard_map.88.refs_0_), channel_id=1, source_target_pairs={{0,128},{64,192},{128,0},{192,64},{1,129},{65,193},{129,1},{193,65... | collective-permute-start | bytes 405512 | tf_op jit(solution)/shard_map/ppermute | solution.py:209
  117.9 14.0 %collective-permute-start.20 = (bf16[528,128]{1,0:T(8,128)(2,1)}, bf16[528,128]{1,0:T(8,128)(2,1)S(1)}, u32[]{:S(2)}, u32[]{:S(2)}) collective-permute-start(bf16[528,128]{1,0:T(8,128)(2,1)} %shard_map.88.refs_0_), channel_id=1, source_target_pairs={{0,192},{64,128},{128,64},{192,0},{1,193},{65,129},{129,65},{193,1... | collective-permute-start | bytes 405512 | tf_op jit(solution)/shard_map/ppermute | solution.py:209
  135.5 11.4 %collective-permute-start.21 = (f32[1,4,128]{2,1,0:T(4,128)}, f32[1,4,128]{2,1,0:T(4,128)S(1)}, u32[]{:S(2)}, u32[]{:S(2)}) collective-permute-start(f32[1,4,128]{2,1,0:T(4,128)} %bitcast.83), channel_id=1, source_target_pairs={{0,1},{1,0},{2,3},{3,2},{4,5},{5,4},{6,7},{7,6},{8,9},{9,8},{10,11... | collective-permute-start | bytes 6152 | tf_op jit(solution)/shard_map/ppermute | solution.py:209
  147.6 4.0 %collective-permute-start.23 = (f32[2,4,128]{2,1,0:T(4,128)S(1)}, f32[2,4,128]{2,1,0:T(4,128)S(1)}, u32[]{:S(2)}, u32[]{:S(2)}) collective-permute-start(f32[2,4,128]{2,1,0:T(4,128)S(1)} %pad_maximum_fusion.3), channel_id=1, source_target_pairs={{0,4},{2,6},{4,0},{6,2},{1,5},{3,7},{5,1},{7,3},{8,12},{10,14},{12... | collective-permute-start | bytes 12296 | tf_op jit(solution)/shard_map/ppermute | solution.py:209
  (22 other events, 122.2 us)
Sparse Core Ops, SparseCore 0:
  11.0 38.8 all-gather.4
  51.7 34.6 all-gather.6

commit v4 on v3

v4 whole, which is shorter than its diff:
```python
import functools

import jax
import jax.numpy as jnp
from jax import lax
from jax.experimental import pallas as pl
from jax.experimental.pallas import tpu as pltpu
from jax.sharding import Mesh, PartitionSpec as P

NODE = ("zl", "x", "c")
EVERY = ("y", "zh", "zl", "x", "c")
TILE = 128
LIMIT = 48 * 2**20


def widen_kernel(values_ref, scales_ref, out_ref):
    blocks = scales_ref.shape[0]
    block = values_ref.shape[1] // blocks
    scales = scales_ref[...].astype(jnp.float32)
    scales = jnp.concatenate([scales] * (8 // blocks), axis=0).T
    for k in range(blocks):
        part = slice(k * block, (k + 1) * block)
        wide = values_ref[:, part].astype(jnp.float32)
        out_ref[:, part] = (wide * scales[:, k : k + 1]).astype(jnp.bfloat16)


def widen_weight(values, scales):
    return pl.pallas_call(
        widen_kernel, out_shape=jax.ShapeDtypeStruct(values.shape, jnp.bfloat16)
    )(values, scales.T)


def norm_kernel(tab_ref, tok_ref, gain_ref, own_ref, oth_ref, inv_ref):
    rows, width = tok_ref.shape
    total = jnp.zeros((rows, TILE), jnp.float32)
    for t in range(width // TILE):
        wide = tok_ref[:, t * TILE : (t + 1) * TILE].astype(jnp.float32)
        total = total + wide * wide
    mean = jnp.sum(total, axis=1, keepdims=True) / width
    inverse = lax.rsqrt(mean + 1e-05)
    inv_ref[...] = inverse
    for side, out_ref in enumerate((own_ref, oth_ref)):
        for r in range(width // TILE // 2):
            at = pl.multiple_of(tab_ref[side, r] * TILE, TILE)
            wide = tok_ref[:, pl.ds(at, TILE)].astype(jnp.float32)
            scaled = wide * inverse * gain_ref[:, pl.ds(at, TILE)]
            out_ref[:, r * TILE : (r + 1) * TILE] = scaled.astype(jnp.bfloat16)


def norm_tiles(tokens, gain, table):
    rows, width = tokens.shape
    step = 64 if rows % 64 == 0 else rows
    half = pl.BlockSpec((step, width // 2), lambda i, tab: (i, 0))
    return pl.pallas_call(
        norm_kernel,
        grid_spec=pltpu.PrefetchScalarGridSpec(
            num_scalar_prefetch=1,
            grid=(rows // step,),
            in_specs=[
                pl.BlockSpec((step, width), lambda i, tab: (i, 0)),
                pl.BlockSpec((1, width), lambda i, tab: (0, 0)),
            ],
            out_specs=[half, half, pl.BlockSpec((step, 1), lambda i, tab: (i, 0))],
        ),
        out_shape=[
            jax.ShapeDtypeStruct((rows, width // 2), jnp.bfloat16),
            jax.ShapeDtypeStruct((rows, width // 2), jnp.bfloat16),
            jax.ShapeDtypeStruct((rows, 1), jnp.float32),
        ],
        compiler_params=pltpu.CompilerParams(vmem_limit_bytes=LIMIT),
        cost_estimate=pl.CostEstimate(
            flops=6 * rows * width, bytes_accessed=4 * rows * width, transcendentals=rows
        ),
    )(table, tokens, gain)


def grad_kernel(own_ref, got_ref, cot_own_ref, cot_got_ref, *out_refs):
    span = 2 * TILE
    half = cot_own_ref.shape[0] // 2
    cot_own = cot_own_ref[...]
    cot_got = cot_got_ref[...]
    for pair in range(own_ref.shape[1] // span):
        part = slice(pair * span, (pair + 1) * span)
        grads = jnp.dot(cot_own, own_ref[:, part], preferred_element_type=jnp.float32)
        grads += jnp.dot(cot_got, got_ref[:, part], preferred_element_type=jnp.float32)
        for which in range(2):
            tile = pair * 2 + which
            z, y1, rest = tile // 16, tile // 8 % 2, tile % 8
            for side, (sent, at) in enumerate(((y1, z * 8 + rest), (z, y1 * 8 + rest))):
                piece = grads[side * half : (side + 1) * half, which * TILE : (which + 1) * TILE]
                if sent:
                    out_refs[side][at] = piece.astype(jnp.bfloat16)
                else:
                    out_refs[2 + side][at] = piece


def grad_tiles(own, got, cot_own, cot_got):
    rows, width = own.shape
    columns = cot_own.shape[0]
    tiles = width // TILE // 2
    shape = (tiles, columns // 2, TILE)
    outs = pl.pallas_call(
        grad_kernel,
        out_shape=[jax.ShapeDtypeStruct(shape, jnp.bfloat16)] * 2
        + [jax.ShapeDtypeStruct(shape, jnp.float32)] * 2,
        compiler_params=pltpu.CompilerParams(vmem_limit_bytes=LIMIT),
        cost_estimate=pl.CostEstimate(
            flops=4 * rows * width * columns,
            bytes_accessed=4 * rows * width + 6 * columns * tiles * TILE,
            transcendentals=0,
        ),
    )(own, got, cot_own, cot_got)
    return outs[:2], outs[2:]


def block_in(tab_ref, tok_ref, block, sem, k):
    span = block.shape[2]
    at = pl.multiple_of(tab_ref[k] * span, span)
    return pltpu.make_async_copy(tok_ref.at[:, pl.ds(at, span)], block.at[k], sem.at[k])


def forward_kernel(tab_ref, tok_ref, inv_ref, gain_ref, cot_ref, *refs):
    w_refs, (proj_ref, moment_ref, acc, block, sem) = refs[:-5], refs[-5:]
    count, _, span = block.shape
    for k in range(count):
        block_in(tab_ref, tok_ref, block, sem, k).start()
    inverse = inv_ref[...]
    acc[...] = jnp.zeros_like(acc)
    for k in range(count):
        block_in(tab_ref, tok_ref, block, sem, k).wait()
        at = pl.multiple_of(tab_ref[k] * span, span)
        wide = block[k].astype(jnp.float32)
        normed = (wide * inverse * gain_ref[:, pl.ds(at, span)]).astype(jnp.bfloat16)
        acc[...] += jnp.dot(normed, w_refs[k // 2][k % 2], preferred_element_type=jnp.float32)
    keys = acc[...]
    proj_ref[...] = keys.astype(jnp.bfloat16)
    inner = jnp.sum(cot_ref[...].astype(jnp.float32) * keys, axis=1, keepdims=True)
    moment_ref[...] = inverse * inverse * inner / (count * span)


def backward_kernel(tab_ref, tok_ref, inv_ref, gain_ref, cot_ref, moment_ref, *refs):
    w_refs, (grads_ref, block, out, sem, out_sem) = refs[:-5], refs[-5:]
    count, _, span = block.shape

    def block_out(k):
        at = pl.multiple_of(tab_ref[k] * span, span)
        return pltpu.make_async_copy(out.at[k], grads_ref.at[:, pl.ds(at, span)], out_sem.at[k])

    for k in range(count):
        block_in(tab_ref, tok_ref, block, sem, k).start()
    inverse, moment, cot = inv_ref[...], moment_ref[...], cot_ref[...]
    for k in range(count):
        partial = lax.dot_general(
            cot, w_refs[k // 2][k % 2], (((1,), (1,)), ((), ())), preferred_element_type=jnp.float32
        )
        block_in(tab_ref, tok_ref, block, sem, k).wait()
        at = pl.multiple_of(tab_ref[k] * span, span)
        wide = block[k].astype(jnp.float32)
        grads = inverse * gain_ref[:, pl.ds(at, span)] * partial - wide * moment
        out[k] = grads.astype(jnp.bfloat16)
        block_out(k).start()
    for k in range(count):
        block_out(k).wait()


def forward(tokens, inverse, gain, cotangent, weights, table):
    rows, width = tokens.shape
    columns = cotangent.shape[1]
    span = weights[0].shape[1]
    count = width // span
    vmem = pl.BlockSpec(memory_space=pltpu.VMEM)
    return pl.pallas_call(
        forward_kernel,
        in_specs=[pl.BlockSpec(memory_space=pltpu.SMEM), pl.BlockSpec(memory_space=pl.ANY)]
        + [vmem] * (3 + len(weights)),
        out_specs=[vmem] * 2,
        out_shape=[
            jax.ShapeDtypeStruct((rows, columns), jnp.bfloat16),
            jax.ShapeDtypeStruct((rows, 1), jnp.float32),
        ],
        scratch_shapes=[
            pltpu.VMEM((rows, columns), jnp.float32),
            pltpu.VMEM((count, rows, span), jnp.bfloat16),
            pltpu.SemaphoreType.DMA((count,)),
        ],
        compiler_params=pltpu.CompilerParams(vmem_limit_bytes=LIMIT),
        cost_estimate=pl.CostEstimate(
            flops=2 * rows * width * columns,
            bytes_accessed=2 * rows * width + 2 * width * columns,
            transcendentals=0,
        ),
    )(table, tokens, inverse, gain, cotangent, *weights)


def backward(tokens, inverse, gain, cotangent, moment, weights, table):
    rows, width = tokens.shape
    columns = cotangent.shape[1]
    span = weights[0].shape[1]
    count = width // span
    vmem = pl.BlockSpec(memory_space=pltpu.VMEM)
    return pl.pallas_call(
        backward_kernel,
        in_specs=[pl.BlockSpec(memory_space=pltpu.SMEM), pl.BlockSpec(memory_space=pl.ANY)]
        + [vmem] * (4 + len(weights)),
        out_specs=pl.BlockSpec(memory_space=pl.ANY),
        out_shape=jax.ShapeDtypeStruct((rows, width), jnp.bfloat16),
        scratch_shapes=[
            pltpu.VMEM((count, rows, span), jnp.bfloat16),
            pltpu.VMEM((count, rows, span), jnp.bfloat16),
            pltpu.SemaphoreType.DMA((count,)),
            pltpu.SemaphoreType.DMA((count,)),
        ],
        compiler_params=pltpu.CompilerParams(vmem_limit_bytes=LIMIT),
        cost_estimate=pl.CostEstimate(
            flops=2 * rows * width * columns,
            bytes_accessed=4 * rows * width + 2 * width * columns,
            transcendentals=0,
        ),
    )(table, tokens, inverse, gain, cotangent, moment, *weights)


def swap(array, axis):
    return lax.ppermute(array, axis, [(0, 1), (1, 0)])


def pair(array, axis, step):
    size = lax.axis_size(axis)
    masks = (1, 3) if step == 0 else (3, 1)
    moves = [(a * 2 + c, (a ^ masks[c]) * 2 + c) for a in range(size) for c in range(2)]
    return lax.ppermute(array, (axis, "c"), moves)


def pair_z(array):
    size = lax.axis_size("zh") * lax.axis_size("zl")
    moves = []
    for z in range(size):
        moves.append((z * 2, (z ^ 1) * 2))
        moves.append((z * 2 + 1, (z + (1 if z % 2 else -1)) % size * 2 + 1))
    return lax.ppermute(array, ("zh", "zl", "c"), moves)


def halve(total):
    half = total.shape[0] // 2
    return total[half:].astype(jnp.bfloat16), total[:half]


def add(kept, got):
    return kept + got.astype(jnp.float32)


def tie(first, *others):
    return lax.optimization_barrier((first, *others))[0]


PIECES = (
    ((0, 0, 0), (0, 0, 1), (1, 0, 0), (1, 0, 1), (0, 1, 0), (0, 1, 1), (0, 2, 1), (0, 2, 0))
    + ((1, 1, 0), (1, 1, 1), (1, 2, 1), (1, 2, 0), (0, 3, 0), (1, 3, 0), (0, 3, 1), (1, 3, 1))
)


def pack_kernel(tab_ref, sent_ref, got_ref, weight_ref, gain_ref, out_ref, *, devices):
    columns = sent_ref.shape[0]
    mine = (sent_ref[...].astype(jnp.float32) + got_ref[...].astype(jnp.float32)) / devices
    out_ref[:columns, :] = mine.astype(jnp.bfloat16)
    rows = pl.ds(pl.multiple_of(tab_ref[0] * TILE, TILE), TILE)
    weight = weight_ref[rows, :].astype(jnp.float32).T
    gain = gain_ref[:, pl.ds(pl.multiple_of(tab_ref[1] * TILE, TILE), TILE)]
    part = jnp.sum(weight * mine, axis=0, keepdims=True) / gain
    high = part.astype(jnp.bfloat16).astype(jnp.float32)
    tail = out_ref.shape[0] - columns
    row = lax.broadcasted_iota(jnp.int32, (tail, TILE), 0)
    ends = jnp.where(row == 0, high, jnp.where(row == 1, part - high, 0.0))
    out_ref[columns:, :] = ends.astype(jnp.bfloat16)


def pack(sent, got, weight, gain, table, devices):
    vmem = pl.BlockSpec(memory_space=pltpu.VMEM)
    return pl.pallas_call(
        functools.partial(pack_kernel, devices=devices),
        in_specs=[pl.BlockSpec(memory_space=pltpu.SMEM)] + [vmem] * 4,
        out_specs=vmem,
        out_shape=jax.ShapeDtypeStruct((sent.shape[0] + 16, TILE), jnp.bfloat16),
    )(table, sent, got, weight, gain)


def finish_kernel(tab_ref, near_ref, far_ref, weight_ref, gain_ref):
    columns = weight_ref.shape[1]
    for k in range(4):
        part = (near_ref, far_ref)[k // 2].at[k % 2]
        rows = pl.ds(pl.multiple_of(tab_ref[k] * TILE, TILE), TILE)
        weight_ref[rows, :] = part[:columns, :].astype(jnp.float32).T
        ends = part[columns:, :].astype(jnp.float32)
        gain_ref[pl.ds(tab_ref[k], 1), :] = ends[0:1] + ends[1:2]


def finish(parts, table):
    vmem = pl.BlockSpec(memory_space=pltpu.VMEM)
    columns = parts[0].shape[1] - 16
    return pl.pallas_call(
        finish_kernel,
        in_specs=[pl.BlockSpec(memory_space=pltpu.SMEM)] + [vmem] * 2,
        out_specs=[vmem] * 2,
        out_shape=[
            jax.ShapeDtypeStruct((4 * TILE, columns), jnp.float32),
            jax.ShapeDtypeStruct((4, TILE), jnp.float32),
        ],
    )(table, *parts)


def order_kernel(tab_ref, in_ref, out_ref):
    for node in range(in_ref.shape[0]):
        out_ref[node] = in_ref[tab_ref[node]]


def order(rows, table):
    vmem = pl.BlockSpec(memory_space=pltpu.VMEM)
    return pl.pallas_call(
        order_kernel,
        in_specs=[pl.BlockSpec(memory_space=pltpu.SMEM), vmem],
        out_specs=vmem,
        out_shape=jax.ShapeDtypeStruct(rows.shape, rows.dtype),
    )(table, rows)


def shards(tokens, norm_gain, weight_values, weight_scale, key_cotangent):
    y, zl, x, c = (lax.axis_index(a) for a in ("y", "zl", "x", "c"))
    width = tokens.shape[1]
    columns = weight_values.shape[1]
    gain = norm_gain.reshape(1, width)
    devices = 1
    for axis in EVERY:
        devices *= lax.axis_size(axis)

    def offset(core, first, second):
        masks = (1 + 2 * core, 3 - 2 * core)
        return first * masks[0] ^ second * masks[1]

    label = jnp.arange(32, dtype=jnp.int32)
    bits = [label // 16] + [label // k % 2 for k in (8, 4, 2, 1)]
    tables = []
    for core in (c, 1 - c):
        chip = (zl ^ bits[0]) * 4 + (x ^ offset(core, bits[3], bits[4]))
        tables.append((chip * 2 + core) * 4 + (y ^ offset(core, bits[1], bits[2])))
    shards_at = jnp.stack(
        [((zl ^ z) * 4 + (x ^ offset(c, k % 2, k // 2))) * 2 + (c ^ lane) for z, k, lane in PIECES]
    ).astype(jnp.int32)

    own = widen_weight(weight_values, weight_scale)
    own_c = swap(own, "c")
    up = pair_z(own)
    cot_own = key_cotangent.T
    cot_got = swap(cot_own, "c")
    mine, other, inverse = norm_tiles(tie(tokens, own, cot_own), gain, jnp.stack(tables))
    got = swap(other, "c")
    got, up = lax.optimization_barrier((got, up))
    base = jnp.stack([own, own_c])
    near = pair(base, "x", 0)
    up_c = swap(up, "c")
    sent, kept = grad_tiles(mine, got, cot_own, cot_got)

    first = sent[0]
    second, near, up_c = lax.optimization_barrier((sent[1], near, up_c))
    moved = (pair(first, "y", 0), pair_z(second))
    near_c = swap(near, "c")
    above = jnp.stack([up, up_c])
    above_near = pair(above, "x", 0)
    (first, kept_first), (second, kept_second) = (halve(add(k, m)) for k, m in zip(kept, moved))
    second, near_c, above_near = lax.optimization_barrier((second, near_c, above_near))
    moved = (pair_z(first), pair(second, "y", 0))
    above_near_c = swap(above_near, "c")
    far = pair(jnp.stack([near_c[1], above_near_c[1]]), "x", 0)
    (first, kept_first), (second, kept_second) = (
        halve(add(k, m)) for k, m in zip((kept_first, kept_second), moved)
    )
    moved = pair(jnp.stack([first, second]), "y", 1)
    total = jnp.stack([add(kept_first, moved[0]), add(kept_second, moved[1])], axis=1)
    send, kept = halve(total)
    send, far = lax.optimization_barrier((send, far))
    moved = pair(send, "x", 0)
    far_c = swap(far, "c")
    send, kept = halve(add(kept, moved))
    send, far_c = lax.optimization_barrier((send, far_c))
    weights = [base, above, near, near_c, above_near, above_near_c, far, far_c]

    moved = pair(send, "x", 1)
    projected, moment = forward(tokens, inverse, gain, key_cotangent, weights, shards_at)
    moved, moment = lax.optimization_barrier((moved, moment))
    send = add(kept, moved).astype(jnp.bfloat16).reshape(columns, TILE)
    moved = pair(send, "zh", 0)
    send = (send.astype(jnp.float32) + moved.astype(jnp.float32)).astype(jnp.bfloat16)
    moved = pair(send, "zh", 1)

    node = (zl * 4 + x) * 2 + c
    at = jnp.stack([y, node * 4 + y]).astype(jnp.int32)
    packed = pack(send, moved, own, gain, at, devices)[None]
    pieces = jnp.concatenate([packed, pair(packed, "y", 0)])
    pieces, moment = lax.optimization_barrier((pieces, moment))
    moved = pair(pieces, "y", 1)
    token_grads = backward(tokens, inverse, gain, key_cotangent, moment, weights, shards_at)
    moved = tie(moved, token_grads)
    quarters = jnp.stack([y ^ offset(c, k % 2, k // 2) for k in range(4)]).astype(jnp.int32)
    weight_grads, gains = finish((pieces, moved), quarters)
    gains = gains[None]
    for move in (
        lambda a: swap(a, "c"),
        lambda a: pair(a, "x", 0),
        lambda a: pair(a, "x", 1),
        lambda a: swap(a, "zl"),
    ):
        gains = jnp.concatenate([gains, move(gains)])
    nodes = jnp.arange(16, dtype=jnp.int32)
    across = nodes // 2 % 4 ^ x
    high, mixed = across // 2, across % 2 ^ across // 2
    step0, step1 = jnp.where(c == 0, mixed, high), jnp.where(c == 0, high, mixed)
    relative = (nodes // 8 ^ zl) * 8 + step1 * 4 + step0 * 2 + (nodes % 2 ^ c)
    gain_grads = order(gains, relative.astype(jnp.int32)).reshape(width)
    return (projected, token_grads, weight_grads, gain_grads)


def solution(mesh):
    fine = Mesh(mesh.devices.reshape(4, 4, 2, 4, 2), EVERY)
    rows = P(EVERY, None)
    return jax.shard_map(
        shards,
        mesh=fine,
        in_specs=(rows, P(), P(NODE, None), P(NODE, None), rows),
        out_specs=(rows, rows, P(NODE, None), P()),
        check_vma=False,
    )
```

time: 166 us -> 163 us (0.982)
  between operations: 14.4 us -> 1.06 us
  waiting for transfers between devices: 47.3 us -> 56.6 us
  starting transfers between devices: 44.1 us -> 40.4 us
  other arithmetic: 5.43 us -> 8.53 us
  Pallas kernels: 38.9 us -> 40.6 us
    ppermute x26, waiting for transfers between devices: 47.2 us -> 56.6 us  [the longest x14 47.2 us: pair(): return lax.ppermute(array, (axis, 'c'), moves)]
    ppermute x26, starting transfers between devices: 44 us -> 40.4 us  [the longest x14 19 us: pair(): return lax.ppermute(array, (axis, 'c'), moves)]
    pallas_call x1, Pallas kernels: 9.4 us -> 12.3 us  [backward(): pl.pallas_call(backward_kernel, in_specs=[pl.BlockSpec(memory_space=pltpu...]
    concatenate x1 -> x4, other arithmetic: 0.68 us -> 3.05 us  [the longest x3 2.06 us: shards(): gains = jnp.concatenate([gains, move(gains)])]
    unnamed x42 -> x57, local copies, waits for them, and re-layouts: 15.2 us -> 13.5 us
    add x10 -> x7, other arithmetic: 3.62 us -> 2.37 us  [the longest x5 1.81 us: add(): return kept + got.astype(jnp.float32)]
  transfers between devices with their start and end apart: 28 -> 26, of which waited for: 14 -> 16; matrix products, arithmetic and copies ran while one was open for 4% -> 4% of each run, Pallas kernels for 19% -> 17%
where the time goes in v4:
time: 163 us; the launch traced here: 162 us
  waiting for transfers between devices  56.6 us (35%)
  Pallas kernels  40.6 us (25%)
  starting transfers between devices  40.4 us (25%)
  local copies, waits for them, and re-layouts  14.7 us (9%)
  other arithmetic  8.53 us (5%)
    ppermute x14, waiting for transfers between devices, pair(): return lax.ppermute(array, (axis, 'c'), moves)  47.2 us
    ppermute x14, starting transfers between devices, pair(): return lax.ppermute(array, (axis, 'c'), moves)  19 us
    unnamed x57, local copies, waits for them, and re-layouts  13.5 us
    pallas_call x1, Pallas kernels, backward(): pl.pallas_call(backward_kernel, in_specs=[pl.BlockSpec(memory_space=pltpu...  12.3 us
    ppermute x9, starting transfers between devices, swap(): return lax.ppermute(array, axis, [(0, 1), (1, 0)])  12 us
    ppermute x3, starting transfers between devices, pair_z(): return lax.ppermute(array, ('zh', 'zl', 'c'), moves)  9.34 us
    pallas_call x1, Pallas kernels, forward(): pl.pallas_call(forward_kernel, in_specs=[pl.BlockSpec(memory_space=pltpu....  7.52 us
    pallas_call x1, Pallas kernels, grad_tiles(): pl.pallas_call(grad_kernel, out_shape=[jax.ShapeDtypeStruct(shape, jnp.bf...  7.03 us
  transfers between devices with their start and end apart: 26, of which 16 were waited for; matrix products, arithmetic and copies ran while one was open for 4% of the time, Pallas kernels for 17%

profile of v4, /device:TPU:1, one launch (start us, length us, event | category | flops | bytes accessed | tf_op | source)
XLA Modules:
  0.0 161.9 jit_solution(9528882710838666867)
XLA Ops:
  4.9 5.9 %shard_map.85 = (bf16[320,4096]{1,0:T(8,128)(2,1)S(1)}, bf16[320,4096]{1,0:T(8,128)(2,1)S(1)}, f32[320,1]{1,0:T(8,128)S(1)}) custom-call(s32[2,32]{1,0:T(2,128)S(1)} %pad_add_fusion.tab_ref, bf16[320,8192]{1,0:T(8,128)(2,1)} %tok_ref.4, f32[1,8192]{1,0:T(1,128)S(1)} %bitcast.53), custom_call_target="tpu_custom_call" | custom-call | flops 15728640 | bytes 10485760 | tf_op jit(solution)/shard_map/pallas_call | solution.py:54
  13.0 3.2 %collective-permute-start.1 = (bf16[320,4096]{1,0:T(8,128)(2,1)S(1)}, bf16[320,4096]{1,0:T(8,128)(2,1)S(1)}, u32[]{:S(2)}, u32[]{:S(2)}) collective-permute-start(bf16[320,4096]{1,0:T(8,128)(2,1)S(1)} %get-tuple-element.35), channel_id=1, source_target_pairs={{0,1},{1,0},{2,3},{3,2},{4,5},{5,4},{6,7},{7,6},{8,9},{9,8},{10,11... | collective-permute-start | bytes 7864328 | tf_op jit(solution)/shard_map/ppermute | solution.py:223
  16.2 3.8 %collective-permute-start.2 = (bf16[512,512]{1,0:T(8,128)(2,1)S(1)}, bf16[512,512]{1,0:T(8,128)(2,1)S(1)}, u32[]{:S(2)}, u32[]{:S(2)}) collective-permute-start(bf16[512,512]{1,0:T(8,128)(2,1)S(1)} %copy-done.21), channel_id=1, source_target_pairs={{0,8},{1,57},{8,0},{9,17},{16,24},{17,9},{24,16},{25,33},{32,40},{... | collective-permute-start | bytes 1572872 | tf_op jit(solution)/shard_map/ppermute | solution.py:239
  22.7 3.9 %collective-permute-done.2 = bf16[512,512]{1,0:T(8,128)(2,1)S(1)} collective-permute-done((bf16[512,512]{1,0:T(8,128)(2,1)S(1)}, bf16[512,512]{1,0:T(8,128)(2,1)S(1)}, u32[]{:S(2)}, u32[]{:S(2)}) %collective-permute-start.2) | collective-permute-done | bytes 524320 | tf_op jit(solution)/shard_map/ppermute | solution.py:239
  28.1 7.0 %shard_map.86 = (bf16[16,256,128]{2,1,0:T(8,128)(2,1)S(1)}, bf16[16,256,128]{2,1,0:T(8,128)(2,1)S(1)}, f32[16,256,128]{2,1,0:T(8,128)S(1)}, f32[16,256,128]{2,1,0:T(8,128)}) custom-call(bf16[320,4096]{1,0:T(8,128)(2,1)} %copy-done.17, bf16[320,4096]{1,0:T(8,128)(2,1)} %copy-done.25, bf16[512,320]{1,0:T(8,128)(2,1)S(1)} %bitcast.57, ...), custom_call_target="tpu_custom_call" | custom-call | flops 2684354560 | bytes 11534336 | tf_op jit(solution)/shard_map/pallas_call | solution.py:102
  35.1 2.8 %collective-permute-start.10 = (bf16[16,256,128]{2,1,0:T(8,128)(2,1)S(1)}, bf16[16,256,128]{2,1,0:T(8,128)(2,1)S(1)}, u32[]{:S(2)}, u32[]{:S(2)}) collective-permute-start(bf16[16,256,128]{2,1,0:T(8,128)(2,1)S(1)} %get-tuple-element.47), channel_id=1, source_target_pairs={{0,64},{1,193},{64,0},{65,129},{128,192},{129,65},{192,128},{193,1... | collective-permute-start | bytes 3145736 | tf_op jit(solution)/shard_map/ppermute | solution.py:230
  38.0 2.7 %collective-permute-start.6 = (bf16[16,256,128]{2,1,0:T(8,128)(2,1)S(1)}, bf16[16,256,128]{2,1,0:T(8,128)(2,1)S(1)}, u32[]{:S(2)}, u32[]{:S(2)}) collective-permute-start(bf16[16,256,128]{2,1,0:T(8,128)(2,1)S(1)} %get-tuple-element.43), channel_id=1, source_target_pairs={{0,8},{1,57},{8,0},{9,17},{16,24},{17,9},{24,16},{25,33},{32,40},{... | collective-permute-start | bytes 3145736 | tf_op jit(solution)/shard_map/ppermute | solution.py:239
  40.8 2.6 %collective-permute-start.8 = (bf16[2,512,512]{2,1,0:T(8,128)(2,1)S(1)}, bf16[2,512,512]{2,1,0:T(8,128)(2,1)S(1)}, u32[]{:S(2)}, u32[]{:S(2)}) collective-permute-start(bf16[2,512,512]{2,1,0:T(8,128)(2,1)S(1)} %pad_maximum_fusion.1.refs_1_), channel_id=1, source_target_pairs={{0,2},{1,7},{2,0},{3,5},{4,6},{5,3},{6,4},{7,1},{8,10},{9,15},{10,... | collective-permute-start | bytes 3145736 | tf_op jit(solution)/shard_map/ppermute | solution.py:230
  43.4 6.8 %collective-permute-done.10 = bf16[16,256,128]{2,1,0:T(8,128)(2,1)S(1)} collective-permute-done((bf16[16,256,128]{2,1,0:T(8,128)(2,1)S(1)}, bf16[16,256,128]{2,1,0:T(8,128)(2,1)S(1)}, u32[]{:S(2)}, u32[]{:S(2)}) %collective-permute-start.10) | collective-permute-done | bytes 1048608 | tf_op jit(solution)/shard_map/ppermute | solution.py:230
  50.5 2.7 %collective-permute-start.11 = (bf16[8,256,128]{2,1,0:T(8,128)(2,1)S(1)}, bf16[8,256,128]{2,1,0:T(8,128)(2,1)S(1)}, u32[]{:S(2)}, u32[]{:S(2)}) collective-permute-start(bf16[8,256,128]{2,1,0:T(8,128)(2,1)S(1)} %slice.119), channel_id=1, source_target_pairs={{0,8},{1,57},{8,0},{9,17},{16,24},{17,9},{24,16},{25,33},{32,40},{... | collective-permute-start | bytes 1572872 | tf_op jit(solution)/shard_map/ppermute | solution.py:239
  60.0 5.5 %collective-permute-done.12 = bf16[8,256,128]{2,1,0:T(8,128)(2,1)S(1)} collective-permute-done((bf16[8,256,128]{2,1,0:T(8,128)(2,1)S(1)}, bf16[8,256,128]{2,1,0:T(8,128)(2,1)S(1)}, u32[]{:S(2)}, u32[]{:S(2)}) %collective-permute-start.12) | collective-permute-done | bytes 524320 | tf_op jit(solution)/shard_map/ppermute | solution.py:230
  66.6 2.8 %collective-permute-start.14 = (bf16[2,512,512]{2,1,0:T(8,128)(2,1)S(1)}, bf16[2,512,512]{2,1,0:T(8,128)(2,1)}, u32[]{:S(2)}, u32[]{:S(2)}) collective-permute-start(bf16[2,512,512]{2,1,0:T(8,128)(2,1)S(1)} %pad_maximum_fusion.2), channel_id=1, source_target_pairs={{0,2},{1,7},{2,0},{3,5},{4,6},{5,3},{6,4},{7,1},{8,10},{9,15},{10,... | collective-permute-start | bytes 3145736 | tf_op jit(solution)/shard_map/ppermute | solution.py:230
  69.5 8.4 %collective-permute-done.13 = bf16[2,4,256,128]{3,2,1,0:T(8,128)(2,1)S(1)} collective-permute-done((bf16[2,4,256,128]{3,2,1,0:T(8,128)(2,1)S(1)}, bf16[2,4,256,128]{3,2,1,0:T(8,128)(2,1)S(1)}, u32[]{:S(2)}, u32[]{:S(2)}) %collective-permute-start.13) | collective-permute-done | bytes 524320 | tf_op jit(solution)/shard_map/ppermute | solution.py:230
  81.8 2.5 %collective-permute-start.15 = (bf16[2,2,256,128]{3,2,0,1:T(8,128)(2,1)}, bf16[2,2,256,128]{3,2,0,1:T(8,128)(2,1)}, u32[]{:S(2)}, u32[]{:S(2)}) collective-permute-start(bf16[2,2,256,128]{3,2,0,1:T(8,128)(2,1)} %fusion.1), channel_id=1, source_target_pairs={{0,2},{1,7},{2,0},{3,5},{4,6},{5,3},{6,4},{7,1},{8,10},{9,15},{10,... | collective-permute-start | bytes 786440 | tf_op jit(solution)/shard_map/ppermute | solution.py:230
  84.4 4.1 %collective-permute-done.15 = bf16[2,2,256,128]{3,2,0,1:T(8,128)(2,1)} collective-permute-done((bf16[2,2,256,128]{3,2,0,1:T(8,128)(2,1)}, bf16[2,2,256,128]{3,2,0,1:T(8,128)(2,1)}, u32[]{:S(2)}, u32[]{:S(2)}) %collective-permute-start.15) | collective-permute-done | bytes 262176 | tf_op jit(solution)/shard_map/ppermute | solution.py:230
  91.0 7.5 %shard_map.87 = (bf16[320,512]{1,0:T(8,128)(2,1)}, f32[320,1]{1,0:T(8,128)S(1)}) custom-call(s32[16]{0:T(128)S(1)} %stack.133.tab_ref, bf16[320,8192]{1,0:T(8,128)(2,1)} %tok_ref.4, f32[320,1]{1,0:T(8,128)S(1)} %copy-done.10, f32[1,8192]{1,0:T(1,128)S(1)} %bitcast.54, bf16[320,512]{1,0:T(8,128)(2,1)S(1)} %copy-done.8, ...), custom_call_target="tpu_custom_call" | custom-call | flops 2684354560 | bytes 13631488 | tf_op jit(solution)/shard_map/pallas_call | solution.py:172
  100.5 4.7 %collective-permute-done.18 = bf16[512,128]{1,0:T(8,128)(2,1)S(1)} collective-permute-done((bf16[512,128]{1,0:T(8,128)(2,1)S(1)}, bf16[512,128]{1,0:T(8,128)(2,1)S(1)}, u32[]{:S(2)}, u32[]{:S(2)}) %collective-permute-start.18) | collective-permute-done | bytes 131104 | tf_op jit(solution)/shard_map/ppermute | solution.py:230
  106.5 5.1 %collective-permute-done.19.got_ref = bf16[512,128]{1,0:T(8,128)(2,1)} collective-permute-done((bf16[512,128]{1,0:T(8,128)(2,1)}, bf16[512,128]{1,0:T(8,128)(2,1)}, u32[]{:S(2)}, u32[]{:S(2)}) %collective-permute-start.19) | collective-permute-done | bytes 131104 | tf_op jit(solution)/shard_map/ppermute | solution.py:230
  116.4 2.6 %collective-permute-done.20 = bf16[1,528,128]{2,1,0:T(8,128)(2,1)} collective-permute-done((bf16[1,528,128]{2,1,0:T(8,128)(2,1)}, bf16[1,528,128]{2,1,0:T(8,128)(2,1)}, u32[]{:S(2)}, u32[]{:S(2)}) %collective-permute-start.20) | collective-permute-done | bytes 135200 | tf_op jit(solution)/shard_map/ppermute | solution.py:230
  125.3 12.3 %shard_map.89 = bf16[320,8192]{1,0:T(8,128)(2,1)} custom-call(s32[16]{0:T(128)S(1)} %stack.133.tab_ref, bf16[320,8192]{1,0:T(8,128)(2,1)} %tok_ref.4, f32[320,1]{1,0:T(8,128)S(1)} %copy-done.11, f32[1,8192]{1,0:T(1,128)S(1)} %bitcast.55, bf16[320,512]{1,0:T(8,128)(2,1)S(1)} %copy-done.8, f32[320,1]{1,0:T(8,128)S(1)} %copy-done.16, ...), custom_call_target="tpu_custom_call" | custom-call | flops 2684354560 | bytes 18874368 | tf_op jit(solution)/shard_map/pallas_call | solution.py:201
  139.8 8.3 %collective-permute-start.22 = (f32[1,4,128]{2,1,0:T(4,128)}, f32[1,4,128]{2,1,0:T(4,128)S(1)}, u32[]{:S(2)}, u32[]{:S(2)}) collective-permute-start(f32[1,4,128]{2,1,0:T(4,128)} %bitcast.66), channel_id=1, source_target_pairs={{0,1},{1,0},{2,3},{3,2},{4,5},{5,4},{6,7},{7,6},{8,9},{9,8},{10,11... | collective-permute-start | bytes 6152 | tf_op jit(solution)/shard_map/ppermute | solution.py:223
  150.4 3.1 %collective-permute-done.23 = f32[2,4,128]{2,1,0:T(4,128)S(1)} collective-permute-done((f32[2,4,128]{2,1,0:T(4,128)S(1)}, f32[2,4,128]{2,1,0:T(4,128)S(1)}, u32[]{:S(2)}, u32[]{:S(2)}) %collective-permute-start.23) | collective-permute-done | bytes 4128 | tf_op jit(solution)/shard_map/ppermute | solution.py:230
  154.2 2.5 %collective-permute-done.24 = f32[4,4,128]{2,1,0:T(4,128)S(1)} collective-permute-done((f32[4,4,128]{2,1,0:T(4,128)S(1)}, f32[4,4,128]{2,1,0:T(4,128)S(1)}, u32[]{:S(2)}, u32[]{:S(2)}) %collective-permute-start.24) | collective-permute-done | bytes 8224 | tf_op jit(solution)/shard_map/ppermute | solution.py:230
  157.3 2.6 %collective-permute-done.25 = f32[8,4,128]{2,1,0:T(4,128)S(1)} collective-permute-done((f32[8,4,128]{2,1,0:T(4,128)S(1)}, f32[8,4,128]{2,1,0:T(4,128)S(1)}, u32[]{:S(2)}, u32[]{:S(2)}) %collective-permute-start.25) | collective-permute-done | bytes 16416 | tf_op jit(solution)/shard_map/ppermute | solution.py:223
  (125 shorter events, 47.4 us)
Async XLA Ops:
  13.0 13.7 %collective-permute-start.1 = (bf16[320,4096]{1,0:T(8,128)(2,1)S(1)}, bf16[320,4096]{1,0:T(8,128)(2,1)S(1)}, u32[]{:S(2)}, u32[]{:S(2)}) collective-permute-start(bf16[320,4096]{1,0:T(8,128)(2,1)S(1)} %get-tuple-element.35), channel_id=1, source_target_pairs={{0,1},{1,0},{2,3},{3,2},{4,5},{5,4},{6,7},{7,6},{8,9},{9,8},{10,11... | collective-permute-start | bytes 7864328 | tf_op jit(solution)/shard_map/ppermute | solution.py:223
  16.2 5.3 %collective-permute-start = (bf16[512,512]{1,0:T(8,128)(2,1)S(1)}, bf16[512,512]{1,0:T(8,128)(2,1)S(1)}, u32[]{:S(2)}, u32[]{:S(2)}) collective-permute-start(bf16[512,512]{1,0:T(8,128)(2,1)S(1)} %copy-done.21), channel_id=1, source_target_pairs={{0,1},{1,0},{2,3},{3,2},{4,5},{5,4},{6,7},{7,6},{8,9},{9,8},{10,11... | collective-permute-start | bytes 1572872 | tf_op jit(solution)/shard_map/ppermute | solution.py:223
  16.2 10.4 %collective-permute-start.2 = (bf16[512,512]{1,0:T(8,128)(2,1)S(1)}, bf16[512,512]{1,0:T(8,128)(2,1)S(1)}, u32[]{:S(2)}, u32[]{:S(2)}) collective-permute-start(bf16[512,512]{1,0:T(8,128)(2,1)S(1)} %copy-done.21), channel_id=1, source_target_pairs={{0,8},{1,57},{8,0},{9,17},{16,24},{17,9},{24,16},{25,33},{32,40},{... | collective-permute-start | bytes 1572872 | tf_op jit(solution)/shard_map/ppermute | solution.py:239
  20.0 6.6 %collective-permute-start.3 = (bf16[512,320]{1,0:T(8,128)(2,1)S(1)}, bf16[512,320]{1,0:T(8,128)(2,1)S(1)}, u32[]{:S(2)}, u32[]{:S(2)}) collective-permute-start(bf16[512,320]{1,0:T(8,128)(2,1)S(1)} %bitcast.56), channel_id=1, source_target_pairs={{0,1},{1,0},{2,3},{3,2},{4,5},{5,4},{6,7},{7,6},{8,9},{9,8},{10,11... | collective-permute-start | bytes 983048 | tf_op jit(solution)/shard_map/ppermute | solution.py:223
  21.6 16.4 %collective-permute-start.4 = (bf16[2,512,512]{2,1,0:T(8,128)(2,1)S(1)}, bf16[2,512,512]{2,1,0:T(8,128)(2,1)S(1)}, u32[]{:S(2)}, u32[]{:S(2)}) collective-permute-start(bf16[2,512,512]{2,1,0:T(8,128)(2,1)S(1)} %pad_maximum_fusion.refs_0_), channel_id=1, source_target_pairs={{0,2},{1,7},{2,0},{3,5},{4,6},{5,3},{6,4},{7,1},{8,10},{9,15},{10,... | collective-permute-start | bytes 3145736 | tf_op jit(solution)/shard_map/ppermute | solution.py:230
  26.6 11.3 %collective-permute-start.5 = (bf16[512,512]{1,0:T(8,128)(2,1)S(1)}, bf16[512,512]{1,0:T(8,128)(2,1)S(1)}, u32[]{:S(2)}, u32[]{:S(2)}) collective-permute-start(bf16[512,512]{1,0:T(8,128)(2,1)S(1)} %collective-permute-done.2), channel_id=1, source_target_pairs={{0,1},{1,0},{2,3},{3,2},{4,5},{5,4},{6,7},{7,6},{8,9},{9,8},{10,11... | collective-permute-start | bytes 1572872 | tf_op jit(solution)/shard_map/ppermute | solution.py:223
  35.1 15.0 %collective-permute-start.10 = (bf16[16,256,128]{2,1,0:T(8,128)(2,1)S(1)}, bf16[16,256,128]{2,1,0:T(8,128)(2,1)S(1)}, u32[]{:S(2)}, u32[]{:S(2)}) collective-permute-start(bf16[16,256,128]{2,1,0:T(8,128)(2,1)S(1)} %get-tuple-element.47), channel_id=1, source_target_pairs={{0,64},{1,193},{64,0},{65,129},{128,192},{129,65},{192,128},{193,1... | collective-permute-start | bytes 3145736 | tf_op jit(solution)/shard_map/ppermute | solution.py:230
  38.0 15.2 %collective-permute-start.6 = (bf16[16,256,128]{2,1,0:T(8,128)(2,1)S(1)}, bf16[16,256,128]{2,1,0:T(8,128)(2,1)S(1)}, u32[]{:S(2)}, u32[]{:S(2)}) collective-permute-start(bf16[16,256,128]{2,1,0:T(8,128)(2,1)S(1)} %get-tuple-element.43), channel_id=1, source_target_pairs={{0,8},{1,57},{8,0},{9,17},{16,24},{17,9},{24,16},{25,33},{32,40},{... | collective-permute-start | bytes 3145736 | tf_op jit(solution)/shard_map/ppermute | solution.py:239
  40.7 12.9 %collective-permute-start.7 = (bf16[2,512,512]{2,1,0:T(8,128)(2,1)S(1)}, bf16[2,512,512]{2,1,0:T(8,128)(2,1)S(1)}, u32[]{:S(2)}, u32[]{:S(2)}) collective-permute-start(bf16[2,512,512]{2,1,0:T(8,128)(2,1)S(1)} %collective-permute-done.4.refs_2_), channel_id=1, source_target_pairs={{0,1},{1,0},{2,3},{3,2},{4,5},{5,4},{6,7},{7,6},{8,9},{9,8},{10,11... | collective-permute-start | bytes 3145736 | tf_op jit(solution)/shard_map/ppermute | solution.py:223
  40.8 14.9 %collective-permute-start.8 = (bf16[2,512,512]{2,1,0:T(8,128)(2,1)S(1)}, bf16[2,512,512]{2,1,0:T(8,128)(2,1)S(1)}, u32[]{:S(2)}, u32[]{:S(2)}) collective-permute-start(bf16[2,512,512]{2,1,0:T(8,128)(2,1)S(1)} %pad_maximum_fusion.1.refs_1_), channel_id=1, source_target_pairs={{0,2},{1,7},{2,0},{3,5},{4,6},{5,3},{6,4},{7,1},{8,10},{9,15},{10,... | collective-permute-start | bytes 3145736 | tf_op jit(solution)/shard_map/ppermute | solution.py:230
  50.5 9.3 %collective-permute-start.11 = (bf16[8,256,128]{2,1,0:T(8,128)(2,1)S(1)}, bf16[8,256,128]{2,1,0:T(8,128)(2,1)S(1)}, u32[]{:S(2)}, u32[]{:S(2)}) collective-permute-start(bf16[8,256,128]{2,1,0:T(8,128)(2,1)S(1)} %slice.119), channel_id=1, source_target_pairs={{0,8},{1,57},{8,0},{9,17},{16,24},{17,9},{24,16},{25,33},{32,40},{... | collective-permute-start | bytes 1572872 | tf_op jit(solution)/shard_map/ppermute | solution.py:239
  55.8 9.8 %collective-permute-start.9 = (bf16[2,512,512]{2,1,0:T(8,128)(2,1)S(1)}, bf16[2,512,512]{2,1,0:T(8,128)(2,1)S(1)}, u32[]{:S(2)}, u32[]{:S(2)}) collective-permute-start(bf16[2,512,512]{2,1,0:T(8,128)(2,1)S(1)} %collective-permute-done.8.refs_4_), channel_id=1, source_target_pairs={{0,1},{1,0},{2,3},{3,2},{4,5},{5,4},{6,7},{7,6},{8,9},{9,8},{10,11... | collective-permute-start | bytes 3145736 | tf_op jit(solution)/shard_map/ppermute | solution.py:223
  56.2 9.2 %collective-permute-start.12 = (bf16[8,256,128]{2,1,0:T(8,128)(2,1)S(1)}, bf16[8,256,128]{2,1,0:T(8,128)(2,1)S(1)}, u32[]{:S(2)}, u32[]{:S(2)}) collective-permute-start(bf16[8,256,128]{2,1,0:T(8,128)(2,1)S(1)} %slice.120), channel_id=1, source_target_pairs={{0,64},{1,193},{64,0},{65,129},{128,192},{129,65},{192,128},{193,1... | collective-permute-start | bytes 1572872 | tf_op jit(solution)/shard_map/ppermute | solution.py:230
  66.6 15.2 %collective-permute-start.14 = (bf16[2,512,512]{2,1,0:T(8,128)(2,1)S(1)}, bf16[2,512,512]{2,1,0:T(8,128)(2,1)}, u32[]{:S(2)}, u32[]{:S(2)}) collective-permute-start(bf16[2,512,512]{2,1,0:T(8,128)(2,1)S(1)} %pad_maximum_fusion.2), channel_id=1, source_target_pairs={{0,2},{1,7},{2,0},{3,5},{4,6},{5,3},{6,4},{7,1},{8,10},{9,15},{10,... | collective-permute-start | bytes 3145736 | tf_op jit(solution)/shard_map/ppermute | solution.py:230
  69.4 8.5 %collective-permute-start.13 = (bf16[2,4,256,128]{3,2,1,0:T(8,128)(2,1)S(1)}, bf16[2,4,256,128]{3,2,1,0:T(8,128)(2,1)S(1)}, u32[]{:S(2)}, u32[]{:S(2)}) collective-permute-start(bf16[2,4,256,128]{3,2,1,0:T(8,128)(2,1)S(1)} %pad_maximum_fusion.4), channel_id=1, source_target_pairs={{0,192},{1,65},{64,128},{65,1},{128,64},{129,193},{192,0},{193,129... | collective-permute-start | bytes 1572872 | tf_op jit(solution)/shard_map/ppermute | solution.py:230
  81.8 7.9 %collective-permute-start.16 = (bf16[2,512,512]{2,1,0:T(8,128)(2,1)}, bf16[2,512,512]{2,1,0:T(8,128)(2,1)}, u32[]{:S(2)}, u32[]{:S(2)}) collective-permute-start(bf16[2,512,512]{2,1,0:T(8,128)(2,1)} %collective-permute-done.14.refs_6_), channel_id=1, source_target_pairs={{0,1},{1,0},{2,3},{3,2},{4,5},{5,4},{6,7},{7,6},{8,9},{9,8},{10,11... | collective-permute-start | bytes 3145736 | tf_op jit(solution)/shard_map/ppermute | solution.py:223
  81.8 6.7 %collective-permute-start.15 = (bf16[2,2,256,128]{3,2,0,1:T(8,128)(2,1)}, bf16[2,2,256,128]{3,2,0,1:T(8,128)(2,1)}, u32[]{:S(2)}, u32[]{:S(2)}) collective-permute-start(bf16[2,2,256,128]{3,2,0,1:T(8,128)(2,1)} %fusion.1), channel_id=1, source_target_pairs={{0,2},{1,7},{2,0},{3,5},{4,6},{5,3},{6,4},{7,1},{8,10},{9,15},{10,... | collective-permute-start | bytes 786440 | tf_op jit(solution)/shard_map/ppermute | solution.py:230
  89.8 9.4 %collective-permute-start.17 = (bf16[1,2,256,128]{3,2,0,1:T(8,128)(2,1)S(1)}, bf16[1,2,256,128]{3,2,0,1:T(8,128)(2,1)S(1)}, u32[]{:S(2)}, u32[]{:S(2)}) collective-permute-start(bf16[1,2,256,128]{3,2,0,1:T(8,128)(2,1)S(1)} %slice.121), channel_id=1, source_target_pairs={{0,6},{1,3},{2,4},{3,1},{4,2},{5,7},{6,0},{7,5},{8,14},{9,11},{10,... | collective-permute-start | bytes 393224 | tf_op jit(solution)/shard_map/ppermute | solution.py:230
  99.2 6.0 %collective-permute-start.18 = (bf16[512,128]{1,0:T(8,128)(2,1)S(1)}, bf16[512,128]{1,0:T(8,128)(2,1)S(1)}, u32[]{:S(2)}, u32[]{:S(2)}) collective-permute-start(bf16[512,128]{1,0:T(8,128)(2,1)S(1)} %bitcast.61), channel_id=1, source_target_pairs={{0,16},{1,49},{16,0},{17,33},{32,48},{33,17},{48,32},{49,1},{2,18}... | collective-permute-start | bytes 393224 | tf_op jit(solution)/shard_map/ppermute | solution.py:230
  105.9 5.7 %collective-permute-start.19 = (bf16[512,128]{1,0:T(8,128)(2,1)}, bf16[512,128]{1,0:T(8,128)(2,1)}, u32[]{:S(2)}, u32[]{:S(2)}) collective-permute-start(bf16[512,128]{1,0:T(8,128)(2,1)} %add_convert_fusion.sent_ref), channel_id=1, source_target_pairs={{0,48},{1,17},{16,32},{17,1},{32,16},{33,49},{48,0},{49,33},{2,50}... | collective-permute-start | bytes 393224 | tf_op jit(solution)/shard_map/ppermute | solution.py:230
  113.6 5.4 %collective-permute-start.20 = (bf16[1,528,128]{2,1,0:T(8,128)(2,1)}, bf16[1,528,128]{2,1,0:T(8,128)(2,1)}, u32[]{:S(2)}, u32[]{:S(2)}) collective-permute-start(bf16[1,528,128]{2,1,0:T(8,128)(2,1)} %bitcast.59), channel_id=1, source_target_pairs={{0,64},{1,193},{64,0},{65,129},{128,192},{129,65},{192,128},{193,1... | collective-permute-start | bytes 405512 | tf_op jit(solution)/shard_map/ppermute | solution.py:230
  120.0 17.5 %collective-permute-start.21 = (bf16[2,528,128]{2,1,0:T(8,128)(2,1)S(1)}, bf16[2,528,128]{2,1,0:T(8,128)(2,1)}, u32[]{:S(2)}, u32[]{:S(2)}) collective-permute-start(bf16[2,528,128]{2,1,0:T(8,128)(2,1)S(1)} %pad_maximum_fusion.5.near_ref), channel_id=1, source_target_pairs={{0,192},{1,65},{64,128},{65,1},{128,64},{129,193},{192,0},{193,129... | collective-permute-start | bytes 811016 | tf_op jit(solution)/shard_map/ppermute | solution.py:230
  139.8 9.3 %collective-permute-start.22 = (f32[1,4,128]{2,1,0:T(4,128)}, f32[1,4,128]{2,1,0:T(4,128)S(1)}, u32[]{:S(2)}, u32[]{:S(2)}) collective-permute-start(f32[1,4,128]{2,1,0:T(4,128)} %bitcast.66), channel_id=1, source_target_pairs={{0,1},{1,0},{2,3},{3,2},{4,5},{5,4},{6,7},{7,6},{8,9},{9,8},{10,11... | collective-permute-start | bytes 6152 | tf_op jit(solution)/shard_map/ppermute | solution.py:223
  149.8 3.7 %collective-permute-start.23 = (f32[2,4,128]{2,1,0:T(4,128)S(1)}, f32[2,4,128]{2,1,0:T(4,128)S(1)}, u32[]{:S(2)}, u32[]{:S(2)}) collective-permute-start(f32[2,4,128]{2,1,0:T(4,128)S(1)} %pad_maximum_fusion.8), channel_id=1, source_target_pairs={{0,2},{1,7},{2,0},{3,5},{4,6},{5,3},{6,4},{7,1},{8,10},{9,15},{10,... | collective-permute-start | bytes 12296 | tf_op jit(solution)/shard_map/ppermute | solution.py:230
  (29 other events, 147.0 us)

commit v5 on v4

--- a/solution.py
+++ b/solution.py
@@ -10,7 +10,8 @@
 NODE = ("zl", "x", "c")
 EVERY = ("y", "zh", "zl", "x", "c")
 TILE = 128
-LIMIT = 48 * 2**20
+EXTRA = 8
+LIMIT = 16 * 2**20
 
 
 def widen_kernel(values_ref, scales_ref, out_ref):
@@ -119,27 +120,33 @@
     return pltpu.make_async_copy(tok_ref.at[:, pl.ds(at, span)], block.at[k], sem.at[k])
 
 
-def forward_kernel(tab_ref, tok_ref, inv_ref, gain_ref, cot_ref, *refs):
-    w_refs, (proj_ref, moment_ref, acc, block, sem) = refs[:-5], refs[-5:]
+def forward_kernel(tab_ref, tok_ref, inv_ref, gain_ref, *refs):
+    w_refs, acc_in, (acc, block, sem) = refs[:4], refs[4:-3], refs[-3:]
     count, _, span = block.shape
     for k in range(count):
         block_in(tab_ref, tok_ref, block, sem, k).start()
     inverse = inv_ref[...]
-    acc[...] = jnp.zeros_like(acc)
+    acc[...] = acc_in[0][...] if acc_in else jnp.zeros_like(acc)
     for k in range(count):
         block_in(tab_ref, tok_ref, block, sem, k).wait()
         at = pl.multiple_of(tab_ref[k] * span, span)
         wide = block[k].astype(jnp.float32)
         normed = (wide * inverse * gain_ref[:, pl.ds(at, span)]).astype(jnp.bfloat16)
         acc[...] += jnp.dot(normed, w_refs[k // 2][k % 2], preferred_element_type=jnp.float32)
+
+
+def forward_last_kernel(tab_ref, tok_ref, inv_ref, gain_ref, cot_ref, *refs):
+    w_refs, acc_in, proj_ref, moment_ref, acc, block, sem = refs[:4], *refs[4:]
+    forward_kernel(tab_ref, tok_ref, inv_ref, gain_ref, *w_refs, acc_in, acc, block, sem)
     keys = acc[...]
+    inverse = inv_ref[...]
     proj_ref[...] = keys.astype(jnp.bfloat16)
     inner = jnp.sum(cot_ref[...].astype(jnp.float32) * keys, axis=1, keepdims=True)
-    moment_ref[...] = inverse * inverse * inner / (count * span)
+    moment_ref[...] = inverse * inverse * inner / tok_ref.shape[1]
 
 
 def backward_kernel(tab_ref, tok_ref, inv_ref, gain_ref, cot_ref, moment_ref, *refs):
-    w_refs, (grads_ref, block, out, sem, out_sem) = refs[:-5], refs[-5:]
+    w_refs, (grads_ref, block, out, sem, out_sem) = refs[:4], refs[-5:]
     count, _, span = block.shape
 
     def block_out(k):
@@ -163,64 +170,78 @@
         block_out(k).wait()
 
 
-def forward(tokens, inverse, gain, cotangent, weights, table):
+VMEM = pl.BlockSpec(memory_space=pltpu.VMEM)
+SMEM = pl.BlockSpec(memory_space=pltpu.SMEM)
+ANY = pl.BlockSpec(memory_space=pl.ANY)
+
+
+def costs(tokens, columns):
     rows, width = tokens.shape
-    columns = cotangent.shape[1]
-    span = weights[0].shape[1]
-    count = width // span
-    vmem = pl.BlockSpec(memory_space=pltpu.VMEM)
+    return dict(
+        compiler_params=pltpu.CompilerParams(vmem_limit_bytes=LIMIT),
+        cost_estimate=pl.CostEstimate(
+            flops=rows * width * columns,
+            bytes_accessed=2 * rows * width + width * columns,
+            transcendentals=0,
+        ),
+    )
+
+
+def forward(tokens, inverse, gain, weights, table):
+    rows, span, columns = tokens.shape[0], *weights[0].shape[1:]
     return pl.pallas_call(
         forward_kernel,
-        in_specs=[pl.BlockSpec(memory_space=pltpu.SMEM), pl.BlockSpec(memory_space=pl.ANY)]
-        + [vmem] * (3 + len(weights)),
-        out_specs=[vmem] * 2,
+        in_specs=[SMEM, ANY] + [VMEM] * 6,
+        out_specs=VMEM,
+        out_shape=jax.ShapeDtypeStruct((rows, columns), jnp.float32),
+        scratch_shapes=[
+            pltpu.VMEM((8, rows, span), jnp.bfloat16),
+            pltpu.SemaphoreType.DMA((8,)),
+        ],
+        **costs(tokens, columns),
+    )(table, tokens, inverse, gain, *weights)
+
+
+def forward_last(tokens, inverse, gain, cotangent, weights, sums, table):
+    rows, span, columns = tokens.shape[0], *weights[0].shape[1:]
+    return pl.pallas_call(
+        forward_last_kernel,
+        in_specs=[SMEM, ANY] + [VMEM] * 8,
+        out_specs=[VMEM] * 2,
         out_shape=[
             jax.ShapeDtypeStruct((rows, columns), jnp.bfloat16),
             jax.ShapeDtypeStruct((rows, 1), jnp.float32),
         ],
         scratch_shapes=[
             pltpu.VMEM((rows, columns), jnp.float32),
-            pltpu.VMEM((count, rows, span), jnp.bfloat16),
-            pltpu.SemaphoreType.DMA((count,)),
-        ],
-        compiler_params=pltpu.CompilerParams(vmem_limit_bytes=LIMIT),
-        cost_estimate=pl.CostEstimate(
-            flops=2 * rows * width * columns,
-            bytes_accessed=2 * rows * width + 2 * width * columns,
-            transcendentals=0,
-        ),
-    )(table, tokens, inverse, gain, cotangent, *weights)
-
-
-def backward(tokens, inverse, gain, cotangent, moment, weights, table):
-    rows, width = tokens.shape
-    columns = cotangent.shape[1]
-    span = weights[0].shape[1]
-    count = width // span
-    vmem = pl.BlockSpec(memory_space=pltpu.VMEM)
+            pltpu.VMEM((8, rows, span), jnp.bfloat16),
+            pltpu.SemaphoreType.DMA((8,)),
+        ],
+        **costs(tokens, columns),
+    )(table, tokens, inverse, gain, cotangent, *weights, sums)
+
+
+def backward(tokens, inverse, gain, cotangent, moment, weights, table, before=()):
+    rows, span, columns = tokens.shape[0], *weights[0].shape[1:]
     return pl.pallas_call(
         backward_kernel,
-        in_specs=[pl.BlockSpec(memory_space=pltpu.SMEM), pl.BlockSpec(memory_space=pl.ANY)]
-        + [vmem] * (4 + len(weights)),
-        out_specs=pl.BlockSpec(memory_space=pl.ANY),
-        out_shape=jax.ShapeDtypeStruct((rows, width), jnp.bfloat16),
+        in_specs=[SMEM, ANY] + [VMEM] * 8 + [ANY] * len(before),
+        out_specs=ANY,
+        out_shape=jax.ShapeDtypeStruct(tokens.shape, jnp.bfloat16),
         scratch_shapes=[
-            pltpu.VMEM((count, rows, span), jnp.bfloat16),
-            pltpu.VMEM((count, rows, span), jnp.bfloat16),
-            pltpu.SemaphoreType.DMA((count,)),
-            pltpu.SemaphoreType.DMA((count,)),
-        ],
-        compiler_params=pltpu.CompilerParams(vmem_limit_bytes=LIMIT),
-        cost_estimate=pl.CostEstimate(
-            flops=2 * rows * width * columns,
-            bytes_accessed=4 * rows * width + 2 * width * columns,
-            transcendentals=0,
-        ),
-    )(table, tokens, inverse, gain, cotangent, moment, *weights)
+            pltpu.VMEM((8, rows, span), jnp.bfloat16),
+            pltpu.VMEM((8, rows, span), jnp.bfloat16),
+            pltpu.SemaphoreType.DMA((8,)),
+            pltpu.SemaphoreType.DMA((8,)),
+        ],
+        input_output_aliases={10: 0} if before else {},
+        **costs(tokens, columns),
+    )(table, tokens, inverse, gain, cotangent, moment, *weights, *before)
 
 
 def swap(array, axis):
-    return lax.ppermute(array, axis, [(0, 1), (1, 0)])
+    last = lax.axis_size(axis) - 1
+    return lax.ppermute(array, axis, [(a, last - a) for a in range(last + 1)])
 
 
 def pair(array, axis, step):
@@ -228,6 +249,11 @@
     masks = (1, 3) if step == 0 else (3, 1)
     moves = [(a * 2 + c, (a ^ masks[c]) * 2 + c) for a in range(size) for c in range(2)]
     return lax.ppermute(array, (axis, "c"), moves)
+
+
+def across(array, axis):
+    size = lax.axis_size(axis)
+    return lax.ppermute(array, axis, [(a, a ^ 2) for a in range(size)])
 
 
 def pair_z(array):
@@ -258,68 +284,105 @@
 )
 
 
-def pack_kernel(tab_ref, sent_ref, got_ref, weight_ref, gain_ref, out_ref, *, devices):
-    columns = sent_ref.shape[0]
-    mine = (sent_ref[...].astype(jnp.float32) + got_ref[...].astype(jnp.float32)) / devices
-    out_ref[:columns, :] = mine.astype(jnp.bfloat16)
-    rows = pl.ds(pl.multiple_of(tab_ref[0] * TILE, TILE), TILE)
-    weight = weight_ref[rows, :].astype(jnp.float32).T
-    gain = gain_ref[:, pl.ds(pl.multiple_of(tab_ref[1] * TILE, TILE), TILE)]
-    part = jnp.sum(weight * mine, axis=0, keepdims=True) / gain
-    high = part.astype(jnp.bfloat16).astype(jnp.float32)
-    tail = out_ref.shape[0] - columns
-    row = lax.broadcasted_iota(jnp.int32, (tail, TILE), 0)
-    ends = jnp.where(row == 0, high, jnp.where(row == 1, part - high, 0.0))
-    out_ref[columns:, :] = ends.astype(jnp.bfloat16)
-
-
-def pack(sent, got, weight, gain, table, devices):
-    vmem = pl.BlockSpec(memory_space=pltpu.VMEM)
-    return pl.pallas_call(
-        functools.partial(pack_kernel, devices=devices),
-        in_specs=[pl.BlockSpec(memory_space=pltpu.SMEM)] + [vmem] * 4,
-        out_specs=vmem,
-        out_shape=jax.ShapeDtypeStruct((sent.shape[0] + 16, TILE), jnp.bfloat16),
-    )(table, sent, got, weight, gain)
-
-
-def finish_kernel(tab_ref, near_ref, far_ref, weight_ref, gain_ref):
+def write_ends(out_ref, rows):
+    high = rows.astype(jnp.bfloat16).astype(jnp.float32)
+    out_ref[-2 * EXTRA :, :] = jnp.concatenate([high, rows - high]).astype(jnp.bfloat16)
+
+
+def read_ends(ref):
+    ends = ref[-2 * EXTRA :, :].astype(jnp.float32)
+    return ends[:EXTRA] + ends[EXTRA:]
+
+
+def spread_kernel(tab_ref, total_ref, gain_ref, base_ref, near_ref, near_c_ref, far_ref, *refs, devices):
+    out_refs, rows_ref = refs[:4], refs[4]
+    columns = base_ref.shape[2]
+    shards_ = (base_ref.at[0], near_c_ref.at[1], near_ref.at[0], far_ref.at[0])
+    rows = pl.ds(pl.multiple_of(tab_ref[4] * TILE, TILE), TILE)
+    rows_ref[...] = jnp.zeros_like(rows_ref)
+    for k, shard in enumerate(shards_):
+        total = total_ref[k].reshape(columns, TILE)
+        out_refs[k][:columns, :] = total.astype(jnp.bfloat16)
+        weight = shard[rows, :].astype(jnp.float32).T
+        part = jnp.sum(weight * total, axis=0, keepdims=True)
+        gain = gain_ref[:, pl.ds(pl.multiple_of(tab_ref[k] * TILE, TILE), TILE)]
+        rows_ref[pl.ds(tab_ref[5 + k], 1), :] = part / (gain * devices)
+    for out_ref in out_refs:
+        write_ends(out_ref, rows_ref[...])
+
+
+def spread(total, gain, base, near, near_c, far, table, devices):
+    columns = base.shape[2]
+    return pl.pallas_call(
+        functools.partial(spread_kernel, devices=devices),
+        in_specs=[SMEM] + [VMEM] * 6,
+        out_specs=[VMEM] * 4,
+        out_shape=[jax.ShapeDtypeStruct((columns + 2 * EXTRA, TILE), jnp.bfloat16)] * 4,
+        scratch_shapes=[pltpu.VMEM((EXTRA, TILE), jnp.float32)],
+        compiler_params=pltpu.CompilerParams(vmem_limit_bytes=LIMIT),
+    )(table, total, gain, base, near, near_c, far)
+
+
+def in_pairs(terms):
+    while len(terms) > 1:
+        terms = [a + b for a, b in zip(terms[::2], terms[1::2])]
+    return terms[0]
+
+
+def merge_kernel(*refs, scale):
+    parts, out_ref = refs[:-1], refs[-1]
+    columns = out_ref.shape[0] - 2 * EXTRA
+    total = in_pairs([part[:columns, :].astype(jnp.float32) for part in parts])
+    out_ref[:columns, :] = (total * scale).astype(jnp.bfloat16)
+    write_ends(out_ref, in_pairs([read_ends(part) for part in parts]))
+
+
+def merge(parts, scale=1.0):
+    return pl.pallas_call(
+        functools.partial(merge_kernel, scale=scale),
+        in_specs=[VMEM] * len(parts),
+        out_specs=VMEM,
+        out_shape=jax.ShapeDtypeStruct(parts[0].shape, parts[0].dtype),
+    )(*parts)
+
+
+def finish_kernel(tab_ref, *refs):
+    parts, (weight_ref, gain_ref) = refs[:4], refs[4:]
     columns = weight_ref.shape[1]
-    for k in range(4):
-        part = (near_ref, far_ref)[k // 2].at[k % 2]
+    for k, part in enumerate(parts):
         rows = pl.ds(pl.multiple_of(tab_ref[k] * TILE, TILE), TILE)
         weight_ref[rows, :] = part[:columns, :].astype(jnp.float32).T
-        ends = part[columns:, :].astype(jnp.float32)
-        gain_ref[pl.ds(tab_ref[k], 1), :] = ends[0:1] + ends[1:2]
+        gain_ref[tab_ref[k]] = read_ends(part)
 
 
 def finish(parts, table):
-    vmem = pl.BlockSpec(memory_space=pltpu.VMEM)
-    columns = parts[0].shape[1] - 16
+    columns = parts[0].shape[0] - 2 * EXTRA
     return pl.pallas_call(
         finish_kernel,
-        in_specs=[pl.BlockSpec(memory_space=pltpu.SMEM)] + [vmem] * 2,
-        out_specs=[vmem] * 2,
+        in_specs=[SMEM] + [VMEM] * 4,
+        out_specs=[VMEM] * 2,
         out_shape=[
             jax.ShapeDtypeStruct((4 * TILE, columns), jnp.float32),
-            jax.ShapeDtypeStruct((4, TILE), jnp.float32),
+            jax.ShapeDtypeStruct((4, EXTRA, TILE), jnp.float32),
         ],
     )(table, *parts)
 
 
-def order_kernel(tab_ref, in_ref, out_ref):
-    for node in range(in_ref.shape[0]):
-        out_ref[node] = in_ref[tab_ref[node]]
-
-
-def order(rows, table):
-    vmem = pl.BlockSpec(memory_space=pltpu.VMEM)
+def order_kernel(tab_ref, *refs):
+    parts, out_ref = refs[:4], refs[4]
+    for k, part in enumerate(parts):
+        for x in range(4):
+            for y in range(4):
+                out_ref[tab_ref[k] + 2 * x, y : y + 1, :] = part[y, x : x + 1, :]
+
+
+def order(parts, table):
     return pl.pallas_call(
         order_kernel,
-        in_specs=[pl.BlockSpec(memory_space=pltpu.SMEM), vmem],
-        out_specs=vmem,
-        out_shape=jax.ShapeDtypeStruct(rows.shape, rows.dtype),
-    )(table, rows)
+        in_specs=[SMEM] + [VMEM] * 4,
+        out_specs=VMEM,
+        out_shape=jax.ShapeDtypeStruct((16, 4, TILE), jnp.float32),
+    )(table, *parts)
 
 
 def shards(tokens, norm_gain, weight_values, weight_scale, key_cotangent):
@@ -349,11 +412,11 @@
     own_c = swap(own, "c")
     up = pair_z(own)
     cot_own = key_cotangent.T
+    base = jnp.stack([own, own_c])
     cot_got = swap(cot_own, "c")
-    mine, other, inverse = norm_tiles(tie(tokens, own, cot_own), gain, jnp.stack(tables))
+    mine, other, inverse = norm_tiles(tie(tokens, base, cot_own), gain, jnp.stack(tables))
     got = swap(other, "c")
     got, up = lax.optimization_barrier((got, up))
-    base = jnp.stack([own, own_c])
     near = pair(base, "x", 0)
     up_c = swap(up, "c")
     sent, kept = grad_tiles(mine, got, cot_own, cot_got)
@@ -372,48 +435,44 @@
     (first, kept_first), (second, kept_second) = (
         halve(add(k, m)) for k, m in zip((kept_first, kept_second), moved)
     )
-    moved = pair(jnp.stack([first, second]), "y", 1)
+    send, near_c = lax.optimization_barrier((jnp.stack([first, second]), near_c))
+    moved = pair(send, "y", 1)
+    early, late_at = [base, above, near, near_c], shards_at[8:]
+    sums = forward(tokens, inverse, gain, early, shards_at[:8])
+    moved, sums = lax.optimization_barrier((moved, sums))
     total = jnp.stack([add(kept_first, moved[0]), add(kept_second, moved[1])], axis=1)
-    send, kept = halve(total)
-    send, far = lax.optimization_barrier((send, far))
-    moved = pair(send, "x", 0)
+    total, far, sums = lax.optimization_barrier((total, far, sums))
+
+    peer = x ^ offset(c, jnp.arange(4) // 2, jnp.arange(4) % 2)
+    node_tile = ((zl * 4 + peer) * 2 + c) * 4 + y
+    at = jnp.concatenate([node_tile, y[None], peer]).astype(jnp.int32)
+    parts = spread(total, gain, base, near, near_c, far, at, devices)
+    moved = [parts[0], pair(parts[2], "x", 0), pair(parts[1], "x", 1), across(parts[3], "x")]
     far_c = swap(far, "c")
-    send, kept = halve(add(kept, moved))
-    send, far_c = lax.optimization_barrier((send, far_c))
-    weights = [base, above, near, near_c, above_near, above_near_c, far, far_c]
-
-    moved = pair(send, "x", 1)
-    projected, moment = forward(tokens, inverse, gain, key_cotangent, weights, shards_at)
-    moved, moment = lax.optimization_barrier((moved, moment))
-    send = add(kept, moved).astype(jnp.bfloat16).reshape(columns, TILE)
+    late = [above_near, above_near_c, far, far_c]
+    projected, moment = forward_last(tokens, inverse, gain, key_cotangent, late, sums, late_at)
+    moved[3], moment = lax.optimization_barrier((moved[3], moment))
+    send = merge(moved)
+
+    send, moment = lax.optimization_barrier((send, moment))
     moved = pair(send, "zh", 0)
-    send = (send.astype(jnp.float32) + moved.astype(jnp.float32)).astype(jnp.bfloat16)
+    token_grads = backward(tokens, inverse, gain, key_cotangent, moment, early, shards_at[:8])
+    moved, token_grads = lax.optimization_barrier((moved, token_grads))
+    send = merge((send, moved))
+    send, token_grads = lax.optimization_barrier((send, token_grads))
     moved = pair(send, "zh", 1)
-
-    node = (zl * 4 + x) * 2 + c
-    at = jnp.stack([y, node * 4 + y]).astype(jnp.int32)
-    packed = pack(send, moved, own, gain, at, devices)[None]
-    pieces = jnp.concatenate([packed, pair(packed, "y", 0)])
-    pieces, moment = lax.optimization_barrier((pieces, moment))
-    moved = pair(pieces, "y", 1)
-    token_grads = backward(tokens, inverse, gain, key_cotangent, moment, weights, shards_at)
-    moved = tie(moved, token_grads)
+    token_grads = backward(
+        tokens, inverse, gain, key_cotangent, moment, late, late_at, before=(token_grads,)
+    )
+    moved, token_grads = lax.optimization_barrier((moved, token_grads))
+    send = merge((send, moved), 1.0 / devices)
+
+    parts = (send, pair(send, "y", 0), pair(send, "y", 1), across(send, "y"))
     quarters = jnp.stack([y ^ offset(c, k % 2, k // 2) for k in range(4)]).astype(jnp.int32)
-    weight_grads, gains = finish((pieces, moved), quarters)
-    gains = gains[None]
-    for move in (
-        lambda a: swap(a, "c"),
-        lambda a: pair(a, "x", 0),
-        lambda a: pair(a, "x", 1),
-        lambda a: swap(a, "zl"),
-    ):
-        gains = jnp.concatenate([gains, move(gains)])
-    nodes = jnp.arange(16, dtype=jnp.int32)
-    across = nodes // 2 % 4 ^ x
-    high, mixed = across // 2, across % 2 ^ across // 2
-    step0, step1 = jnp.where(c == 0, mixed, high), jnp.where(c == 0, high, mixed)
-    relative = (nodes // 8 ^ zl) * 8 + step1 * 4 + step0 * 2 + (nodes % 2 ^ c)
-    gain_grads = order(gains, relative.astype(jnp.int32)).reshape(width)
+    weight_grads, gains = finish(parts, quarters)
+    gains = (gains, swap(gains, "c"), swap(gains, "zl"), swap(gains, ("zl", "c")))
+    nodes = jnp.stack([(zl ^ k // 2) * 8 + (c ^ k % 2) for k in range(4)]).astype(jnp.int32)
+    gain_grads = order(gains, nodes).reshape(width)
     return (projected, token_grads, weight_grads, gain_grads)
 
 

time: 163 us -> 148 us (0.908)
  waiting for transfers between devices: 56.6 us -> 32.7 us
  local copies, waits for them, and re-layouts: 14.7 us -> 28.7 us
  starting transfers between devices: 40.4 us -> 36.7 us
  other arithmetic: 8.53 us -> 6.48 us
    ppermute x14 -> x12, waiting for transfers between devices: 47.2 us -> 22.5 us  [pair(): return lax.ppermute(array, (axis, 'c'), moves)]
    unnamed x57 -> x73, local copies, waits for them, and re-layouts: 13.5 us -> 28.3 us
    pallas_call x5 -> x10, Pallas kernels: 25.4 us -> 31.3 us  [the longest x2 12.6 us: backward(): pl.pallas_call(backward_kernel, in_specs=[SMEM, ANY] + [VMEM] * 8 + [ANY]...]
    concatenate x4 -> x1, other arithmetic: 3.05 us -> 0.08 us  [shards(): at = jnp.concatenate([node_tile, y[None], peer]).astype(jnp.int32)]
    pallas_call x1, Pallas kernels: 5.94 us -> 3.37 us  [norm_tiles(): pl.pallas_call(norm_kernel, grid_spec=pltpu.PrefetchScalarGridSpec(num_sc...]
    pallas_call x1, Pallas kernels: 7.03 us -> 4.49 us  [grad_tiles(): pl.pallas_call(grad_kernel, out_shape=[jax.ShapeDtypeStruct(shape, jnp.bf...]
    ppermute x14 -> x12, starting transfers between devices: 19 us -> 17.4 us  [pair(): return lax.ppermute(array, (axis, 'c'), moves)]
    ppermute x9 -> x12, starting transfers between devices: 12 us -> 10.7 us  [the longest x10 6.7 us: swap(): return lax.ppermute(array, axis, [(a, last - a) for a in range(last + 1)])]
  transfers between devices with their start and end apart: 26 -> 27, of which waited for: 16 -> 15; matrix products, arithmetic and copies ran while one was open for 4% -> 4% of each run, Pallas kernels for 17% -> 18%
where the time goes in v5:
time: 148 us; the launch traced here: 147 us
  Pallas kernels  41.4 us (28%)
  starting transfers between devices  36.7 us (25%)
  waiting for transfers between devices  32.7 us (22%)
  local copies, waits for them, and re-layouts  28.7 us (19%)
  other arithmetic  6.48 us (4%)
    unnamed x73, local copies, waits for them, and re-layouts  28.3 us
    ppermute x12, waiting for transfers between devices, pair(): return lax.ppermute(array, (axis, 'c'), moves)  22.5 us
    ppermute x12, starting transfers between devices, pair(): return lax.ppermute(array, (axis, 'c'), moves)  17.4 us
    pallas_call x2, Pallas kernels, backward(): pl.pallas_call(backward_kernel, in_specs=[SMEM, ANY] + [VMEM] * 8 + [ANY]...  12.6 us
    ppermute x3, starting transfers between devices, pair_z(): return lax.ppermute(array, ('zh', 'zl', 'c'), moves)  8.55 us
    ppermute x10, starting transfers between devices, swap(): return lax.ppermute(array, axis, [(a, last - a) for a in range(last + 1)])  6.7 us
    ppermute x3, waiting for transfers between devices, pair_z(): return lax.ppermute(array, ('zh', 'zl', 'c'), moves)  6.5 us
    pallas_call x3, Pallas kernels, merge(): pl.pallas_call(functools.partial(merge_kernel, scale=scale), in_specs=[VM...  5.17 us
  transfers between devices with their start and end apart: 27, of which 15 were waited for; matrix products, arithmetic and copies ran while one was open for 4% of the time, Pallas kernels for 18%

profile of v5, /device:TPU:1, one launch (start us, length us, event | category | flops | bytes accessed | tf_op | source)
XLA Modules:
  0.0 147.0 jit_solution(15096211634362190177)
XLA Ops:
  2.9 3.2 %collective-permute-start = (bf16[512,512]{1,0:T(8,128)(2,1)}, bf16[512,512]{1,0:T(8,128)(2,1)S(1)}, u32[]{:S(2)}, u32[]{:S(2)}) collective-permute-start(bf16[512,512]{1,0:T(8,128)(2,1)} %shard_map.84), channel_id=1, source_target_pairs={{0,1},{1,0},{2,3},{3,2},{4,5},{5,4},{6,7},{7,6},{8,9},{9,8},{10,11... | collective-permute-start | bytes 1572872 | tf_op jit(solution)/shard_map/ppermute | solution.py:244
  9.0 2.5 %copy-done = bf16[320,8192]{1,0:T(8,128)(2,1)S(1)} copy-done((bf16[320,8192]{1,0:T(8,128)(2,1)S(1)}, bf16[320,8192]{1,0:T(8,128)(2,1)}, u32[]{:S(2)}) %copy-start) | copy-done | bytes 5242904
  11.5 3.4 %shard_map.85 = (bf16[320,4096]{1,0:T(8,128)(2,1)S(1)}, bf16[320,4096]{1,0:T(8,128)(2,1)S(1)}, f32[320,1]{1,0:T(8,128)S(1)}) custom-call(s32[2,32]{1,0:T(2,128)S(1)} %pad_add_fusion.tab_ref, bf16[320,8192]{1,0:T(8,128)(2,1)S(1)} %copy-done, f32[1,8192]{1,0:T(1,128)S(1)} %bitcast.48), custom_call_target="tpu_custom_call" | custom-call | flops 15728640 | bytes 10485760 | tf_op jit(solution)/shard_map/pallas_call | solution.py:55
  15.3 3.8 %collective-permute-start.2 = (bf16[512,512]{1,0:T(8,128)(2,1)S(1)}, bf16[512,512]{1,0:T(8,128)(2,1)S(1)}, u32[]{:S(2)}, u32[]{:S(2)}) collective-permute-start(bf16[512,512]{1,0:T(8,128)(2,1)S(1)} %copy-done.27), channel_id=1, source_target_pairs={{0,8},{1,57},{8,0},{9,17},{16,24},{17,9},{24,16},{25,33},{32,40},{... | collective-permute-start | bytes 1572872 | tf_op jit(solution)/shard_map/ppermute | solution.py:265
  19.2 2.5 %collective-permute-start.4 = (bf16[2,512,512]{2,1,0:T(8,128)(2,1)S(1)}, bf16[2,512,512]{2,1,0:T(8,128)(2,1)S(1)}, u32[]{:S(2)}, u32[]{:S(2)}) collective-permute-start(bf16[2,512,512]{2,1,0:T(8,128)(2,1)S(1)} %pad_maximum_fusion.refs_0_.base_ref), channel_id=1, source_target_pairs={{0,2},{1,7},{2,0},{3,5},{4,6},{5,3},{6,4},{7,1},{8,10},{9,15},{10,... | collective-permute-start | bytes 3145736 | tf_op jit(solution)/shard_map/ppermute | solution.py:251
  21.7 4.1 %collective-permute-done.2 = bf16[512,512]{1,0:T(8,128)(2,1)S(1)} collective-permute-done((bf16[512,512]{1,0:T(8,128)(2,1)S(1)}, bf16[512,512]{1,0:T(8,128)(2,1)S(1)}, u32[]{:S(2)}, u32[]{:S(2)}) %collective-permute-start.2) | collective-permute-done | bytes 524320 | tf_op jit(solution)/shard_map/ppermute | solution.py:265
  25.8 4.5 %shard_map.86 = (bf16[16,256,128]{2,1,0:T(8,128)(2,1)S(1)}, bf16[16,256,128]{2,1,0:T(8,128)(2,1)S(1)}, f32[16,256,128]{2,1,0:T(8,128)S(1)}, f32[16,256,128]{2,1,0:T(8,128)S(1)}) custom-call(bf16[320,4096]{1,0:T(8,128)(2,1)S(1)} %get-tuple-element.47.own_ref, bf16[320,4096]{1,0:T(8,128)(2,1)S(1)} %collective-permute-done.1.got_ref, ...), custom_call_target="tpu_custom_call" | custom-call | flops 2684354560 | bytes 11534336 | tf_op jit(solution)/shard_map/pallas_call | solution.py:103
  30.3 2.8 %collective-permute-start.10 = (bf16[16,256,128]{2,1,0:T(8,128)(2,1)S(1)}, bf16[16,256,128]{2,1,0:T(8,128)(2,1)S(1)}, u32[]{:S(2)}, u32[]{:S(2)}) collective-permute-start(bf16[16,256,128]{2,1,0:T(8,128)(2,1)S(1)} %get-tuple-element.58), channel_id=1, source_target_pairs={{0,64},{1,193},{64,0},{65,129},{128,192},{129,65},{192,128},{193,1... | collective-permute-start | bytes 3145736 | tf_op jit(solution)/shard_map/ppermute | solution.py:251
  36.0 2.6 %collective-permute-start.8 = (bf16[2,512,512]{2,1,0:T(8,128)(2,1)S(1)}, bf16[2,512,512]{2,1,0:T(8,128)(2,1)S(1)}, u32[]{:S(2)}, u32[]{:S(2)}) collective-permute-start(bf16[2,512,512]{2,1,0:T(8,128)(2,1)S(1)} %pad_maximum_fusion.1.refs_1_), channel_id=1, source_target_pairs={{0,2},{1,7},{2,0},{3,5},{4,6},{5,3},{6,4},{7,1},{8,10},{9,15},{10,... | collective-permute-start | bytes 3145736 | tf_op jit(solution)/shard_map/ppermute | solution.py:251
  38.6 6.7 %collective-permute-done.10 = bf16[16,256,128]{2,1,0:T(8,128)(2,1)S(1)} collective-permute-done((bf16[16,256,128]{2,1,0:T(8,128)(2,1)S(1)}, bf16[16,256,128]{2,1,0:T(8,128)(2,1)S(1)}, u32[]{:S(2)}, u32[]{:S(2)}) %collective-permute-start.10) | collective-permute-done | bytes 1048608 | tf_op jit(solution)/shard_map/ppermute | solution.py:251
  45.6 2.8 %collective-permute-start.11 = (bf16[8,256,128]{2,1,0:T(8,128)(2,1)S(1)}, bf16[8,256,128]{2,1,0:T(8,128)(2,1)S(1)}, u32[]{:S(2)}, u32[]{:S(2)}) collective-permute-start(bf16[8,256,128]{2,1,0:T(8,128)(2,1)S(1)} %slice.84), channel_id=1, source_target_pairs={{0,8},{1,57},{8,0},{9,17},{16,24},{17,9},{24,16},{25,33},{32,40},{... | collective-permute-start | bytes 1572872 | tf_op jit(solution)/shard_map/ppermute | solution.py:265
  55.2 5.1 %collective-permute-done.12 = bf16[8,256,128]{2,1,0:T(8,128)(2,1)S(1)} collective-permute-done((bf16[8,256,128]{2,1,0:T(8,128)(2,1)S(1)}, bf16[8,256,128]{2,1,0:T(8,128)(2,1)S(1)}, u32[]{:S(2)}, u32[]{:S(2)}) %collective-permute-start.12) | collective-permute-done | bytes 524320 | tf_op jit(solution)/shard_map/ppermute | solution.py:251
  62.7 2.5 %collective-permute-start.14 = (bf16[2,512,512]{2,1,0:T(8,128)(2,1)}, bf16[2,512,512]{2,1,0:T(8,128)(2,1)}, u32[]{:S(2)}, u32[]{:S(2)}) collective-permute-start(bf16[2,512,512]{2,1,0:T(8,128)(2,1)} %pad_maximum_fusion.3), channel_id=1, source_target_pairs={{0,2},{1,7},{2,0},{3,5},{4,6},{5,3},{6,4},{7,1},{8,10},{9,15},{10,... | collective-permute-start | bytes 3145736 | tf_op jit(solution)/shard_map/ppermute | solution.py:251
  66.2 2.5 %copy-done.1 = bf16[320,8192]{1,0:T(8,128)(2,1)S(1)} copy-done((bf16[320,8192]{1,0:T(8,128)(2,1)S(1)}, bf16[320,8192]{1,0:T(8,128)(2,1)}, u32[]{:S(2)}) %copy-start.1) | copy-done | bytes 5242904
  71.1 2.9 %shard_map.87.refs_4_ = f32[320,512]{1,0:T(8,128)S(1)} custom-call(s32[8]{0:T(128)S(1)} %stack.152.tab_ref, bf16[320,8192]{1,0:T(8,128)(2,1)S(1)} %copy-done.1, f32[320,1]{1,0:T(8,128)S(1)} %get-tuple-element.46.inv_ref, f32[1,8192]{1,0:T(1,128)S(1)} %bitcast.49, bf16[2,512,512]{2,1,0:T(8,128)(2,1)S(1)} %pad_maximum_fusion.refs_0_.base_ref, ...), custom_call_target="tpu_custom_call" | custom-call | flops 1342177280 | bytes 9437184 | tf_op jit(solution)/shard_map/pallas_call | solution.py:192
  78.0 2.3 %shard_map.89 = (bf16[528,128]{1,0:T(8,128)(2,1)S(1)}, bf16[528,128]{1,0:T(8,128)(2,1)}, bf16[528,128]{1,0:T(8,128)(2,1)}, bf16[528,128]{1,0:T(8,128)(2,1)}) custom-call(s32[9]{0:T(128)S(1)} %pad_add_fusion.1.tab_ref, f32[4,2,256,128]{3,2,1,0:T(8,128)S(1)} %pad_maximum_fusion.2.total_ref, f32[1,8192]{1,0:T(1,128)S(1)} %bitcast.50, ...), custom_call_target="tpu_custom_call" | custom-call | tf_op jit(solution)/shard_map/pallas_call | solution.py:316
  84.1 2.5 %copy-done.2 = bf16[320,8192]{1,0:T(8,128)(2,1)S(1)} copy-done((bf16[320,8192]{1,0:T(8,128)(2,1)S(1)}, bf16[320,8192]{1,0:T(8,128)(2,1)}, u32[]{:S(2)}) %copy-start.2) | copy-done | bytes 5242904
  89.0 4.6 %shard_map.88 = (bf16[320,512]{1,0:T(8,128)(2,1)}, f32[320,1]{1,0:T(8,128)S(1)}) custom-call(s32[8]{0:T(128)S(1)} %stack.133.tab_ref, bf16[320,8192]{1,0:T(8,128)(2,1)S(1)} %copy-done.2, f32[320,1]{1,0:T(8,128)S(1)} %get-tuple-element.46.inv_ref, f32[1,8192]{1,0:T(1,128)S(1)} %bitcast.51, bf16[320,512]{1,0:T(8,128)(2,1)S(1)} %copy-done.17, ...), custom_call_target="tpu_custom_call" | custom-call | flops 1342177280 | bytes 9437184 | tf_op jit(solution)/shard_map/pallas_call | solution.py:207
  96.7 2.5 %copy-done.3 = bf16[320,8192]{1,0:T(8,128)(2,1)S(1)} copy-done((bf16[320,8192]{1,0:T(8,128)(2,1)S(1)}, bf16[320,8192]{1,0:T(8,128)(2,1)}, u32[]{:S(2)}) %copy-start.3) | copy-done | bytes 5242904
  101.6 5.8 %shard_map.91.refs_4_ = bf16[320,8192]{1,0:T(8,128)(2,1)} custom-call(s32[8]{0:T(128)S(1)} %stack.152.tab_ref, bf16[320,8192]{1,0:T(8,128)(2,1)S(1)} %copy-done.3, f32[320,1]{1,0:T(8,128)S(1)} %get-tuple-element.46.inv_ref, f32[1,8192]{1,0:T(1,128)S(1)} %bitcast.52, bf16[320,512]{1,0:T(8,128)(2,1)S(1)} %copy-done.17, ...), custom_call_target="tpu_custom_call" | custom-call | flops 1342177280 | bytes 9437184 | tf_op jit(solution)/shard_map/pallas_call | solution.py:226
  111.1 2.5 %copy-done.4 = bf16[320,8192]{1,0:T(8,128)(2,1)S(1)} copy-done((bf16[320,8192]{1,0:T(8,128)(2,1)S(1)}, bf16[320,8192]{1,0:T(8,128)(2,1)}, u32[]{:S(2)}) %copy-start.4) | copy-done | bytes 5242904
  116.0 6.8 %shard_map.93 = bf16[320,8192]{1,0:T(8,128)(2,1)} custom-call(s32[8]{0:T(128)S(1)} %stack.133.tab_ref, bf16[320,8192]{1,0:T(8,128)(2,1)S(1)} %copy-done.4, f32[320,1]{1,0:T(8,128)S(1)} %get-tuple-element.46.inv_ref, f32[1,8192]{1,0:T(1,128)S(1)} %bitcast.53, bf16[320,512]{1,0:T(8,128)(2,1)S(1)} %copy-done.17, ...), custom_call_target="tpu_custom_call", output_to_operand_aliasing={{}: (10, {})} | custom-call | flops 1342177280 | bytes 9437184 | tf_op jit(solution)/shard_map/pallas_call | solution.py:226
  125.2 2.7 %collective-permute-start.23 = (bf16[528,128]{1,0:T(8,128)(2,1)}, bf16[528,128]{1,0:T(8,128)(2,1)S(1)}, u32[]{:S(2)}, u32[]{:S(2)}) collective-permute-start(bf16[528,128]{1,0:T(8,128)(2,1)} %shard_map.94.refs_0_), channel_id=1, source_target_pairs={{0,128},{64,192},{128,0},{192,64},{1,129},{65,193},{129,1},{193,65... | collective-permute-start | bytes 405512 | tf_op jit(solution)/shard_map/ppermute | solution.py:256
  133.0 3.1 %collective-permute-done.21.refs_1_ = bf16[528,128]{1,0:T(8,128)(2,1)S(1)} collective-permute-done((bf16[528,128]{1,0:T(8,128)(2,1)}, bf16[528,128]{1,0:T(8,128)(2,1)S(1)}, u32[]{:S(2)}, u32[]{:S(2)}) %collective-permute-start.21) | collective-permute-done | bytes 135200 | tf_op jit(solution)/shard_map/ppermute | solution.py:251
  (141 shorter events, 61.3 us)
Async XLA Ops:
  2.9 5.0 %collective-permute-start = (bf16[512,512]{1,0:T(8,128)(2,1)}, bf16[512,512]{1,0:T(8,128)(2,1)S(1)}, u32[]{:S(2)}, u32[]{:S(2)}) collective-permute-start(bf16[512,512]{1,0:T(8,128)(2,1)} %shard_map.84), channel_id=1, source_target_pairs={{0,1},{1,0},{2,3},{3,2},{4,5},{5,4},{6,7},{7,6},{8,9},{9,8},{10,11... | collective-permute-start | bytes 1572872 | tf_op jit(solution)/shard_map/ppermute | solution.py:244
  14.9 10.9 %collective-permute-start.1 = (bf16[320,4096]{1,0:T(8,128)(2,1)S(1)}, bf16[320,4096]{1,0:T(8,128)(2,1)S(1)}, u32[]{:S(2)}, u32[]{:S(2)}) collective-permute-start(bf16[320,4096]{1,0:T(8,128)(2,1)S(1)} %get-tuple-element.48), channel_id=1, source_target_pairs={{0,1},{1,0},{2,3},{3,2},{4,5},{5,4},{6,7},{7,6},{8,9},{9,8},{10,11... | collective-permute-start | bytes 7864328 | tf_op jit(solution)/shard_map/ppermute | solution.py:244
  15.3 10.4 %collective-permute-start.2 = (bf16[512,512]{1,0:T(8,128)(2,1)S(1)}, bf16[512,512]{1,0:T(8,128)(2,1)S(1)}, u32[]{:S(2)}, u32[]{:S(2)}) collective-permute-start(bf16[512,512]{1,0:T(8,128)(2,1)S(1)} %copy-done.27), channel_id=1, source_target_pairs={{0,8},{1,57},{8,0},{9,17},{16,24},{17,9},{24,16},{25,33},{32,40},{... | collective-permute-start | bytes 1572872 | tf_op jit(solution)/shard_map/ppermute | solution.py:265
  19.2 6.6 %collective-permute-start.3 = (bf16[512,320]{1,0:T(8,128)(2,1)S(1)}, bf16[512,320]{1,0:T(8,128)(2,1)S(1)}, u32[]{:S(2)}, u32[]{:S(2)}) collective-permute-start(bf16[512,320]{1,0:T(8,128)(2,1)S(1)} %bitcast.54), channel_id=1, source_target_pairs={{0,1},{1,0},{2,3},{3,2},{4,5},{5,4},{6,7},{7,6},{8,9},{9,8},{10,11... | collective-permute-start | bytes 983048 | tf_op jit(solution)/shard_map/ppermute | solution.py:244
  19.2 14.9 %collective-permute-start.4 = (bf16[2,512,512]{2,1,0:T(8,128)(2,1)S(1)}, bf16[2,512,512]{2,1,0:T(8,128)(2,1)S(1)}, u32[]{:S(2)}, u32[]{:S(2)}) collective-permute-start(bf16[2,512,512]{2,1,0:T(8,128)(2,1)S(1)} %pad_maximum_fusion.refs_0_.base_ref), channel_id=1, source_target_pairs={{0,2},{1,7},{2,0},{3,5},{4,6},{5,3},{6,4},{7,1},{8,10},{9,15},{10,... | collective-permute-start | bytes 3145736 | tf_op jit(solution)/shard_map/ppermute | solution.py:251
  25.8 8.3 %collective-permute-start.5 = (bf16[512,512]{1,0:T(8,128)(2,1)S(1)}, bf16[512,512]{1,0:T(8,128)(2,1)S(1)}, u32[]{:S(2)}, u32[]{:S(2)}) collective-permute-start(bf16[512,512]{1,0:T(8,128)(2,1)S(1)} %collective-permute-done.2), channel_id=1, source_target_pairs={{0,1},{1,0},{2,3},{3,2},{4,5},{5,4},{6,7},{7,6},{8,9},{9,8},{10,11... | collective-permute-start | bytes 1572872 | tf_op jit(solution)/shard_map/ppermute | solution.py:244
  30.3 15.0 %collective-permute-start.10 = (bf16[16,256,128]{2,1,0:T(8,128)(2,1)S(1)}, bf16[16,256,128]{2,1,0:T(8,128)(2,1)S(1)}, u32[]{:S(2)}, u32[]{:S(2)}) collective-permute-start(bf16[16,256,128]{2,1,0:T(8,128)(2,1)S(1)} %get-tuple-element.58), channel_id=1, source_target_pairs={{0,64},{1,193},{64,0},{65,129},{128,192},{129,65},{192,128},{193,1... | collective-permute-start | bytes 3145736 | tf_op jit(solution)/shard_map/ppermute | solution.py:251
  34.1 14.9 %collective-permute-start.6 = (bf16[16,256,128]{2,1,0:T(8,128)(2,1)S(1)}, bf16[16,256,128]{2,1,0:T(8,128)(2,1)S(1)}, u32[]{:S(2)}, u32[]{:S(2)}) collective-permute-start(bf16[16,256,128]{2,1,0:T(8,128)(2,1)S(1)} %get-tuple-element.53), channel_id=1, source_target_pairs={{0,8},{1,57},{8,0},{9,17},{16,24},{17,9},{24,16},{25,33},{32,40},{... | collective-permute-start | bytes 3145736 | tf_op jit(solution)/shard_map/ppermute | solution.py:265
  36.0 14.9 %collective-permute-start.8 = (bf16[2,512,512]{2,1,0:T(8,128)(2,1)S(1)}, bf16[2,512,512]{2,1,0:T(8,128)(2,1)S(1)}, u32[]{:S(2)}, u32[]{:S(2)}) collective-permute-start(bf16[2,512,512]{2,1,0:T(8,128)(2,1)S(1)} %pad_maximum_fusion.1.refs_1_), channel_id=1, source_target_pairs={{0,2},{1,7},{2,0},{3,5},{4,6},{5,3},{6,4},{7,1},{8,10},{9,15},{10,... | collective-permute-start | bytes 3145736 | tf_op jit(solution)/shard_map/ppermute | solution.py:251
  38.6 12.4 %collective-permute-start.7 = (bf16[2,512,512]{2,1,0:T(8,128)(2,1)S(1)}, bf16[2,512,512]{2,1,0:T(8,128)(2,1)S(1)}, u32[]{:S(2)}, u32[]{:S(2)}) collective-permute-start(bf16[2,512,512]{2,1,0:T(8,128)(2,1)S(1)} %collective-permute-done.4.refs_2_.near_ref), channel_id=1, source_target_pairs={{0,1},{1,0},{2,3},{3,2},{4,5},{5,4},{6,7},{7,6},{8,9},{9,8},{10,11... | collective-permute-start | bytes 3145736 | tf_op jit(solution)/shard_map/ppermute | solution.py:244
  45.6 9.4 %collective-permute-start.11 = (bf16[8,256,128]{2,1,0:T(8,128)(2,1)S(1)}, bf16[8,256,128]{2,1,0:T(8,128)(2,1)S(1)}, u32[]{:S(2)}, u32[]{:S(2)}) collective-permute-start(bf16[8,256,128]{2,1,0:T(8,128)(2,1)S(1)} %slice.84), channel_id=1, source_target_pairs={{0,8},{1,57},{8,0},{9,17},{16,24},{17,9},{24,16},{25,33},{32,40},{... | collective-permute-start | bytes 1572872 | tf_op jit(solution)/shard_map/ppermute | solution.py:265
  51.0 9.3 %collective-permute-start.12 = (bf16[8,256,128]{2,1,0:T(8,128)(2,1)S(1)}, bf16[8,256,128]{2,1,0:T(8,128)(2,1)S(1)}, u32[]{:S(2)}, u32[]{:S(2)}) collective-permute-start(bf16[8,256,128]{2,1,0:T(8,128)(2,1)S(1)} %slice.85), channel_id=1, source_target_pairs={{0,64},{1,193},{64,0},{65,129},{128,192},{129,65},{192,128},{193,1... | collective-permute-start | bytes 1572872 | tf_op jit(solution)/shard_map/ppermute | solution.py:251
  53.1 8.5 %collective-permute-start.9 = (bf16[2,512,512]{2,1,0:T(8,128)(2,1)S(1)}, bf16[2,512,512]{2,1,0:T(8,128)(2,1)S(1)}, u32[]{:S(2)}, u32[]{:S(2)}) collective-permute-start(bf16[2,512,512]{2,1,0:T(8,128)(2,1)S(1)} %collective-permute-done.8.refs_0_), channel_id=1, source_target_pairs={{0,1},{1,0},{2,3},{3,2},{4,5},{5,4},{6,7},{7,6},{8,9},{9,8},{10,11... | collective-permute-start | bytes 3145736 | tf_op jit(solution)/shard_map/ppermute | solution.py:244
  62.7 15.2 %collective-permute-start.14 = (bf16[2,512,512]{2,1,0:T(8,128)(2,1)}, bf16[2,512,512]{2,1,0:T(8,128)(2,1)}, u32[]{:S(2)}, u32[]{:S(2)}) collective-permute-start(bf16[2,512,512]{2,1,0:T(8,128)(2,1)} %pad_maximum_fusion.3), channel_id=1, source_target_pairs={{0,2},{1,7},{2,0},{3,5},{4,6},{5,3},{6,4},{7,1},{8,10},{9,15},{10,... | collective-permute-start | bytes 3145736 | tf_op jit(solution)/shard_map/ppermute | solution.py:251
  66.1 8.6 %collective-permute-start.13 = (bf16[2,4,256,128]{3,2,1,0:T(8,128)(2,1)}, bf16[2,4,256,128]{3,2,1,0:T(8,128)(2,1)}, u32[]{:S(2)}, u32[]{:S(2)}) collective-permute-start(bf16[2,4,256,128]{3,2,1,0:T(8,128)(2,1)} %pad_maximum_fusion.4), channel_id=1, source_target_pairs={{0,192},{1,65},{64,128},{65,1},{128,64},{129,193},{192,0},{193,129... | collective-permute-start | bytes 1572872 | tf_op jit(solution)/shard_map/ppermute | solution.py:251
  77.9 6.2 %collective-permute-start.15 = (bf16[2,512,512]{2,1,0:T(8,128)(2,1)}, bf16[2,512,512]{2,1,0:T(8,128)(2,1)}, u32[]{:S(2)}, u32[]{:S(2)}) collective-permute-start(bf16[2,512,512]{2,1,0:T(8,128)(2,1)} %collective-permute-done.14.refs_2_.far_ref), channel_id=1, source_target_pairs={{0,1},{1,0},{2,3},{3,2},{4,5},{5,4},{6,7},{7,6},{8,9},{9,8},{10,11... | collective-permute-start | bytes 3145736 | tf_op jit(solution)/shard_map/ppermute | solution.py:244
  80.9 12.7 %collective-permute-start.18 = (bf16[528,128]{1,0:T(8,128)(2,1)}, bf16[528,128]{1,0:T(8,128)(2,1)}, u32[]{:S(2)}, u32[]{:S(2)}) collective-permute-start(bf16[528,128]{1,0:T(8,128)(2,1)} %get-tuple-element.72), channel_id=1, source_target_pairs={{0,4},{2,6},{4,0},{6,2},{1,5},{3,7},{5,1},{7,3},{8,12},{10,14},{12... | collective-permute-start | bytes 405512 | tf_op jit(solution)/shard_map/ppermute | solution.py:256
  82.2 11.4 %collective-permute-start.16 = (bf16[528,128]{1,0:T(8,128)(2,1)}, bf16[528,128]{1,0:T(8,128)(2,1)}, u32[]{:S(2)}, u32[]{:S(2)}) collective-permute-start(bf16[528,128]{1,0:T(8,128)(2,1)} %get-tuple-element.70), channel_id=1, source_target_pairs={{0,2},{1,7},{2,0},{3,5},{4,6},{5,3},{6,4},{7,1},{8,10},{9,15},{10,... | collective-permute-start | bytes 405512 | tf_op jit(solution)/shard_map/ppermute | solution.py:251
  83.4 10.3 %collective-permute-start.17 = (bf16[528,128]{1,0:T(8,128)(2,1)}, bf16[528,128]{1,0:T(8,128)(2,1)}, u32[]{:S(2)}, u32[]{:S(2)}) collective-permute-start(bf16[528,128]{1,0:T(8,128)(2,1)} %get-tuple-element.71), channel_id=1, source_target_pairs={{0,6},{1,3},{2,4},{3,1},{4,2},{5,7},{6,0},{7,5},{8,14},{9,11},{10,... | collective-permute-start | bytes 405512 | tf_op jit(solution)/shard_map/ppermute | solution.py:251
  95.5 11.9 %collective-permute-start.19 = (bf16[528,128]{1,0:T(8,128)(2,1)}, bf16[528,128]{1,0:T(8,128)(2,1)S(1)}, u32[]{:S(2)}, u32[]{:S(2)}) collective-permute-start(bf16[528,128]{1,0:T(8,128)(2,1)} %shard_map.90.refs_0_), channel_id=1, source_target_pairs={{0,16},{1,49},{16,0},{17,33},{32,48},{33,17},{48,32},{49,1},{2,18}... | collective-permute-start | bytes 405512 | tf_op jit(solution)/shard_map/ppermute | solution.py:251
  109.7 13.1 %collective-permute-start.20 = (bf16[528,128]{1,0:T(8,128)(2,1)}, bf16[528,128]{1,0:T(8,128)(2,1)S(1)}, u32[]{:S(2)}, u32[]{:S(2)}) collective-permute-start(bf16[528,128]{1,0:T(8,128)(2,1)} %shard_map.92.refs_0_), channel_id=1, source_target_pairs={{0,48},{1,17},{16,32},{17,1},{32,16},{33,49},{48,0},{49,33},{2,50}... | collective-permute-start | bytes 405512 | tf_op jit(solution)/shard_map/ppermute | solution.py:251
  125.2 5.6 %collective-permute-start.23 = (bf16[528,128]{1,0:T(8,128)(2,1)}, bf16[528,128]{1,0:T(8,128)(2,1)S(1)}, u32[]{:S(2)}, u32[]{:S(2)}) collective-permute-start(bf16[528,128]{1,0:T(8,128)(2,1)} %shard_map.94.refs_0_), channel_id=1, source_target_pairs={{0,128},{64,192},{128,0},{192,64},{1,129},{65,193},{129,1},{193,65... | collective-permute-start | bytes 405512 | tf_op jit(solution)/shard_map/ppermute | solution.py:256
  127.9 5.1 %collective-permute-start.22 = (bf16[528,128]{1,0:T(8,128)(2,1)}, bf16[528,128]{1,0:T(8,128)(2,1)S(1)}, u32[]{:S(2)}, u32[]{:S(2)}) collective-permute-start(bf16[528,128]{1,0:T(8,128)(2,1)} %shard_map.94.refs_0_), channel_id=1, source_target_pairs={{0,192},{1,65},{64,128},{65,1},{128,64},{129,193},{192,0},{193,129... | collective-permute-start | bytes 405512 | tf_op jit(solution)/shard_map/ppermute | solution.py:251
  128.4 7.7 %collective-permute-start.21 = (bf16[528,128]{1,0:T(8,128)(2,1)}, bf16[528,128]{1,0:T(8,128)(2,1)S(1)}, u32[]{:S(2)}, u32[]{:S(2)}) collective-permute-start(bf16[528,128]{1,0:T(8,128)(2,1)} %shard_map.94.refs_0_), channel_id=1, source_target_pairs={{0,64},{1,193},{64,0},{65,129},{128,192},{129,65},{192,128},{193,1... | collective-permute-start | bytes 405512 | tf_op jit(solution)/shard_map/ppermute | solution.py:251
  (40 other events, 121.0 us)

commit v6 on v5

--- a/solution.py
+++ b/solution.py
@@ -12,6 +12,8 @@
 TILE = 128
 EXTRA = 8
 LIMIT = 16 * 2**20
+SMALL = 8 * 2**20
+QUICK = pl.CostEstimate(flops=1, bytes_accessed=1, transcendentals=0)
 
 
 def widen_kernel(values_ref, scales_ref, out_ref):
@@ -27,7 +29,9 @@
 
 def widen_weight(values, scales):
     return pl.pallas_call(
-        widen_kernel, out_shape=jax.ShapeDtypeStruct(values.shape, jnp.bfloat16)
+        widen_kernel,
+        out_shape=jax.ShapeDtypeStruct(values.shape, jnp.bfloat16),
+        compiler_params=pltpu.CompilerParams(vmem_limit_bytes=SMALL),
     )(values, scales.T)
 
 
@@ -69,9 +73,7 @@
             jax.ShapeDtypeStruct((rows, 1), jnp.float32),
         ],
         compiler_params=pltpu.CompilerParams(vmem_limit_bytes=LIMIT),
-        cost_estimate=pl.CostEstimate(
-            flops=6 * rows * width, bytes_accessed=4 * rows * width, transcendentals=rows
-        ),
+        cost_estimate=QUICK,
     )(table, tokens, gain)
 
 
@@ -105,11 +107,7 @@
         out_shape=[jax.ShapeDtypeStruct(shape, jnp.bfloat16)] * 2
         + [jax.ShapeDtypeStruct(shape, jnp.float32)] * 2,
         compiler_params=pltpu.CompilerParams(vmem_limit_bytes=LIMIT),
-        cost_estimate=pl.CostEstimate(
-            flops=4 * rows * width * columns,
-            bytes_accessed=4 * rows * width + 6 * columns * tiles * TILE,
-            transcendentals=0,
-        ),
+        cost_estimate=QUICK,
     )(own, got, cot_own, cot_got)
     return outs[:2], outs[2:]
 
@@ -120,8 +118,16 @@
     return pltpu.make_async_copy(tok_ref.at[:, pl.ds(at, span)], block.at[k], sem.at[k])
 
 
+def shards_of(refs):
+    return [ref.at[k] for ref in refs for k in range(ref.shape[0])]
+
+
 def forward_kernel(tab_ref, tok_ref, inv_ref, gain_ref, *refs):
     w_refs, acc_in, (acc, block, sem) = refs[:4], refs[4:-3], refs[-3:]
+    forward_steps(tab_ref, tok_ref, inv_ref, gain_ref, shards_of(w_refs), acc_in, acc, block, sem)
+
+
+def forward_steps(tab_ref, tok_ref, inv_ref, gain_ref, weights, acc_in, acc, block, sem):
     count, _, span = block.shape
     for k in range(count):
         block_in(tab_ref, tok_ref, block, sem, k).start()
@@ -132,12 +138,13 @@
         at = pl.multiple_of(tab_ref[k] * span, span)
         wide = block[k].astype(jnp.float32)
         normed = (wide * inverse * gain_ref[:, pl.ds(at, span)]).astype(jnp.bfloat16)
-        acc[...] += jnp.dot(normed, w_refs[k // 2][k % 2], preferred_element_type=jnp.float32)
+        acc[...] += jnp.dot(normed, weights[k][...], preferred_element_type=jnp.float32)
 
 
 def forward_last_kernel(tab_ref, tok_ref, inv_ref, gain_ref, cot_ref, *refs):
-    w_refs, acc_in, proj_ref, moment_ref, acc, block, sem = refs[:4], *refs[4:]
-    forward_kernel(tab_ref, tok_ref, inv_ref, gain_ref, *w_refs, acc_in, acc, block, sem)
+    w_refs, (acc_in, proj_ref, moment_ref, acc, block, sem) = refs[:-6], refs[-6:]
+    weights = shards_of(w_refs)
+    forward_steps(tab_ref, tok_ref, inv_ref, gain_ref, weights, (acc_in,), acc, block, sem)
     keys = acc[...]
     inverse = inv_ref[...]
     proj_ref[...] = keys.astype(jnp.bfloat16)
@@ -145,8 +152,8 @@
     moment_ref[...] = inverse * inverse * inner / tok_ref.shape[1]
 
 
-def backward_kernel(tab_ref, tok_ref, inv_ref, gain_ref, cot_ref, moment_ref, *refs):
-    w_refs, (grads_ref, block, out, sem, out_sem) = refs[:4], refs[-5:]
+def backward_kernel(tab_ref, tok_ref, inv_ref, gain_ref, cot_ref, moment_ref, *refs, count):
+    weights, (grads_ref, block, out, sem, out_sem) = shards_of(refs[:count]), refs[-5:]
     count, _, span = block.shape
 
     def block_out(k):
@@ -158,7 +165,7 @@
     inverse, moment, cot = inv_ref[...], moment_ref[...], cot_ref[...]
     for k in range(count):
         partial = lax.dot_general(
-            cot, w_refs[k // 2][k % 2], (((1,), (1,)), ((), ())), preferred_element_type=jnp.float32
+            cot, weights[k][...], (((1,), (1,)), ((), ())), preferred_element_type=jnp.float32
         )
         block_in(tab_ref, tok_ref, block, sem, k).wait()
         at = pl.multiple_of(tab_ref[k] * span, span)
@@ -206,7 +213,7 @@
     rows, span, columns = tokens.shape[0], *weights[0].shape[1:]
     return pl.pallas_call(
         forward_last_kernel,
-        in_specs=[SMEM, ANY] + [VMEM] * 8,
+        in_specs=[SMEM, ANY] + [VMEM] * (4 + len(weights)),
         out_specs=[VMEM] * 2,
         out_shape=[
             jax.ShapeDtypeStruct((rows, columns), jnp.bfloat16),
@@ -224,8 +231,8 @@
 def backward(tokens, inverse, gain, cotangent, moment, weights, table, before=()):
     rows, span, columns = tokens.shape[0], *weights[0].shape[1:]
     return pl.pallas_call(
-        backward_kernel,
-        in_specs=[SMEM, ANY] + [VMEM] * 8 + [ANY] * len(before),
+        functools.partial(backward_kernel, count=len(weights)),
+        in_specs=[SMEM, ANY] + [VMEM] * (4 + len(weights)) + [ANY] * len(before),
         out_specs=ANY,
         out_shape=jax.ShapeDtypeStruct(tokens.shape, jnp.bfloat16),
         scratch_shapes=[
@@ -234,7 +241,7 @@
             pltpu.SemaphoreType.DMA((8,)),
             pltpu.SemaphoreType.DMA((8,)),
         ],
-        input_output_aliases={10: 0} if before else {},
+        input_output_aliases={6 + len(weights): 0} if before else {},
         **costs(tokens, columns),
     )(table, tokens, inverse, gain, cotangent, moment, *weights, *before)
 
@@ -343,6 +350,7 @@
         in_specs=[VMEM] * len(parts),
         out_specs=VMEM,
         out_shape=jax.ShapeDtypeStruct(parts[0].shape, parts[0].dtype),
+        compiler_params=pltpu.CompilerParams(vmem_limit_bytes=SMALL),
     )(*parts)
 
 
@@ -365,6 +373,7 @@
             jax.ShapeDtypeStruct((4 * TILE, columns), jnp.float32),
             jax.ShapeDtypeStruct((4, EXTRA, TILE), jnp.float32),
         ],
+        compiler_params=pltpu.CompilerParams(vmem_limit_bytes=SMALL),
     )(table, *parts)
 
 
@@ -382,6 +391,7 @@
         in_specs=[SMEM] + [VMEM] * 4,
         out_specs=VMEM,
         out_shape=jax.ShapeDtypeStruct((16, 4, TILE), jnp.float32),
+        compiler_params=pltpu.CompilerParams(vmem_limit_bytes=SMALL),
     )(table, *parts)
 
 
@@ -414,42 +424,43 @@
     cot_own = key_cotangent.T
     base = jnp.stack([own, own_c])
     cot_got = swap(cot_own, "c")
-    mine, other, inverse = norm_tiles(tie(tokens, base, cot_own), gain, jnp.stack(tables))
+    mine, other, inverse = norm_tiles(tokens, gain, tie(jnp.stack(tables), base, cot_own))
     got = swap(other, "c")
-    got, up = lax.optimization_barrier((got, up))
     near = pair(base, "x", 0)
-    up_c = swap(up, "c")
     sent, kept = grad_tiles(mine, got, cot_own, cot_got)
 
     first = sent[0]
-    second, near, up_c = lax.optimization_barrier((sent[1], near, up_c))
-    moved = (pair(first, "y", 0), pair_z(second))
+    second, near, up = lax.optimization_barrier((sent[1], near, up))
+    moved = [pair(first, "y", 0), pair_z(second)]
     near_c = swap(near, "c")
-    above = jnp.stack([up, up_c])
+    above = jnp.stack([up, swap(up, "c")])
     above_near = pair(above, "x", 0)
+    far = pair(near_c[1:], "x", 0)
     (first, kept_first), (second, kept_second) = (halve(add(k, m)) for k, m in zip(kept, moved))
-    second, near_c, above_near = lax.optimization_barrier((second, near_c, above_near))
-    moved = (pair_z(first), pair(second, "y", 0))
+
+    second, near_c, above = lax.optimization_barrier((second, near_c, above))
+    moved = [pair_z(first), pair(second, "y", 0)]
+    early, late_at = [base, above, near, near_c], shards_at[8:]
+    sums = forward(tokens, inverse, gain, early, shards_at[:8])
+    moved[1], sums, above_near, far = lax.optimization_barrier((moved[1], sums, above_near, far))
     above_near_c = swap(above_near, "c")
-    far = pair(jnp.stack([near_c[1], above_near_c[1]]), "x", 0)
+    above_far = pair(above_near_c[1:], "x", 0)
     (first, kept_first), (second, kept_second) = (
         halve(add(k, m)) for k, m in zip((kept_first, kept_second), moved)
     )
-    send, near_c = lax.optimization_barrier((jnp.stack([first, second]), near_c))
-    moved = pair(send, "y", 1)
-    early, late_at = [base, above, near, near_c], shards_at[8:]
-    sums = forward(tokens, inverse, gain, early, shards_at[:8])
-    moved, sums = lax.optimization_barrier((moved, sums))
+
+    moved = pair(jnp.stack([first, second]), "y", 1)
+    far_c = swap(far, "c")
+    moved, above_far, far_c = lax.optimization_barrier((moved, above_far, far_c))
     total = jnp.stack([add(kept_first, moved[0]), add(kept_second, moved[1])], axis=1)
-    total, far, sums = lax.optimization_barrier((total, far, sums))
 
     peer = x ^ offset(c, jnp.arange(4) // 2, jnp.arange(4) % 2)
     node_tile = ((zl * 4 + peer) * 2 + c) * 4 + y
     at = jnp.concatenate([node_tile, y[None], peer]).astype(jnp.int32)
-    parts = spread(total, gain, base, near, near_c, far, at, devices)
+    parts = list(spread(total, gain, base, near, near_c, far, at, devices))
+    parts[0], above_far = lax.optimization_barrier((parts[0], above_far))
     moved = [parts[0], pair(parts[2], "x", 0), pair(parts[1], "x", 1), across(parts[3], "x")]
-    far_c = swap(far, "c")
-    late = [above_near, above_near_c, far, far_c]
+    late = [above_near, above_near_c, far, above_far, far_c, swap(above_far, "c")]
     projected, moment = forward_last(tokens, inverse, gain, key_cotangent, late, sums, late_at)
     moved[3], moment = lax.optimization_barrier((moved[3], moment))
     send = merge(moved)

time: 148 us -> 132 us (0.89)
  local copies, waits for them, and re-layouts: 28.7 us -> 19.9 us
  Pallas kernels: 41.4 us -> 36.4 us
  starting transfers between devices: 36.7 us -> 40.7 us
  waiting for transfers between devices: 32.7 us -> 28.9 us
  other arithmetic: 6.48 us -> 4.71 us
    unnamed x73 -> x47, local copies, waits for them, and re-layouts: 28.3 us -> 16.8 us
    ppermute x12 -> x13, waiting for transfers between devices: 22.5 us -> 16.8 us  [pair(): return lax.ppermute(array, (axis, 'c'), moves)]
    pallas_call x3, Pallas kernels: 5.17 us -> 1.21 us  [merge(): pl.pallas_call(functools.partial(merge_kernel, scale=scale), in_specs=[VM...]
    ppermute x3, starting transfers between devices: 8.55 us -> 12.1 us  [pair_z(): return lax.ppermute(array, ('zh', 'zl', 'c'), moves)]
    ppermute x10 -> x11, waiting for transfers between devices: 2.29 us -> 5.3 us  [swap(): return lax.ppermute(array, axis, [(a, last - a) for a in range(last + 1)])]
    ppermute x12 -> x13, starting transfers between devices: 17.4 us -> 20.1 us  [pair(): return lax.ppermute(array, (axis, 'c'), moves)]
    add x4, other arithmetic: 0.62 us -> 3.06 us  [add(): return kept + got.astype(jnp.float32)]
    ppermute x2, starting transfers between devices: 4.03 us -> 1.74 us  [across(): return lax.ppermute(array, axis, [(a, a ^ 2) for a in range(size)])]
  transfers between devices with their start and end apart: 27 -> 29, of which waited for: 15 -> 13; matrix products, arithmetic and copies ran while one was open for 4% -> 7% of each run, Pallas kernels for 18% -> 20%
where the time goes in v6:
time: 132 us
  starting transfers between devices  40.7 us (31%)
  Pallas kernels  36.4 us (28%)
  waiting for transfers between devices  28.9 us (22%)
  local copies, waits for them, and re-layouts  19.9 us (15%)
  other arithmetic  4.71 us (4%)
    ppermute x13, starting transfers between devices, pair(): return lax.ppermute(array, (axis, 'c'), moves)  20.1 us
    unnamed x47, local copies, waits for them, and re-layouts  16.8 us
    ppermute x13, waiting for transfers between devices, pair(): return lax.ppermute(array, (axis, 'c'), moves)  16.8 us
    pallas_call x2, Pallas kernels, backward(): pl.pallas_call(functools.partial(backward_kernel, count=len(weights)), in...  13.4 us
    ppermute x3, starting transfers between devices, pair_z(): return lax.ppermute(array, ('zh', 'zl', 'c'), moves)  12.1 us
    ppermute x11, starting transfers between devices, swap(): return lax.ppermute(array, axis, [(a, last - a) for a in range(last + 1)])  6.76 us
    ppermute x11, waiting for transfers between devices, swap(): return lax.ppermute(array, axis, [(a, last - a) for a in range(last + 1)])  5.3 us
    pallas_call x1, Pallas kernels, forward_last(): pl.pallas_call(forward_last_kernel, in_specs=[SMEM, ANY] + [VMEM] * (4 +...  4.77 us
  transfers between devices with their start and end apart: 29, of which 13 were waited for; matrix products, arithmetic and copies ran while one was open for 7% of the time, Pallas kernels for 20%

profile of v6, /device:TPU:1, one launch (start us, length us, event | category | flops | bytes accessed | tf_op | source)
XLA Modules:
  0.0 131.6 jit_solution(7021381221391157265)
XLA Ops:
  2.8 3.3 %collective-permute-start = (bf16[512,512]{1,0:T(8,128)(2,1)S(1)}, bf16[512,512]{1,0:T(8,128)(2,1)S(1)}, u32[]{:S(2)}, u32[]{:S(2)}) collective-permute-start(bf16[512,512]{1,0:T(8,128)(2,1)S(1)} %shard_map.84), channel_id=1, source_target_pairs={{0,1},{1,0},{2,3},{3,2},{4,5},{5,4},{6,7},{7,6},{8,9},{9,8},{10,11... | collective-permute-start | bytes 1572872 | tf_op jit(solution)/shard_map/ppermute | solution.py:251
  7.7 2.5 %copy-done = bf16[320,8192]{1,0:T(8,128)(2,1)S(1)} copy-done((bf16[320,8192]{1,0:T(8,128)(2,1)S(1)}, bf16[320,8192]{1,0:T(8,128)(2,1)}, u32[]{:S(2)}) %copy-start) | copy-done | bytes 5242904
  10.2 3.4 %shard_map.85 = (bf16[320,4096]{1,0:T(8,128)(2,1)S(1)}, bf16[320,4096]{1,0:T(8,128)(2,1)S(1)}, f32[320,1]{1,0:T(8,128)S(1)}) custom-call(s32[2,32]{1,0:T(2,128)S(1)} %pad_add_fusion.tab_ref, bf16[320,8192]{1,0:T(8,128)(2,1)S(1)} %copy-done, f32[1,8192]{1,0:T(1,128)S(1)} %bitcast.51), custom_call_target="tpu_custom_call" | custom-call | flops 1 | bytes 1 | tf_op jit(solution)/shard_map/pallas_call | solution.py:59
  14.8 5.6 %collective-permute-start.4 = (bf16[512,512]{1,0:T(8,128)(2,1)S(1)}, bf16[512,512]{1,0:T(8,128)(2,1)S(1)}, u32[]{:S(2)}, u32[]{:S(2)}) collective-permute-start(bf16[512,512]{1,0:T(8,128)(2,1)S(1)} %shard_map.84), channel_id=1, source_target_pairs={{0,8},{1,57},{8,0},{9,17},{16,24},{17,9},{24,16},{25,33},{32,40},{... | collective-permute-start | bytes 1572872 | tf_op jit(solution)/shard_map/ppermute | solution.py:272
  22.1 4.5 %shard_map.86 = (bf16[16,256,128]{2,1,0:T(8,128)(2,1)S(1)}, bf16[16,256,128]{2,1,0:T(8,128)(2,1)S(1)}, f32[16,256,128]{2,1,0:T(8,128)S(1)}, f32[16,256,128]{2,1,0:T(8,128)S(1)}) custom-call(bf16[320,4096]{1,0:T(8,128)(2,1)S(1)} %get-tuple-element.47.own_ref, bf16[320,4096]{1,0:T(8,128)(2,1)S(1)} %collective-permute-done.1.got_ref, ...), custom_call_target="tpu_custom_call" | custom-call | flops 1 | bytes 1 | tf_op jit(solution)/shard_map/pallas_call | solution.py:105
  28.9 3.8 %collective-permute-start.5 = (bf16[16,256,128]{2,1,0:T(8,128)(2,1)S(1)}, bf16[16,256,128]{2,1,0:T(8,128)(2,1)S(1)}, u32[]{:S(2)}, u32[]{:S(2)}) collective-permute-start(bf16[16,256,128]{2,1,0:T(8,128)(2,1)S(1)} %get-tuple-element.51), channel_id=1, source_target_pairs={{0,8},{1,57},{8,0},{9,17},{16,24},{17,9},{24,16},{25,33},{32,40},{... | collective-permute-start | bytes 3145736 | tf_op jit(solution)/shard_map/ppermute | solution.py:272
  32.8 2.7 %collective-permute-start.12 = (bf16[16,256,128]{2,1,0:T(8,128)(2,1)S(1)}, bf16[16,256,128]{2,1,0:T(8,128)(2,1)S(1)}, u32[]{:S(2)}, u32[]{:S(2)}) collective-permute-start(bf16[16,256,128]{2,1,0:T(8,128)(2,1)S(1)} %get-tuple-element.60), channel_id=1, source_target_pairs={{0,64},{1,193},{64,0},{65,129},{128,192},{129,65},{192,128},{193,1... | collective-permute-start | bytes 3145736 | tf_op jit(solution)/shard_map/ppermute | solution.py:258
  38.5 2.5 %collective-permute-start.9 = (bf16[2,512,512]{2,1,0:T(8,128)(2,1)}, bf16[2,512,512]{2,1,0:T(8,128)(2,1)}, u32[]{:S(2)}, u32[]{:S(2)}) collective-permute-start(bf16[2,512,512]{2,1,0:T(8,128)(2,1)} %pad_maximum_fusion.1.refs_1_), channel_id=1, source_target_pairs={{0,2},{1,7},{2,0},{3,5},{4,6},{5,3},{6,4},{7,1},{8,10},{9,15},{10,... | collective-permute-start | bytes 3145736 | tf_op jit(solution)/shard_map/ppermute | solution.py:258
  41.0 4.0 %collective-permute-done.5 = bf16[16,256,128]{2,1,0:T(8,128)(2,1)S(1)} collective-permute-done((bf16[16,256,128]{2,1,0:T(8,128)(2,1)S(1)}, bf16[16,256,128]{2,1,0:T(8,128)(2,1)S(1)}, u32[]{:S(2)}, u32[]{:S(2)}) %collective-permute-start.5) | collective-permute-done | bytes 1048608 | tf_op jit(solution)/shard_map/ppermute | solution.py:272
  47.0 2.5 %collective-permute-start.10 = (bf16[1,512,512]{2,1,0:T(8,128)(2,1)}, bf16[1,512,512]{2,1,0:T(8,128)(2,1)}, u32[]{:S(2)}, u32[]{:S(2)}) collective-permute-start(bf16[1,512,512]{2,1,0:T(8,128)(2,1)} %slice.58), channel_id=1, source_target_pairs={{0,2},{1,7},{2,0},{3,5},{4,6},{5,3},{6,4},{7,1},{8,10},{9,15},{10,... | collective-permute-start | bytes 1572872 | tf_op jit(solution)/shard_map/ppermute | solution.py:258
  49.5 2.7 %collective-permute-start.8 = (bf16[8,256,128]{2,1,0:T(8,128)(2,1)}, bf16[8,256,128]{2,1,0:T(8,128)(2,1)}, u32[]{:S(2)}, u32[]{:S(2)}) collective-permute-start(bf16[8,256,128]{2,1,0:T(8,128)(2,1)} %slice.86), channel_id=1, source_target_pairs={{0,64},{1,193},{64,0},{65,129},{128,192},{129,65},{192,128},{193,1... | collective-permute-start | bytes 1572872 | tf_op jit(solution)/shard_map/ppermute | solution.py:258
  54.0 2.7 %collective-permute-start.13 = (bf16[8,256,128]{2,1,0:T(8,128)(2,1)}, bf16[8,256,128]{2,1,0:T(8,128)(2,1)}, u32[]{:S(2)}, u32[]{:S(2)}) collective-permute-start(bf16[8,256,128]{2,1,0:T(8,128)(2,1)} %slice.85), channel_id=1, source_target_pairs={{0,8},{1,57},{8,0},{9,17},{16,24},{17,9},{24,16},{25,33},{32,40},{... | collective-permute-start | bytes 1572872 | tf_op jit(solution)/shard_map/ppermute | solution.py:272
  56.8 2.5 %copy-done.1 = bf16[320,8192]{1,0:T(8,128)(2,1)S(1)} copy-done((bf16[320,8192]{1,0:T(8,128)(2,1)S(1)}, bf16[320,8192]{1,0:T(8,128)(2,1)}, u32[]{:S(2)}) %copy-start.1) | copy-done | bytes 5242904
  59.2 3.7 %shard_map.87.refs_6_ = f32[320,512]{1,0:T(8,128)S(1)} custom-call(s32[8]{0:T(128)S(1)} %stack.146.tab_ref, bf16[320,8192]{1,0:T(8,128)(2,1)S(1)} %copy-done.1, f32[320,1]{1,0:T(8,128)S(1)} %get-tuple-element.46.inv_ref, f32[1,8192]{1,0:T(1,128)S(1)} %bitcast.52, bf16[2,512,512]{2,1,0:T(8,128)(2,1)S(1)} %pad_maximum_fusion.refs_0_.base_ref, ...), custom_call_target="tpu_custom_call" | custom-call | flops 1342177280 | bytes 9437184 | tf_op jit(solution)/shard_map/pallas_call | solution.py:199
  67.9 7.1 %collective-permute-done.14 = bf16[2,4,256,128]{3,2,1,0:T(8,128)(2,1)S(1)} collective-permute-done((bf16[2,4,256,128]{3,2,1,0:T(8,128)(2,1)S(1)}, bf16[2,4,256,128]{3,2,1,0:T(8,128)(2,1)S(1)}, u32[]{:S(2)}, u32[]{:S(2)}) %collective-permute-start.14) | collective-permute-done | bytes 524320 | tf_op jit(solution)/shard_map/ppermute | solution.py:258
  77.2 2.1 %shard_map.88 = (bf16[528,128]{1,0:T(8,128)(2,1)S(1)}, bf16[528,128]{1,0:T(8,128)(2,1)}, bf16[528,128]{1,0:T(8,128)(2,1)}, bf16[528,128]{1,0:T(8,128)(2,1)}) custom-call(s32[9]{0:T(128)S(1)} %pad_add_fusion.1.tab_ref, f32[4,2,256,128]{3,2,1,0:T(8,128)S(1)} %pad_maximum_fusion.2.total_ref, f32[1,8192]{1,0:T(1,128)S(1)} %bitcast.53, ...), custom_call_target="tpu_custom_call" | custom-call | tf_op jit(solution)/shard_map/pallas_call | solution.py:323
  80.6 2.1 %collective-permute-start.18 = (bf16[528,128]{1,0:T(8,128)(2,1)}, bf16[528,128]{1,0:T(8,128)(2,1)}, u32[]{:S(2)}, u32[]{:S(2)}) collective-permute-start(bf16[528,128]{1,0:T(8,128)(2,1)} %get-tuple-element.70), channel_id=1, source_target_pairs={{0,2},{1,7},{2,0},{3,5},{4,6},{5,3},{6,4},{7,1},{8,10},{9,15},{10,... | collective-permute-start | bytes 405512 | tf_op jit(solution)/shard_map/ppermute | solution.py:258
  83.3 2.5 %copy-done.2 = bf16[320,8192]{1,0:T(8,128)(2,1)S(1)} copy-done((bf16[320,8192]{1,0:T(8,128)(2,1)S(1)}, bf16[320,8192]{1,0:T(8,128)(2,1)}, u32[]{:S(2)}) %copy-start.2) | copy-done | bytes 5242904
  90.1 4.8 %shard_map.89 = (bf16[320,512]{1,0:T(8,128)(2,1)}, f32[320,1]{1,0:T(8,128)S(1)}) custom-call(s32[8]{0:T(128)S(1)} %stack.130.tab_ref, bf16[320,8192]{1,0:T(8,128)(2,1)S(1)} %copy-done.2, f32[320,1]{1,0:T(8,128)S(1)} %copy-done.8, f32[1,8192]{1,0:T(1,128)S(1)} %bitcast.54, bf16[320,512]{1,0:T(8,128)(2,1)S(1)} %copy-done.6, ...), custom_call_target="tpu_custom_call" | custom-call | flops 1342177280 | bytes 9437184 | tf_op jit(solution)/shard_map/pallas_call | solution.py:214
  96.1 2.4 %collective-permute-start.21 = (bf16[528,128]{1,0:T(8,128)(2,1)S(1)}, bf16[528,128]{1,0:T(8,128)(2,1)S(1)}, u32[]{:S(2)}, u32[]{:S(2)}) collective-permute-start(bf16[528,128]{1,0:T(8,128)(2,1)S(1)} %shard_map.90.refs_0_), channel_id=1, source_target_pairs={{0,16},{1,49},{16,0},{17,33},{32,48},{33,17},{48,32},{49,1},{2,18}... | collective-permute-start | bytes 405512 | tf_op jit(solution)/shard_map/ppermute | solution.py:258
  98.4 6.5 %shard_map.91.refs_6_ = bf16[320,8192]{1,0:T(8,128)(2,1)} custom-call(s32[8]{0:T(128)S(1)} %stack.146.tab_ref, bf16[320,8192]{1,0:T(8,128)(2,1)S(1)} %copy-done.2, f32[320,1]{1,0:T(8,128)S(1)} %copy-done.8, f32[1,8192]{1,0:T(1,128)S(1)} %bitcast.55, bf16[320,512]{1,0:T(8,128)(2,1)S(1)} %copy-done.6, f32[320,1]{1,0:T(8,128)S(1)} %get-tuple-element.77.moment_ref, ...), custom_call_target="tpu_custom_call" | custom-call | flops 1342177280 | bytes 9437184 | tf_op jit(solution)/shard_map/pallas_call | solution.py:233
  107.0 6.9 %shard_map.93 = bf16[320,8192]{1,0:T(8,128)(2,1)} custom-call(s32[8]{0:T(128)S(1)} %stack.130.tab_ref, bf16[320,8192]{1,0:T(8,128)(2,1)S(1)} %copy-done.2, f32[320,1]{1,0:T(8,128)S(1)} %copy-done.8, f32[1,8192]{1,0:T(1,128)S(1)} %bitcast.56, bf16[320,512]{1,0:T(8,128)(2,1)S(1)} %copy-done.6, ...), custom_call_target="tpu_custom_call", output_to_operand_aliasing={{}: (12, {})} | custom-call | flops 1342177280 | bytes 9437184 | tf_op jit(solution)/shard_map/pallas_call | solution.py:233
  119.5 2.4 %collective-permute-done.24.refs_2_ = bf16[528,128]{1,0:T(8,128)(2,1)S(1)} collective-permute-done((bf16[528,128]{1,0:T(8,128)(2,1)S(1)}, bf16[528,128]{1,0:T(8,128)(2,1)S(1)}, u32[]{:S(2)}, u32[]{:S(2)}) %collective-permute-start.24) | collective-permute-done | bytes 135200 | tf_op jit(solution)/shard_map/ppermute | solution.py:258
  121.9 3.3 %collective-permute-done.23.refs_1_ = bf16[528,128]{1,0:T(8,128)(2,1)S(1)} collective-permute-done((bf16[528,128]{1,0:T(8,128)(2,1)S(1)}, bf16[528,128]{1,0:T(8,128)(2,1)S(1)}, u32[]{:S(2)}, u32[]{:S(2)}) %collective-permute-start.23) | collective-permute-done | bytes 135200 | tf_op jit(solution)/shard_map/ppermute | solution.py:258
  (117 shorter events, 44.2 us)
Async XLA Ops:
  2.8 4.9 %collective-permute-start = (bf16[512,512]{1,0:T(8,128)(2,1)S(1)}, bf16[512,512]{1,0:T(8,128)(2,1)S(1)}, u32[]{:S(2)}, u32[]{:S(2)}) collective-permute-start(bf16[512,512]{1,0:T(8,128)(2,1)S(1)} %shard_map.84), channel_id=1, source_target_pairs={{0,1},{1,0},{2,3},{3,2},{4,5},{5,4},{6,7},{7,6},{8,9},{9,8},{10,11... | collective-permute-start | bytes 1572872 | tf_op jit(solution)/shard_map/ppermute | solution.py:251
  13.6 8.5 %collective-permute-start.1 = (bf16[320,4096]{1,0:T(8,128)(2,1)S(1)}, bf16[320,4096]{1,0:T(8,128)(2,1)S(1)}, u32[]{:S(2)}, u32[]{:S(2)}) collective-permute-start(bf16[320,4096]{1,0:T(8,128)(2,1)S(1)} %get-tuple-element.48), channel_id=1, source_target_pairs={{0,1},{1,0},{2,3},{3,2},{4,5},{5,4},{6,7},{7,6},{8,9},{9,8},{10,11... | collective-permute-start | bytes 7864328 | tf_op jit(solution)/shard_map/ppermute | solution.py:251
  14.1 14.9 %collective-permute-start.3 = (bf16[2,512,512]{2,1,0:T(8,128)(2,1)S(1)}, bf16[2,512,512]{2,1,0:T(8,128)(2,1)S(1)}, u32[]{:S(2)}, u32[]{:S(2)}) collective-permute-start(bf16[2,512,512]{2,1,0:T(8,128)(2,1)S(1)} %pad_maximum_fusion.refs_0_.base_ref), channel_id=1, source_target_pairs={{0,2},{1,7},{2,0},{3,5},{4,6},{5,3},{6,4},{7,1},{8,10},{9,15},{10,... | collective-permute-start | bytes 3145736 | tf_op jit(solution)/shard_map/ppermute | solution.py:258
  14.8 12.1 %collective-permute-start.4 = (bf16[512,512]{1,0:T(8,128)(2,1)S(1)}, bf16[512,512]{1,0:T(8,128)(2,1)S(1)}, u32[]{:S(2)}, u32[]{:S(2)}) collective-permute-start(bf16[512,512]{1,0:T(8,128)(2,1)S(1)} %shard_map.84), channel_id=1, source_target_pairs={{0,8},{1,57},{8,0},{9,17},{16,24},{17,9},{24,16},{25,33},{32,40},{... | collective-permute-start | bytes 1572872 | tf_op jit(solution)/shard_map/ppermute | solution.py:272
  28.9 16.0 %collective-permute-start.5 = (bf16[16,256,128]{2,1,0:T(8,128)(2,1)S(1)}, bf16[16,256,128]{2,1,0:T(8,128)(2,1)S(1)}, u32[]{:S(2)}, u32[]{:S(2)}) collective-permute-start(bf16[16,256,128]{2,1,0:T(8,128)(2,1)S(1)} %get-tuple-element.51), channel_id=1, source_target_pairs={{0,8},{1,57},{8,0},{9,17},{16,24},{17,9},{24,16},{25,33},{32,40},{... | collective-permute-start | bytes 3145736 | tf_op jit(solution)/shard_map/ppermute | solution.py:272
  32.8 13.4 %collective-permute-start.6 = (bf16[2,512,512]{2,1,0:T(8,128)(2,1)S(1)}, bf16[2,512,512]{2,1,0:T(8,128)(2,1)S(1)}, u32[]{:S(2)}, u32[]{:S(2)}) collective-permute-start(bf16[2,512,512]{2,1,0:T(8,128)(2,1)S(1)} %collective-permute-done.3.refs_2_.near_ref), channel_id=1, source_target_pairs={{0,1},{1,0},{2,3},{3,2},{4,5},{5,4},{6,7},{7,6},{8,9},{9,8},{10,11... | collective-permute-start | bytes 3145736 | tf_op jit(solution)/shard_map/ppermute | solution.py:251
  32.8 19.4 %collective-permute-start.12 = (bf16[16,256,128]{2,1,0:T(8,128)(2,1)S(1)}, bf16[16,256,128]{2,1,0:T(8,128)(2,1)S(1)}, u32[]{:S(2)}, u32[]{:S(2)}) collective-permute-start(bf16[16,256,128]{2,1,0:T(8,128)(2,1)S(1)} %get-tuple-element.60), channel_id=1, source_target_pairs={{0,64},{1,193},{64,0},{65,129},{128,192},{129,65},{192,128},{193,1... | collective-permute-start | bytes 3145736 | tf_op jit(solution)/shard_map/ppermute | solution.py:258
  38.5 24.5 %collective-permute-start.9 = (bf16[2,512,512]{2,1,0:T(8,128)(2,1)}, bf16[2,512,512]{2,1,0:T(8,128)(2,1)}, u32[]{:S(2)}, u32[]{:S(2)}) collective-permute-start(bf16[2,512,512]{2,1,0:T(8,128)(2,1)} %pad_maximum_fusion.1.refs_1_), channel_id=1, source_target_pairs={{0,2},{1,7},{2,0},{3,5},{4,6},{5,3},{6,4},{7,1},{8,10},{9,15},{10,... | collective-permute-start | bytes 3145736 | tf_op jit(solution)/shard_map/ppermute | solution.py:258
  47.0 16.0 %collective-permute-start.10 = (bf16[1,512,512]{2,1,0:T(8,128)(2,1)}, bf16[1,512,512]{2,1,0:T(8,128)(2,1)}, u32[]{:S(2)}, u32[]{:S(2)}) collective-permute-start(bf16[1,512,512]{2,1,0:T(8,128)(2,1)} %slice.58), channel_id=1, source_target_pairs={{0,2},{1,7},{2,0},{3,5},{4,6},{5,3},{6,4},{7,1},{8,10},{9,15},{10,... | collective-permute-start | bytes 1572872 | tf_op jit(solution)/shard_map/ppermute | solution.py:258
  49.5 13.5 %collective-permute-start.8 = (bf16[8,256,128]{2,1,0:T(8,128)(2,1)}, bf16[8,256,128]{2,1,0:T(8,128)(2,1)}, u32[]{:S(2)}, u32[]{:S(2)}) collective-permute-start(bf16[8,256,128]{2,1,0:T(8,128)(2,1)} %slice.86), channel_id=1, source_target_pairs={{0,64},{1,193},{64,0},{65,129},{128,192},{129,65},{192,128},{193,1... | collective-permute-start | bytes 1572872 | tf_op jit(solution)/shard_map/ppermute | solution.py:258
  54.0 9.6 %collective-permute-start.13 = (bf16[8,256,128]{2,1,0:T(8,128)(2,1)}, bf16[8,256,128]{2,1,0:T(8,128)(2,1)}, u32[]{:S(2)}, u32[]{:S(2)}) collective-permute-start(bf16[8,256,128]{2,1,0:T(8,128)(2,1)} %slice.85), channel_id=1, source_target_pairs={{0,8},{1,57},{8,0},{9,17},{16,24},{17,9},{24,16},{25,33},{32,40},{... | collective-permute-start | bytes 1572872 | tf_op jit(solution)/shard_map/ppermute | solution.py:272
  63.0 3.5 %collective-permute-start.11 = (bf16[2,512,512]{2,1,0:T(8,128)(2,1)}, bf16[2,512,512]{2,1,0:T(8,128)(2,1)S(1)}, u32[]{:S(2)}, u32[]{:S(2)}) collective-permute-start(bf16[2,512,512]{2,1,0:T(8,128)(2,1)} %collective-permute-done.9.refs_0_), channel_id=1, source_target_pairs={{0,1},{1,0},{2,3},{3,2},{4,5},{5,4},{6,7},{7,6},{8,9},{9,8},{10,11... | collective-permute-start | bytes 3145736 | tf_op jit(solution)/shard_map/ppermute | solution.py:251
  66.4 8.5 %collective-permute-start.14 = (bf16[2,4,256,128]{3,2,1,0:T(8,128)(2,1)S(1)}, bf16[2,4,256,128]{3,2,1,0:T(8,128)(2,1)S(1)}, u32[]{:S(2)}, u32[]{:S(2)}) collective-permute-start(bf16[2,4,256,128]{3,2,1,0:T(8,128)(2,1)S(1)} %pad_maximum_fusion.3), channel_id=1, source_target_pairs={{0,192},{1,65},{64,128},{65,1},{128,64},{129,193},{192,0},{193,129... | collective-permute-start | bytes 1572872 | tf_op jit(solution)/shard_map/ppermute | solution.py:258
  67.6 9.4 %collective-permute-start.15 = (bf16[1,512,512]{2,1,0:T(8,128)(2,1)S(1)}, bf16[1,512,512]{2,1,0:T(8,128)(2,1)}, u32[]{:S(2)}, u32[]{:S(2)}) collective-permute-start(bf16[1,512,512]{2,1,0:T(8,128)(2,1)S(1)} %slice.65), channel_id=1, source_target_pairs={{0,2},{1,7},{2,0},{3,5},{4,6},{5,3},{6,4},{7,1},{8,10},{9,15},{10,... | collective-permute-start | bytes 1572872 | tf_op jit(solution)/shard_map/ppermute | solution.py:258
  79.9 3.4 %collective-permute-start.17 = (bf16[1,512,512]{2,1,0:T(8,128)(2,1)}, bf16[1,512,512]{2,1,0:T(8,128)(2,1)}, u32[]{:S(2)}, u32[]{:S(2)}) collective-permute-start(bf16[1,512,512]{2,1,0:T(8,128)(2,1)} %collective-permute-done.15.refs_3_), channel_id=1, source_target_pairs={{0,1},{1,0},{2,3},{3,2},{4,5},{5,4},{6,7},{7,6},{8,9},{9,8},{10,11... | collective-permute-start | bytes 1572872 | tf_op jit(solution)/shard_map/ppermute | solution.py:251
  80.6 14.3 %collective-permute-start.20 = (bf16[528,128]{1,0:T(8,128)(2,1)}, bf16[528,128]{1,0:T(8,128)(2,1)}, u32[]{:S(2)}, u32[]{:S(2)}) collective-permute-start(bf16[528,128]{1,0:T(8,128)(2,1)} %get-tuple-element.72), channel_id=1, source_target_pairs={{0,4},{2,6},{4,0},{6,2},{1,5},{3,7},{5,1},{7,3},{8,12},{10,14},{12... | collective-permute-start | bytes 405512 | tf_op jit(solution)/shard_map/ppermute | solution.py:263
  80.6 14.3 %collective-permute-start.18 = (bf16[528,128]{1,0:T(8,128)(2,1)}, bf16[528,128]{1,0:T(8,128)(2,1)}, u32[]{:S(2)}, u32[]{:S(2)}) collective-permute-start(bf16[528,128]{1,0:T(8,128)(2,1)} %get-tuple-element.70), channel_id=1, source_target_pairs={{0,2},{1,7},{2,0},{3,5},{4,6},{5,3},{6,4},{7,1},{8,10},{9,15},{10,... | collective-permute-start | bytes 405512 | tf_op jit(solution)/shard_map/ppermute | solution.py:258
  82.7 12.2 %collective-permute-start.19 = (bf16[528,128]{1,0:T(8,128)(2,1)}, bf16[528,128]{1,0:T(8,128)(2,1)}, u32[]{:S(2)}, u32[]{:S(2)}) collective-permute-start(bf16[528,128]{1,0:T(8,128)(2,1)} %get-tuple-element.71), channel_id=1, source_target_pairs={{0,6},{1,3},{2,4},{3,1},{4,2},{5,7},{6,0},{7,5},{8,14},{9,11},{10,... | collective-permute-start | bytes 405512 | tf_op jit(solution)/shard_map/ppermute | solution.py:258
  96.1 8.9 %collective-permute-start.21 = (bf16[528,128]{1,0:T(8,128)(2,1)S(1)}, bf16[528,128]{1,0:T(8,128)(2,1)S(1)}, u32[]{:S(2)}, u32[]{:S(2)}) collective-permute-start(bf16[528,128]{1,0:T(8,128)(2,1)S(1)} %shard_map.90.refs_0_), channel_id=1, source_target_pairs={{0,16},{1,49},{16,0},{17,33},{32,48},{33,17},{48,32},{49,1},{2,18}... | collective-permute-start | bytes 405512 | tf_op jit(solution)/shard_map/ppermute | solution.py:258
  105.0 9.0 %collective-permute-start.22 = (bf16[528,128]{1,0:T(8,128)(2,1)S(1)}, bf16[528,128]{1,0:T(8,128)(2,1)S(1)}, u32[]{:S(2)}, u32[]{:S(2)}) collective-permute-start(bf16[528,128]{1,0:T(8,128)(2,1)S(1)} %shard_map.92.refs_0_), channel_id=1, source_target_pairs={{0,48},{1,17},{16,32},{17,1},{32,16},{33,49},{48,0},{49,33},{2,50}... | collective-permute-start | bytes 405512 | tf_op jit(solution)/shard_map/ppermute | solution.py:258
  114.0 5.5 %collective-permute-start.25 = (bf16[528,128]{1,0:T(8,128)(2,1)S(1)}, bf16[528,128]{1,0:T(8,128)(2,1)S(1)}, u32[]{:S(2)}, u32[]{:S(2)}) collective-permute-start(bf16[528,128]{1,0:T(8,128)(2,1)S(1)} %shard_map.94.refs_0_), channel_id=1, source_target_pairs={{0,128},{64,192},{128,0},{192,64},{1,129},{65,193},{129,1},{193,65... | collective-permute-start | bytes 405512 | tf_op jit(solution)/shard_map/ppermute | solution.py:263
  115.8 6.1 %collective-permute-start.24 = (bf16[528,128]{1,0:T(8,128)(2,1)S(1)}, bf16[528,128]{1,0:T(8,128)(2,1)S(1)}, u32[]{:S(2)}, u32[]{:S(2)}) collective-permute-start(bf16[528,128]{1,0:T(8,128)(2,1)S(1)} %shard_map.94.refs_0_), channel_id=1, source_target_pairs={{0,192},{1,65},{64,128},{65,1},{128,64},{129,193},{192,0},{193,129... | collective-permute-start | bytes 405512 | tf_op jit(solution)/shard_map/ppermute | solution.py:258
  117.4 7.8 %collective-permute-start.23 = (bf16[528,128]{1,0:T(8,128)(2,1)S(1)}, bf16[528,128]{1,0:T(8,128)(2,1)S(1)}, u32[]{:S(2)}, u32[]{:S(2)}) collective-permute-start(bf16[528,128]{1,0:T(8,128)(2,1)S(1)} %shard_map.94.refs_0_), channel_id=1, source_target_pairs={{0,64},{1,193},{64,0},{65,129},{128,192},{129,65},{192,128},{193,1... | collective-permute-start | bytes 405512 | tf_op jit(solution)/shard_map/ppermute | solution.py:258
  126.9 3.6 %collective-permute-start.28 = (f32[4,8,128]{2,1,0:T(8,128)S(1)}, f32[4,8,128]{2,1,0:T(8,128)S(1)}, u32[]{:S(2)}, u32[]{:S(2)}) collective-permute-start(f32[4,8,128]{2,1,0:T(8,128)S(1)} %get-tuple-element.85.refs_0_), channel_id=1, source_target_pairs={{0,9},{1,8},{8,1},{9,0},{2,11},{3,10},{10,3},{11,2},{4,13},{5,12},... | collective-permute-start | bytes 49160 | tf_op jit(solution)/shard_map/ppermute | solution.py:251
  (28 other events, 137.5 us)

commit v7 on v6

--- a/solution.py
+++ b/solution.py
@@ -14,6 +14,9 @@
 LIMIT = 16 * 2**20
 SMALL = 8 * 2**20
 QUICK = pl.CostEstimate(flops=1, bytes_accessed=1, transcendentals=0)
+VMEM = pl.BlockSpec(memory_space=pltpu.VMEM)
+SMEM = pl.BlockSpec(memory_space=pltpu.SMEM)
+HBM = pl.BlockSpec(memory_space=pltpu.HBM)
 
 
 def widen_kernel(values_ref, scales_ref, out_ref):
@@ -35,42 +38,47 @@
     )(values, scales.T)
 
 
-def norm_kernel(tab_ref, tok_ref, gain_ref, own_ref, oth_ref, inv_ref):
-    rows, width = tok_ref.shape
-    total = jnp.zeros((rows, TILE), jnp.float32)
-    for t in range(width // TILE):
-        wide = tok_ref[:, t * TILE : (t + 1) * TILE].astype(jnp.float32)
-        total = total + wide * wide
-    mean = jnp.sum(total, axis=1, keepdims=True) / width
-    inverse = lax.rsqrt(mean + 1e-05)
-    inv_ref[...] = inverse
-    for side, out_ref in enumerate((own_ref, oth_ref)):
-        for r in range(width // TILE // 2):
-            at = pl.multiple_of(tab_ref[side, r] * TILE, TILE)
-            wide = tok_ref[:, pl.ds(at, TILE)].astype(jnp.float32)
-            scaled = wide * inverse * gain_ref[:, pl.ds(at, TILE)]
-            out_ref[:, r * TILE : (r + 1) * TILE] = scaled.astype(jnp.bfloat16)
+def norm_kernel(tab_ref, tok_ref, gain_ref, own_ref, oth_ref, inv_ref, block, sem):
+    count, rows, width = block.shape
+
+    def block_in(k):
+        return pltpu.make_async_copy(tok_ref.at[pl.ds(k * rows, rows)], block.at[k], sem.at[k])
+
+    for k in range(count):
+        block_in(k).start()
+    for k in range(count):
+        block_in(k).wait()
+        part = slice(k * rows, (k + 1) * rows)
+        total = jnp.zeros((rows, TILE), jnp.float32)
+        for t in range(width // TILE):
+            wide = block[k, :, t * TILE : (t + 1) * TILE].astype(jnp.float32)
+            total = total + wide * wide
+        mean = jnp.sum(total, axis=1, keepdims=True) / width
+        inverse = lax.rsqrt(mean + 1e-05)
+        inv_ref[part, :] = inverse
+        for side, out_ref in enumerate((own_ref, oth_ref)):
+            for r in range(width // TILE // 2):
+                at = pl.multiple_of(tab_ref[side, r] * TILE, TILE)
+                wide = block[k, :, pl.ds(at, TILE)].astype(jnp.float32)
+                scaled = wide * inverse * gain_ref[:, pl.ds(at, TILE)]
+                out_ref[part, r * TILE : (r + 1) * TILE] = scaled.astype(jnp.bfloat16)
 
 
 def norm_tiles(tokens, gain, table):
     rows, width = tokens.shape
     step = 64 if rows % 64 == 0 else rows
-    half = pl.BlockSpec((step, width // 2), lambda i, tab: (i, 0))
     return pl.pallas_call(
         norm_kernel,
-        grid_spec=pltpu.PrefetchScalarGridSpec(
-            num_scalar_prefetch=1,
-            grid=(rows // step,),
-            in_specs=[
-                pl.BlockSpec((step, width), lambda i, tab: (i, 0)),
-                pl.BlockSpec((1, width), lambda i, tab: (0, 0)),
-            ],
-            out_specs=[half, half, pl.BlockSpec((step, 1), lambda i, tab: (i, 0))],
-        ),
+        in_specs=[SMEM, HBM, VMEM],
+        out_specs=[VMEM] * 3,
         out_shape=[
             jax.ShapeDtypeStruct((rows, width // 2), jnp.bfloat16),
             jax.ShapeDtypeStruct((rows, width // 2), jnp.bfloat16),
             jax.ShapeDtypeStruct((rows, 1), jnp.float32),
+        ],
+        scratch_shapes=[
+            pltpu.VMEM((rows // step, step, width), jnp.bfloat16),
+            pltpu.SemaphoreType.DMA((rows // step,)),
         ],
         compiler_params=pltpu.CompilerParams(vmem_limit_bytes=LIMIT),
         cost_estimate=QUICK,
@@ -112,39 +120,61 @@
     return outs[:2], outs[2:]
 
 
-def block_in(tab_ref, tok_ref, block, sem, k):
-    span = block.shape[2]
-    at = pl.multiple_of(tab_ref[k] * span, span)
-    return pltpu.make_async_copy(tok_ref.at[:, pl.ds(at, span)], block.at[k], sem.at[k])
-
-
-def shards_of(refs):
-    return [ref.at[k] for ref in refs for k in range(ref.shape[0])]
+class Inputs:
+    def __init__(self, tab_ref, tok_ref, w_refs, block, weight, sem, weight_sem):
+        shards_ = [ref.at[k] for ref in w_refs for k in range(ref.shape[0])]
+        self.count, _, self.span = block.shape
+        self.tab_ref, self.block, self.weight = tab_ref, block, weight
+        self.copies = []
+        for k in range(self.count):
+            self.copies.append(
+                (
+                    pltpu.make_async_copy(tok_ref.at[:, self.columns(k)], block.at[k], sem.at[k]),
+                    pltpu.make_async_copy(shards_[k], weight.at[k], weight_sem.at[k]),
+                )
+            )
+        for pair_ in self.copies:
+            for copy in pair_:
+                copy.start()
+
+    def columns(self, k):
+        return pl.ds(pl.multiple_of(self.tab_ref[k] * self.span, self.span), self.span)
+
+    def wait(self, k):
+        for copy in self.copies[k]:
+            copy.wait()
+
+    @staticmethod
+    def scratch(rows, span, columns, count):
+        return [
+            pltpu.VMEM((count, rows, span), jnp.bfloat16),
+            pltpu.VMEM((count, span, columns), jnp.bfloat16),
+            pltpu.SemaphoreType.DMA((count,)),
+            pltpu.SemaphoreType.DMA((count,)),
+        ]
+
+
+def forward_steps(inputs, inv_ref, gain_ref, acc):
+    inverse = inv_ref[...]
+    for k in range(inputs.count):
+        inputs.wait(k)
+        wide = inputs.block[k].astype(jnp.float32)
+        normed = (wide * inverse * gain_ref[:, inputs.columns(k)]).astype(jnp.bfloat16)
+        acc[...] += jnp.dot(normed, inputs.weight[k], preferred_element_type=jnp.float32)
 
 
 def forward_kernel(tab_ref, tok_ref, inv_ref, gain_ref, *refs):
-    w_refs, acc_in, (acc, block, sem) = refs[:4], refs[4:-3], refs[-3:]
-    forward_steps(tab_ref, tok_ref, inv_ref, gain_ref, shards_of(w_refs), acc_in, acc, block, sem)
-
-
-def forward_steps(tab_ref, tok_ref, inv_ref, gain_ref, weights, acc_in, acc, block, sem):
-    count, _, span = block.shape
-    for k in range(count):
-        block_in(tab_ref, tok_ref, block, sem, k).start()
-    inverse = inv_ref[...]
-    acc[...] = acc_in[0][...] if acc_in else jnp.zeros_like(acc)
-    for k in range(count):
-        block_in(tab_ref, tok_ref, block, sem, k).wait()
-        at = pl.multiple_of(tab_ref[k] * span, span)
-        wide = block[k].astype(jnp.float32)
-        normed = (wide * inverse * gain_ref[:, pl.ds(at, span)]).astype(jnp.bfloat16)
-        acc[...] += jnp.dot(normed, weights[k][...], preferred_element_type=jnp.float32)
-
-
-def forward_last_kernel(tab_ref, tok_ref, inv_ref, gain_ref, cot_ref, *refs):
-    w_refs, (acc_in, proj_ref, moment_ref, acc, block, sem) = refs[:-6], refs[-6:]
-    weights = shards_of(w_refs)
-    forward_steps(tab_ref, tok_ref, inv_ref, gain_ref, weights, (acc_in,), acc, block, sem)
+    w_refs, (acc, *scratch) = refs[:-5], refs[-5:]
+    inputs = Inputs(tab_ref, tok_ref, w_refs, *scratch)
+    acc[...] = jnp.zeros_like(acc)
+    forward_steps(inputs, inv_ref, gain_ref, acc)
+
+
+def forward_last_kernel(tab_ref, tok_ref, inv_ref, gain_ref, cot_ref, acc_in, *refs):
+    w_refs, (proj_ref, moment_ref, acc, *scratch) = refs[:-7], refs[-7:]
+    inputs = Inputs(tab_ref, tok_ref, w_refs, *scratch)
+    acc[...] = acc_in[...]
+    forward_steps(inputs, inv_ref, gain_ref, acc)
     keys = acc[...]
     inverse = inv_ref[...]
     proj_ref[...] = keys.astype(jnp.bfloat16)
@@ -153,33 +183,26 @@
 
 
 def backward_kernel(tab_ref, tok_ref, inv_ref, gain_ref, cot_ref, moment_ref, *refs, count):
-    weights, (grads_ref, block, out, sem, out_sem) = shards_of(refs[:count]), refs[-5:]
-    count, _, span = block.shape
+    w_refs, (grads_ref, out, out_sem, *scratch) = refs[:count], refs[-7:]
+    inputs = Inputs(tab_ref, tok_ref, w_refs, *scratch)
 
     def block_out(k):
-        at = pl.multiple_of(tab_ref[k] * span, span)
-        return pltpu.make_async_copy(out.at[k], grads_ref.at[:, pl.ds(at, span)], out_sem.at[k])
-
-    for k in range(count):
-        block_in(tab_ref, tok_ref, block, sem, k).start()
+        return pltpu.make_async_copy(
+            out.at[k], grads_ref.at[:, inputs.columns(k)], out_sem.at[k]
+        )
+
     inverse, moment, cot = inv_ref[...], moment_ref[...], cot_ref[...]
-    for k in range(count):
+    for k in range(inputs.count):
+        inputs.wait(k)
         partial = lax.dot_general(
-            cot, weights[k][...], (((1,), (1,)), ((), ())), preferred_element_type=jnp.float32
+            cot, inputs.weight[k], (((1,), (1,)), ((), ())), preferred_element_type=jnp.float32
         )
-        block_in(tab_ref, tok_ref, block, sem, k).wait()
-        at = pl.multiple_of(tab_ref[k] * span, span)
-        wide = block[k].astype(jnp.float32)
-        grads = inverse * gain_ref[:, pl.ds(at, span)] * partial - wide * moment
+        wide = inputs.block[k].astype(jnp.float32)
+        grads = inverse * gain_ref[:, inputs.columns(k)] * partial - wide * moment
         out[k] = grads.astype(jnp.bfloat16)
         block_out(k).start()
-    for k in range(count):
+    for k in range(inputs.count):
         block_out(k).wait()
-
-
-VMEM = pl.BlockSpec(memory_space=pltpu.VMEM)
-SMEM = pl.BlockSpec(memory_space=pltpu.SMEM)
-ANY = pl.BlockSpec(memory_space=pl.ANY)
 
 
 def costs(tokens, columns):
@@ -198,13 +221,10 @@
     rows, span, columns = tokens.shape[0], *weights[0].shape[1:]
     return pl.pallas_call(
         forward_kernel,
-        in_specs=[SMEM, ANY] + [VMEM] * 6,
+        in_specs=[SMEM, HBM] + [VMEM] * 2 + [HBM] * len(weights),
         out_specs=VMEM,
         out_shape=jax.ShapeDtypeStruct((rows, columns), jnp.float32),
-        scratch_shapes=[
-            pltpu.VMEM((8, rows, span), jnp.bfloat16),
-            pltpu.SemaphoreType.DMA((8,)),
-        ],
+        scratch_shapes=Inputs.scratch(rows, span, columns, table.shape[0]),
         **costs(tokens, columns),
     )(table, tokens, inverse, gain, *weights)
 
@@ -213,34 +233,31 @@
     rows, span, columns = tokens.shape[0], *weights[0].shape[1:]
     return pl.pallas_call(
         forward_last_kernel,
-        in_specs=[SMEM, ANY] + [VMEM] * (4 + len(weights)),
+        in_specs=[SMEM, HBM] + [VMEM] * 4 + [HBM] * len(weights),
         out_specs=[VMEM] * 2,
         out_shape=[
             jax.ShapeDtypeStruct((rows, columns), jnp.bfloat16),
             jax.ShapeDtypeStruct((rows, 1), jnp.float32),
         ],
-        scratch_shapes=[
-            pltpu.VMEM((rows, columns), jnp.float32),
-            pltpu.VMEM((8, rows, span), jnp.bfloat16),
-            pltpu.SemaphoreType.DMA((8,)),
-        ],
+        scratch_shapes=[pltpu.VMEM((rows, columns), jnp.float32)]
+        + Inputs.scratch(rows, span, columns, table.shape[0]),
         **costs(tokens, columns),
-    )(table, tokens, inverse, gain, cotangent, *weights, sums)
+    )(table, tokens, inverse, gain, cotangent, sums, *weights)
 
 
 def backward(tokens, inverse, gain, cotangent, moment, weights, table, before=()):
     rows, span, columns = tokens.shape[0], *weights[0].shape[1:]
+    count = table.shape[0]
     return pl.pallas_call(
         functools.partial(backward_kernel, count=len(weights)),
-        in_specs=[SMEM, ANY] + [VMEM] * (4 + len(weights)) + [ANY] * len(before),
-        out_specs=ANY,
+        in_specs=[SMEM, HBM] + [VMEM] * 4 + [HBM] * (len(weights) + len(before)),
+        out_specs=HBM,
         out_shape=jax.ShapeDtypeStruct(tokens.shape, jnp.bfloat16),
         scratch_shapes=[
-            pltpu.VMEM((8, rows, span), jnp.bfloat16),
-            pltpu.VMEM((8, rows, span), jnp.bfloat16),
-            pltpu.SemaphoreType.DMA((8,)),
-            pltpu.SemaphoreType.DMA((8,)),
-        ],
+            pltpu.VMEM((count, rows, span), jnp.bfloat16),
+            pltpu.SemaphoreType.DMA((count,)),
+        ]
+        + Inputs.scratch(rows, span, columns, count),
         input_output_aliases={6 + len(weights): 0} if before else {},
         **costs(tokens, columns),
     )(table, tokens, inverse, gain, cotangent, moment, *weights, *before)
@@ -285,10 +302,11 @@
     return lax.optimization_barrier((first, *others))[0]
 
 
-PIECES = (
-    ((0, 0, 0), (0, 0, 1), (1, 0, 0), (1, 0, 1), (0, 1, 0), (0, 1, 1), (0, 2, 1), (0, 2, 0))
-    + ((1, 1, 0), (1, 1, 1), (1, 2, 1), (1, 2, 0), (0, 3, 0), (1, 3, 0), (0, 3, 1), (1, 3, 1))
-)
+BASE, ABOVE = (((z, 0, 0), (z, 0, 1)) for z in (0, 1))
+NEAR, ABOVE_NEAR = (((z, 1, 0), (z, 1, 1)) for z in (0, 1))
+NEAR_C, ABOVE_NEAR_C = (((z, 2, 1), (z, 2, 0)) for z in (0, 1))
+FAR, ABOVE_FAR = (((z, 3, 0),) for z in (0, 1))
+FAR_C, ABOVE_FAR_C = (((z, 3, 1),) for z in (0, 1))
 
 
 def write_ends(out_ref, rows):
@@ -302,16 +320,22 @@
 
 
 def spread_kernel(tab_ref, total_ref, gain_ref, base_ref, near_ref, near_c_ref, far_ref, *refs, devices):
-    out_refs, rows_ref = refs[:4], refs[4]
+    out_refs, (rows_ref, weight, sem) = refs[:4], refs[4:]
     columns = base_ref.shape[2]
-    shards_ = (base_ref.at[0], near_c_ref.at[1], near_ref.at[0], far_ref.at[0])
     rows = pl.ds(pl.multiple_of(tab_ref[4] * TILE, TILE), TILE)
+    copies = [
+        pltpu.make_async_copy(shard.at[rows], weight.at[k], sem.at[k])
+        for k, shard in enumerate((base_ref.at[0], near_c_ref.at[1], near_ref.at[0], far_ref.at[0]))
+    ]
+    for copy in copies:
+        copy.start()
     rows_ref[...] = jnp.zeros_like(rows_ref)
-    for k, shard in enumerate(shards_):
+    for k in range(4):
+        out_refs[k][:columns, :] = total_ref[k].reshape(columns, TILE).astype(jnp.bfloat16)
+    for k in range(4):
+        copies[k].wait()
         total = total_ref[k].reshape(columns, TILE)
-        out_refs[k][:columns, :] = total.astype(jnp.bfloat16)
-        weight = shard[rows, :].astype(jnp.float32).T
-        part = jnp.sum(weight * total, axis=0, keepdims=True)
+        part = jnp.sum(weight[k].astype(jnp.float32).T * total, axis=0, keepdims=True)
         gain = gain_ref[:, pl.ds(pl.multiple_of(tab_ref[k] * TILE, TILE), TILE)]
         rows_ref[pl.ds(tab_ref[5 + k], 1), :] = part / (gain * devices)
     for out_ref in out_refs:
@@ -322,10 +346,14 @@
     columns = base.shape[2]
     return pl.pallas_call(
         functools.partial(spread_kernel, devices=devices),
-        in_specs=[SMEM] + [VMEM] * 6,
+        in_specs=[SMEM] + [VMEM] * 2 + [HBM] * 4,
         out_specs=[VMEM] * 4,
         out_shape=[jax.ShapeDtypeStruct((columns + 2 * EXTRA, TILE), jnp.bfloat16)] * 4,
-        scratch_shapes=[pltpu.VMEM((EXTRA, TILE), jnp.float32)],
+        scratch_shapes=[
+            pltpu.VMEM((EXTRA, TILE), jnp.float32),
+            pltpu.VMEM((4, TILE, columns), jnp.bfloat16),
+            pltpu.SemaphoreType.DMA((4,)),
+        ],
         compiler_params=pltpu.CompilerParams(vmem_limit_bytes=LIMIT),
     )(table, total, gain, base, near, near_c, far)
 
@@ -414,9 +442,10 @@
     for core in (c, 1 - c):
         chip = (zl ^ bits[0]) * 4 + (x ^ offset(core, bits[3], bits[4]))
         tables.append((chip * 2 + core) * 4 + (y ^ offset(core, bits[1], bits[2])))
-    shards_at = jnp.stack(
-        [((zl ^ z) * 4 + (x ^ offset(c, k % 2, k // 2))) * 2 + (c ^ lane) for z, k, lane in PIECES]
-    ).astype(jnp.int32)
+
+    def nodes_of(pieces):
+        at = [((zl ^ z) * 4 + (x ^ offset(c, k % 2, k // 2))) * 2 + (c ^ lane) for z, k, lane in pieces]
+        return jnp.stack(at).astype(jnp.int32)
 
     own = widen_weight(weight_values, weight_scale)
     own_c = swap(own, "c")
@@ -429,19 +458,17 @@
     near = pair(base, "x", 0)
     sent, kept = grad_tiles(mine, got, cot_own, cot_got)
 
-    first = sent[0]
-    second, near, up = lax.optimization_barrier((sent[1], near, up))
-    moved = [pair(first, "y", 0), pair_z(second)]
+    moved = [pair(sent[0], "y", 0), pair_z(sent[1])]
+    (first, kept_first), (second, kept_second) = (halve(add(k, m)) for k, m in zip(kept, moved))
+
+    first, near, up = lax.optimization_barrier((first, near, up))
+    moved = [pair_z(first), pair(second, "y", 0)]
     near_c = swap(near, "c")
     above = jnp.stack([up, swap(up, "c")])
     above_near = pair(above, "x", 0)
     far = pair(near_c[1:], "x", 0)
-    (first, kept_first), (second, kept_second) = (halve(add(k, m)) for k, m in zip(kept, moved))
-
-    second, near_c, above = lax.optimization_barrier((second, near_c, above))
-    moved = [pair_z(first), pair(second, "y", 0)]
-    early, late_at = [base, above, near, near_c], shards_at[8:]
-    sums = forward(tokens, inverse, gain, early, shards_at[:8])
+    early = [base, above, near, near_c]
+    sums = forward(tokens, inverse, gain, early, nodes_of(BASE + ABOVE + NEAR + NEAR_C))
     moved[1], sums, above_near, far = lax.optimization_barrier((moved[1], sums, above_near, far))
     above_near_c = swap(above_near, "c")
     above_far = pair(above_near_c[1:], "x", 0)
@@ -460,26 +487,39 @@
     parts = list(spread(total, gain, base, near, near_c, far, at, devices))
     parts[0], above_far = lax.optimization_barrier((parts[0], above_far))
     moved = [parts[0], pair(parts[2], "x", 0), pair(parts[1], "x", 1), across(parts[3], "x")]
-    late = [above_near, above_near_c, far, above_far, far_c, swap(above_far, "c")]
+    above_far_c = swap(above_far, "c")
+    late = [above_near, above_near_c, far, above_far, far_c, above_far_c]
+    late_at = nodes_of(ABOVE_NEAR + ABOVE_NEAR_C + FAR + ABOVE_FAR + FAR_C + ABOVE_FAR_C)
     projected, moment = forward_last(tokens, inverse, gain, key_cotangent, late, sums, late_at)
     moved[3], moment = lax.optimization_barrier((moved[3], moment))
     send = merge(moved)
 
+    def part_of_grads(before, weights, pieces):
+        return backward(
+            tokens, inverse, gain, key_cotangent, moment, weights, nodes_of(pieces), before
+        )
+
     send, moment = lax.optimization_barrier((send, moment))
     moved = pair(send, "zh", 0)
-    token_grads = backward(tokens, inverse, gain, key_cotangent, moment, early, shards_at[:8])
+    token_grads = part_of_grads((), [base, above, near], BASE + ABOVE + NEAR)
     moved, token_grads = lax.optimization_barrier((moved, token_grads))
     send = merge((send, moved))
     send, token_grads = lax.optimization_barrier((send, token_grads))
     moved = pair(send, "zh", 1)
-    token_grads = backward(
-        tokens, inverse, gain, key_cotangent, moment, late, late_at, before=(token_grads,)
+    token_grads = part_of_grads(
+        (token_grads,), [near_c, above_near, far], NEAR_C + ABOVE_NEAR + FAR
     )
     moved, token_grads = lax.optimization_barrier((moved, token_grads))
     send = merge((send, moved), 1.0 / devices)
 
     parts = (send, pair(send, "y", 0), pair(send, "y", 1), across(send, "y"))
     quarters = jnp.stack([y ^ offset(c, k % 2, k // 2) for k in range(4)]).astype(jnp.int32)
+    token_grads = part_of_grads(
+        (tie(token_grads, send),),
+        [above_near_c, above_far, far_c, above_far_c],
+        ABOVE_NEAR_C + ABOVE_FAR + FAR_C + ABOVE_FAR_C,
+    )
+    parts, token_grads = lax.optimization_barrier((parts, token_grads))
     weight_grads, gains = finish(parts, quarters)
     gains = (gains, swap(gains, "c"), swap(gains, "zl"), swap(gains, ("zl", "c")))
     nodes = jnp.stack([(zl ^ k // 2) * 8 + (c ^ k % 2) for k in range(4)]).astype(jnp.int32)

time: 132 us -> 145 us (1.098)
  local copies, waits for them, and re-layouts: 19.9 us -> 32.6 us
    unnamed x47 -> x69, local copies, waits for them, and re-layouts: 16.8 us -> 29.2 us
    ppermute x3, starting transfers between devices: 12.1 us -> 8.28 us  [pair_z(): return lax.ppermute(array, ('zh', 'zl', 'c'), moves)]
    ppermute x11, waiting for transfers between devices: 5.3 us -> 8.67 us  [swap(): return lax.ppermute(array, axis, [(a, last - a) for a in range(last + 1)])]
    ppermute x13, waiting for transfers between devices: 16.8 us -> 13.8 us  [pair(): return lax.ppermute(array, (axis, 'c'), moves)]
    ppermute x11, starting transfers between devices: 6.76 us -> 9.71 us  [swap(): return lax.ppermute(array, axis, [(a, last - a) for a in range(last + 1)])]
    pallas_call x3, Pallas kernels: 1.21 us -> 3.73 us  [merge(): pl.pallas_call(functools.partial(merge_kernel, scale=scale), in_specs=[VM...]
    ppermute x2, waiting for transfers between devices: 2.04 us -> 0.01 us  [across(): return lax.ppermute(array, axis, [(a, a ^ 2) for a in range(size)])]
    pallas_call x2 -> x3, Pallas kernels: 13.4 us -> 11.6 us  [backward(): pl.pallas_call(functools.partial(backward_kernel, count=len(weights)), in...]
  transfers between devices with their start and end apart: 29 -> 29, of which waited for: 13 -> 10; matrix products, arithmetic and copies ran while one was open for 7% -> 6% of each run, Pallas kernels for 20% -> 14%
where the time goes in v7:
time: 145 us; the launch traced here: 144 us
  starting transfers between devices  40.2 us (28%)
  Pallas kernels  37.6 us (26%)
  local copies, waits for them, and re-layouts  32.6 us (22%)
  waiting for transfers between devices  28 us (19%)
  other arithmetic  4.43 us (3%)
    unnamed x69, local copies, waits for them, and re-layouts  29.2 us
    ppermute x13, starting transfers between devices, pair(): return lax.ppermute(array, (axis, 'c'), moves)  18.7 us
    ppermute x13, waiting for transfers between devices, pair(): return lax.ppermute(array, (axis, 'c'), moves)  13.8 us
    pallas_call x3, Pallas kernels, backward(): pl.pallas_call(functools.partial(backward_kernel, count=len(weights)), in...  11.6 us
    ppermute x11, starting transfers between devices, swap(): return lax.ppermute(array, axis, [(a, last - a) for a in range(last + 1)])  9.71 us
    ppermute x11, waiting for transfers between devices, swap(): return lax.ppermute(array, axis, [(a, last - a) for a in range(last + 1)])  8.67 us
    ppermute x3, starting transfers between devices, pair_z(): return lax.ppermute(array, ('zh', 'zl', 'c'), moves)  8.28 us
    ppermute x3, waiting for transfers between devices, pair_z(): return lax.ppermute(array, ('zh', 'zl', 'c'), moves)  5.55 us
  transfers between devices with their start and end apart: 29, of which 10 were waited for; matrix products, arithmetic and copies ran while one was open for 6% of the time, Pallas kernels for 14%

profile of v7, /device:TPU:1, one launch (start us, length us, event | category | flops | bytes accessed | tf_op | source)
XLA Modules:
  0.0 143.9 jit_solution(6665056642440566145)
XLA Ops:
  2.8 3.3 %collective-permute-start = (bf16[512,512]{1,0:T(8,128)(2,1)S(1)}, bf16[512,512]{1,0:T(8,128)(2,1)S(1)}, u32[]{:S(2)}, u32[]{:S(2)}) collective-permute-start(bf16[512,512]{1,0:T(8,128)(2,1)S(1)} %shard_map.84), channel_id=1, source_target_pairs={{0,1},{1,0},{2,3},{3,2},{4,5},{5,4},{6,7},{7,6},{8,9},{9,8},{10,11... | collective-permute-start | bytes 1572872 | tf_op jit(solution)/shard_map/ppermute | solution.py:268
  7.7 2.5 %copy-done = bf16[320,8192]{1,0:T(8,128)(2,1)S(1)} copy-done((bf16[320,8192]{1,0:T(8,128)(2,1)S(1)}, bf16[320,8192]{1,0:T(8,128)(2,1)}, u32[]{:S(2)}) %copy-start) | copy-done | bytes 5242904
  10.2 3.7 %shard_map.85 = (bf16[320,4096]{1,0:T(8,128)(2,1)S(1)}, bf16[320,4096]{1,0:T(8,128)(2,1)S(1)}, f32[320,1]{1,0:T(8,128)S(1)}) custom-call(s32[2,32]{1,0:T(2,128)S(1)} %pad_add_fusion.tab_ref, bf16[320,8192]{1,0:T(8,128)(2,1)S(1)} %copy-done, f32[1,8192]{1,0:T(1,128)S(1)} %bitcast.49), custom_call_target="tpu_custom_call" | custom-call | flops 1 | bytes 1 | tf_op jit(solution)/shard_map/pallas_call | solution.py:70
  14.5 5.0 %collective-permute-done.2.cot_got_ref = bf16[512,320]{1,0:T(8,128)(2,1)S(1)} collective-permute-done((bf16[512,320]{1,0:T(8,128)(2,1)S(1)}, bf16[512,320]{1,0:T(8,128)(2,1)S(1)}, u32[]{:S(2)}, u32[]{:S(2)}) %collective-permute-start.2) | collective-permute-done | bytes 327712 | tf_op jit(solution)/shard_map/ppermute | solution.py:268
  19.5 4.5 %shard_map.86 = (bf16[16,256,128]{2,1,0:T(8,128)(2,1)S(1)}, bf16[16,256,128]{2,1,0:T(8,128)(2,1)S(1)}, f32[16,256,128]{2,1,0:T(8,128)S(1)}, f32[16,256,128]{2,1,0:T(8,128)S(1)}) custom-call(bf16[320,4096]{1,0:T(8,128)(2,1)S(1)} %get-tuple-element.50.own_ref, bf16[320,4096]{1,0:T(8,128)(2,1)S(1)} %collective-permute-done.1.got_ref, ...), custom_call_target="tpu_custom_call" | custom-call | flops 1 | bytes 1 | tf_op jit(solution)/shard_map/pallas_call | solution.py:113
  25.1 2.5 %collective-permute-start.6 = (bf16[2,512,512]{2,1,0:T(8,128)(2,1)S(1)}, bf16[2,512,512]{2,1,0:T(8,128)(2,1)S(1)}, u32[]{:S(2)}, u32[]{:S(2)}) collective-permute-start(bf16[2,512,512]{2,1,0:T(8,128)(2,1)S(1)} %pad_maximum_fusion.refs_0_.base_ref), channel_id=1, source_target_pairs={{0,2},{1,7},{2,0},{3,5},{4,6},{5,3},{6,4},{7,1},{8,10},{9,15},{10,... | collective-permute-start | bytes 3145736 | tf_op jit(solution)/shard_map/ppermute | solution.py:275
  27.6 5.6 %collective-permute-start.7 = (bf16[512,512]{1,0:T(8,128)(2,1)S(1)}, bf16[512,512]{1,0:T(8,128)(2,1)S(1)}, u32[]{:S(2)}, u32[]{:S(2)}) collective-permute-start(bf16[512,512]{1,0:T(8,128)(2,1)S(1)} %shard_map.84), channel_id=1, source_target_pairs={{0,8},{1,57},{8,0},{9,17},{16,24},{17,9},{24,16},{25,33},{32,40},{... | collective-permute-start | bytes 1572872 | tf_op jit(solution)/shard_map/ppermute | solution.py:289
  33.2 5.8 %collective-permute-done.5 = bf16[16,256,128]{2,1,0:T(8,128)(2,1)S(1)} collective-permute-done((bf16[16,256,128]{2,1,0:T(8,128)(2,1)S(1)}, bf16[16,256,128]{2,1,0:T(8,128)(2,1)S(1)}, u32[]{:S(2)}, u32[]{:S(2)}) %collective-permute-start.5) | collective-permute-done | bytes 1048608 | tf_op jit(solution)/shard_map/ppermute | solution.py:275
  45.4 5.5 %collective-permute-done.3 = bf16[16,256,128]{2,1,0:T(8,128)(2,1)S(1)} collective-permute-done((bf16[16,256,128]{2,1,0:T(8,128)(2,1)S(1)}, bf16[16,256,128]{2,1,0:T(8,128)(2,1)S(1)}, u32[]{:S(2)}, u32[]{:S(2)}) %collective-permute-start.3) | collective-permute-done | bytes 1048608 | tf_op jit(solution)/shard_map/ppermute | solution.py:289
  53.7 2.7 %collective-permute-start.13 = (bf16[8,256,128]{2,1,0:T(8,128)(2,1)}, bf16[8,256,128]{2,1,0:T(8,128)(2,1)}, u32[]{:S(2)}, u32[]{:S(2)}) collective-permute-start(bf16[8,256,128]{2,1,0:T(8,128)(2,1)} %slice.80), channel_id=1, source_target_pairs={{0,8},{1,57},{8,0},{9,17},{16,24},{17,9},{24,16},{25,33},{32,40},{... | collective-permute-start | bytes 1572872 | tf_op jit(solution)/shard_map/ppermute | solution.py:289
  56.5 2.5 %copy-done.1 = bf16[320,8192]{1,0:T(8,128)(2,1)S(1)} copy-done((bf16[320,8192]{1,0:T(8,128)(2,1)S(1)}, bf16[320,8192]{1,0:T(8,128)(2,1)}, u32[]{:S(2)}) %copy-start.1) | copy-done | bytes 5242904
  58.9 3.4 %shard_map.87.acc_in = f32[320,512]{1,0:T(8,128)S(1)} custom-call(s32[8]{0:T(128)S(1)} %stack.169.tab_ref, bf16[320,8192]{1,0:T(8,128)(2,1)S(1)} %copy-done.1, f32[320,1]{1,0:T(8,128)S(1)} %get-tuple-element.49.inv_ref, f32[1,8192]{1,0:T(1,128)S(1)} %bitcast.50, bf16[2,512,512]{2,1,0:T(8,128)(2,1)S(1)} %pad_maximum_fusion.refs_0_.base_ref, ...), custom_call_target="tpu_custom_call" | custom-call | flops 1342177280 | bytes 9437184 | tf_op jit(solution)/shard_map/pallas_call | solution.py:222
  71.1 4.2 %collective-permute-done.14 = bf16[2,4,256,128]{3,2,1,0:T(8,128)(2,1)S(1)} collective-permute-done((bf16[2,4,256,128]{3,2,1,0:T(8,128)(2,1)S(1)}, bf16[2,4,256,128]{3,2,1,0:T(8,128)(2,1)S(1)}, u32[]{:S(2)}, u32[]{:S(2)}) %collective-permute-start.14) | collective-permute-done | bytes 524320 | tf_op jit(solution)/shard_map/ppermute | solution.py:275
  78.5 2.9 %shard_map.88 = (bf16[528,128]{1,0:T(8,128)(2,1)S(1)}, bf16[528,128]{1,0:T(8,128)(2,1)}, bf16[528,128]{1,0:T(8,128)(2,1)}, bf16[528,128]{1,0:T(8,128)(2,1)}) custom-call(s32[9]{0:T(128)S(1)} %pad_add_fusion.1.tab_ref, f32[4,2,256,128]{3,2,1,0:T(8,128)S(1)} %pad_maximum_fusion.2.total_ref, f32[1,8192]{1,0:T(1,128)S(1)} %bitcast.51, ...), custom_call_target="tpu_custom_call" | custom-call | tf_op jit(solution)/shard_map/pallas_call | solution.py:347
  85.1 2.5 %copy-done.2 = bf16[320,8192]{1,0:T(8,128)(2,1)S(1)} copy-done((bf16[320,8192]{1,0:T(8,128)(2,1)S(1)}, bf16[320,8192]{1,0:T(8,128)(2,1)}, u32[]{:S(2)}) %copy-start.2) | copy-done | bytes 5242904
  91.8 4.5 %shard_map.89 = (bf16[320,512]{1,0:T(8,128)(2,1)}, f32[320,1]{1,0:T(8,128)S(1)}) custom-call(s32[8]{0:T(128)S(1)} %stack.156.tab_ref, bf16[320,8192]{1,0:T(8,128)(2,1)S(1)} %copy-done.2, f32[320,1]{1,0:T(8,128)S(1)} %copy-done.11, f32[1,8192]{1,0:T(1,128)S(1)} %bitcast.52, bf16[320,512]{1,0:T(8,128)(2,1)S(1)} %copy-done.6, f32[320,512]{1,0:T(8,128)S(1)} %copy-done.15, ...), custom_call_target="tpu_custom_call" | custom-call | flops 1342177280 | bytes 9437184 | tf_op jit(solution)/shard_map/pallas_call | solution.py:234
  98.8 6.0 %collective-permute-start.21 = (bf16[528,128]{1,0:T(8,128)(2,1)}, bf16[528,128]{1,0:T(8,128)(2,1)}, u32[]{:S(2)}, u32[]{:S(2)}) collective-permute-start(bf16[528,128]{1,0:T(8,128)(2,1)} %shard_map.90.refs_0_), channel_id=1, source_target_pairs={{0,16},{1,49},{16,0},{17,33},{32,48},{33,17},{48,32},{49,1},{2,18}... | collective-permute-start | bytes 405512 | tf_op jit(solution)/shard_map/ppermute | solution.py:275
  104.9 2.5 %copy-done.3 = bf16[320,8192]{1,0:T(8,128)(2,1)S(1)} copy-done((bf16[320,8192]{1,0:T(8,128)(2,1)S(1)}, bf16[320,8192]{1,0:T(8,128)(2,1)}, u32[]{:S(2)}) %copy-start.3) | copy-done | bytes 5242904
  109.2 4.1 %shard_map.91.refs_3_ = bf16[320,8192]{1,0:T(8,128)(2,1)} custom-call(s32[6]{0:T(128)S(1)} %stack.179.tab_ref, bf16[320,8192]{1,0:T(8,128)(2,1)S(1)} %copy-done.3, f32[320,1]{1,0:T(8,128)S(1)} %copy-done.12, f32[1,8192]{1,0:T(1,128)S(1)} %bitcast.53, bf16[320,512]{1,0:T(8,128)(2,1)S(1)} %copy-done.6, f32[320,1]{1,0:T(8,128)S(1)} %copy-done.21, ...), custom_call_target="tpu_custom_call" | custom-call | flops 1342177280 | bytes 9437184 | tf_op jit(solution)/shard_map/pallas_call | solution.py:251
  115.7 2.5 %copy-done.4 = bf16[320,8192]{1,0:T(8,128)(2,1)S(1)} copy-done((bf16[320,8192]{1,0:T(8,128)(2,1)S(1)}, bf16[320,8192]{1,0:T(8,128)(2,1)}, u32[]{:S(2)}) %copy-start.4) | copy-done | bytes 5242904
  120.0 3.7 %shard_map.93.refs_4_ = bf16[320,8192]{1,0:T(8,128)(2,1)} custom-call(s32[5]{0:T(128)S(1)} %stack.180.tab_ref, bf16[320,8192]{1,0:T(8,128)(2,1)S(1)} %copy-done.4, f32[320,1]{1,0:T(8,128)S(1)} %copy-done.13, f32[1,8192]{1,0:T(1,128)S(1)} %bitcast.54, bf16[320,512]{1,0:T(8,128)(2,1)S(1)} %copy-done.6, ...), custom_call_target="tpu_custom_call", output_to_operand_aliasing={{}: (9, {})} | custom-call | flops 1342177280 | bytes 9437184 | tf_op jit(solution)/shard_map/pallas_call | solution.py:251
  129.2 2.5 %copy-done.5 = bf16[320,8192]{1,0:T(8,128)(2,1)S(1)} copy-done((bf16[320,8192]{1,0:T(8,128)(2,1)S(1)}, bf16[320,8192]{1,0:T(8,128)(2,1)}, u32[]{:S(2)}) %copy-start.5) | copy-done | bytes 5242904
  131.7 3.7 %shard_map.95 = bf16[320,8192]{1,0:T(8,128)(2,1)} custom-call(s32[5]{0:T(128)S(1)} %stack.181.tab_ref, bf16[320,8192]{1,0:T(8,128)(2,1)S(1)} %copy-done.5, f32[320,1]{1,0:T(8,128)S(1)} %copy-done.13, f32[1,8192]{1,0:T(1,128)S(1)} %bitcast.55, bf16[320,512]{1,0:T(8,128)(2,1)S(1)} %copy-done.6, ...), custom_call_target="tpu_custom_call", output_to_operand_aliasing={{}: (10, {})} | custom-call | flops 1342177280 | bytes 9437184 | tf_op jit(solution)/shard_map/pallas_call | solution.py:251
  137.1 2.7 %collective-permute-start.28 = (f32[4,8,128]{2,1,0:T(8,128)S(1)}, f32[4,8,128]{2,1,0:T(8,128)S(1)}, u32[]{:S(2)}, u32[]{:S(2)}) collective-permute-start(f32[4,8,128]{2,1,0:T(8,128)S(1)} %get-tuple-element.91.refs_0_), channel_id=1, source_target_pairs={{0,9},{1,8},{8,1},{9,0},{2,11},{3,10},{10,3},{11,2},{4,13},{5,12},... | collective-permute-start | bytes 49160 | tf_op jit(solution)/shard_map/ppermute | solution.py:268
  (143 shorter events, 54.1 us)
Async XLA Ops:
  2.8 4.9 %collective-permute-start = (bf16[512,512]{1,0:T(8,128)(2,1)S(1)}, bf16[512,512]{1,0:T(8,128)(2,1)S(1)}, u32[]{:S(2)}, u32[]{:S(2)}) collective-permute-start(bf16[512,512]{1,0:T(8,128)(2,1)S(1)} %shard_map.84), channel_id=1, source_target_pairs={{0,1},{1,0},{2,3},{3,2},{4,5},{5,4},{6,7},{7,6},{8,9},{9,8},{10,11... | collective-permute-start | bytes 1572872 | tf_op jit(solution)/shard_map/ppermute | solution.py:268
  13.9 5.6 %collective-permute-start.1 = (bf16[320,4096]{1,0:T(8,128)(2,1)S(1)}, bf16[320,4096]{1,0:T(8,128)(2,1)S(1)}, u32[]{:S(2)}, u32[]{:S(2)}) collective-permute-start(bf16[320,4096]{1,0:T(8,128)(2,1)S(1)} %get-tuple-element.51), channel_id=1, source_target_pairs={{0,1},{1,0},{2,3},{3,2},{4,5},{5,4},{6,7},{7,6},{8,9},{9,8},{10,11... | collective-permute-start | bytes 7864328 | tf_op jit(solution)/shard_map/ppermute | solution.py:268
  14.4 5.1 %collective-permute-start.2 = (bf16[512,320]{1,0:T(8,128)(2,1)S(1)}, bf16[512,320]{1,0:T(8,128)(2,1)S(1)}, u32[]{:S(2)}, u32[]{:S(2)}) collective-permute-start(bf16[512,320]{1,0:T(8,128)(2,1)S(1)} %bitcast.56), channel_id=1, source_target_pairs={{0,1},{1,0},{2,3},{3,2},{4,5},{5,4},{6,7},{7,6},{8,9},{9,8},{10,11... | collective-permute-start | bytes 983048 | tf_op jit(solution)/shard_map/ppermute | solution.py:268
  24.0 14.9 %collective-permute-start.5 = (bf16[16,256,128]{2,1,0:T(8,128)(2,1)S(1)}, bf16[16,256,128]{2,1,0:T(8,128)(2,1)S(1)}, u32[]{:S(2)}, u32[]{:S(2)}) collective-permute-start(bf16[16,256,128]{2,1,0:T(8,128)(2,1)S(1)} %get-tuple-element.55), channel_id=1, source_target_pairs={{0,64},{1,193},{64,0},{65,129},{128,192},{129,65},{192,128},{193,1... | collective-permute-start | bytes 3145736 | tf_op jit(solution)/shard_map/ppermute | solution.py:275
  25.1 15.2 %collective-permute-start.6 = (bf16[2,512,512]{2,1,0:T(8,128)(2,1)S(1)}, bf16[2,512,512]{2,1,0:T(8,128)(2,1)S(1)}, u32[]{:S(2)}, u32[]{:S(2)}) collective-permute-start(bf16[2,512,512]{2,1,0:T(8,128)(2,1)S(1)} %pad_maximum_fusion.refs_0_.base_ref), channel_id=1, source_target_pairs={{0,2},{1,7},{2,0},{3,5},{4,6},{5,3},{6,4},{7,1},{8,10},{9,15},{10,... | collective-permute-start | bytes 3145736 | tf_op jit(solution)/shard_map/ppermute | solution.py:275
  27.6 12.7 %collective-permute-start.7 = (bf16[512,512]{1,0:T(8,128)(2,1)S(1)}, bf16[512,512]{1,0:T(8,128)(2,1)S(1)}, u32[]{:S(2)}, u32[]{:S(2)}) collective-permute-start(bf16[512,512]{1,0:T(8,128)(2,1)S(1)} %shard_map.84), channel_id=1, source_target_pairs={{0,8},{1,57},{8,0},{9,17},{16,24},{17,9},{24,16},{25,33},{32,40},{... | collective-permute-start | bytes 1572872 | tf_op jit(solution)/shard_map/ppermute | solution.py:289
  33.1 17.8 %collective-permute-start.3 = (bf16[16,256,128]{2,1,0:T(8,128)(2,1)S(1)}, bf16[16,256,128]{2,1,0:T(8,128)(2,1)S(1)}, u32[]{:S(2)}, u32[]{:S(2)}) collective-permute-start(bf16[16,256,128]{2,1,0:T(8,128)(2,1)S(1)} %get-tuple-element.53), channel_id=1, source_target_pairs={{0,8},{1,57},{8,0},{9,17},{16,24},{17,9},{24,16},{25,33},{32,40},{... | collective-permute-start | bytes 3145736 | tf_op jit(solution)/shard_map/ppermute | solution.py:289
  40.6 11.7 %collective-permute-start.9 = (bf16[2,512,512]{2,1,0:T(8,128)(2,1)S(1)}, bf16[2,512,512]{2,1,0:T(8,128)(2,1)S(1)}, u32[]{:S(2)}, u32[]{:S(2)}) collective-permute-start(bf16[2,512,512]{2,1,0:T(8,128)(2,1)S(1)} %collective-permute-done.6.refs_2_.near_ref), channel_id=1, source_target_pairs={{0,1},{1,0},{2,3},{3,2},{4,5},{5,4},{6,7},{7,6},{8,9},{9,8},{10,11... | collective-permute-start | bytes 3145736 | tf_op jit(solution)/shard_map/ppermute | solution.py:268
  43.3 19.1 %collective-permute-start.10 = (bf16[2,512,512]{2,1,0:T(8,128)(2,1)}, bf16[2,512,512]{2,1,0:T(8,128)(2,1)}, u32[]{:S(2)}, u32[]{:S(2)}) collective-permute-start(bf16[2,512,512]{2,1,0:T(8,128)(2,1)} %pad_maximum_fusion.1.refs_1_), channel_id=1, source_target_pairs={{0,2},{1,7},{2,0},{3,5},{4,6},{5,3},{6,4},{7,1},{8,10},{9,15},{10,... | collective-permute-start | bytes 3145736 | tf_op jit(solution)/shard_map/ppermute | solution.py:275
  52.2 10.2 %collective-permute-start.4 = (bf16[8,256,128]{2,1,0:T(8,128)(2,1)}, bf16[8,256,128]{2,1,0:T(8,128)(2,1)}, u32[]{:S(2)}, u32[]{:S(2)}) collective-permute-start(bf16[8,256,128]{2,1,0:T(8,128)(2,1)} %slice.81), channel_id=1, source_target_pairs={{0,64},{1,193},{64,0},{65,129},{128,192},{129,65},{192,128},{193,1... | collective-permute-start | bytes 1572872 | tf_op jit(solution)/shard_map/ppermute | solution.py:275
  53.5 10.6 %collective-permute-start.11 = (bf16[1,512,512]{2,1,0:T(8,128)(2,1)}, bf16[1,512,512]{2,1,0:T(8,128)(2,1)}, u32[]{:S(2)}, u32[]{:S(2)}) collective-permute-start(bf16[1,512,512]{2,1,0:T(8,128)(2,1)} %slice.54), channel_id=1, source_target_pairs={{0,2},{1,7},{2,0},{3,5},{4,6},{5,3},{6,4},{7,1},{8,10},{9,15},{10,... | collective-permute-start | bytes 1572872 | tf_op jit(solution)/shard_map/ppermute | solution.py:275
  53.7 10.6 %collective-permute-start.13 = (bf16[8,256,128]{2,1,0:T(8,128)(2,1)}, bf16[8,256,128]{2,1,0:T(8,128)(2,1)}, u32[]{:S(2)}, u32[]{:S(2)}) collective-permute-start(bf16[8,256,128]{2,1,0:T(8,128)(2,1)} %slice.80), channel_id=1, source_target_pairs={{0,8},{1,57},{8,0},{9,17},{16,24},{17,9},{24,16},{25,33},{32,40},{... | collective-permute-start | bytes 1572872 | tf_op jit(solution)/shard_map/ppermute | solution.py:289
  64.1 4.7 %collective-permute-start.12 = (bf16[2,512,512]{2,1,0:T(8,128)(2,1)}, bf16[2,512,512]{2,1,0:T(8,128)(2,1)S(1)}, u32[]{:S(2)}, u32[]{:S(2)}) collective-permute-start(bf16[2,512,512]{2,1,0:T(8,128)(2,1)} %collective-permute-done.10.refs_0_.refs_1_), channel_id=1, source_target_pairs={{0,1},{1,0},{2,3},{3,2},{4,5},{5,4},{6,7},{7,6},{8,9},{9,8},{10,11... | collective-permute-start | bytes 3145736 | tf_op jit(solution)/shard_map/ppermute | solution.py:268
  66.8 8.5 %collective-permute-start.14 = (bf16[2,4,256,128]{3,2,1,0:T(8,128)(2,1)S(1)}, bf16[2,4,256,128]{3,2,1,0:T(8,128)(2,1)S(1)}, u32[]{:S(2)}, u32[]{:S(2)}) collective-permute-start(bf16[2,4,256,128]{3,2,1,0:T(8,128)(2,1)S(1)} %pad_maximum_fusion.3), channel_id=1, source_target_pairs={{0,192},{1,65},{64,128},{65,1},{128,64},{129,193},{192,0},{193,129... | collective-permute-start | bytes 1572872 | tf_op jit(solution)/shard_map/ppermute | solution.py:275
  67.3 8.0 %collective-permute-start.16 = (bf16[1,512,512]{2,1,0:T(8,128)(2,1)}, bf16[1,512,512]{2,1,0:T(8,128)(2,1)S(1)}, u32[]{:S(2)}, u32[]{:S(2)}) collective-permute-start(bf16[1,512,512]{2,1,0:T(8,128)(2,1)} %collective-permute-done.11.far_ref.refs_2_), channel_id=1, source_target_pairs={{0,1},{1,0},{2,3},{3,2},{4,5},{5,4},{6,7},{7,6},{8,9},{9,8},{10,11... | collective-permute-start | bytes 1572872 | tf_op jit(solution)/shard_map/ppermute | solution.py:268
  68.8 9.4 %collective-permute-start.15 = (bf16[1,512,512]{2,1,0:T(8,128)(2,1)S(1)}, bf16[1,512,512]{2,1,0:T(8,128)(2,1)}, u32[]{:S(2)}, u32[]{:S(2)}) collective-permute-start(bf16[1,512,512]{2,1,0:T(8,128)(2,1)S(1)} %slice.60), channel_id=1, source_target_pairs={{0,2},{1,7},{2,0},{3,5},{4,6},{5,3},{6,4},{7,1},{8,10},{9,15},{10,... | collective-permute-start | bytes 1572872 | tf_op jit(solution)/shard_map/ppermute | solution.py:275
  82.1 14.9 %collective-permute-start.20 = (bf16[528,128]{1,0:T(8,128)(2,1)}, bf16[528,128]{1,0:T(8,128)(2,1)}, u32[]{:S(2)}, u32[]{:S(2)}) collective-permute-start(bf16[528,128]{1,0:T(8,128)(2,1)} %get-tuple-element.72), channel_id=1, source_target_pairs={{0,4},{2,6},{4,0},{6,2},{1,5},{3,7},{5,1},{7,3},{8,12},{10,14},{12... | collective-permute-start | bytes 405512 | tf_op jit(solution)/shard_map/ppermute | solution.py:280
  84.1 12.9 %collective-permute-start.18 = (bf16[528,128]{1,0:T(8,128)(2,1)}, bf16[528,128]{1,0:T(8,128)(2,1)}, u32[]{:S(2)}, u32[]{:S(2)}) collective-permute-start(bf16[528,128]{1,0:T(8,128)(2,1)} %get-tuple-element.70), channel_id=1, source_target_pairs={{0,2},{1,7},{2,0},{3,5},{4,6},{5,3},{6,4},{7,1},{8,10},{9,15},{10,... | collective-permute-start | bytes 405512 | tf_op jit(solution)/shard_map/ppermute | solution.py:275
  85.0 12.0 %collective-permute-start.19 = (bf16[528,128]{1,0:T(8,128)(2,1)}, bf16[528,128]{1,0:T(8,128)(2,1)}, u32[]{:S(2)}, u32[]{:S(2)}) collective-permute-start(bf16[528,128]{1,0:T(8,128)(2,1)} %get-tuple-element.71), channel_id=1, source_target_pairs={{0,6},{1,3},{2,4},{3,1},{4,2},{5,7},{6,0},{7,5},{8,14},{9,11},{10,... | collective-permute-start | bytes 405512 | tf_op jit(solution)/shard_map/ppermute | solution.py:275
  98.8 14.6 %collective-permute-start.21 = (bf16[528,128]{1,0:T(8,128)(2,1)}, bf16[528,128]{1,0:T(8,128)(2,1)}, u32[]{:S(2)}, u32[]{:S(2)}) collective-permute-start(bf16[528,128]{1,0:T(8,128)(2,1)} %shard_map.90.refs_0_), channel_id=1, source_target_pairs={{0,16},{1,49},{16,0},{17,33},{32,48},{33,17},{48,32},{49,1},{2,18}... | collective-permute-start | bytes 405512 | tf_op jit(solution)/shard_map/ppermute | solution.py:275
  114.4 9.4 %collective-permute-start.22 = (bf16[528,128]{1,0:T(8,128)(2,1)S(1)}, bf16[528,128]{1,0:T(8,128)(2,1)}, u32[]{:S(2)}, u32[]{:S(2)}) collective-permute-start(bf16[528,128]{1,0:T(8,128)(2,1)S(1)} %shard_map.92.refs_0_), channel_id=1, source_target_pairs={{0,48},{1,17},{16,32},{17,1},{32,16},{33,49},{48,0},{49,33},{2,50}... | collective-permute-start | bytes 405512 | tf_op jit(solution)/shard_map/ppermute | solution.py:275
  125.7 9.7 %collective-permute-start.25 = (bf16[528,128]{1,0:T(8,128)(2,1)S(1)}, bf16[528,128]{1,0:T(8,128)(2,1)S(1)}, u32[]{:S(2)}, u32[]{:S(2)}) collective-permute-start(bf16[528,128]{1,0:T(8,128)(2,1)S(1)} %shard_map.94.refs_0_), channel_id=1, source_target_pairs={{0,128},{64,192},{128,0},{192,64},{1,129},{65,193},{129,1},{193,65... | collective-permute-start | bytes 405512 | tf_op jit(solution)/shard_map/ppermute | solution.py:280
  127.1 8.3 %collective-permute-start.24 = (bf16[528,128]{1,0:T(8,128)(2,1)S(1)}, bf16[528,128]{1,0:T(8,128)(2,1)S(1)}, u32[]{:S(2)}, u32[]{:S(2)}) collective-permute-start(bf16[528,128]{1,0:T(8,128)(2,1)S(1)} %shard_map.94.refs_0_), channel_id=1, source_target_pairs={{0,192},{1,65},{64,128},{65,1},{128,64},{129,193},{192,0},{193,129... | collective-permute-start | bytes 405512 | tf_op jit(solution)/shard_map/ppermute | solution.py:275
  127.8 7.6 %collective-permute-start.23 = (bf16[528,128]{1,0:T(8,128)(2,1)S(1)}, bf16[528,128]{1,0:T(8,128)(2,1)S(1)}, u32[]{:S(2)}, u32[]{:S(2)}) collective-permute-start(bf16[528,128]{1,0:T(8,128)(2,1)S(1)} %shard_map.94.refs_0_), channel_id=1, source_target_pairs={{0,64},{1,193},{64,0},{65,129},{128,192},{129,65},{192,128},{193,1... | collective-permute-start | bytes 405512 | tf_op jit(solution)/shard_map/ppermute | solution.py:275
  (39 other events, 175.6 us)

commit v8 on v7

--- a/solution.py
+++ b/solution.py
@@ -82,14 +82,15 @@
         ],
         compiler_params=pltpu.CompilerParams(vmem_limit_bytes=LIMIT),
         cost_estimate=QUICK,
-    )(table, tokens, gain)
-
-
-def grad_kernel(own_ref, got_ref, cot_own_ref, cot_got_ref, *out_refs):
+    )(table, *in_hbm(tokens), gain)
+
+
+def grad_kernel(own_ref, got_ref, cot_own_ref, cot_got_ref, sent_ref, kept_ref, *, side):
     span = 2 * TILE
     half = cot_own_ref.shape[0] // 2
-    cot_own = cot_own_ref[...]
-    cot_got = cot_got_ref[...]
+    rows = slice(side * half, (side + 1) * half)
+    cot_own = cot_own_ref[rows, :]
+    cot_got = cot_got_ref[rows, :]
     for pair in range(own_ref.shape[1] // span):
         part = slice(pair * span, (pair + 1) * span)
         grads = jnp.dot(cot_own, own_ref[:, part], preferred_element_type=jnp.float32)
@@ -97,27 +98,26 @@
         for which in range(2):
             tile = pair * 2 + which
             z, y1, rest = tile // 16, tile // 8 % 2, tile % 8
-            for side, (sent, at) in enumerate(((y1, z * 8 + rest), (z, y1 * 8 + rest))):
-                piece = grads[side * half : (side + 1) * half, which * TILE : (which + 1) * TILE]
-                if sent:
-                    out_refs[side][at] = piece.astype(jnp.bfloat16)
-                else:
-                    out_refs[2 + side][at] = piece
-
-
-def grad_tiles(own, got, cot_own, cot_got):
-    rows, width = own.shape
-    columns = cot_own.shape[0]
-    tiles = width // TILE // 2
-    shape = (tiles, columns // 2, TILE)
-    outs = pl.pallas_call(
-        grad_kernel,
-        out_shape=[jax.ShapeDtypeStruct(shape, jnp.bfloat16)] * 2
-        + [jax.ShapeDtypeStruct(shape, jnp.float32)] * 2,
+            sent, at = ((y1, z * 8 + rest), (z, y1 * 8 + rest))[side]
+            piece = grads[:, which * TILE : (which + 1) * TILE]
+            if sent:
+                sent_ref[at] = piece.astype(jnp.bfloat16)
+            else:
+                kept_ref[at] = piece
+
+
+def grad_tiles(own, got, cot_own, cot_got, side):
+    width = own.shape[1]
+    shape = (width // TILE // 2, cot_own.shape[0] // 2, TILE)
+    return pl.pallas_call(
+        functools.partial(grad_kernel, side=side),
+        out_shape=[
+            jax.ShapeDtypeStruct(shape, jnp.bfloat16),
+            jax.ShapeDtypeStruct(shape, jnp.float32),
+        ],
         compiler_params=pltpu.CompilerParams(vmem_limit_bytes=LIMIT),
         cost_estimate=QUICK,
     )(own, got, cot_own, cot_got)
-    return outs[:2], outs[2:]
 
 
 class Inputs:
@@ -205,6 +205,10 @@
         block_out(k).wait()
 
 
+def in_hbm(*arrays):
+    return [pltpu.with_memory_space_constraint(array, pltpu.HBM) for array in arrays]
+
+
 def costs(tokens, columns):
     rows, width = tokens.shape
     return dict(
@@ -226,7 +230,7 @@
         out_shape=jax.ShapeDtypeStruct((rows, columns), jnp.float32),
         scratch_shapes=Inputs.scratch(rows, span, columns, table.shape[0]),
         **costs(tokens, columns),
-    )(table, tokens, inverse, gain, *weights)
+    )(table, *in_hbm(tokens), inverse, gain, *in_hbm(*weights))
 
 
 def forward_last(tokens, inverse, gain, cotangent, weights, sums, table):
@@ -242,7 +246,7 @@
         scratch_shapes=[pltpu.VMEM((rows, columns), jnp.float32)]
         + Inputs.scratch(rows, span, columns, table.shape[0]),
         **costs(tokens, columns),
-    )(table, tokens, inverse, gain, cotangent, sums, *weights)
+    )(table, *in_hbm(tokens), inverse, gain, cotangent, sums, *in_hbm(*weights))
 
 
 def backward(tokens, inverse, gain, cotangent, moment, weights, table, before=()):
@@ -260,7 +264,7 @@
         + Inputs.scratch(rows, span, columns, count),
         input_output_aliases={6 + len(weights): 0} if before else {},
         **costs(tokens, columns),
-    )(table, tokens, inverse, gain, cotangent, moment, *weights, *before)
+    )(table, *in_hbm(tokens), inverse, gain, cotangent, moment, *in_hbm(*weights, *before))
 
 
 def swap(array, axis):
@@ -289,13 +293,13 @@
     return lax.ppermute(array, ("zh", "zl", "c"), moves)
 
 
-def halve(total):
-    half = total.shape[0] // 2
-    return total[half:].astype(jnp.bfloat16), total[:half]
-
-
 def add(kept, got):
     return kept + got.astype(jnp.float32)
+
+
+def add_halves(kept, got):
+    half = kept.shape[0] // 2
+    return add(kept[half:], got[half:]).astype(jnp.bfloat16), add(kept[:half], got[:half])
 
 
 def tie(first, *others):
@@ -355,7 +359,7 @@
             pltpu.SemaphoreType.DMA((4,)),
         ],
         compiler_params=pltpu.CompilerParams(vmem_limit_bytes=LIMIT),
-    )(table, total, gain, base, near, near_c, far)
+    )(table, total, gain, *in_hbm(base, near, near_c, far))
 
 
 def in_pairs(terms):
@@ -456,24 +460,28 @@
     mine, other, inverse = norm_tiles(tokens, gain, tie(jnp.stack(tables), base, cot_own))
     got = swap(other, "c")
     near = pair(base, "x", 0)
-    sent, kept = grad_tiles(mine, got, cot_own, cot_got)
-
-    moved = [pair(sent[0], "y", 0), pair_z(sent[1])]
-    (first, kept_first), (second, kept_second) = (halve(add(k, m)) for k, m in zip(kept, moved))
-
-    first, near, up = lax.optimization_barrier((first, near, up))
+
+    first, kept_first = grad_tiles(mine, got, cot_own, cot_got, 0)
+    mine, up, first = lax.optimization_barrier((mine, up, first))
+    second, kept_second = grad_tiles(mine, got, cot_own, cot_got, 1)
+    moved = [pair(first, "y", 0), pair_z(second)]
+    above = jnp.stack([up, swap(up, "c")])
+    above_near = pair(above, "x", 0)
+    (first, kept_first), (second, kept_second) = map(
+        add_halves, (kept_first, kept_second), moved
+    )
+
+    first, near = lax.optimization_barrier((first, near))
     moved = [pair_z(first), pair(second, "y", 0)]
     near_c = swap(near, "c")
-    above = jnp.stack([up, swap(up, "c")])
-    above_near = pair(above, "x", 0)
     far = pair(near_c[1:], "x", 0)
     early = [base, above, near, near_c]
     sums = forward(tokens, inverse, gain, early, nodes_of(BASE + ABOVE + NEAR + NEAR_C))
-    moved[1], sums, above_near, far = lax.optimization_barrier((moved[1], sums, above_near, far))
+    moved[1], sums, above_near = lax.optimization_barrier((moved[1], sums, above_near))
     above_near_c = swap(above_near, "c")
     above_far = pair(above_near_c[1:], "x", 0)
-    (first, kept_first), (second, kept_second) = (
-        halve(add(k, m)) for k, m in zip((kept_first, kept_second), moved)
+    (first, kept_first), (second, kept_second) = map(
+        add_halves, (kept_first, kept_second), moved
     )
 
     moved = pair(jnp.stack([first, second]), "y", 1)

time: 145 us -> 123 us (0.85)
  local copies, waits for them, and re-layouts: 32.6 us -> 7.06 us
  other arithmetic: 4.43 us -> 6.26 us
  starting transfers between devices: 40.2 us -> 41.8 us
    unnamed x69 -> x25, local copies, waits for them, and re-layouts: 29.2 us -> 5.53 us
    ppermute x13, waiting for transfers between devices: 13.8 us -> 21.2 us  [pair(): return lax.ppermute(array, (axis, 'c'), moves)]
    ppermute x11, waiting for transfers between devices: 8.67 us -> 4.13 us  [swap(): return lax.ppermute(array, axis, [(a, last - a) for a in range(last + 1)])]
    pallas_call x3, Pallas kernels: 3.73 us -> 0.17 us  [merge(): pl.pallas_call(functools.partial(merge_kernel, scale=scale), in_specs=[VM...]
    ppermute x13, starting transfers between devices: 18.7 us -> 21.2 us  [pair(): return lax.ppermute(array, (axis, 'c'), moves)]
    pallas_call x3, Pallas kernels: 11.6 us -> 13.7 us  [backward(): pl.pallas_call(functools.partial(backward_kernel, count=len(weights)), in...]
    slice x2 -> x0, local copies, waits for them, and re-layouts: 2.03 us -> none  [halve(): return (total[half:].astype(jnp.bfloat16), total[:half])]
    ppermute x3, waiting for transfers between devices: 5.55 us -> 3.78 us  [pair_z(): return lax.ppermute(array, ('zh', 'zl', 'c'), moves)]
  transfers between devices with their start and end apart: 29 -> 29, of which waited for: 10 -> 15; matrix products, arithmetic and copies ran while one was open for 6% -> 6% of each run, Pallas kernels for 14% -> 22%
where the time goes in v8:
time: 123 us
  starting transfers between devices  41.8 us (34%)
  Pallas kernels  37.5 us (30%)
  waiting for transfers between devices  29.1 us (24%)
  local copies, waits for them, and re-layouts  7.06 us (6%)
  other arithmetic  6.26 us (5%)
    ppermute x13, waiting for transfers between devices, pair(): return lax.ppermute(array, (axis, 'c'), moves)  21.2 us
    ppermute x13, starting transfers between devices, pair(): return lax.ppermute(array, (axis, 'c'), moves)  21.2 us
    pallas_call x3, Pallas kernels, backward(): pl.pallas_call(functools.partial(backward_kernel, count=len(weights)), in...  13.7 us
    ppermute x3, starting transfers between devices, pair_z(): return lax.ppermute(array, ('zh', 'zl', 'c'), moves)  9.29 us
    ppermute x11, starting transfers between devices, swap(): return lax.ppermute(array, axis, [(a, last - a) for a in range(last + 1)])  8.49 us
    unnamed x25, local copies, waits for them, and re-layouts  5.53 us
    pallas_call x1, Pallas kernels, forward_last(): pl.pallas_call(forward_last_kernel, in_specs=[SMEM, HBM] + [VMEM] * 4 + [...  4.91 us
    pallas_call x2, Pallas kernels, grad_tiles(): pl.pallas_call(functools.partial(grad_kernel, side=side), out_shape=[jax....  4.65 us
  transfers between devices with their start and end apart: 29, of which 15 were waited for; matrix products, arithmetic and copies ran while one was open for 6% of the time, Pallas kernels for 22%

profile of v8, /device:TPU:1, one launch (start us, length us, event | category | flops | bytes accessed | tf_op | source)
XLA Modules:
  0.0 122.7 jit_solution(17712636470247119735)
XLA Ops:
  2.8 3.3 %collective-permute-start = (bf16[512,512]{1,0:T(8,128)(2,1)S(1)}, bf16[512,512]{1,0:T(8,128)(2,1)S(1)}, u32[]{:S(2)}, u32[]{:S(2)}) collective-permute-start(bf16[512,512]{1,0:T(8,128)(2,1)S(1)} %shard_map.84), channel_id=1, source_target_pairs={{0,1},{1,0},{2,3},{3,2},{4,5},{5,4},{6,7},{7,6},{8,9},{9,8},{10,11... | collective-permute-start | bytes 1572872 | tf_op jit(solution)/shard_map/ppermute | solution.py:272
  7.7 4.6 %shard_map.85 = (bf16[320,4096]{1,0:T(8,128)(2,1)S(1)}, bf16[320,4096]{1,0:T(8,128)(2,1)S(1)}, f32[320,1]{1,0:T(8,128)S(1)}) custom-call(s32[2,32]{1,0:T(2,128)S(1)} %pad_add_fusion.tab_ref, bf16[320,8192]{1,0:T(8,128)(2,1)} %tok_ref.11, f32[1,8192]{1,0:T(1,128)S(1)} %bitcast.52), custom_call_target="tpu_custom_call" | custom-call | flops 1 | bytes 1 | tf_op jit(solution)/shard_map/pallas_call | solution.py:70
  12.8 3.8 %collective-permute-start.1 = (bf16[512,512]{1,0:T(8,128)(2,1)S(1)}, bf16[512,512]{1,0:T(8,128)(2,1)S(1)}, u32[]{:S(2)}, u32[]{:S(2)}) collective-permute-start(bf16[512,512]{1,0:T(8,128)(2,1)S(1)} %shard_map.84), channel_id=1, source_target_pairs={{0,8},{1,57},{8,0},{9,17},{16,24},{17,9},{24,16},{25,33},{32,40},{... | collective-permute-start | bytes 1572872 | tf_op jit(solution)/shard_map/ppermute | solution.py:293
  18.3 2.3 %shard_map.86 = (bf16[16,256,128]{2,1,0:T(8,128)(2,1)S(1)}, f32[16,256,128]{2,1,0:T(8,128)S(1)}) custom-call(bf16[320,4096]{1,0:T(8,128)(2,1)S(1)} %get-tuple-element.54.own_ref, bf16[320,4096]{1,0:T(8,128)(2,1)S(1)} %collective-permute-done.2.got_ref, bf16[512,320]{1,0:T(8,128)(2,1)S(1)} %bitcast.49, bf16[512,320]{1,0:T(8,128)(2,1)S(1)} %collective-permute-done.3.cot_got_ref), custom_call_target="tpu_custom_call" | custom-call | flops 1 | bytes 1 | tf_op jit(solution)/shard_map/pallas_call | solution.py:112
  20.7 2.5 %collective-permute-done.1 = bf16[512,512]{1,0:T(8,128)(2,1)S(1)} collective-permute-done((bf16[512,512]{1,0:T(8,128)(2,1)S(1)}, bf16[512,512]{1,0:T(8,128)(2,1)S(1)}, u32[]{:S(2)}, u32[]{:S(2)}) %collective-permute-start.1) | collective-permute-done | bytes 524320 | tf_op jit(solution)/shard_map/ppermute | solution.py:293
  23.2 2.7 %collective-permute-start.7 = (bf16[16,256,128]{2,1,0:T(8,128)(2,1)S(1)}, bf16[16,256,128]{2,1,0:T(8,128)(2,1)S(1)}, u32[]{:S(2)}, u32[]{:S(2)}) collective-permute-start(bf16[16,256,128]{2,1,0:T(8,128)(2,1)S(1)} %get-tuple-element.59), channel_id=1, source_target_pairs={{0,64},{1,193},{64,0},{65,129},{128,192},{129,65},{192,128},{193,1... | collective-permute-start | bytes 3145736 | tf_op jit(solution)/shard_map/ppermute | solution.py:279
  25.9 2.5 %collective-permute-start.8 = (bf16[2,512,512]{2,1,0:T(8,128)(2,1)S(1)}, bf16[2,512,512]{2,1,0:T(8,128)(2,1)}, u32[]{:S(2)}, u32[]{:S(2)}) collective-permute-start(bf16[2,512,512]{2,1,0:T(8,128)(2,1)S(1)} %pad_maximum_fusion.refs_0_.base_ref), channel_id=1, source_target_pairs={{0,2},{1,7},{2,0},{3,5},{4,6},{5,3},{6,4},{7,1},{8,10},{9,15},{10,... | collective-permute-start | bytes 3145736 | tf_op jit(solution)/shard_map/ppermute | solution.py:279
  28.4 2.3 %shard_map.87 = (bf16[16,256,128]{2,1,0:T(8,128)(2,1)S(1)}, f32[16,256,128]{2,1,0:T(8,128)S(1)}) custom-call(bf16[320,4096]{1,0:T(8,128)(2,1)S(1)} %get-tuple-element.54.own_ref, bf16[320,4096]{1,0:T(8,128)(2,1)S(1)} %collective-permute-done.2.got_ref, bf16[512,320]{1,0:T(8,128)(2,1)S(1)} %bitcast.50, bf16[512,320]{1,0:T(8,128)(2,1)S(1)} %collective-permute-done.3.cot_got_ref), custom_call_target="tpu_custom_call" | custom-call | flops 1 | bytes 1 | tf_op jit(solution)/shard_map/pallas_call | solution.py:112
  30.7 2.8 %collective-permute-start.4 = (bf16[16,256,128]{2,1,0:T(8,128)(2,1)S(1)}, bf16[16,256,128]{2,1,0:T(8,128)(2,1)S(1)}, u32[]{:S(2)}, u32[]{:S(2)}) collective-permute-start(bf16[16,256,128]{2,1,0:T(8,128)(2,1)S(1)} %get-tuple-element.56), channel_id=1, source_target_pairs={{0,8},{1,57},{8,0},{9,17},{16,24},{17,9},{24,16},{25,33},{32,40},{... | collective-permute-start | bytes 3145736 | tf_op jit(solution)/shard_map/ppermute | solution.py:293
  33.5 4.6 %collective-permute-done.7 = bf16[16,256,128]{2,1,0:T(8,128)(2,1)S(1)} collective-permute-done((bf16[16,256,128]{2,1,0:T(8,128)(2,1)S(1)}, bf16[16,256,128]{2,1,0:T(8,128)(2,1)S(1)}, u32[]{:S(2)}, u32[]{:S(2)}) %collective-permute-start.7) | collective-permute-done | bytes 1048608 | tf_op jit(solution)/shard_map/ppermute | solution.py:279
  42.0 2.5 %collective-permute-start.10 = (bf16[2,512,512]{2,1,0:T(8,128)(2,1)}, bf16[2,512,512]{2,1,0:T(8,128)(2,1)}, u32[]{:S(2)}, u32[]{:S(2)}) collective-permute-start(bf16[2,512,512]{2,1,0:T(8,128)(2,1)} %pad_maximum_fusion.1.refs_1_), channel_id=1, source_target_pairs={{0,2},{1,7},{2,0},{3,5},{4,6},{5,3},{6,4},{7,1},{8,10},{9,15},{10,... | collective-permute-start | bytes 3145736 | tf_op jit(solution)/shard_map/ppermute | solution.py:279
  47.1 2.7 %collective-permute-start.13 = (bf16[8,256,128]{2,1,0:T(8,128)(2,1)S(1)}, bf16[8,256,128]{2,1,0:T(8,128)(2,1)S(1)}, u32[]{:S(2)}, u32[]{:S(2)}) collective-permute-start(bf16[8,256,128]{2,1,0:T(8,128)(2,1)S(1)} %get-tuple-element.63), channel_id=1, source_target_pairs={{0,8},{1,57},{8,0},{9,17},{16,24},{17,9},{24,16},{25,33},{32,40},{... | collective-permute-start | bytes 1572872 | tf_op jit(solution)/shard_map/ppermute | solution.py:293
  50.8 4.1 %shard_map.88.acc_in = f32[320,512]{1,0:T(8,128)S(1)} custom-call(s32[8]{0:T(128)S(1)} %stack.169.tab_ref, bf16[320,8192]{1,0:T(8,128)(2,1)} %tok_ref.11, f32[320,1]{1,0:T(8,128)S(1)} %get-tuple-element.50.inv_ref, f32[1,8192]{1,0:T(1,128)S(1)} %bitcast.53, bf16[2,512,512]{2,1,0:T(8,128)(2,1)} %copy-done.4, bf16[2,512,512]{2,1,0:T(8,128)(2,1)} %pad_maximum_fusion.1.refs_1_, ...), custom_call_target="tpu_custom_call" | custom-call | flops 1342177280 | bytes 9437184 | tf_op jit(solution)/shard_map/pallas_call | solution.py:226
  58.7 2.6 %collective-permute-start.12 = (bf16[1,512,512]{2,1,0:T(8,128)(2,1)S(1)}, bf16[1,512,512]{2,1,0:T(8,128)(2,1)S(1)}, u32[]{:S(2)}, u32[]{:S(2)}) collective-permute-start(bf16[1,512,512]{2,1,0:T(8,128)(2,1)S(1)} %slice.82), channel_id=1, source_target_pairs={{0,2},{1,7},{2,0},{3,5},{4,6},{5,3},{6,4},{7,1},{8,10},{9,15},{10,... | collective-permute-start | bytes 1572872 | tf_op jit(solution)/shard_map/ppermute | solution.py:279
  62.5 5.8 %collective-permute-done.12.far_ref.refs_2_ = bf16[1,512,512]{2,1,0:T(8,128)(2,1)S(1)} collective-permute-done((bf16[1,512,512]{2,1,0:T(8,128)(2,1)S(1)}, bf16[1,512,512]{2,1,0:T(8,128)(2,1)S(1)}, u32[]{:S(2)}, u32[]{:S(2)}) %collective-permute-start.12) | collective-permute-done | bytes 524320 | tf_op jit(solution)/shard_map/ppermute | solution.py:279
  68.3 2.6 %collective-permute-start.15 = (bf16[1,512,512]{2,1,0:T(8,128)(2,1)S(1)}, bf16[1,512,512]{2,1,0:T(8,128)(2,1)}, u32[]{:S(2)}, u32[]{:S(2)}) collective-permute-start(bf16[1,512,512]{2,1,0:T(8,128)(2,1)S(1)} %slice.90), channel_id=1, source_target_pairs={{0,2},{1,7},{2,0},{3,5},{4,6},{5,3},{6,4},{7,1},{8,10},{9,15},{10,... | collective-permute-start | bytes 1572872 | tf_op jit(solution)/shard_map/ppermute | solution.py:279
  71.8 6.0 %collective-permute-done.15.refs_3_.refs_1_ = bf16[1,512,512]{2,1,0:T(8,128)(2,1)} collective-permute-done((bf16[1,512,512]{2,1,0:T(8,128)(2,1)S(1)}, bf16[1,512,512]{2,1,0:T(8,128)(2,1)}, u32[]{:S(2)}, u32[]{:S(2)}) %collective-permute-start.15) | collective-permute-done | bytes 524320 | tf_op jit(solution)/shard_map/ppermute | solution.py:279
  85.6 4.9 %shard_map.90 = (bf16[320,512]{1,0:T(8,128)(2,1)}, f32[320,1]{1,0:T(8,128)S(1)}) custom-call(s32[8]{0:T(128)S(1)} %stack.156.tab_ref, bf16[320,8192]{1,0:T(8,128)(2,1)} %tok_ref.11, f32[320,1]{1,0:T(8,128)S(1)} %get-tuple-element.50.inv_ref, f32[1,8192]{1,0:T(1,128)S(1)} %bitcast.55, bf16[320,512]{1,0:T(8,128)(2,1)S(1)} %copy-done, ...), custom_call_target="tpu_custom_call" | custom-call | flops 1342177280 | bytes 9437184 | tf_op jit(solution)/shard_map/pallas_call | solution.py:238
  91.4 2.5 %collective-permute-start.21 = (bf16[528,128]{1,0:T(8,128)(2,1)S(1)}, bf16[528,128]{1,0:T(8,128)(2,1)S(1)}, u32[]{:S(2)}, u32[]{:S(2)}) collective-permute-start(bf16[528,128]{1,0:T(8,128)(2,1)S(1)} %shard_map.91.refs_0_), channel_id=1, source_target_pairs={{0,16},{1,49},{16,0},{17,33},{32,48},{33,17},{48,32},{49,1},{2,18}... | collective-permute-start | bytes 405512 | tf_op jit(solution)/shard_map/ppermute | solution.py:279
  94.0 4.9 %shard_map.92.refs_3_ = bf16[320,8192]{1,0:T(8,128)(2,1)} custom-call(s32[6]{0:T(128)S(1)} %stack.179.tab_ref, bf16[320,8192]{1,0:T(8,128)(2,1)} %tok_ref.11, f32[320,1]{1,0:T(8,128)S(1)} %get-tuple-element.50.inv_ref, f32[1,8192]{1,0:T(1,128)S(1)} %bitcast.56, bf16[320,512]{1,0:T(8,128)(2,1)S(1)} %copy-done, f32[320,1]{1,0:T(8,128)S(1)} %get-tuple-element.79.moment_ref, ...), custom_call_target="tpu_custom_call" | custom-call | flops 1342177280 | bytes 9437184 | tf_op jit(solution)/shard_map/pallas_call | solution.py:255
  98.9 2.2 %collective-permute-start.22 = (bf16[528,128]{1,0:T(8,128)(2,1)S(1)}, bf16[528,128]{1,0:T(8,128)(2,1)S(1)}, u32[]{:S(2)}, u32[]{:S(2)}) collective-permute-start(bf16[528,128]{1,0:T(8,128)(2,1)S(1)} %shard_map.93.refs_0_), channel_id=1, source_target_pairs={{0,48},{1,17},{16,32},{17,1},{32,16},{33,49},{48,0},{49,33},{2,50}... | collective-permute-start | bytes 405512 | tf_op jit(solution)/shard_map/ppermute | solution.py:279
  101.2 4.4 %shard_map.94.refs_4_ = bf16[320,8192]{1,0:T(8,128)(2,1)} custom-call(s32[5]{0:T(128)S(1)} %stack.180.tab_ref, bf16[320,8192]{1,0:T(8,128)(2,1)} %tok_ref.11, f32[320,1]{1,0:T(8,128)S(1)} %get-tuple-element.50.inv_ref, f32[1,8192]{1,0:T(1,128)S(1)} %bitcast.57, bf16[320,512]{1,0:T(8,128)(2,1)S(1)} %copy-done, ...), custom_call_target="tpu_custom_call", output_to_operand_aliasing={{}: (9, {})} | custom-call | flops 1342177280 | bytes 9437184 | tf_op jit(solution)/shard_map/pallas_call | solution.py:255
  109.2 4.4 %shard_map.96 = bf16[320,8192]{1,0:T(8,128)(2,1)} custom-call(s32[5]{0:T(128)S(1)} %stack.181.tab_ref, bf16[320,8192]{1,0:T(8,128)(2,1)} %tok_ref.11, f32[320,1]{1,0:T(8,128)S(1)} %get-tuple-element.50.inv_ref, f32[1,8192]{1,0:T(1,128)S(1)} %bitcast.58, bf16[320,512]{1,0:T(8,128)(2,1)S(1)} %copy-done, ...), custom_call_target="tpu_custom_call", output_to_operand_aliasing={{}: (10, {})} | custom-call | flops 1342177280 | bytes 9437184 | tf_op jit(solution)/shard_map/pallas_call | solution.py:255
  115.6 2.9 %collective-permute-start.28 = (f32[4,8,128]{2,1,0:T(8,128)S(1)}, f32[4,8,128]{2,1,0:T(8,128)S(1)}, u32[]{:S(2)}, u32[]{:S(2)}) collective-permute-start(f32[4,8,128]{2,1,0:T(8,128)S(1)} %get-tuple-element.93.refs_0_), channel_id=1, source_target_pairs={{0,9},{1,8},{8,1},{9,0},{2,11},{3,10},{10,3},{11,2},{4,13},{5,12},... | collective-permute-start | bytes 49160 | tf_op jit(solution)/shard_map/ppermute | solution.py:272
  (96 shorter events, 37.9 us)
Async XLA Ops:
  2.8 4.9 %collective-permute-start = (bf16[512,512]{1,0:T(8,128)(2,1)S(1)}, bf16[512,512]{1,0:T(8,128)(2,1)S(1)}, u32[]{:S(2)}, u32[]{:S(2)}) collective-permute-start(bf16[512,512]{1,0:T(8,128)(2,1)S(1)} %shard_map.84), channel_id=1, source_target_pairs={{0,1},{1,0},{2,3},{3,2},{4,5},{5,4},{6,7},{7,6},{8,9},{9,8},{10,11... | collective-permute-start | bytes 1572872 | tf_op jit(solution)/shard_map/ppermute | solution.py:272
  12.3 6.0 %collective-permute-start.2 = (bf16[320,4096]{1,0:T(8,128)(2,1)S(1)}, bf16[320,4096]{1,0:T(8,128)(2,1)S(1)}, u32[]{:S(2)}, u32[]{:S(2)}) collective-permute-start(bf16[320,4096]{1,0:T(8,128)(2,1)S(1)} %get-tuple-element.52), channel_id=1, source_target_pairs={{0,1},{1,0},{2,3},{3,2},{4,5},{5,4},{6,7},{7,6},{8,9},{9,8},{10,11... | collective-permute-start | bytes 7864328 | tf_op jit(solution)/shard_map/ppermute | solution.py:272
  12.8 10.4 %collective-permute-start.1 = (bf16[512,512]{1,0:T(8,128)(2,1)S(1)}, bf16[512,512]{1,0:T(8,128)(2,1)S(1)}, u32[]{:S(2)}, u32[]{:S(2)}) collective-permute-start(bf16[512,512]{1,0:T(8,128)(2,1)S(1)} %shard_map.84), channel_id=1, source_target_pairs={{0,8},{1,57},{8,0},{9,17},{16,24},{17,9},{24,16},{25,33},{32,40},{... | collective-permute-start | bytes 1572872 | tf_op jit(solution)/shard_map/ppermute | solution.py:293
  23.2 14.9 %collective-permute-start.7 = (bf16[16,256,128]{2,1,0:T(8,128)(2,1)S(1)}, bf16[16,256,128]{2,1,0:T(8,128)(2,1)S(1)}, u32[]{:S(2)}, u32[]{:S(2)}) collective-permute-start(bf16[16,256,128]{2,1,0:T(8,128)(2,1)S(1)} %get-tuple-element.59), channel_id=1, source_target_pairs={{0,64},{1,193},{64,0},{65,129},{128,192},{129,65},{192,128},{193,1... | collective-permute-start | bytes 3145736 | tf_op jit(solution)/shard_map/ppermute | solution.py:279
  25.9 15.0 %collective-permute-start.8 = (bf16[2,512,512]{2,1,0:T(8,128)(2,1)S(1)}, bf16[2,512,512]{2,1,0:T(8,128)(2,1)}, u32[]{:S(2)}, u32[]{:S(2)}) collective-permute-start(bf16[2,512,512]{2,1,0:T(8,128)(2,1)S(1)} %pad_maximum_fusion.refs_0_.base_ref), channel_id=1, source_target_pairs={{0,2},{1,7},{2,0},{3,5},{4,6},{5,3},{6,4},{7,1},{8,10},{9,15},{10,... | collective-permute-start | bytes 3145736 | tf_op jit(solution)/shard_map/ppermute | solution.py:279
  30.7 14.9 %collective-permute-start.4 = (bf16[16,256,128]{2,1,0:T(8,128)(2,1)S(1)}, bf16[16,256,128]{2,1,0:T(8,128)(2,1)S(1)}, u32[]{:S(2)}, u32[]{:S(2)}) collective-permute-start(bf16[16,256,128]{2,1,0:T(8,128)(2,1)S(1)} %get-tuple-element.56), channel_id=1, source_target_pairs={{0,8},{1,57},{8,0},{9,17},{16,24},{17,9},{24,16},{25,33},{32,40},{... | collective-permute-start | bytes 3145736 | tf_op jit(solution)/shard_map/ppermute | solution.py:293
  33.5 7.4 %collective-permute-start.6 = (bf16[512,512]{1,0:T(8,128)(2,1)S(1)}, bf16[512,512]{1,0:T(8,128)(2,1)S(1)}, u32[]{:S(2)}, u32[]{:S(2)}) collective-permute-start(bf16[512,512]{1,0:T(8,128)(2,1)S(1)} %collective-permute-done.1), channel_id=1, source_target_pairs={{0,1},{1,0},{2,3},{3,2},{4,5},{5,4},{6,7},{7,6},{8,9},{9,8},{10,11... | collective-permute-start | bytes 1572872 | tf_op jit(solution)/shard_map/ppermute | solution.py:272
  40.9 8.9 %collective-permute-start.9 = (bf16[2,512,512]{2,1,0:T(8,128)(2,1)}, bf16[2,512,512]{2,1,0:T(8,128)(2,1)S(1)}, u32[]{:S(2)}, u32[]{:S(2)}) collective-permute-start(bf16[2,512,512]{2,1,0:T(8,128)(2,1)} %collective-permute-done.8.refs_2_.near_ref), channel_id=1, source_target_pairs={{0,1},{1,0},{2,3},{3,2},{4,5},{5,4},{6,7},{7,6},{8,9},{9,8},{10,11... | collective-permute-start | bytes 3145736 | tf_op jit(solution)/shard_map/ppermute | solution.py:272
  42.0 15.2 %collective-permute-start.10 = (bf16[2,512,512]{2,1,0:T(8,128)(2,1)}, bf16[2,512,512]{2,1,0:T(8,128)(2,1)}, u32[]{:S(2)}, u32[]{:S(2)}) collective-permute-start(bf16[2,512,512]{2,1,0:T(8,128)(2,1)} %pad_maximum_fusion.1.refs_1_), channel_id=1, source_target_pairs={{0,2},{1,7},{2,0},{3,5},{4,6},{5,3},{6,4},{7,1},{8,10},{9,15},{10,... | collective-permute-start | bytes 3145736 | tf_op jit(solution)/shard_map/ppermute | solution.py:279
  47.0 9.6 %collective-permute-start.5 = (bf16[8,256,128]{2,1,0:T(8,128)(2,1)}, bf16[8,256,128]{2,1,0:T(8,128)(2,1)}, u32[]{:S(2)}, u32[]{:S(2)}) collective-permute-start(bf16[8,256,128]{2,1,0:T(8,128)(2,1)} %get-tuple-element.99), channel_id=1, source_target_pairs={{0,64},{1,193},{64,0},{65,129},{128,192},{129,65},{192,128},{193,1... | collective-permute-start | bytes 1572872 | tf_op jit(solution)/shard_map/ppermute | solution.py:279
  47.1 14.1 %collective-permute-start.13 = (bf16[8,256,128]{2,1,0:T(8,128)(2,1)S(1)}, bf16[8,256,128]{2,1,0:T(8,128)(2,1)S(1)}, u32[]{:S(2)}, u32[]{:S(2)}) collective-permute-start(bf16[8,256,128]{2,1,0:T(8,128)(2,1)S(1)} %get-tuple-element.63), channel_id=1, source_target_pairs={{0,8},{1,57},{8,0},{9,17},{16,24},{17,9},{24,16},{25,33},{32,40},{... | collective-permute-start | bytes 1572872 | tf_op jit(solution)/shard_map/ppermute | solution.py:293
  57.1 11.2 %collective-permute-start.11 = (bf16[2,512,512]{2,1,0:T(8,128)(2,1)}, bf16[2,512,512]{2,1,0:T(8,128)(2,1)S(1)}, u32[]{:S(2)}, u32[]{:S(2)}) collective-permute-start(bf16[2,512,512]{2,1,0:T(8,128)(2,1)} %collective-permute-done.10.refs_0_.refs_1_), channel_id=1, source_target_pairs={{0,1},{1,0},{2,3},{3,2},{4,5},{5,4},{6,7},{7,6},{8,9},{9,8},{10,11... | collective-permute-start | bytes 3145736 | tf_op jit(solution)/shard_map/ppermute | solution.py:272
  58.7 9.6 %collective-permute-start.12 = (bf16[1,512,512]{2,1,0:T(8,128)(2,1)S(1)}, bf16[1,512,512]{2,1,0:T(8,128)(2,1)S(1)}, u32[]{:S(2)}, u32[]{:S(2)}) collective-permute-start(bf16[1,512,512]{2,1,0:T(8,128)(2,1)S(1)} %slice.82), channel_id=1, source_target_pairs={{0,2},{1,7},{2,0},{3,5},{4,6},{5,3},{6,4},{7,1},{8,10},{9,15},{10,... | collective-permute-start | bytes 1572872 | tf_op jit(solution)/shard_map/ppermute | solution.py:279
  62.4 8.6 %collective-permute-start.14 = (bf16[2,4,256,128]{3,2,1,0:T(8,128)(2,1)S(1)}, bf16[2,4,256,128]{3,2,1,0:T(8,128)(2,1)S(1)}, u32[]{:S(2)}, u32[]{:S(2)}) collective-permute-start(bf16[2,4,256,128]{3,2,1,0:T(8,128)(2,1)S(1)} %pad_maximum_fusion.3), channel_id=1, source_target_pairs={{0,192},{1,65},{64,128},{65,1},{128,64},{129,193},{192,0},{193,129... | collective-permute-start | bytes 1572872 | tf_op jit(solution)/shard_map/ppermute | solution.py:279
  68.3 9.4 %collective-permute-start.15 = (bf16[1,512,512]{2,1,0:T(8,128)(2,1)S(1)}, bf16[1,512,512]{2,1,0:T(8,128)(2,1)}, u32[]{:S(2)}, u32[]{:S(2)}) collective-permute-start(bf16[1,512,512]{2,1,0:T(8,128)(2,1)S(1)} %slice.90), channel_id=1, source_target_pairs={{0,2},{1,7},{2,0},{3,5},{4,6},{5,3},{6,4},{7,1},{8,10},{9,15},{10,... | collective-permute-start | bytes 1572872 | tf_op jit(solution)/shard_map/ppermute | solution.py:279
  81.7 8.9 %collective-permute-start.20 = (bf16[528,128]{1,0:T(8,128)(2,1)S(1)}, bf16[528,128]{1,0:T(8,128)(2,1)S(1)}, u32[]{:S(2)}, u32[]{:S(2)}) collective-permute-start(bf16[528,128]{1,0:T(8,128)(2,1)S(1)} %get-tuple-element.74), channel_id=1, source_target_pairs={{0,4},{2,6},{4,0},{6,2},{1,5},{3,7},{5,1},{7,3},{8,12},{10,14},{12... | collective-permute-start | bytes 405512 | tf_op jit(solution)/shard_map/ppermute | solution.py:284
  83.6 7.0 %collective-permute-start.18 = (bf16[528,128]{1,0:T(8,128)(2,1)S(1)}, bf16[528,128]{1,0:T(8,128)(2,1)S(1)}, u32[]{:S(2)}, u32[]{:S(2)}) collective-permute-start(bf16[528,128]{1,0:T(8,128)(2,1)S(1)} %get-tuple-element.72), channel_id=1, source_target_pairs={{0,2},{1,7},{2,0},{3,5},{4,6},{5,3},{6,4},{7,1},{8,10},{9,15},{10,... | collective-permute-start | bytes 405512 | tf_op jit(solution)/shard_map/ppermute | solution.py:279
  84.2 7.2 %collective-permute-start.19 = (bf16[528,128]{1,0:T(8,128)(2,1)S(1)}, bf16[528,128]{1,0:T(8,128)(2,1)S(1)}, u32[]{:S(2)}, u32[]{:S(2)}) collective-permute-start(bf16[528,128]{1,0:T(8,128)(2,1)S(1)} %get-tuple-element.73), channel_id=1, source_target_pairs={{0,6},{1,3},{2,4},{3,1},{4,2},{5,7},{6,0},{7,5},{8,14},{9,11},{10,... | collective-permute-start | bytes 405512 | tf_op jit(solution)/shard_map/ppermute | solution.py:279
  91.4 7.5 %collective-permute-start.21 = (bf16[528,128]{1,0:T(8,128)(2,1)S(1)}, bf16[528,128]{1,0:T(8,128)(2,1)S(1)}, u32[]{:S(2)}, u32[]{:S(2)}) collective-permute-start(bf16[528,128]{1,0:T(8,128)(2,1)S(1)} %shard_map.91.refs_0_), channel_id=1, source_target_pairs={{0,16},{1,49},{16,0},{17,33},{32,48},{33,17},{48,32},{49,1},{2,18}... | collective-permute-start | bytes 405512 | tf_op jit(solution)/shard_map/ppermute | solution.py:279
  98.9 6.7 %collective-permute-start.22 = (bf16[528,128]{1,0:T(8,128)(2,1)S(1)}, bf16[528,128]{1,0:T(8,128)(2,1)S(1)}, u32[]{:S(2)}, u32[]{:S(2)}) collective-permute-start(bf16[528,128]{1,0:T(8,128)(2,1)S(1)} %shard_map.93.refs_0_), channel_id=1, source_target_pairs={{0,48},{1,17},{16,32},{17,1},{32,16},{33,49},{48,0},{49,33},{2,50}... | collective-permute-start | bytes 405512 | tf_op jit(solution)/shard_map/ppermute | solution.py:279
  105.7 8.0 %collective-permute-start.25 = (bf16[528,128]{1,0:T(8,128)(2,1)S(1)}, bf16[528,128]{1,0:T(8,128)(2,1)S(1)}, u32[]{:S(2)}, u32[]{:S(2)}) collective-permute-start(bf16[528,128]{1,0:T(8,128)(2,1)S(1)} %shard_map.95.refs_0_), channel_id=1, source_target_pairs={{0,128},{64,192},{128,0},{192,64},{1,129},{65,193},{129,1},{193,65... | collective-permute-start | bytes 405512 | tf_op jit(solution)/shard_map/ppermute | solution.py:284
  106.6 7.1 %collective-permute-start.24 = (bf16[528,128]{1,0:T(8,128)(2,1)S(1)}, bf16[528,128]{1,0:T(8,128)(2,1)S(1)}, u32[]{:S(2)}, u32[]{:S(2)}) collective-permute-start(bf16[528,128]{1,0:T(8,128)(2,1)S(1)} %shard_map.95.refs_0_), channel_id=1, source_target_pairs={{0,192},{1,65},{64,128},{65,1},{128,64},{129,193},{192,0},{193,129... | collective-permute-start | bytes 405512 | tf_op jit(solution)/shard_map/ppermute | solution.py:279
  107.6 6.3 %collective-permute-start.23 = (bf16[528,128]{1,0:T(8,128)(2,1)S(1)}, bf16[528,128]{1,0:T(8,128)(2,1)S(1)}, u32[]{:S(2)}, u32[]{:S(2)}) collective-permute-start(bf16[528,128]{1,0:T(8,128)(2,1)S(1)} %shard_map.95.refs_0_), channel_id=1, source_target_pairs={{0,64},{1,193},{64,0},{65,129},{128,192},{129,65},{192,128},{193,1... | collective-permute-start | bytes 405512 | tf_op jit(solution)/shard_map/ppermute | solution.py:279
  115.6 4.3 %collective-permute-start.28 = (f32[4,8,128]{2,1,0:T(8,128)S(1)}, f32[4,8,128]{2,1,0:T(8,128)S(1)}, u32[]{:S(2)}, u32[]{:S(2)}) collective-permute-start(f32[4,8,128]{2,1,0:T(8,128)S(1)} %get-tuple-element.93.refs_0_), channel_id=1, source_target_pairs={{0,9},{1,8},{8,1},{9,0},{2,11},{3,10},{10,3},{11,2},{4,13},{5,12},... | collective-permute-start | bytes 49160 | tf_op jit(solution)/shard_map/ppermute | solution.py:272
  (17 other events, 91.8 us)

commit v9 on v8

--- a/solution.py
+++ b/solution.py
@@ -477,16 +477,17 @@
     far = pair(near_c[1:], "x", 0)
     early = [base, above, near, near_c]
     sums = forward(tokens, inverse, gain, early, nodes_of(BASE + ABOVE + NEAR + NEAR_C))
-    moved[1], sums, above_near = lax.optimization_barrier((moved[1], sums, above_near))
-    above_near_c = swap(above_near, "c")
-    above_far = pair(above_near_c[1:], "x", 0)
+    moved[1], sums, above_near, far = lax.optimization_barrier((moved[1], sums, above_near, far))
     (first, kept_first), (second, kept_second) = map(
         add_halves, (kept_first, kept_second), moved
     )
 
-    moved = pair(jnp.stack([first, second]), "y", 1)
+    send, above_near, far = lax.optimization_barrier((jnp.stack([first, second]), above_near, far))
+    moved = pair(send, "y", 1)
+    above_near_c = swap(above_near, "c")
+    above_far = pair(above_near_c[1:], "x", 0)
     far_c = swap(far, "c")
-    moved, above_far, far_c = lax.optimization_barrier((moved, above_far, far_c))
+    moved, far_c, above_near_c = lax.optimization_barrier((moved, far_c, above_near_c))
     total = jnp.stack([add(kept_first, moved[0]), add(kept_second, moved[1])], axis=1)
 
     peer = x ^ offset(c, jnp.arange(4) // 2, jnp.arange(4) % 2)

time: 123 us -> 120 us (0.976)
  waiting for transfers between devices: 29.1 us -> 25.5 us
  local copies, waits for them, and re-layouts: 7.06 us -> 5.11 us
  other arithmetic: 6.26 us -> 8.05 us
    ppermute x13, waiting for transfers between devices: 21.2 us -> 15.9 us  [pair(): return lax.ppermute(array, (axis, 'c'), moves)]
    ppermute x11, starting transfers between devices: 8.49 us -> 10.4 us  [swap(): return lax.ppermute(array, axis, [(a, last - a) for a in range(last + 1)])]
    unnamed x25 -> x29, local copies, waits for them, and re-layouts: 5.53 us -> 3.75 us
    ppermute x3, waiting for transfers between devices: 3.78 us -> 5.37 us  [pair_z(): return lax.ppermute(array, ('zh', 'zl', 'c'), moves)]
    another operation x3, other arithmetic: 1.13 us -> 2.4 us  [shards(): jnp.stack([first, second])]
  transfers between devices with their start and end apart: 29 -> 29, of which waited for: 15 -> 14; matrix products, arithmetic and copies ran while one was open for 6% -> 8% of each run, Pallas kernels for 22% -> 25%
where the time goes in v9:
time: 120 us
  starting transfers between devices  42.4 us (35%)
  Pallas kernels  37.5 us (31%)
  waiting for transfers between devices  25.5 us (21%)
  other arithmetic  8.05 us (7%)
  local copies, waits for them, and re-layouts  5.11 us (4%)
    ppermute x13, starting transfers between devices, pair(): return lax.ppermute(array, (axis, 'c'), moves)  20.5 us
    ppermute x13, waiting for transfers between devices, pair(): return lax.ppermute(array, (axis, 'c'), moves)  15.9 us
    pallas_call x3, Pallas kernels, backward(): pl.pallas_call(functools.partial(backward_kernel, count=len(weights)), in...  13.7 us
    ppermute x11, starting transfers between devices, swap(): return lax.ppermute(array, axis, [(a, last - a) for a in range(last + 1)])  10.4 us
    ppermute x3, starting transfers between devices, pair_z(): return lax.ppermute(array, ('zh', 'zl', 'c'), moves)  9.29 us
    ppermute x3, waiting for transfers between devices, pair_z(): return lax.ppermute(array, ('zh', 'zl', 'c'), moves)  5.37 us
    pallas_call x1, Pallas kernels, forward_last(): pl.pallas_call(forward_last_kernel, in_specs=[SMEM, HBM] + [VMEM] * 4 + [...  4.92 us
    pallas_call x2, Pallas kernels, grad_tiles(): pl.pallas_call(functools.partial(grad_kernel, side=side), out_shape=[jax....  4.71 us
  transfers between devices with their start and end apart: 29, of which 14 were waited for; matrix products, arithmetic and copies ran while one was open for 8% of the time, Pallas kernels for 25%

profile of v9, /device:TPU:1, one launch (start us, length us, event | category | flops | bytes accessed | tf_op | source)
XLA Modules:
  0.0 119.6 jit_solution(15442089139410923686)
XLA Ops:
  2.8 3.3 %collective-permute-start = (bf16[512,512]{1,0:T(8,128)(2,1)S(1)}, bf16[512,512]{1,0:T(8,128)(2,1)S(1)}, u32[]{:S(2)}, u32[]{:S(2)}) collective-permute-start(bf16[512,512]{1,0:T(8,128)(2,1)S(1)} %shard_map.84), channel_id=1, source_target_pairs={{0,1},{1,0},{2,3},{3,2},{4,5},{5,4},{6,7},{7,6},{8,9},{9,8},{10,11... | collective-permute-start | bytes 1572872 | tf_op jit(solution)/shard_map/ppermute | solution.py:272
  7.7 4.6 %shard_map.85 = (bf16[320,4096]{1,0:T(8,128)(2,1)S(1)}, bf16[320,4096]{1,0:T(8,128)(2,1)S(1)}, f32[320,1]{1,0:T(8,128)S(1)}) custom-call(s32[2,32]{1,0:T(2,128)S(1)} %pad_add_fusion.tab_ref, bf16[320,8192]{1,0:T(8,128)(2,1)} %tok_ref.11, f32[1,8192]{1,0:T(1,128)S(1)} %bitcast.52), custom_call_target="tpu_custom_call" | custom-call | flops 1 | bytes 1 | tf_op jit(solution)/shard_map/pallas_call | solution.py:70
  12.8 3.8 %collective-permute-start.1 = (bf16[512,512]{1,0:T(8,128)(2,1)S(1)}, bf16[512,512]{1,0:T(8,128)(2,1)S(1)}, u32[]{:S(2)}, u32[]{:S(2)}) collective-permute-start(bf16[512,512]{1,0:T(8,128)(2,1)S(1)} %shard_map.84), channel_id=1, source_target_pairs={{0,8},{1,57},{8,0},{9,17},{16,24},{17,9},{24,16},{25,33},{32,40},{... | collective-permute-start | bytes 1572872 | tf_op jit(solution)/shard_map/ppermute | solution.py:293
  18.3 2.4 %shard_map.86 = (bf16[16,256,128]{2,1,0:T(8,128)(2,1)S(1)}, f32[16,256,128]{2,1,0:T(8,128)S(1)}) custom-call(bf16[320,4096]{1,0:T(8,128)(2,1)S(1)} %get-tuple-element.58.own_ref, bf16[320,4096]{1,0:T(8,128)(2,1)S(1)} %collective-permute-done.2.got_ref, bf16[512,320]{1,0:T(8,128)(2,1)S(1)} %bitcast.49, bf16[512,320]{1,0:T(8,128)(2,1)S(1)} %collective-permute-done.3.cot_got_ref), custom_call_target="tpu_custom_call" | custom-call | flops 1 | bytes 1 | tf_op jit(solution)/shard_map/pallas_call | solution.py:112
  20.7 2.5 %collective-permute-done.1 = bf16[512,512]{1,0:T(8,128)(2,1)S(1)} collective-permute-done((bf16[512,512]{1,0:T(8,128)(2,1)S(1)}, bf16[512,512]{1,0:T(8,128)(2,1)S(1)}, u32[]{:S(2)}, u32[]{:S(2)}) %collective-permute-start.1) | collective-permute-done | bytes 524320 | tf_op jit(solution)/shard_map/ppermute | solution.py:293
  23.2 2.7 %collective-permute-start.7 = (bf16[16,256,128]{2,1,0:T(8,128)(2,1)S(1)}, bf16[16,256,128]{2,1,0:T(8,128)(2,1)S(1)}, u32[]{:S(2)}, u32[]{:S(2)}) collective-permute-start(bf16[16,256,128]{2,1,0:T(8,128)(2,1)S(1)} %get-tuple-element.63), channel_id=1, source_target_pairs={{0,64},{1,193},{64,0},{65,129},{128,192},{129,65},{192,128},{193,1... | collective-permute-start | bytes 3145736 | tf_op jit(solution)/shard_map/ppermute | solution.py:279
  25.9 2.5 %collective-permute-start.8 = (bf16[2,512,512]{2,1,0:T(8,128)(2,1)S(1)}, bf16[2,512,512]{2,1,0:T(8,128)(2,1)S(1)}, u32[]{:S(2)}, u32[]{:S(2)}) collective-permute-start(bf16[2,512,512]{2,1,0:T(8,128)(2,1)S(1)} %pad_maximum_fusion.refs_0_.base_ref), channel_id=1, source_target_pairs={{0,2},{1,7},{2,0},{3,5},{4,6},{5,3},{6,4},{7,1},{8,10},{9,15},{10,... | collective-permute-start | bytes 3145736 | tf_op jit(solution)/shard_map/ppermute | solution.py:279
  28.4 2.3 %shard_map.87 = (bf16[16,256,128]{2,1,0:T(8,128)(2,1)S(1)}, f32[16,256,128]{2,1,0:T(8,128)S(1)}) custom-call(bf16[320,4096]{1,0:T(8,128)(2,1)S(1)} %get-tuple-element.58.own_ref, bf16[320,4096]{1,0:T(8,128)(2,1)S(1)} %collective-permute-done.2.got_ref, bf16[512,320]{1,0:T(8,128)(2,1)S(1)} %bitcast.50, bf16[512,320]{1,0:T(8,128)(2,1)S(1)} %collective-permute-done.3.cot_got_ref), custom_call_target="tpu_custom_call" | custom-call | flops 1 | bytes 1 | tf_op jit(solution)/shard_map/pallas_call | solution.py:112
  30.8 2.8 %collective-permute-start.4 = (bf16[16,256,128]{2,1,0:T(8,128)(2,1)S(1)}, bf16[16,256,128]{2,1,0:T(8,128)(2,1)S(1)}, u32[]{:S(2)}, u32[]{:S(2)}) collective-permute-start(bf16[16,256,128]{2,1,0:T(8,128)(2,1)S(1)} %get-tuple-element.60), channel_id=1, source_target_pairs={{0,8},{1,57},{8,0},{9,17},{16,24},{17,9},{24,16},{25,33},{32,40},{... | collective-permute-start | bytes 3145736 | tf_op jit(solution)/shard_map/ppermute | solution.py:293
  33.5 4.6 %collective-permute-done.7 = bf16[16,256,128]{2,1,0:T(8,128)(2,1)S(1)} collective-permute-done((bf16[16,256,128]{2,1,0:T(8,128)(2,1)S(1)}, bf16[16,256,128]{2,1,0:T(8,128)(2,1)S(1)}, u32[]{:S(2)}, u32[]{:S(2)}) %collective-permute-start.7) | collective-permute-done | bytes 1048608 | tf_op jit(solution)/shard_map/ppermute | solution.py:279
  42.0 2.5 %collective-permute-start.10 = (bf16[2,512,512]{2,1,0:T(8,128)(2,1)}, bf16[2,512,512]{2,1,0:T(8,128)(2,1)}, u32[]{:S(2)}, u32[]{:S(2)}) collective-permute-start(bf16[2,512,512]{2,1,0:T(8,128)(2,1)} %pad_maximum_fusion.1.refs_1_), channel_id=1, source_target_pairs={{0,2},{1,7},{2,0},{3,5},{4,6},{5,3},{6,4},{7,1},{8,10},{9,15},{10,... | collective-permute-start | bytes 3145736 | tf_op jit(solution)/shard_map/ppermute | solution.py:279
  44.5 2.7 %collective-permute-start.12 = (bf16[8,256,128]{2,1,0:T(8,128)(2,1)S(1)}, bf16[8,256,128]{2,1,0:T(8,128)(2,1)}, u32[]{:S(2)}, u32[]{:S(2)}) collective-permute-start(bf16[8,256,128]{2,1,0:T(8,128)(2,1)S(1)} %get-tuple-element.66), channel_id=1, source_target_pairs={{0,8},{1,57},{8,0},{9,17},{16,24},{17,9},{24,16},{25,33},{32,40},{... | collective-permute-start | bytes 1572872 | tf_op jit(solution)/shard_map/ppermute | solution.py:293
  50.9 2.9 %collective-permute-done.12 = bf16[8,256,128]{2,1,0:T(8,128)(2,1)} collective-permute-done((bf16[8,256,128]{2,1,0:T(8,128)(2,1)S(1)}, bf16[8,256,128]{2,1,0:T(8,128)(2,1)}, u32[]{:S(2)}, u32[]{:S(2)}) %collective-permute-start.12) | collective-permute-done | bytes 524320 | tf_op jit(solution)/shard_map/ppermute | solution.py:293
  55.0 4.0 %shard_map.88.acc_in = f32[320,512]{1,0:T(8,128)S(1)} custom-call(s32[8]{0:T(128)S(1)} %stack.169.tab_ref, bf16[320,8192]{1,0:T(8,128)(2,1)} %tok_ref.11, f32[320,1]{1,0:T(8,128)S(1)} %get-tuple-element.54.inv_ref, f32[1,8192]{1,0:T(1,128)S(1)} %bitcast.53, bf16[2,512,512]{2,1,0:T(8,128)(2,1)} %copy-done.4, bf16[2,512,512]{2,1,0:T(8,128)(2,1)} %pad_maximum_fusion.1.refs_1_, ...), custom_call_target="tpu_custom_call" | custom-call | flops 1342177280 | bytes 9437184 | tf_op jit(solution)/shard_map/pallas_call | solution.py:226
  59.1 3.6 %collective-permute-done.11.far_ref.refs_2_ = bf16[1,512,512]{2,1,0:T(8,128)(2,1)S(1)} collective-permute-done((bf16[1,512,512]{2,1,0:T(8,128)(2,1)}, bf16[1,512,512]{2,1,0:T(8,128)(2,1)S(1)}, u32[]{:S(2)}, u32[]{:S(2)}) %collective-permute-start.11) | collective-permute-done | bytes 524320 | tf_op jit(solution)/shard_map/ppermute | solution.py:279
  66.9 2.6 %collective-permute-start.16 = (bf16[1,512,512]{2,1,0:T(8,128)(2,1)S(1)}, bf16[1,512,512]{2,1,0:T(8,128)(2,1)S(1)}, u32[]{:S(2)}, u32[]{:S(2)}) collective-permute-start(bf16[1,512,512]{2,1,0:T(8,128)(2,1)S(1)} %slice.91), channel_id=1, source_target_pairs={{0,2},{1,7},{2,0},{3,5},{4,6},{5,3},{6,4},{7,1},{8,10},{9,15},{10,... | collective-permute-start | bytes 1572872 | tf_op jit(solution)/shard_map/ppermute | solution.py:279
  69.6 3.1 %collective-permute-done.13 = bf16[2,4,256,128]{3,2,1,0:T(8,128)(2,1)S(1)} collective-permute-done((bf16[2,4,256,128]{3,2,1,0:T(8,128)(2,1)S(1)}, bf16[2,4,256,128]{3,2,1,0:T(8,128)(2,1)S(1)}, u32[]{:S(2)}, u32[]{:S(2)}) %collective-permute-start.13) | collective-permute-done | bytes 524320 | tf_op jit(solution)/shard_map/ppermute | solution.py:279
  76.4 2.3 %collective-permute-start.17 = (bf16[1,512,512]{2,1,0:T(8,128)(2,1)S(1)}, bf16[1,512,512]{2,1,0:T(8,128)(2,1)S(1)}, u32[]{:S(2)}, u32[]{:S(2)}) collective-permute-start(bf16[1,512,512]{2,1,0:T(8,128)(2,1)S(1)} %collective-permute-done.16.refs_3_.refs_1_), channel_id=1, source_target_pairs={{0,1},{1,0},{2,3},{3,2},{4,5},{5,4},{6,7},{7,6},{8,9},{9,8},{10,11... | collective-permute-start | bytes 1572872 | tf_op jit(solution)/shard_map/ppermute | solution.py:272
  82.7 4.9 %shard_map.90 = (bf16[320,512]{1,0:T(8,128)(2,1)}, f32[320,1]{1,0:T(8,128)S(1)}) custom-call(s32[8]{0:T(128)S(1)} %stack.156.tab_ref, bf16[320,8192]{1,0:T(8,128)(2,1)} %tok_ref.11, f32[320,1]{1,0:T(8,128)S(1)} %get-tuple-element.54.inv_ref, f32[1,8192]{1,0:T(1,128)S(1)} %bitcast.55, bf16[320,512]{1,0:T(8,128)(2,1)S(1)} %copy-done, ...), custom_call_target="tpu_custom_call" | custom-call | flops 1342177280 | bytes 9437184 | tf_op jit(solution)/shard_map/pallas_call | solution.py:238
  88.5 2.5 %collective-permute-start.21 = (bf16[528,128]{1,0:T(8,128)(2,1)S(1)}, bf16[528,128]{1,0:T(8,128)(2,1)S(1)}, u32[]{:S(2)}, u32[]{:S(2)}) collective-permute-start(bf16[528,128]{1,0:T(8,128)(2,1)S(1)} %shard_map.91.refs_0_), channel_id=1, source_target_pairs={{0,16},{1,49},{16,0},{17,33},{32,48},{33,17},{48,32},{49,1},{2,18}... | collective-permute-start | bytes 405512 | tf_op jit(solution)/shard_map/ppermute | solution.py:279
  91.1 4.8 %shard_map.92.refs_3_ = bf16[320,8192]{1,0:T(8,128)(2,1)} custom-call(s32[6]{0:T(128)S(1)} %stack.179.tab_ref, bf16[320,8192]{1,0:T(8,128)(2,1)} %tok_ref.11, f32[320,1]{1,0:T(8,128)S(1)} %get-tuple-element.54.inv_ref, f32[1,8192]{1,0:T(1,128)S(1)} %bitcast.56, bf16[320,512]{1,0:T(8,128)(2,1)S(1)} %copy-done, f32[320,1]{1,0:T(8,128)S(1)} %get-tuple-element.87.moment_ref, ...), custom_call_target="tpu_custom_call" | custom-call | flops 1342177280 | bytes 9437184 | tf_op jit(solution)/shard_map/pallas_call | solution.py:255
  98.3 4.4 %shard_map.94.refs_4_ = bf16[320,8192]{1,0:T(8,128)(2,1)} custom-call(s32[5]{0:T(128)S(1)} %stack.180.tab_ref, bf16[320,8192]{1,0:T(8,128)(2,1)} %tok_ref.11, f32[320,1]{1,0:T(8,128)S(1)} %get-tuple-element.54.inv_ref, f32[1,8192]{1,0:T(1,128)S(1)} %bitcast.57, bf16[320,512]{1,0:T(8,128)(2,1)S(1)} %copy-done, ...), custom_call_target="tpu_custom_call", output_to_operand_aliasing={{}: (9, {})} | custom-call | flops 1342177280 | bytes 9437184 | tf_op jit(solution)/shard_map/pallas_call | solution.py:255
  106.3 4.4 %shard_map.96 = bf16[320,8192]{1,0:T(8,128)(2,1)} custom-call(s32[5]{0:T(128)S(1)} %stack.181.tab_ref, bf16[320,8192]{1,0:T(8,128)(2,1)} %tok_ref.11, f32[320,1]{1,0:T(8,128)S(1)} %get-tuple-element.54.inv_ref, f32[1,8192]{1,0:T(1,128)S(1)} %bitcast.58, bf16[320,512]{1,0:T(8,128)(2,1)S(1)} %copy-done, ...), custom_call_target="tpu_custom_call", output_to_operand_aliasing={{}: (10, {})} | custom-call | flops 1342177280 | bytes 9437184 | tf_op jit(solution)/shard_map/pallas_call | solution.py:255
  110.8 2.3 %collective-permute-done.23.refs_1_ = bf16[528,128]{1,0:T(8,128)(2,1)S(1)} collective-permute-done((bf16[528,128]{1,0:T(8,128)(2,1)S(1)}, bf16[528,128]{1,0:T(8,128)(2,1)S(1)}, u32[]{:S(2)}, u32[]{:S(2)}) %collective-permute-start.23) | collective-permute-done | bytes 135200 | tf_op jit(solution)/shard_map/ppermute | solution.py:279
  (100 shorter events, 40.0 us)
Async XLA Ops:
  2.8 4.9 %collective-permute-start = (bf16[512,512]{1,0:T(8,128)(2,1)S(1)}, bf16[512,512]{1,0:T(8,128)(2,1)S(1)}, u32[]{:S(2)}, u32[]{:S(2)}) collective-permute-start(bf16[512,512]{1,0:T(8,128)(2,1)S(1)} %shard_map.84), channel_id=1, source_target_pairs={{0,1},{1,0},{2,3},{3,2},{4,5},{5,4},{6,7},{7,6},{8,9},{9,8},{10,11... | collective-permute-start | bytes 1572872 | tf_op jit(solution)/shard_map/ppermute | solution.py:272
  12.3 6.0 %collective-permute-start.2 = (bf16[320,4096]{1,0:T(8,128)(2,1)S(1)}, bf16[320,4096]{1,0:T(8,128)(2,1)S(1)}, u32[]{:S(2)}, u32[]{:S(2)}) collective-permute-start(bf16[320,4096]{1,0:T(8,128)(2,1)S(1)} %get-tuple-element.56), channel_id=1, source_target_pairs={{0,1},{1,0},{2,3},{3,2},{4,5},{5,4},{6,7},{7,6},{8,9},{9,8},{10,11... | collective-permute-start | bytes 7864328 | tf_op jit(solution)/shard_map/ppermute | solution.py:272
  12.8 10.4 %collective-permute-start.1 = (bf16[512,512]{1,0:T(8,128)(2,1)S(1)}, bf16[512,512]{1,0:T(8,128)(2,1)S(1)}, u32[]{:S(2)}, u32[]{:S(2)}) collective-permute-start(bf16[512,512]{1,0:T(8,128)(2,1)S(1)} %shard_map.84), channel_id=1, source_target_pairs={{0,8},{1,57},{8,0},{9,17},{16,24},{17,9},{24,16},{25,33},{32,40},{... | collective-permute-start | bytes 1572872 | tf_op jit(solution)/shard_map/ppermute | solution.py:293
  23.2 14.9 %collective-permute-start.7 = (bf16[16,256,128]{2,1,0:T(8,128)(2,1)S(1)}, bf16[16,256,128]{2,1,0:T(8,128)(2,1)S(1)}, u32[]{:S(2)}, u32[]{:S(2)}) collective-permute-start(bf16[16,256,128]{2,1,0:T(8,128)(2,1)S(1)} %get-tuple-element.63), channel_id=1, source_target_pairs={{0,64},{1,193},{64,0},{65,129},{128,192},{129,65},{192,128},{193,1... | collective-permute-start | bytes 3145736 | tf_op jit(solution)/shard_map/ppermute | solution.py:279
  25.9 14.9 %collective-permute-start.8 = (bf16[2,512,512]{2,1,0:T(8,128)(2,1)S(1)}, bf16[2,512,512]{2,1,0:T(8,128)(2,1)S(1)}, u32[]{:S(2)}, u32[]{:S(2)}) collective-permute-start(bf16[2,512,512]{2,1,0:T(8,128)(2,1)S(1)} %pad_maximum_fusion.refs_0_.base_ref), channel_id=1, source_target_pairs={{0,2},{1,7},{2,0},{3,5},{4,6},{5,3},{6,4},{7,1},{8,10},{9,15},{10,... | collective-permute-start | bytes 3145736 | tf_op jit(solution)/shard_map/ppermute | solution.py:279
  28.4 12.4 %collective-permute-start.6 = (bf16[512,512]{1,0:T(8,128)(2,1)S(1)}, bf16[512,512]{1,0:T(8,128)(2,1)S(1)}, u32[]{:S(2)}, u32[]{:S(2)}) collective-permute-start(bf16[512,512]{1,0:T(8,128)(2,1)S(1)} %collective-permute-done.1), channel_id=1, source_target_pairs={{0,1},{1,0},{2,3},{3,2},{4,5},{5,4},{6,7},{7,6},{8,9},{9,8},{10,11... | collective-permute-start | bytes 1572872 | tf_op jit(solution)/shard_map/ppermute | solution.py:272
  30.8 16.4 %collective-permute-start.4 = (bf16[16,256,128]{2,1,0:T(8,128)(2,1)S(1)}, bf16[16,256,128]{2,1,0:T(8,128)(2,1)S(1)}, u32[]{:S(2)}, u32[]{:S(2)}) collective-permute-start(bf16[16,256,128]{2,1,0:T(8,128)(2,1)S(1)} %get-tuple-element.60), channel_id=1, source_target_pairs={{0,8},{1,57},{8,0},{9,17},{16,24},{17,9},{24,16},{25,33},{32,40},{... | collective-permute-start | bytes 3145736 | tf_op jit(solution)/shard_map/ppermute | solution.py:293
  40.8 9.0 %collective-permute-start.9 = (bf16[2,512,512]{2,1,0:T(8,128)(2,1)S(1)}, bf16[2,512,512]{2,1,0:T(8,128)(2,1)S(1)}, u32[]{:S(2)}, u32[]{:S(2)}) collective-permute-start(bf16[2,512,512]{2,1,0:T(8,128)(2,1)S(1)} %collective-permute-done.8.refs_2_.near_ref), channel_id=1, source_target_pairs={{0,1},{1,0},{2,3},{3,2},{4,5},{5,4},{6,7},{7,6},{8,9},{9,8},{10,11... | collective-permute-start | bytes 3145736 | tf_op jit(solution)/shard_map/ppermute | solution.py:272
  42.0 17.0 %collective-permute-start.10 = (bf16[2,512,512]{2,1,0:T(8,128)(2,1)}, bf16[2,512,512]{2,1,0:T(8,128)(2,1)}, u32[]{:S(2)}, u32[]{:S(2)}) collective-permute-start(bf16[2,512,512]{2,1,0:T(8,128)(2,1)} %pad_maximum_fusion.1.refs_1_), channel_id=1, source_target_pairs={{0,2},{1,7},{2,0},{3,5},{4,6},{5,3},{6,4},{7,1},{8,10},{9,15},{10,... | collective-permute-start | bytes 3145736 | tf_op jit(solution)/shard_map/ppermute | solution.py:279
  44.5 9.3 %collective-permute-start.12 = (bf16[8,256,128]{2,1,0:T(8,128)(2,1)S(1)}, bf16[8,256,128]{2,1,0:T(8,128)(2,1)}, u32[]{:S(2)}, u32[]{:S(2)}) collective-permute-start(bf16[8,256,128]{2,1,0:T(8,128)(2,1)S(1)} %get-tuple-element.66), channel_id=1, source_target_pairs={{0,8},{1,57},{8,0},{9,17},{16,24},{17,9},{24,16},{25,33},{32,40},{... | collective-permute-start | bytes 1572872 | tf_op jit(solution)/shard_map/ppermute | solution.py:293
  48.6 10.5 %collective-permute-start.5 = (bf16[8,256,128]{2,1,0:T(8,128)(2,1)}, bf16[8,256,128]{2,1,0:T(8,128)(2,1)}, u32[]{:S(2)}, u32[]{:S(2)}) collective-permute-start(bf16[8,256,128]{2,1,0:T(8,128)(2,1)} %get-tuple-element.107), channel_id=1, source_target_pairs={{0,64},{1,193},{64,0},{65,129},{128,192},{129,65},{192,128},{193,1... | collective-permute-start | bytes 1572872 | tf_op jit(solution)/shard_map/ppermute | solution.py:279
  50.7 12.0 %collective-permute-start.11 = (bf16[1,512,512]{2,1,0:T(8,128)(2,1)}, bf16[1,512,512]{2,1,0:T(8,128)(2,1)S(1)}, u32[]{:S(2)}, u32[]{:S(2)}) collective-permute-start(bf16[1,512,512]{2,1,0:T(8,128)(2,1)} %slice.82), channel_id=1, source_target_pairs={{0,2},{1,7},{2,0},{3,5},{4,6},{5,3},{6,4},{7,1},{8,10},{9,15},{10,... | collective-permute-start | bytes 1572872 | tf_op jit(solution)/shard_map/ppermute | solution.py:279
  64.4 8.3 %collective-permute-start.13 = (bf16[2,4,256,128]{3,2,1,0:T(8,128)(2,1)S(1)}, bf16[2,4,256,128]{3,2,1,0:T(8,128)(2,1)S(1)}, u32[]{:S(2)}, u32[]{:S(2)}) collective-permute-start(bf16[2,4,256,128]{3,2,1,0:T(8,128)(2,1)S(1)} %pad_maximum_fusion.3), channel_id=1, source_target_pairs={{0,192},{1,65},{64,128},{65,1},{128,64},{129,193},{192,0},{193,129... | collective-permute-start | bytes 1572872 | tf_op jit(solution)/shard_map/ppermute | solution.py:279
  64.4 8.3 %collective-permute-start.14 = (bf16[1,512,512]{2,1,0:T(8,128)(2,1)S(1)}, bf16[1,512,512]{2,1,0:T(8,128)(2,1)S(1)}, u32[]{:S(2)}, u32[]{:S(2)}) collective-permute-start(bf16[1,512,512]{2,1,0:T(8,128)(2,1)S(1)} %collective-permute-done.11.far_ref.refs_2_), channel_id=1, source_target_pairs={{0,1},{1,0},{2,3},{3,2},{4,5},{5,4},{6,7},{7,6},{8,9},{9,8},{10,11... | collective-permute-start | bytes 1572872 | tf_op jit(solution)/shard_map/ppermute | solution.py:272
  66.9 9.4 %collective-permute-start.16 = (bf16[1,512,512]{2,1,0:T(8,128)(2,1)S(1)}, bf16[1,512,512]{2,1,0:T(8,128)(2,1)S(1)}, u32[]{:S(2)}, u32[]{:S(2)}) collective-permute-start(bf16[1,512,512]{2,1,0:T(8,128)(2,1)S(1)} %slice.91), channel_id=1, source_target_pairs={{0,2},{1,7},{2,0},{3,5},{4,6},{5,3},{6,4},{7,1},{8,10},{9,15},{10,... | collective-permute-start | bytes 1572872 | tf_op jit(solution)/shard_map/ppermute | solution.py:279
  76.4 5.5 %collective-permute-start.17 = (bf16[1,512,512]{2,1,0:T(8,128)(2,1)S(1)}, bf16[1,512,512]{2,1,0:T(8,128)(2,1)S(1)}, u32[]{:S(2)}, u32[]{:S(2)}) collective-permute-start(bf16[1,512,512]{2,1,0:T(8,128)(2,1)S(1)} %collective-permute-done.16.refs_3_.refs_1_), channel_id=1, source_target_pairs={{0,1},{1,0},{2,3},{3,2},{4,5},{5,4},{6,7},{7,6},{8,9},{9,8},{10,11... | collective-permute-start | bytes 1572872 | tf_op jit(solution)/shard_map/ppermute | solution.py:272
  78.7 8.9 %collective-permute-start.20 = (bf16[528,128]{1,0:T(8,128)(2,1)S(1)}, bf16[528,128]{1,0:T(8,128)(2,1)S(1)}, u32[]{:S(2)}, u32[]{:S(2)}) collective-permute-start(bf16[528,128]{1,0:T(8,128)(2,1)S(1)} %get-tuple-element.82), channel_id=1, source_target_pairs={{0,4},{2,6},{4,0},{6,2},{1,5},{3,7},{5,1},{7,3},{8,12},{10,14},{12... | collective-permute-start | bytes 405512 | tf_op jit(solution)/shard_map/ppermute | solution.py:284
  80.6 7.1 %collective-permute-start.18 = (bf16[528,128]{1,0:T(8,128)(2,1)S(1)}, bf16[528,128]{1,0:T(8,128)(2,1)S(1)}, u32[]{:S(2)}, u32[]{:S(2)}) collective-permute-start(bf16[528,128]{1,0:T(8,128)(2,1)S(1)} %get-tuple-element.80), channel_id=1, source_target_pairs={{0,2},{1,7},{2,0},{3,5},{4,6},{5,3},{6,4},{7,1},{8,10},{9,15},{10,... | collective-permute-start | bytes 405512 | tf_op jit(solution)/shard_map/ppermute | solution.py:279
  81.4 7.1 %collective-permute-start.19 = (bf16[528,128]{1,0:T(8,128)(2,1)S(1)}, bf16[528,128]{1,0:T(8,128)(2,1)S(1)}, u32[]{:S(2)}, u32[]{:S(2)}) collective-permute-start(bf16[528,128]{1,0:T(8,128)(2,1)S(1)} %get-tuple-element.81), channel_id=1, source_target_pairs={{0,6},{1,3},{2,4},{3,1},{4,2},{5,7},{6,0},{7,5},{8,14},{9,11},{10,... | collective-permute-start | bytes 405512 | tf_op jit(solution)/shard_map/ppermute | solution.py:279
  88.5 7.5 %collective-permute-start.21 = (bf16[528,128]{1,0:T(8,128)(2,1)S(1)}, bf16[528,128]{1,0:T(8,128)(2,1)S(1)}, u32[]{:S(2)}, u32[]{:S(2)}) collective-permute-start(bf16[528,128]{1,0:T(8,128)(2,1)S(1)} %shard_map.91.refs_0_), channel_id=1, source_target_pairs={{0,16},{1,49},{16,0},{17,33},{32,48},{33,17},{48,32},{49,1},{2,18}... | collective-permute-start | bytes 405512 | tf_op jit(solution)/shard_map/ppermute | solution.py:279
  96.0 6.7 %collective-permute-start.22 = (bf16[528,128]{1,0:T(8,128)(2,1)S(1)}, bf16[528,128]{1,0:T(8,128)(2,1)S(1)}, u32[]{:S(2)}, u32[]{:S(2)}) collective-permute-start(bf16[528,128]{1,0:T(8,128)(2,1)S(1)} %shard_map.93.refs_0_), channel_id=1, source_target_pairs={{0,48},{1,17},{16,32},{17,1},{32,16},{33,49},{48,0},{49,33},{2,50}... | collective-permute-start | bytes 405512 | tf_op jit(solution)/shard_map/ppermute | solution.py:279
  102.8 8.0 %collective-permute-start.25 = (bf16[528,128]{1,0:T(8,128)(2,1)S(1)}, bf16[528,128]{1,0:T(8,128)(2,1)S(1)}, u32[]{:S(2)}, u32[]{:S(2)}) collective-permute-start(bf16[528,128]{1,0:T(8,128)(2,1)S(1)} %shard_map.95.refs_0_), channel_id=1, source_target_pairs={{0,128},{64,192},{128,0},{192,64},{1,129},{65,193},{129,1},{193,65... | collective-permute-start | bytes 405512 | tf_op jit(solution)/shard_map/ppermute | solution.py:284
  103.2 7.6 %collective-permute-start.24 = (bf16[528,128]{1,0:T(8,128)(2,1)S(1)}, bf16[528,128]{1,0:T(8,128)(2,1)S(1)}, u32[]{:S(2)}, u32[]{:S(2)}) collective-permute-start(bf16[528,128]{1,0:T(8,128)(2,1)S(1)} %shard_map.95.refs_0_), channel_id=1, source_target_pairs={{0,192},{1,65},{64,128},{65,1},{128,64},{129,193},{192,0},{193,129... | collective-permute-start | bytes 405512 | tf_op jit(solution)/shard_map/ppermute | solution.py:279
  105.3 7.8 %collective-permute-start.23 = (bf16[528,128]{1,0:T(8,128)(2,1)S(1)}, bf16[528,128]{1,0:T(8,128)(2,1)S(1)}, u32[]{:S(2)}, u32[]{:S(2)}) collective-permute-start(bf16[528,128]{1,0:T(8,128)(2,1)S(1)} %shard_map.95.refs_0_), channel_id=1, source_target_pairs={{0,64},{1,193},{64,0},{65,129},{128,192},{129,65},{192,128},{193,1... | collective-permute-start | bytes 405512 | tf_op jit(solution)/shard_map/ppermute | solution.py:279
  (19 other events, 108.8 us)

commit v10 on v9

--- a/solution.py
+++ b/solution.py
@@ -451,14 +451,15 @@
         at = [((zl ^ z) * 4 + (x ^ offset(c, k % 2, k // 2))) * 2 + (c ^ lane) for z, k, lane in pieces]
         return jnp.stack(at).astype(jnp.int32)
 
-    own = widen_weight(weight_values, weight_scale)
+    mine, other, inverse = norm_tiles(tokens, gain, jnp.stack(tables))
+    got = swap(other, "c")
+
+    own = widen_weight(tie(weight_values, inverse), weight_scale)
     own_c = swap(own, "c")
     up = pair_z(own)
-    cot_own = key_cotangent.T
+    cot_own = tie(key_cotangent, inverse).T
     base = jnp.stack([own, own_c])
     cot_got = swap(cot_own, "c")
-    mine, other, inverse = norm_tiles(tokens, gain, tie(jnp.stack(tables), base, cot_own))
-    got = swap(other, "c")
     near = pair(base, "x", 0)
 
     first, kept_first = grad_tiles(mine, got, cot_own, cot_got, 0)
@@ -477,12 +478,12 @@
     far = pair(near_c[1:], "x", 0)
     early = [base, above, near, near_c]
     sums = forward(tokens, inverse, gain, early, nodes_of(BASE + ABOVE + NEAR + NEAR_C))
-    moved[1], sums, above_near, far = lax.optimization_barrier((moved[1], sums, above_near, far))
+    moved[1], sums, above_near = lax.optimization_barrier((moved[1], sums, above_near))
     (first, kept_first), (second, kept_second) = map(
         add_halves, (kept_first, kept_second), moved
     )
 
-    send, above_near, far = lax.optimization_barrier((jnp.stack([first, second]), above_near, far))
+    send, above_near = lax.optimization_barrier((jnp.stack([first, second]), above_near))
     moved = pair(send, "y", 1)
     above_near_c = swap(above_near, "c")
     above_far = pair(above_near_c[1:], "x", 0)

time: 120 us -> 125 us (1.042)
  starting transfers between devices: 42.4 us -> 36.2 us
  waiting for transfers between devices: 25.5 us -> 31.6 us
  Pallas kernels: 37.5 us -> 43.2 us
    ppermute x13, waiting for transfers between devices: 15.9 us -> 21.5 us  [pair(): return lax.ppermute(array, (axis, 'c'), moves)]
    pallas_call x2, Pallas kernels: 4.71 us -> 8.14 us  [grad_tiles(): pl.pallas_call(functools.partial(grad_kernel, side=side), out_shape=[jax....]
    ppermute x11, starting transfers between devices: 10.4 us -> 6.95 us  [swap(): return lax.ppermute(array, axis, [(a, last - a) for a in range(last + 1)])]
    ppermute x13, starting transfers between devices: 20.5 us -> 17.8 us  [pair(): return lax.ppermute(array, (axis, 'c'), moves)]
    pallas_call x1, Pallas kernels: 4.56 us -> 6.04 us  [norm_tiles(): pl.pallas_call(norm_kernel, in_specs=[SMEM, HBM, VMEM], out_specs=[VMEM]...]
    unnamed x29 -> x22, local copies, waits for them, and re-layouts: 3.75 us -> 2.58 us
  transfers between devices with their start and end apart: 29 -> 29, of which waited for: 14 -> 12; matrix products, arithmetic and copies ran while one was open for 8% -> 7% of each run, Pallas kernels for 25% -> 27%
where the time goes in v10:
time: 125 us
  Pallas kernels  43.2 us (35%)
  starting transfers between devices  36.2 us (29%)
  waiting for transfers between devices  31.6 us (25%)
  other arithmetic  8.59 us (7%)
  local copies, waits for them, and re-layouts  4.33 us (3%)
    ppermute x13, waiting for transfers between devices, pair(): return lax.ppermute(array, (axis, 'c'), moves)  21.5 us
    ppermute x13, starting transfers between devices, pair(): return lax.ppermute(array, (axis, 'c'), moves)  17.8 us
    pallas_call x3, Pallas kernels, backward(): pl.pallas_call(functools.partial(backward_kernel, count=len(weights)), in...  13.7 us
    ppermute x3, starting transfers between devices, pair_z(): return lax.ppermute(array, ('zh', 'zl', 'c'), moves)  9.26 us
    pallas_call x2, Pallas kernels, grad_tiles(): pl.pallas_call(functools.partial(grad_kernel, side=side), out_shape=[jax....  8.14 us
    ppermute x11, starting transfers between devices, swap(): return lax.ppermute(array, axis, [(a, last - a) for a in range(last + 1)])  6.95 us
    pallas_call x1, Pallas kernels, norm_tiles(): pl.pallas_call(norm_kernel, in_specs=[SMEM, HBM, VMEM], out_specs=[VMEM]...  6.04 us
    ppermute x11, waiting for transfers between devices, swap(): return lax.ppermute(array, axis, [(a, last - a) for a in range(last + 1)])  5.11 us
  transfers between devices with their start and end apart: 29, of which 12 were waited for; matrix products, arithmetic and copies ran while one was open for 7% of the time, Pallas kernels for 27%

profile of v10, /device:TPU:1, one launch (start us, length us, event | category | flops | bytes accessed | tf_op | source)
XLA Modules:
  0.0 124.9 jit_solution(6208819674607642498)
XLA Ops:
  1.5 6.0 %shard_map.84 = (bf16[320,4096]{1,0:T(8,128)(2,1)S(1)}, bf16[320,4096]{1,0:T(8,128)(2,1)}, f32[320,1]{1,0:T(8,128)S(1)}) custom-call(s32[2,32]{1,0:T(2,128)S(1)} %pad_add_fusion.tab_ref, bf16[320,8192]{1,0:T(8,128)(2,1)} %tok_ref.11, f32[1,8192]{1,0:T(1,128)S(1)} %bitcast.51), custom_call_target="tpu_custom_call" | custom-call | flops 1 | bytes 1 | tf_op jit(solution)/shard_map/pallas_call | solution.py:70
  7.5 3.3 %collective-permute-start.1 = (bf16[320,4096]{1,0:T(8,128)(2,1)}, bf16[320,4096]{1,0:T(8,128)(2,1)}, u32[]{:S(2)}, u32[]{:S(2)}) collective-permute-start(bf16[320,4096]{1,0:T(8,128)(2,1)} %get-tuple-element.55), channel_id=1, source_target_pairs={{0,1},{1,0},{2,3},{3,2},{4,5},{5,4},{6,7},{7,6},{8,9},{9,8},{10,11... | collective-permute-start | bytes 7864328 | tf_op jit(solution)/shard_map/ppermute | solution.py:272
  12.0 3.8 %collective-permute-start = (bf16[512,512]{1,0:T(8,128)(2,1)}, bf16[512,512]{1,0:T(8,128)(2,1)}, u32[]{:S(2)}, u32[]{:S(2)}) collective-permute-start(bf16[512,512]{1,0:T(8,128)(2,1)} %shard_map.85), channel_id=1, source_target_pairs={{0,8},{1,57},{8,0},{9,17},{16,24},{17,9},{24,16},{25,33},{32,40},{... | collective-permute-start | bytes 1572872 | tf_op jit(solution)/shard_map/ppermute | solution.py:293
  18.3 4.1 %shard_map.86 = (bf16[16,256,128]{2,1,0:T(8,128)(2,1)S(1)}, f32[16,256,128]{2,1,0:T(8,128)S(1)}) custom-call(bf16[320,4096]{1,0:T(8,128)(2,1)S(1)} %get-tuple-element.58.own_ref, bf16[320,4096]{1,0:T(8,128)(2,1)} %collective-permute-done.1.got_ref, bf16[512,320]{1,0:T(8,128)(2,1)S(1)} %bitcast.49, bf16[512,320]{1,0:T(8,128)(2,1)S(1)} %collective-permute-done.2.cot_got_ref), custom_call_target="tpu_custom_call" | custom-call | flops 1 | bytes 1 | tf_op jit(solution)/shard_map/pallas_call | solution.py:112
  22.7 2.7 %collective-permute-start.7 = (bf16[16,256,128]{2,1,0:T(8,128)(2,1)S(1)}, bf16[16,256,128]{2,1,0:T(8,128)(2,1)S(1)}, u32[]{:S(2)}, u32[]{:S(2)}) collective-permute-start(bf16[16,256,128]{2,1,0:T(8,128)(2,1)S(1)} %get-tuple-element.63), channel_id=1, source_target_pairs={{0,64},{1,193},{64,0},{65,129},{128,192},{129,65},{192,128},{193,1... | collective-permute-start | bytes 3145736 | tf_op jit(solution)/shard_map/ppermute | solution.py:279
  26.8 2.6 %collective-permute-start.8 = (bf16[2,512,512]{2,1,0:T(8,128)(2,1)S(1)}, bf16[2,512,512]{2,1,0:T(8,128)(2,1)}, u32[]{:S(2)}, u32[]{:S(2)}) collective-permute-start(bf16[2,512,512]{2,1,0:T(8,128)(2,1)S(1)} %pad_maximum_fusion.refs_0_.base_ref), channel_id=1, source_target_pairs={{0,2},{1,7},{2,0},{3,5},{4,6},{5,3},{6,4},{7,1},{8,10},{9,15},{10,... | collective-permute-start | bytes 3145736 | tf_op jit(solution)/shard_map/ppermute | solution.py:279
  29.4 4.1 %shard_map.87 = (bf16[16,256,128]{2,1,0:T(8,128)(2,1)S(1)}, f32[16,256,128]{2,1,0:T(8,128)S(1)}) custom-call(bf16[320,4096]{1,0:T(8,128)(2,1)S(1)} %get-tuple-element.58.own_ref, bf16[320,4096]{1,0:T(8,128)(2,1)} %collective-permute-done.1.got_ref, bf16[512,320]{1,0:T(8,128)(2,1)S(1)} %bitcast.50, bf16[512,320]{1,0:T(8,128)(2,1)S(1)} %collective-permute-done.2.cot_got_ref), custom_call_target="tpu_custom_call" | custom-call | flops 1 | bytes 1 | tf_op jit(solution)/shard_map/pallas_call | solution.py:112
  33.4 2.7 %collective-permute-start.3 = (bf16[16,256,128]{2,1,0:T(8,128)(2,1)S(1)}, bf16[16,256,128]{2,1,0:T(8,128)(2,1)S(1)}, u32[]{:S(2)}, u32[]{:S(2)}) collective-permute-start(bf16[16,256,128]{2,1,0:T(8,128)(2,1)S(1)} %get-tuple-element.60), channel_id=1, source_target_pairs={{0,8},{1,57},{8,0},{9,17},{16,24},{17,9},{24,16},{25,33},{32,40},{... | collective-permute-start | bytes 3145736 | tf_op jit(solution)/shard_map/ppermute | solution.py:293
  37.9 4.0 %collective-permute-done.8.refs_2_.near_ref = bf16[2,512,512]{2,1,0:T(8,128)(2,1)} collective-permute-done((bf16[2,512,512]{2,1,0:T(8,128)(2,1)S(1)}, bf16[2,512,512]{2,1,0:T(8,128)(2,1)}, u32[]{:S(2)}, u32[]{:S(2)}) %collective-permute-start.8) | collective-permute-done | bytes 1048608 | tf_op jit(solution)/shard_map/ppermute | solution.py:279
  41.8 2.1 %pad_maximum_fusion.1.refs_1_ = bf16[2,512,512]{2,1,0:T(8,128)(2,1)} fusion(bf16[1,512,512]{2,1,0:T(8,128)(2,1)S(1)} %bitcast.59, bf16[1,512,512]{2,1,0:T(8,128)(2,1)} %bitcast.21), kind=kLoop, calls=%fused_computation.1 | loop fusion | flops 524288 | bytes 2097152 | tf_op jit(solution)/shard_map/stack | solution.py:469
  44.0 2.5 %collective-permute-start.10 = (bf16[2,512,512]{2,1,0:T(8,128)(2,1)}, bf16[2,512,512]{2,1,0:T(8,128)(2,1)}, u32[]{:S(2)}, u32[]{:S(2)}) collective-permute-start(bf16[2,512,512]{2,1,0:T(8,128)(2,1)} %pad_maximum_fusion.1.refs_1_), channel_id=1, source_target_pairs={{0,2},{1,7},{2,0},{3,5},{4,6},{5,3},{6,4},{7,1},{8,10},{9,15},{10,... | collective-permute-start | bytes 3145736 | tf_op jit(solution)/shard_map/ppermute | solution.py:279
  46.4 2.7 %collective-permute-start.11 = (bf16[8,256,128]{2,1,0:T(8,128)(2,1)S(1)}, bf16[8,256,128]{2,1,0:T(8,128)(2,1)}, u32[]{:S(2)}, u32[]{:S(2)}) collective-permute-start(bf16[8,256,128]{2,1,0:T(8,128)(2,1)S(1)} %get-tuple-element.66), channel_id=1, source_target_pairs={{0,8},{1,57},{8,0},{9,17},{16,24},{17,9},{24,16},{25,33},{32,40},{... | collective-permute-start | bytes 1572872 | tf_op jit(solution)/shard_map/ppermute | solution.py:293
  51.2 4.6 %collective-permute-done.11 = bf16[8,256,128]{2,1,0:T(8,128)(2,1)} collective-permute-done((bf16[8,256,128]{2,1,0:T(8,128)(2,1)S(1)}, bf16[8,256,128]{2,1,0:T(8,128)(2,1)}, u32[]{:S(2)}, u32[]{:S(2)}) %collective-permute-start.11) | collective-permute-done | bytes 524320 | tf_op jit(solution)/shard_map/ppermute | solution.py:293
  57.9 4.0 %shard_map.88.acc_in = f32[320,512]{1,0:T(8,128)S(1)} custom-call(s32[8]{0:T(128)S(1)} %stack.166.tab_ref, bf16[320,8192]{1,0:T(8,128)(2,1)} %tok_ref.11, f32[320,1]{1,0:T(8,128)S(1)} %get-tuple-element.52.inv_ref, f32[1,8192]{1,0:T(1,128)S(1)} %bitcast.52, bf16[2,512,512]{2,1,0:T(8,128)(2,1)} %copy-done.5, bf16[2,512,512]{2,1,0:T(8,128)(2,1)} %pad_maximum_fusion.1.refs_1_, ...), custom_call_target="tpu_custom_call" | custom-call | flops 1342177280 | bytes 9437184 | tf_op jit(solution)/shard_map/pallas_call | solution.py:226
  64.7 9.1 %collective-permute-done.13.far_ref.refs_2_ = bf16[1,512,512]{2,1,0:T(8,128)(2,1)S(1)} collective-permute-done((bf16[1,512,512]{2,1,0:T(8,128)(2,1)S(1)}, bf16[1,512,512]{2,1,0:T(8,128)(2,1)S(1)}, u32[]{:S(2)}, u32[]{:S(2)}) %collective-permute-start.13) | collective-permute-done | bytes 524320 | tf_op jit(solution)/shard_map/ppermute | solution.py:279
  77.1 2.1 %shard_map.89 = (bf16[528,128]{1,0:T(8,128)(2,1)S(1)}, bf16[528,128]{1,0:T(8,128)(2,1)S(1)}, bf16[528,128]{1,0:T(8,128)(2,1)S(1)}, bf16[528,128]{1,0:T(8,128)(2,1)S(1)}) custom-call(s32[9]{0:T(128)S(1)} %pad_add_fusion.1.tab_ref, f32[4,2,256,128]{3,2,1,0:T(8,128)S(1)} %pad_maximum_fusion.2.total_ref, f32[1,8192]{1,0:T(1,128)S(1)} %bitcast.53, ...), custom_call_target="tpu_custom_call" | custom-call | tf_op jit(solution)/shard_map/pallas_call | solution.py:351
  79.3 4.1 %collective-permute-done.16.refs_3_.refs_1_ = bf16[1,512,512]{2,1,0:T(8,128)(2,1)} collective-permute-done((bf16[1,512,512]{2,1,0:T(8,128)(2,1)S(1)}, bf16[1,512,512]{2,1,0:T(8,128)(2,1)}, u32[]{:S(2)}, u32[]{:S(2)}) %collective-permute-start.16) | collective-permute-done | bytes 524320 | tf_op jit(solution)/shard_map/ppermute | solution.py:279
  87.3 4.9 %shard_map.90 = (bf16[320,512]{1,0:T(8,128)(2,1)}, f32[320,1]{1,0:T(8,128)S(1)}) custom-call(s32[8]{0:T(128)S(1)} %stack.156.tab_ref, bf16[320,8192]{1,0:T(8,128)(2,1)} %tok_ref.11, f32[320,1]{1,0:T(8,128)S(1)} %get-tuple-element.52.inv_ref, f32[1,8192]{1,0:T(1,128)S(1)} %bitcast.54, bf16[320,512]{1,0:T(8,128)(2,1)S(1)} %copy-done, ...), custom_call_target="tpu_custom_call" | custom-call | flops 1342177280 | bytes 9437184 | tf_op jit(solution)/shard_map/pallas_call | solution.py:238
  95.4 4.8 %shard_map.92.refs_3_ = bf16[320,8192]{1,0:T(8,128)(2,1)} custom-call(s32[6]{0:T(128)S(1)} %stack.179.tab_ref, bf16[320,8192]{1,0:T(8,128)(2,1)} %tok_ref.11, f32[320,1]{1,0:T(8,128)S(1)} %get-tuple-element.52.inv_ref, f32[1,8192]{1,0:T(1,128)S(1)} %bitcast.55, bf16[320,512]{1,0:T(8,128)(2,1)S(1)} %copy-done, f32[320,1]{1,0:T(8,128)S(1)} %get-tuple-element.85.moment_ref, ...), custom_call_target="tpu_custom_call" | custom-call | flops 1342177280 | bytes 9437184 | tf_op jit(solution)/shard_map/pallas_call | solution.py:255
  100.3 3.1 %collective-permute-start.22 = (bf16[528,128]{1,0:T(8,128)(2,1)S(1)}, bf16[528,128]{1,0:T(8,128)(2,1)S(1)}, u32[]{:S(2)}, u32[]{:S(2)}) collective-permute-start(bf16[528,128]{1,0:T(8,128)(2,1)S(1)} %shard_map.93.refs_0_), channel_id=1, source_target_pairs={{0,48},{1,17},{16,32},{17,1},{32,16},{33,49},{48,0},{49,33},{2,50}... | collective-permute-start | bytes 405512 | tf_op jit(solution)/shard_map/ppermute | solution.py:279
  103.5 4.4 %shard_map.94.refs_4_ = bf16[320,8192]{1,0:T(8,128)(2,1)} custom-call(s32[5]{0:T(128)S(1)} %stack.180.tab_ref, bf16[320,8192]{1,0:T(8,128)(2,1)} %tok_ref.11, f32[320,1]{1,0:T(8,128)S(1)} %get-tuple-element.52.inv_ref, f32[1,8192]{1,0:T(1,128)S(1)} %bitcast.56, bf16[320,512]{1,0:T(8,128)(2,1)S(1)} %copy-done, ...), custom_call_target="tpu_custom_call", output_to_operand_aliasing={{}: (9, {})} | custom-call | flops 1342177280 | bytes 9437184 | tf_op jit(solution)/shard_map/pallas_call | solution.py:255
  109.3 2.0 %collective-permute-start.23 = (bf16[528,128]{1,0:T(8,128)(2,1)S(1)}, bf16[528,128]{1,0:T(8,128)(2,1)S(1)}, u32[]{:S(2)}, u32[]{:S(2)}) collective-permute-start(bf16[528,128]{1,0:T(8,128)(2,1)S(1)} %shard_map.95.refs_0_), channel_id=1, source_target_pairs={{0,64},{1,193},{64,0},{65,129},{128,192},{129,65},{192,128},{193,1... | collective-permute-start | bytes 405512 | tf_op jit(solution)/shard_map/ppermute | solution.py:279
  111.5 4.4 %shard_map.96 = bf16[320,8192]{1,0:T(8,128)(2,1)} custom-call(s32[5]{0:T(128)S(1)} %stack.181.tab_ref, bf16[320,8192]{1,0:T(8,128)(2,1)} %tok_ref.11, f32[320,1]{1,0:T(8,128)S(1)} %get-tuple-element.52.inv_ref, f32[1,8192]{1,0:T(1,128)S(1)} %bitcast.57, bf16[320,512]{1,0:T(8,128)(2,1)S(1)} %copy-done, ...), custom_call_target="tpu_custom_call", output_to_operand_aliasing={{}: (10, {})} | custom-call | flops 1342177280 | bytes 9437184 | tf_op jit(solution)/shard_map/pallas_call | solution.py:255
  117.4 1.7 %shard_map.97 = (f32[512,512]{1,0:T(8,128)}, f32[4,8,128]{2,1,0:T(8,128)S(1)}) custom-call(s32[4]{0:T(128)S(1)} %pad_add_fusion.2.tab_ref, bf16[528,128]{1,0:T(8,128)(2,1)S(1)} %shard_map.95.refs_0_, bf16[528,128]{1,0:T(8,128)(2,1)S(1)} %collective-permute-done.23.refs_1_, bf16[528,128]{1,0:T(8,128)(2,1)S(1)} %collective-permute-done.24.refs_2_, ...), custom_call_target="tpu_custom_call" | custom-call | tf_op jit(solution)/shard_map/pallas_call | solution.py:400
  (94 shorter events, 33.8 us)
Async XLA Ops:
  7.5 10.8 %collective-permute-start.1 = (bf16[320,4096]{1,0:T(8,128)(2,1)}, bf16[320,4096]{1,0:T(8,128)(2,1)}, u32[]{:S(2)}, u32[]{:S(2)}) collective-permute-start(bf16[320,4096]{1,0:T(8,128)(2,1)} %get-tuple-element.55), channel_id=1, source_target_pairs={{0,1},{1,0},{2,3},{3,2},{4,5},{5,4},{6,7},{7,6},{8,9},{9,8},{10,11... | collective-permute-start | bytes 7864328 | tf_op jit(solution)/shard_map/ppermute | solution.py:272
  12.0 10.7 %collective-permute-start = (bf16[512,512]{1,0:T(8,128)(2,1)}, bf16[512,512]{1,0:T(8,128)(2,1)}, u32[]{:S(2)}, u32[]{:S(2)}) collective-permute-start(bf16[512,512]{1,0:T(8,128)(2,1)} %shard_map.85), channel_id=1, source_target_pairs={{0,8},{1,57},{8,0},{9,17},{16,24},{17,9},{24,16},{25,33},{32,40},{... | collective-permute-start | bytes 1572872 | tf_op jit(solution)/shard_map/ppermute | solution.py:293
  15.9 9.6 %collective-permute-start.5 = (bf16[512,512]{1,0:T(8,128)(2,1)}, bf16[512,512]{1,0:T(8,128)(2,1)}, u32[]{:S(2)}, u32[]{:S(2)}) collective-permute-start(bf16[512,512]{1,0:T(8,128)(2,1)} %shard_map.85), channel_id=1, source_target_pairs={{0,1},{1,0},{2,3},{3,2},{4,5},{5,4},{6,7},{7,6},{8,9},{9,8},{10,11... | collective-permute-start | bytes 1572872 | tf_op jit(solution)/shard_map/ppermute | solution.py:272
  22.7 14.9 %collective-permute-start.7 = (bf16[16,256,128]{2,1,0:T(8,128)(2,1)S(1)}, bf16[16,256,128]{2,1,0:T(8,128)(2,1)S(1)}, u32[]{:S(2)}, u32[]{:S(2)}) collective-permute-start(bf16[16,256,128]{2,1,0:T(8,128)(2,1)S(1)} %get-tuple-element.63), channel_id=1, source_target_pairs={{0,64},{1,193},{64,0},{65,129},{128,192},{129,65},{192,128},{193,1... | collective-permute-start | bytes 3145736 | tf_op jit(solution)/shard_map/ppermute | solution.py:279
  26.8 15.1 %collective-permute-start.8 = (bf16[2,512,512]{2,1,0:T(8,128)(2,1)S(1)}, bf16[2,512,512]{2,1,0:T(8,128)(2,1)}, u32[]{:S(2)}, u32[]{:S(2)}) collective-permute-start(bf16[2,512,512]{2,1,0:T(8,128)(2,1)S(1)} %pad_maximum_fusion.refs_0_.base_ref), channel_id=1, source_target_pairs={{0,2},{1,7},{2,0},{3,5},{4,6},{5,3},{6,4},{7,1},{8,10},{9,15},{10,... | collective-permute-start | bytes 3145736 | tf_op jit(solution)/shard_map/ppermute | solution.py:279
  33.4 15.7 %collective-permute-start.3 = (bf16[16,256,128]{2,1,0:T(8,128)(2,1)S(1)}, bf16[16,256,128]{2,1,0:T(8,128)(2,1)S(1)}, u32[]{:S(2)}, u32[]{:S(2)}) collective-permute-start(bf16[16,256,128]{2,1,0:T(8,128)(2,1)S(1)} %get-tuple-element.60), channel_id=1, source_target_pairs={{0,8},{1,57},{8,0},{9,17},{16,24},{17,9},{24,16},{25,33},{32,40},{... | collective-permute-start | bytes 3145736 | tf_op jit(solution)/shard_map/ppermute | solution.py:293
  36.2 5.7 %collective-permute-start.6 = (bf16[512,512]{1,0:T(8,128)(2,1)}, bf16[512,512]{1,0:T(8,128)(2,1)S(1)}, u32[]{:S(2)}, u32[]{:S(2)}) collective-permute-start(bf16[512,512]{1,0:T(8,128)(2,1)} %collective-permute-done), channel_id=1, source_target_pairs={{0,1},{1,0},{2,3},{3,2},{4,5},{5,4},{6,7},{7,6},{8,9},{9,8},{10,11... | collective-permute-start | bytes 1572872 | tf_op jit(solution)/shard_map/ppermute | solution.py:272
  41.8 15.0 %collective-permute-start.9 = (bf16[2,512,512]{2,1,0:T(8,128)(2,1)}, bf16[2,512,512]{2,1,0:T(8,128)(2,1)S(1)}, u32[]{:S(2)}, u32[]{:S(2)}) collective-permute-start(bf16[2,512,512]{2,1,0:T(8,128)(2,1)} %collective-permute-done.8.refs_2_.near_ref), channel_id=1, source_target_pairs={{0,1},{1,0},{2,3},{3,2},{4,5},{5,4},{6,7},{7,6},{8,9},{9,8},{10,11... | collective-permute-start | bytes 3145736 | tf_op jit(solution)/shard_map/ppermute | solution.py:272
  44.0 17.9 %collective-permute-start.10 = (bf16[2,512,512]{2,1,0:T(8,128)(2,1)}, bf16[2,512,512]{2,1,0:T(8,128)(2,1)}, u32[]{:S(2)}, u32[]{:S(2)}) collective-permute-start(bf16[2,512,512]{2,1,0:T(8,128)(2,1)} %pad_maximum_fusion.1.refs_1_), channel_id=1, source_target_pairs={{0,2},{1,7},{2,0},{3,5},{4,6},{5,3},{6,4},{7,1},{8,10},{9,15},{10,... | collective-permute-start | bytes 3145736 | tf_op jit(solution)/shard_map/ppermute | solution.py:279
  46.4 9.3 %collective-permute-start.11 = (bf16[8,256,128]{2,1,0:T(8,128)(2,1)S(1)}, bf16[8,256,128]{2,1,0:T(8,128)(2,1)}, u32[]{:S(2)}, u32[]{:S(2)}) collective-permute-start(bf16[8,256,128]{2,1,0:T(8,128)(2,1)S(1)} %get-tuple-element.66), channel_id=1, source_target_pairs={{0,8},{1,57},{8,0},{9,17},{16,24},{17,9},{24,16},{25,33},{32,40},{... | collective-permute-start | bytes 1572872 | tf_op jit(solution)/shard_map/ppermute | solution.py:293
  50.5 11.4 %collective-permute-start.4 = (bf16[8,256,128]{2,1,0:T(8,128)(2,1)}, bf16[8,256,128]{2,1,0:T(8,128)(2,1)}, u32[]{:S(2)}, u32[]{:S(2)}) collective-permute-start(bf16[8,256,128]{2,1,0:T(8,128)(2,1)} %get-tuple-element.105), channel_id=1, source_target_pairs={{0,64},{1,193},{64,0},{65,129},{128,192},{129,65},{192,128},{193,1... | collective-permute-start | bytes 1572872 | tf_op jit(solution)/shard_map/ppermute | solution.py:279
  63.0 11.0 %collective-permute-start.15 = (bf16[2,512,512]{2,1,0:T(8,128)(2,1)}, bf16[2,512,512]{2,1,0:T(8,128)(2,1)S(1)}, u32[]{:S(2)}, u32[]{:S(2)}) collective-permute-start(bf16[2,512,512]{2,1,0:T(8,128)(2,1)} %collective-permute-done.10.refs_0_.refs_1_), channel_id=1, source_target_pairs={{0,1},{1,0},{2,3},{3,2},{4,5},{5,4},{6,7},{7,6},{8,9},{9,8},{10,11... | collective-permute-start | bytes 3145736 | tf_op jit(solution)/shard_map/ppermute | solution.py:272
  64.1 9.6 %collective-permute-start.13 = (bf16[1,512,512]{2,1,0:T(8,128)(2,1)S(1)}, bf16[1,512,512]{2,1,0:T(8,128)(2,1)S(1)}, u32[]{:S(2)}, u32[]{:S(2)}) collective-permute-start(bf16[1,512,512]{2,1,0:T(8,128)(2,1)S(1)} %slice.87), channel_id=1, source_target_pairs={{0,2},{1,7},{2,0},{3,5},{4,6},{5,3},{6,4},{7,1},{8,10},{9,15},{10,... | collective-permute-start | bytes 1572872 | tf_op jit(solution)/shard_map/ppermute | solution.py:279
  64.7 9.8 %collective-permute-start.12 = (bf16[2,4,256,128]{3,2,1,0:T(8,128)(2,1)S(1)}, bf16[2,4,256,128]{3,2,1,0:T(8,128)(2,1)S(1)}, u32[]{:S(2)}, u32[]{:S(2)}) collective-permute-start(bf16[2,4,256,128]{3,2,1,0:T(8,128)(2,1)S(1)} %pad_maximum_fusion.3), channel_id=1, source_target_pairs={{0,192},{1,65},{64,128},{65,1},{128,64},{129,193},{192,0},{193,129... | collective-permute-start | bytes 1572872 | tf_op jit(solution)/shard_map/ppermute | solution.py:279
  74.0 9.4 %collective-permute-start.16 = (bf16[1,512,512]{2,1,0:T(8,128)(2,1)S(1)}, bf16[1,512,512]{2,1,0:T(8,128)(2,1)}, u32[]{:S(2)}, u32[]{:S(2)}) collective-permute-start(bf16[1,512,512]{2,1,0:T(8,128)(2,1)S(1)} %slice.91), channel_id=1, source_target_pairs={{0,2},{1,7},{2,0},{3,5},{4,6},{5,3},{6,4},{7,1},{8,10},{9,15},{10,... | collective-permute-start | bytes 1572872 | tf_op jit(solution)/shard_map/ppermute | solution.py:279
  83.7 8.5 %collective-permute-start.20 = (bf16[528,128]{1,0:T(8,128)(2,1)S(1)}, bf16[528,128]{1,0:T(8,128)(2,1)S(1)}, u32[]{:S(2)}, u32[]{:S(2)}) collective-permute-start(bf16[528,128]{1,0:T(8,128)(2,1)S(1)} %get-tuple-element.80), channel_id=1, source_target_pairs={{0,4},{2,6},{4,0},{6,2},{1,5},{3,7},{5,1},{7,3},{8,12},{10,14},{12... | collective-permute-start | bytes 405512 | tf_op jit(solution)/shard_map/ppermute | solution.py:284
  84.8 8.9 %collective-permute-start.18 = (bf16[528,128]{1,0:T(8,128)(2,1)S(1)}, bf16[528,128]{1,0:T(8,128)(2,1)S(1)}, u32[]{:S(2)}, u32[]{:S(2)}) collective-permute-start(bf16[528,128]{1,0:T(8,128)(2,1)S(1)} %get-tuple-element.78), channel_id=1, source_target_pairs={{0,2},{1,7},{2,0},{3,5},{4,6},{5,3},{6,4},{7,1},{8,10},{9,15},{10,... | collective-permute-start | bytes 405512 | tf_op jit(solution)/shard_map/ppermute | solution.py:279
  85.8 7.8 %collective-permute-start.19 = (bf16[528,128]{1,0:T(8,128)(2,1)S(1)}, bf16[528,128]{1,0:T(8,128)(2,1)S(1)}, u32[]{:S(2)}, u32[]{:S(2)}) collective-permute-start(bf16[528,128]{1,0:T(8,128)(2,1)S(1)} %get-tuple-element.79), channel_id=1, source_target_pairs={{0,6},{1,3},{2,4},{3,1},{4,2},{5,7},{6,0},{7,5},{8,14},{9,11},{10,... | collective-permute-start | bytes 405512 | tf_op jit(solution)/shard_map/ppermute | solution.py:279
  93.7 6.6 %collective-permute-start.21 = (bf16[528,128]{1,0:T(8,128)(2,1)S(1)}, bf16[528,128]{1,0:T(8,128)(2,1)S(1)}, u32[]{:S(2)}, u32[]{:S(2)}) collective-permute-start(bf16[528,128]{1,0:T(8,128)(2,1)S(1)} %shard_map.91.refs_0_), channel_id=1, source_target_pairs={{0,16},{1,49},{16,0},{17,33},{32,48},{33,17},{48,32},{49,1},{2,18}... | collective-permute-start | bytes 405512 | tf_op jit(solution)/shard_map/ppermute | solution.py:279
  100.3 7.6 %collective-permute-start.22 = (bf16[528,128]{1,0:T(8,128)(2,1)S(1)}, bf16[528,128]{1,0:T(8,128)(2,1)S(1)}, u32[]{:S(2)}, u32[]{:S(2)}) collective-permute-start(bf16[528,128]{1,0:T(8,128)(2,1)S(1)} %shard_map.93.refs_0_), channel_id=1, source_target_pairs={{0,48},{1,17},{16,32},{17,1},{32,16},{33,49},{48,0},{49,33},{2,50}... | collective-permute-start | bytes 405512 | tf_op jit(solution)/shard_map/ppermute | solution.py:279
  108.0 8.0 %collective-permute-start.25 = (bf16[528,128]{1,0:T(8,128)(2,1)S(1)}, bf16[528,128]{1,0:T(8,128)(2,1)S(1)}, u32[]{:S(2)}, u32[]{:S(2)}) collective-permute-start(bf16[528,128]{1,0:T(8,128)(2,1)S(1)} %shard_map.95.refs_0_), channel_id=1, source_target_pairs={{0,128},{64,192},{128,0},{192,64},{1,129},{65,193},{129,1},{193,65... | collective-permute-start | bytes 405512 | tf_op jit(solution)/shard_map/ppermute | solution.py:284
  109.2 6.8 %collective-permute-start.24 = (bf16[528,128]{1,0:T(8,128)(2,1)S(1)}, bf16[528,128]{1,0:T(8,128)(2,1)S(1)}, u32[]{:S(2)}, u32[]{:S(2)}) collective-permute-start(bf16[528,128]{1,0:T(8,128)(2,1)S(1)} %shard_map.95.refs_0_), channel_id=1, source_target_pairs={{0,192},{1,65},{64,128},{65,1},{128,64},{129,193},{192,0},{193,129... | collective-permute-start | bytes 405512 | tf_op jit(solution)/shard_map/ppermute | solution.py:279
  109.3 8.1 %collective-permute-start.23 = (bf16[528,128]{1,0:T(8,128)(2,1)S(1)}, bf16[528,128]{1,0:T(8,128)(2,1)S(1)}, u32[]{:S(2)}, u32[]{:S(2)}) collective-permute-start(bf16[528,128]{1,0:T(8,128)(2,1)S(1)} %shard_map.95.refs_0_), channel_id=1, source_target_pairs={{0,64},{1,193},{64,0},{65,129},{128,192},{129,65},{192,128},{193,1... | collective-permute-start | bytes 405512 | tf_op jit(solution)/shard_map/ppermute | solution.py:279
  119.1 3.2 %collective-permute-start.28 = (f32[4,8,128]{2,1,0:T(8,128)S(1)}, f32[4,8,128]{2,1,0:T(8,128)S(1)}, u32[]{:S(2)}, u32[]{:S(2)}) collective-permute-start(f32[4,8,128]{2,1,0:T(8,128)S(1)} %get-tuple-element.99.refs_0_), channel_id=1, source_target_pairs={{0,9},{1,8},{8,1},{9,0},{2,11},{3,10},{10,3},{11,2},{4,13},{5,12},... | collective-permute-start | bytes 49160 | tf_op jit(solution)/shard_map/ppermute | solution.py:272
  (16 other events, 75.1 us)

commit v11 on v9

--- a/solution.py
+++ b/solution.py
@@ -457,7 +457,7 @@
     cot_own = key_cotangent.T
     base = jnp.stack([own, own_c])
     cot_got = swap(cot_own, "c")
-    mine, other, inverse = norm_tiles(tokens, gain, tie(jnp.stack(tables), base, cot_own))
+    mine, other, inverse = norm_tiles(tokens, gain, tie(jnp.stack(tables), own))
     got = swap(other, "c")
     near = pair(base, "x", 0)
 
@@ -466,6 +466,7 @@
     second, kept_second = grad_tiles(mine, got, cot_own, cot_got, 1)
     moved = [pair(first, "y", 0), pair_z(second)]
     above = jnp.stack([up, swap(up, "c")])
+    moved[0], above = lax.optimization_barrier((moved[0], above))
     above_near = pair(above, "x", 0)
     (first, kept_first), (second, kept_second) = map(
         add_halves, (kept_first, kept_second), moved

time: 120 us -> 123 us (1.025)
  waiting for transfers between devices: 25.5 us -> 18.8 us
  Pallas kernels: 37.5 us -> 43.2 us
  other arithmetic: 8.05 us -> 10.1 us
  starting transfers between devices: 42.4 us -> 44.2 us
    ppermute x13, waiting for transfers between devices: 15.9 us -> 10.1 us  [pair(): return lax.ppermute(array, (axis, 'c'), moves)]
    pallas_call x2, Pallas kernels: 4.71 us -> 8.12 us  [grad_tiles(): pl.pallas_call(functools.partial(grad_kernel, side=side), out_shape=[jax....]
    ppermute x3, waiting for transfers between devices: 5.37 us -> 3.25 us  [pair_z(): return lax.ppermute(array, ('zh', 'zl', 'c'), moves)]
    pallas_call x1, Pallas kernels: 4.56 us -> 6.04 us  [norm_tiles(): pl.pallas_call(norm_kernel, in_specs=[SMEM, HBM, VMEM], out_specs=[VMEM]...]
    unnamed x29 -> x31, local copies, waits for them, and re-layouts: 3.75 us -> 3.53 us
  transfers between devices with their start and end apart: 29 -> 29, of which waited for: 14 -> 14; matrix products, arithmetic and copies ran while one was open for 8% -> 8% of each run, Pallas kernels for 25% -> 27%
where the time goes in v11:
time: 123 us; the launch traced here: 122 us
  starting transfers between devices  44.2 us (36%)
  Pallas kernels  43.2 us (35%)
  waiting for transfers between devices  18.8 us (15%)
  other arithmetic  10.1 us (8%)
  local copies, waits for them, and re-layouts  4.89 us (4%)
    ppermute x13, starting transfers between devices, pair(): return lax.ppermute(array, (axis, 'c'), moves)  21.4 us
    pallas_call x3, Pallas kernels, backward(): pl.pallas_call(functools.partial(backward_kernel, count=len(weights)), in...  13.7 us
    ppermute x11, starting transfers between devices, swap(): return lax.ppermute(array, axis, [(a, last - a) for a in range(last + 1)])  10.8 us
    ppermute x13, waiting for transfers between devices, pair(): return lax.ppermute(array, (axis, 'c'), moves)  10.1 us
    ppermute x3, starting transfers between devices, pair_z(): return lax.ppermute(array, ('zh', 'zl', 'c'), moves)  9.82 us
    pallas_call x2, Pallas kernels, grad_tiles(): pl.pallas_call(functools.partial(grad_kernel, side=side), out_shape=[jax....  8.12 us
    pallas_call x1, Pallas kernels, norm_tiles(): pl.pallas_call(norm_kernel, in_specs=[SMEM, HBM, VMEM], out_specs=[VMEM]...  6.04 us
    ppermute x11, waiting for transfers between devices, swap(): return lax.ppermute(array, axis, [(a, last - a) for a in range(last + 1)])  5.48 us
  transfers between devices with their start and end apart: 29, of which 14 were waited for; matrix products, arithmetic and copies ran while one was open for 8% of the time, Pallas kernels for 27%

profile of v11, /device:TPU:1, one launch (start us, length us, event | category | flops | bytes accessed | tf_op | source)
XLA Modules:
  0.0 122.1 jit_solution(1274805600555405993)
XLA Ops:
  4.4 6.0 %shard_map.85 = (bf16[320,4096]{1,0:T(8,128)(2,1)S(1)}, bf16[320,4096]{1,0:T(8,128)(2,1)}, f32[320,1]{1,0:T(8,128)S(1)}) custom-call(s32[2,32]{1,0:T(2,128)S(1)} %pad_add_fusion.tab_ref, bf16[320,8192]{1,0:T(8,128)(2,1)} %tok_ref.11, f32[1,8192]{1,0:T(1,128)S(1)} %bitcast.51), custom_call_target="tpu_custom_call" | custom-call | flops 1 | bytes 1 | tf_op jit(solution)/shard_map/pallas_call | solution.py:70
  10.4 3.3 %collective-permute-start.1 = (bf16[320,4096]{1,0:T(8,128)(2,1)}, bf16[320,4096]{1,0:T(8,128)(2,1)}, u32[]{:S(2)}, u32[]{:S(2)}) collective-permute-start(bf16[320,4096]{1,0:T(8,128)(2,1)} %get-tuple-element.58), channel_id=1, source_target_pairs={{0,1},{1,0},{2,3},{3,2},{4,5},{5,4},{6,7},{7,6},{8,9},{9,8},{10,11... | collective-permute-start | bytes 7864328 | tf_op jit(solution)/shard_map/ppermute | solution.py:272
  13.7 3.8 %collective-permute-start = (bf16[512,512]{1,0:T(8,128)(2,1)}, bf16[512,512]{1,0:T(8,128)(2,1)}, u32[]{:S(2)}, u32[]{:S(2)}) collective-permute-start(bf16[512,512]{1,0:T(8,128)(2,1)} %shard_map.84), channel_id=1, source_target_pairs={{0,8},{1,57},{8,0},{9,17},{16,24},{17,9},{24,16},{25,33},{32,40},{... | collective-permute-start | bytes 1572872 | tf_op jit(solution)/shard_map/ppermute | solution.py:293
  20.1 4.1 %shard_map.86 = (bf16[16,256,128]{2,1,0:T(8,128)(2,1)S(1)}, f32[16,256,128]{2,1,0:T(8,128)S(1)}) custom-call(bf16[320,4096]{1,0:T(8,128)(2,1)S(1)} %get-tuple-element.60.own_ref, bf16[320,4096]{1,0:T(8,128)(2,1)} %collective-permute-done.1.got_ref, bf16[512,320]{1,0:T(8,128)(2,1)S(1)} %bitcast.49, bf16[512,320]{1,0:T(8,128)(2,1)S(1)} %collective-permute-done.2.cot_got_ref), custom_call_target="tpu_custom_call" | custom-call | flops 1 | bytes 1 | tf_op jit(solution)/shard_map/pallas_call | solution.py:112
  24.5 2.7 %collective-permute-start.6 = (bf16[16,256,128]{2,1,0:T(8,128)(2,1)S(1)}, bf16[16,256,128]{2,1,0:T(8,128)(2,1)S(1)}, u32[]{:S(2)}, u32[]{:S(2)}) collective-permute-start(bf16[16,256,128]{2,1,0:T(8,128)(2,1)S(1)} %get-tuple-element.63), channel_id=1, source_target_pairs={{0,64},{1,193},{64,0},{65,129},{128,192},{129,65},{192,128},{193,1... | collective-permute-start | bytes 3145736 | tf_op jit(solution)/shard_map/ppermute | solution.py:279
  28.5 2.6 %collective-permute-start.8 = (bf16[2,512,512]{2,1,0:T(8,128)(2,1)S(1)}, bf16[2,512,512]{2,1,0:T(8,128)(2,1)S(1)}, u32[]{:S(2)}, u32[]{:S(2)}) collective-permute-start(bf16[2,512,512]{2,1,0:T(8,128)(2,1)S(1)} %pad_maximum_fusion.refs_0_.base_ref), channel_id=1, source_target_pairs={{0,2},{1,7},{2,0},{3,5},{4,6},{5,3},{6,4},{7,1},{8,10},{9,15},{10,... | collective-permute-start | bytes 3145736 | tf_op jit(solution)/shard_map/ppermute | solution.py:279
  31.1 4.1 %shard_map.87 = (bf16[16,256,128]{2,1,0:T(8,128)(2,1)S(1)}, f32[16,256,128]{2,1,0:T(8,128)S(1)}) custom-call(bf16[320,4096]{1,0:T(8,128)(2,1)S(1)} %get-tuple-element.60.own_ref, bf16[320,4096]{1,0:T(8,128)(2,1)} %collective-permute-done.1.got_ref, bf16[512,320]{1,0:T(8,128)(2,1)S(1)} %bitcast.50, bf16[512,320]{1,0:T(8,128)(2,1)S(1)} %collective-permute-done.2.cot_got_ref), custom_call_target="tpu_custom_call" | custom-call | flops 1 | bytes 1 | tf_op jit(solution)/shard_map/pallas_call | solution.py:112
  35.2 3.0 %collective-permute-start.3 = (bf16[16,256,128]{2,1,0:T(8,128)(2,1)S(1)}, bf16[16,256,128]{2,1,0:T(8,128)(2,1)S(1)}, u32[]{:S(2)}, u32[]{:S(2)}) collective-permute-start(bf16[16,256,128]{2,1,0:T(8,128)(2,1)S(1)} %get-tuple-element.62), channel_id=1, source_target_pairs={{0,8},{1,57},{8,0},{9,17},{16,24},{17,9},{24,16},{25,33},{32,40},{... | collective-permute-start | bytes 3145736 | tf_op jit(solution)/shard_map/ppermute | solution.py:293
  38.2 2.1 %pad_maximum_fusion.1.refs_1_ = bf16[2,512,512]{2,1,0:T(8,128)(2,1)} fusion(bf16[1,512,512]{2,1,0:T(8,128)(2,1)S(1)} %bitcast.59, bf16[1,512,512]{2,1,0:T(8,128)(2,1)} %bitcast.21), kind=kLoop, calls=%fused_computation.1 | loop fusion | flops 524288 | bytes 2097152 | tf_op jit(solution)/shard_map/stack | solution.py:468
  43.5 2.5 %collective-permute-start.10 = (bf16[2,512,512]{2,1,0:T(8,128)(2,1)}, bf16[2,512,512]{2,1,0:T(8,128)(2,1)}, u32[]{:S(2)}, u32[]{:S(2)}) collective-permute-start(bf16[2,512,512]{2,1,0:T(8,128)(2,1)} %pad_maximum_fusion.1.refs_1_), channel_id=1, source_target_pairs={{0,2},{1,7},{2,0},{3,5},{4,6},{5,3},{6,4},{7,1},{8,10},{9,15},{10,... | collective-permute-start | bytes 3145736 | tf_op jit(solution)/shard_map/ppermute | solution.py:279
  45.9 2.9 %collective-permute-start.12 = (bf16[8,256,128]{2,1,0:T(8,128)(2,1)S(1)}, bf16[8,256,128]{2,1,0:T(8,128)(2,1)}, u32[]{:S(2)}, u32[]{:S(2)}) collective-permute-start(bf16[8,256,128]{2,1,0:T(8,128)(2,1)S(1)} %get-tuple-element.70), channel_id=1, source_target_pairs={{0,8},{1,57},{8,0},{9,17},{16,24},{17,9},{24,16},{25,33},{32,40},{... | collective-permute-start | bytes 1572872 | tf_op jit(solution)/shard_map/ppermute | solution.py:293
  57.3 4.0 %shard_map.88.acc_in = f32[320,512]{1,0:T(8,128)S(1)} custom-call(s32[8]{0:T(128)S(1)} %stack.166.tab_ref, bf16[320,8192]{1,0:T(8,128)(2,1)} %tok_ref.11, f32[320,1]{1,0:T(8,128)S(1)} %get-tuple-element.56.inv_ref, f32[1,8192]{1,0:T(1,128)S(1)} %bitcast.52, bf16[2,512,512]{2,1,0:T(8,128)(2,1)} %copy-done.5, bf16[2,512,512]{2,1,0:T(8,128)(2,1)} %pad_maximum_fusion.1.refs_1_, ...), custom_call_target="tpu_custom_call" | custom-call | flops 1342177280 | bytes 9437184 | tf_op jit(solution)/shard_map/pallas_call | solution.py:226
  61.3 2.8 %collective-permute-done.11.far_ref.refs_2_ = bf16[1,512,512]{2,1,0:T(8,128)(2,1)S(1)} collective-permute-done((bf16[1,512,512]{2,1,0:T(8,128)(2,1)}, bf16[1,512,512]{2,1,0:T(8,128)(2,1)S(1)}, u32[]{:S(2)}, u32[]{:S(2)}) %collective-permute-start.11) | collective-permute-done | bytes 524320 | tf_op jit(solution)/shard_map/ppermute | solution.py:279
  68.5 2.6 %collective-permute-start.16 = (bf16[1,512,512]{2,1,0:T(8,128)(2,1)S(1)}, bf16[1,512,512]{2,1,0:T(8,128)(2,1)S(1)}, u32[]{:S(2)}, u32[]{:S(2)}) collective-permute-start(bf16[1,512,512]{2,1,0:T(8,128)(2,1)S(1)} %slice.89), channel_id=1, source_target_pairs={{0,2},{1,7},{2,0},{3,5},{4,6},{5,3},{6,4},{7,1},{8,10},{9,15},{10,... | collective-permute-start | bytes 1572872 | tf_op jit(solution)/shard_map/ppermute | solution.py:279
  71.1 3.1 %collective-permute-done.13 = bf16[2,4,256,128]{3,2,1,0:T(8,128)(2,1)S(1)} collective-permute-done((bf16[2,4,256,128]{3,2,1,0:T(8,128)(2,1)S(1)}, bf16[2,4,256,128]{3,2,1,0:T(8,128)(2,1)S(1)}, u32[]{:S(2)}, u32[]{:S(2)}) %collective-permute-start.13) | collective-permute-done | bytes 524320 | tf_op jit(solution)/shard_map/ppermute | solution.py:279
  75.8 2.1 %shard_map.89 = (bf16[528,128]{1,0:T(8,128)(2,1)S(1)}, bf16[528,128]{1,0:T(8,128)(2,1)S(1)}, bf16[528,128]{1,0:T(8,128)(2,1)S(1)}, bf16[528,128]{1,0:T(8,128)(2,1)S(1)}) custom-call(s32[9]{0:T(128)S(1)} %pad_add_fusion.1.tab_ref, f32[4,2,256,128]{3,2,1,0:T(8,128)S(1)} %pad_maximum_fusion.2.total_ref, f32[1,8192]{1,0:T(1,128)S(1)} %bitcast.53, ...), custom_call_target="tpu_custom_call" | custom-call | tf_op jit(solution)/shard_map/pallas_call | solution.py:351
  77.9 2.3 %collective-permute-start.17 = (bf16[1,512,512]{2,1,0:T(8,128)(2,1)S(1)}, bf16[1,512,512]{2,1,0:T(8,128)(2,1)S(1)}, u32[]{:S(2)}, u32[]{:S(2)}) collective-permute-start(bf16[1,512,512]{2,1,0:T(8,128)(2,1)S(1)} %collective-permute-done.16.refs_3_.refs_1_), channel_id=1, source_target_pairs={{0,1},{1,0},{2,3},{3,2},{4,5},{5,4},{6,7},{7,6},{8,9},{9,8},{10,11... | collective-permute-start | bytes 1572872 | tf_op jit(solution)/shard_map/ppermute | solution.py:272
  84.2 4.9 %shard_map.90 = (bf16[320,512]{1,0:T(8,128)(2,1)}, f32[320,1]{1,0:T(8,128)S(1)}) custom-call(s32[8]{0:T(128)S(1)} %stack.156.tab_ref, bf16[320,8192]{1,0:T(8,128)(2,1)} %tok_ref.11, f32[320,1]{1,0:T(8,128)S(1)} %get-tuple-element.56.inv_ref, f32[1,8192]{1,0:T(1,128)S(1)} %bitcast.54, bf16[320,512]{1,0:T(8,128)(2,1)S(1)} %copy-done, ...), custom_call_target="tpu_custom_call" | custom-call | flops 1342177280 | bytes 9437184 | tf_op jit(solution)/shard_map/pallas_call | solution.py:238
  90.0 3.7 %collective-permute-start.21 = (bf16[528,128]{1,0:T(8,128)(2,1)S(1)}, bf16[528,128]{1,0:T(8,128)(2,1)S(1)}, u32[]{:S(2)}, u32[]{:S(2)}) collective-permute-start(bf16[528,128]{1,0:T(8,128)(2,1)S(1)} %shard_map.91.refs_0_), channel_id=1, source_target_pairs={{0,16},{1,49},{16,0},{17,33},{32,48},{33,17},{48,32},{49,1},{2,18}... | collective-permute-start | bytes 405512 | tf_op jit(solution)/shard_map/ppermute | solution.py:279
  93.7 4.8 %shard_map.92.refs_3_ = bf16[320,8192]{1,0:T(8,128)(2,1)} custom-call(s32[6]{0:T(128)S(1)} %stack.179.tab_ref, bf16[320,8192]{1,0:T(8,128)(2,1)} %tok_ref.11, f32[320,1]{1,0:T(8,128)S(1)} %get-tuple-element.56.inv_ref, f32[1,8192]{1,0:T(1,128)S(1)} %bitcast.55, bf16[320,512]{1,0:T(8,128)(2,1)S(1)} %copy-done, f32[320,1]{1,0:T(8,128)S(1)} %get-tuple-element.91.moment_ref, ...), custom_call_target="tpu_custom_call" | custom-call | flops 1342177280 | bytes 9437184 | tf_op jit(solution)/shard_map/pallas_call | solution.py:255
  100.0 4.4 %shard_map.94.refs_4_ = bf16[320,8192]{1,0:T(8,128)(2,1)} custom-call(s32[5]{0:T(128)S(1)} %stack.180.tab_ref, bf16[320,8192]{1,0:T(8,128)(2,1)} %tok_ref.11, f32[320,1]{1,0:T(8,128)S(1)} %get-tuple-element.56.inv_ref, f32[1,8192]{1,0:T(1,128)S(1)} %bitcast.56, bf16[320,512]{1,0:T(8,128)(2,1)S(1)} %copy-done, ...), custom_call_target="tpu_custom_call", output_to_operand_aliasing={{}: (9, {})} | custom-call | flops 1342177280 | bytes 9437184 | tf_op jit(solution)/shard_map/pallas_call | solution.py:255
  106.3 2.0 %collective-permute-start.23 = (bf16[528,128]{1,0:T(8,128)(2,1)S(1)}, bf16[528,128]{1,0:T(8,128)(2,1)S(1)}, u32[]{:S(2)}, u32[]{:S(2)}) collective-permute-start(bf16[528,128]{1,0:T(8,128)(2,1)S(1)} %shard_map.95.refs_0_), channel_id=1, source_target_pairs={{0,64},{1,193},{64,0},{65,129},{128,192},{129,65},{192,128},{193,1... | collective-permute-start | bytes 405512 | tf_op jit(solution)/shard_map/ppermute | solution.py:279
  108.5 4.4 %shard_map.96 = bf16[320,8192]{1,0:T(8,128)(2,1)} custom-call(s32[5]{0:T(128)S(1)} %stack.181.tab_ref, bf16[320,8192]{1,0:T(8,128)(2,1)} %tok_ref.11, f32[320,1]{1,0:T(8,128)S(1)} %get-tuple-element.56.inv_ref, f32[1,8192]{1,0:T(1,128)S(1)} %bitcast.57, bf16[320,512]{1,0:T(8,128)(2,1)S(1)} %copy-done, ...), custom_call_target="tpu_custom_call", output_to_operand_aliasing={{}: (10, {})} | custom-call | flops 1342177280 | bytes 9437184 | tf_op jit(solution)/shard_map/pallas_call | solution.py:255
  115.5 2.5 %collective-permute-start.28 = (f32[4,8,128]{2,1,0:T(8,128)S(1)}, f32[4,8,128]{2,1,0:T(8,128)S(1)}, u32[]{:S(2)}, u32[]{:S(2)}) collective-permute-start(f32[4,8,128]{2,1,0:T(8,128)S(1)} %get-tuple-element.105.refs_0_), channel_id=1, source_target_pairs={{0,9},{1,8},{8,1},{9,0},{2,11},{3,10},{10,3},{11,2},{4,13},{5,12},... | collective-permute-start | bytes 49160 | tf_op jit(solution)/shard_map/ppermute | solution.py:272
  (102 shorter events, 40.2 us)
Async XLA Ops:
  10.4 9.7 %collective-permute-start.1 = (bf16[320,4096]{1,0:T(8,128)(2,1)}, bf16[320,4096]{1,0:T(8,128)(2,1)}, u32[]{:S(2)}, u32[]{:S(2)}) collective-permute-start(bf16[320,4096]{1,0:T(8,128)(2,1)} %get-tuple-element.58), channel_id=1, source_target_pairs={{0,1},{1,0},{2,3},{3,2},{4,5},{5,4},{6,7},{7,6},{8,9},{9,8},{10,11... | collective-permute-start | bytes 7864328 | tf_op jit(solution)/shard_map/ppermute | solution.py:272
  13.7 10.7 %collective-permute-start = (bf16[512,512]{1,0:T(8,128)(2,1)}, bf16[512,512]{1,0:T(8,128)(2,1)}, u32[]{:S(2)}, u32[]{:S(2)}) collective-permute-start(bf16[512,512]{1,0:T(8,128)(2,1)} %shard_map.84), channel_id=1, source_target_pairs={{0,8},{1,57},{8,0},{9,17},{16,24},{17,9},{24,16},{25,33},{32,40},{... | collective-permute-start | bytes 1572872 | tf_op jit(solution)/shard_map/ppermute | solution.py:293
  17.6 9.6 %collective-permute-start.5 = (bf16[512,512]{1,0:T(8,128)(2,1)}, bf16[512,512]{1,0:T(8,128)(2,1)}, u32[]{:S(2)}, u32[]{:S(2)}) collective-permute-start(bf16[512,512]{1,0:T(8,128)(2,1)} %shard_map.84), channel_id=1, source_target_pairs={{0,1},{1,0},{2,3},{3,2},{4,5},{5,4},{6,7},{7,6},{8,9},{9,8},{10,11... | collective-permute-start | bytes 1572872 | tf_op jit(solution)/shard_map/ppermute | solution.py:272
  24.5 15.8 %collective-permute-start.6 = (bf16[16,256,128]{2,1,0:T(8,128)(2,1)S(1)}, bf16[16,256,128]{2,1,0:T(8,128)(2,1)S(1)}, u32[]{:S(2)}, u32[]{:S(2)}) collective-permute-start(bf16[16,256,128]{2,1,0:T(8,128)(2,1)S(1)} %get-tuple-element.63), channel_id=1, source_target_pairs={{0,64},{1,193},{64,0},{65,129},{128,192},{129,65},{192,128},{193,1... | collective-permute-start | bytes 3145736 | tf_op jit(solution)/shard_map/ppermute | solution.py:279
  28.5 14.9 %collective-permute-start.8 = (bf16[2,512,512]{2,1,0:T(8,128)(2,1)S(1)}, bf16[2,512,512]{2,1,0:T(8,128)(2,1)S(1)}, u32[]{:S(2)}, u32[]{:S(2)}) collective-permute-start(bf16[2,512,512]{2,1,0:T(8,128)(2,1)S(1)} %pad_maximum_fusion.refs_0_.base_ref), channel_id=1, source_target_pairs={{0,2},{1,7},{2,0},{3,5},{4,6},{5,3},{6,4},{7,1},{8,10},{9,15},{10,... | collective-permute-start | bytes 3145736 | tf_op jit(solution)/shard_map/ppermute | solution.py:279
  31.1 7.1 %collective-permute-start.7 = (bf16[512,512]{1,0:T(8,128)(2,1)}, bf16[512,512]{1,0:T(8,128)(2,1)S(1)}, u32[]{:S(2)}, u32[]{:S(2)}) collective-permute-start(bf16[512,512]{1,0:T(8,128)(2,1)} %collective-permute-done), channel_id=1, source_target_pairs={{0,1},{1,0},{2,3},{3,2},{4,5},{5,4},{6,7},{7,6},{8,9},{9,8},{10,11... | collective-permute-start | bytes 1572872 | tf_op jit(solution)/shard_map/ppermute | solution.py:272
  35.2 15.2 %collective-permute-start.3 = (bf16[16,256,128]{2,1,0:T(8,128)(2,1)S(1)}, bf16[16,256,128]{2,1,0:T(8,128)(2,1)S(1)}, u32[]{:S(2)}, u32[]{:S(2)}) collective-permute-start(bf16[16,256,128]{2,1,0:T(8,128)(2,1)S(1)} %get-tuple-element.62), channel_id=1, source_target_pairs={{0,8},{1,57},{8,0},{9,17},{16,24},{17,9},{24,16},{25,33},{32,40},{... | collective-permute-start | bytes 3145736 | tf_op jit(solution)/shard_map/ppermute | solution.py:293
  43.5 8.4 %collective-permute-start.9 = (bf16[2,512,512]{2,1,0:T(8,128)(2,1)S(1)}, bf16[2,512,512]{2,1,0:T(8,128)(2,1)S(1)}, u32[]{:S(2)}, u32[]{:S(2)}) collective-permute-start(bf16[2,512,512]{2,1,0:T(8,128)(2,1)S(1)} %collective-permute-done.8.refs_2_.near_ref), channel_id=1, source_target_pairs={{0,1},{1,0},{2,3},{3,2},{4,5},{5,4},{6,7},{7,6},{8,9},{9,8},{10,11... | collective-permute-start | bytes 3145736 | tf_op jit(solution)/shard_map/ppermute | solution.py:272
  43.5 17.9 %collective-permute-start.10 = (bf16[2,512,512]{2,1,0:T(8,128)(2,1)}, bf16[2,512,512]{2,1,0:T(8,128)(2,1)}, u32[]{:S(2)}, u32[]{:S(2)}) collective-permute-start(bf16[2,512,512]{2,1,0:T(8,128)(2,1)} %pad_maximum_fusion.1.refs_1_), channel_id=1, source_target_pairs={{0,2},{1,7},{2,0},{3,5},{4,6},{5,3},{6,4},{7,1},{8,10},{9,15},{10,... | collective-permute-start | bytes 3145736 | tf_op jit(solution)/shard_map/ppermute | solution.py:279
  45.9 10.2 %collective-permute-start.12 = (bf16[8,256,128]{2,1,0:T(8,128)(2,1)S(1)}, bf16[8,256,128]{2,1,0:T(8,128)(2,1)}, u32[]{:S(2)}, u32[]{:S(2)}) collective-permute-start(bf16[8,256,128]{2,1,0:T(8,128)(2,1)S(1)} %get-tuple-element.70), channel_id=1, source_target_pairs={{0,8},{1,57},{8,0},{9,17},{16,24},{17,9},{24,16},{25,33},{32,40},{... | collective-permute-start | bytes 1572872 | tf_op jit(solution)/shard_map/ppermute | solution.py:293
  51.8 9.6 %collective-permute-start.4 = (bf16[8,256,128]{2,1,0:T(8,128)(2,1)}, bf16[8,256,128]{2,1,0:T(8,128)(2,1)}, u32[]{:S(2)}, u32[]{:S(2)}) collective-permute-start(bf16[8,256,128]{2,1,0:T(8,128)(2,1)} %get-tuple-element.111), channel_id=1, source_target_pairs={{0,64},{1,193},{64,0},{65,129},{128,192},{129,65},{192,128},{193,1... | collective-permute-start | bytes 1572872 | tf_op jit(solution)/shard_map/ppermute | solution.py:279
  52.8 11.4 %collective-permute-start.11 = (bf16[1,512,512]{2,1,0:T(8,128)(2,1)}, bf16[1,512,512]{2,1,0:T(8,128)(2,1)S(1)}, u32[]{:S(2)}, u32[]{:S(2)}) collective-permute-start(bf16[1,512,512]{2,1,0:T(8,128)(2,1)} %slice.81), channel_id=1, source_target_pairs={{0,2},{1,7},{2,0},{3,5},{4,6},{5,3},{6,4},{7,1},{8,10},{9,15},{10,... | collective-permute-start | bytes 1572872 | tf_op jit(solution)/shard_map/ppermute | solution.py:279
  65.9 8.3 %collective-permute-start.13 = (bf16[2,4,256,128]{3,2,1,0:T(8,128)(2,1)S(1)}, bf16[2,4,256,128]{3,2,1,0:T(8,128)(2,1)S(1)}, u32[]{:S(2)}, u32[]{:S(2)}) collective-permute-start(bf16[2,4,256,128]{3,2,1,0:T(8,128)(2,1)S(1)} %pad_maximum_fusion.3), channel_id=1, source_target_pairs={{0,192},{1,65},{64,128},{65,1},{128,64},{129,193},{192,0},{193,129... | collective-permute-start | bytes 1572872 | tf_op jit(solution)/shard_map/ppermute | solution.py:279
  65.9 8.3 %collective-permute-start.14 = (bf16[1,512,512]{2,1,0:T(8,128)(2,1)S(1)}, bf16[1,512,512]{2,1,0:T(8,128)(2,1)S(1)}, u32[]{:S(2)}, u32[]{:S(2)}) collective-permute-start(bf16[1,512,512]{2,1,0:T(8,128)(2,1)S(1)} %collective-permute-done.11.far_ref.refs_2_), channel_id=1, source_target_pairs={{0,1},{1,0},{2,3},{3,2},{4,5},{5,4},{6,7},{7,6},{8,9},{9,8},{10,11... | collective-permute-start | bytes 1572872 | tf_op jit(solution)/shard_map/ppermute | solution.py:272
  68.5 9.5 %collective-permute-start.16 = (bf16[1,512,512]{2,1,0:T(8,128)(2,1)S(1)}, bf16[1,512,512]{2,1,0:T(8,128)(2,1)S(1)}, u32[]{:S(2)}, u32[]{:S(2)}) collective-permute-start(bf16[1,512,512]{2,1,0:T(8,128)(2,1)S(1)} %slice.89), channel_id=1, source_target_pairs={{0,2},{1,7},{2,0},{3,5},{4,6},{5,3},{6,4},{7,1},{8,10},{9,15},{10,... | collective-permute-start | bytes 1572872 | tf_op jit(solution)/shard_map/ppermute | solution.py:279
  77.9 5.4 %collective-permute-start.17 = (bf16[1,512,512]{2,1,0:T(8,128)(2,1)S(1)}, bf16[1,512,512]{2,1,0:T(8,128)(2,1)S(1)}, u32[]{:S(2)}, u32[]{:S(2)}) collective-permute-start(bf16[1,512,512]{2,1,0:T(8,128)(2,1)S(1)} %collective-permute-done.16.refs_3_.refs_1_), channel_id=1, source_target_pairs={{0,1},{1,0},{2,3},{3,2},{4,5},{5,4},{6,7},{7,6},{8,9},{9,8},{10,11... | collective-permute-start | bytes 1572872 | tf_op jit(solution)/shard_map/ppermute | solution.py:272
  80.2 8.9 %collective-permute-start.20 = (bf16[528,128]{1,0:T(8,128)(2,1)S(1)}, bf16[528,128]{1,0:T(8,128)(2,1)S(1)}, u32[]{:S(2)}, u32[]{:S(2)}) collective-permute-start(bf16[528,128]{1,0:T(8,128)(2,1)S(1)} %get-tuple-element.86), channel_id=1, source_target_pairs={{0,4},{2,6},{4,0},{6,2},{1,5},{3,7},{5,1},{7,3},{8,12},{10,14},{12... | collective-permute-start | bytes 405512 | tf_op jit(solution)/shard_map/ppermute | solution.py:284
  82.1 7.0 %collective-permute-start.18 = (bf16[528,128]{1,0:T(8,128)(2,1)S(1)}, bf16[528,128]{1,0:T(8,128)(2,1)S(1)}, u32[]{:S(2)}, u32[]{:S(2)}) collective-permute-start(bf16[528,128]{1,0:T(8,128)(2,1)S(1)} %get-tuple-element.84), channel_id=1, source_target_pairs={{0,2},{1,7},{2,0},{3,5},{4,6},{5,3},{6,4},{7,1},{8,10},{9,15},{10,... | collective-permute-start | bytes 405512 | tf_op jit(solution)/shard_map/ppermute | solution.py:279
  82.9 7.0 %collective-permute-start.19 = (bf16[528,128]{1,0:T(8,128)(2,1)S(1)}, bf16[528,128]{1,0:T(8,128)(2,1)S(1)}, u32[]{:S(2)}, u32[]{:S(2)}) collective-permute-start(bf16[528,128]{1,0:T(8,128)(2,1)S(1)} %get-tuple-element.85), channel_id=1, source_target_pairs={{0,6},{1,3},{2,4},{3,1},{4,2},{5,7},{6,0},{7,5},{8,14},{9,11},{10,... | collective-permute-start | bytes 405512 | tf_op jit(solution)/shard_map/ppermute | solution.py:279
  90.0 8.6 %collective-permute-start.21 = (bf16[528,128]{1,0:T(8,128)(2,1)S(1)}, bf16[528,128]{1,0:T(8,128)(2,1)S(1)}, u32[]{:S(2)}, u32[]{:S(2)}) collective-permute-start(bf16[528,128]{1,0:T(8,128)(2,1)S(1)} %shard_map.91.refs_0_), channel_id=1, source_target_pairs={{0,16},{1,49},{16,0},{17,33},{32,48},{33,17},{48,32},{49,1},{2,18}... | collective-permute-start | bytes 405512 | tf_op jit(solution)/shard_map/ppermute | solution.py:279
  98.7 6.3 %collective-permute-start.22 = (bf16[528,128]{1,0:T(8,128)(2,1)S(1)}, bf16[528,128]{1,0:T(8,128)(2,1)S(1)}, u32[]{:S(2)}, u32[]{:S(2)}) collective-permute-start(bf16[528,128]{1,0:T(8,128)(2,1)S(1)} %shard_map.93.refs_0_), channel_id=1, source_target_pairs={{0,48},{1,17},{16,32},{17,1},{32,16},{33,49},{48,0},{49,33},{2,50}... | collective-permute-start | bytes 405512 | tf_op jit(solution)/shard_map/ppermute | solution.py:279
  105.0 8.0 %collective-permute-start.25 = (bf16[528,128]{1,0:T(8,128)(2,1)S(1)}, bf16[528,128]{1,0:T(8,128)(2,1)S(1)}, u32[]{:S(2)}, u32[]{:S(2)}) collective-permute-start(bf16[528,128]{1,0:T(8,128)(2,1)S(1)} %shard_map.95.refs_0_), channel_id=1, source_target_pairs={{0,128},{64,192},{128,0},{192,64},{1,129},{65,193},{129,1},{193,65... | collective-permute-start | bytes 405512 | tf_op jit(solution)/shard_map/ppermute | solution.py:284
  105.3 7.7 %collective-permute-start.24 = (bf16[528,128]{1,0:T(8,128)(2,1)S(1)}, bf16[528,128]{1,0:T(8,128)(2,1)S(1)}, u32[]{:S(2)}, u32[]{:S(2)}) collective-permute-start(bf16[528,128]{1,0:T(8,128)(2,1)S(1)} %shard_map.95.refs_0_), channel_id=1, source_target_pairs={{0,192},{1,65},{64,128},{65,1},{128,64},{129,193},{192,0},{193,129... | collective-permute-start | bytes 405512 | tf_op jit(solution)/shard_map/ppermute | solution.py:279
  106.3 7.5 %collective-permute-start.23 = (bf16[528,128]{1,0:T(8,128)(2,1)S(1)}, bf16[528,128]{1,0:T(8,128)(2,1)S(1)}, u32[]{:S(2)}, u32[]{:S(2)}) collective-permute-start(bf16[528,128]{1,0:T(8,128)(2,1)S(1)} %shard_map.95.refs_0_), channel_id=1, source_target_pairs={{0,64},{1,193},{64,0},{65,129},{128,192},{129,65},{192,128},{193,1... | collective-permute-start | bytes 405512 | tf_op jit(solution)/shard_map/ppermute | solution.py:279
  (20 other events, 104.9 us)
